TPU v7x, 32 devices: a whole 2x2x4 slice. The times are simulated.
32 devices in a mesh: group: 4 (over y, core), dp: 4 (over z), tensor: 2 (over x).
Axes of the slice: x: 2, y: 2, z: 4, core: 2. Of those that a mesh axis runs over, the one named last changes fastest.
Arguments:
- patches: bfloat16 [2, 4, 4, 1568, 1536], P(None, 'group', 'dp'), may hold values from -6 to 6
- visible: int32 [2, 4, 4, 160], P(None, 'group', 'dp'), may hold values from 0 to 1567, as said below
- frames_valid: int32 [2, 4, 4], P(None, 'group', 'dp'), may hold values from 1 to 8, as said below
- clip_valid: int32 [2, 4, 4], P(None, 'group', 'dp'), may hold values from 0 to 1, as said below
- rep_weights: float32 [2076672], P('dp'), may hold values from -6 to 6
- ten_weights: float32 [2, 4423680], P('tensor', 'dp'), may hold values from -6 to 6
- rep_m: float32 [4, 2076672], P('group', 'dp'), may hold values from -1 to 1
- rep_v: float32 [4, 2076672], P('group', 'dp'), may hold values from 0 to 1
- ten_m: float32 [4, 2, 4423680], P('group', 'tensor', 'dp'), may hold values from -1 to 1
- ten_v: float32 [4, 2, 4423680], P('group', 'tensor', 'dp'), may hold values from 0 to 1
- rep_outer: float32 [2076672], P('dp'), may hold values from -1 to 1
- ten_outer: float32 [2, 4423680], P('tensor', 'dp'), may hold values from -1 to 1
Outputs:
- loss_sum: float32 [2, 4], P(None, 'group')
- loss_count: float32 [2, 4], P(None, 'group')
- clip_norm: float32 [2, 4], P(None, 'group')
- rep_first: float32 [4, 2076672], P('group', 'dp')
- rep_second: float32 [4, 2076672], P('group', 'dp')
- ten_first: float32 [4, 2, 4423680], P('group', 'tensor', 'dp')
- ten_second: float32 [4, 2, 4423680], P('group', 'tensor', 'dp')
- rep_diff: float32 [2076672], P('dp')
- ten_diff: float32 [2, 4423680], P('tensor', 'dp')
- rep_momentum: float32 [2076672], P('dp')
- ten_momentum: float32 [2, 4423680], P('tensor', 'dp')
- rep_master: float32 [2076672], P('dp')
- ten_master: float32 [2, 4423680], P('tensor', 'dp')
Inputs may be any that keep to these rules, and one draw needn't show every extreme that they name: `visible`: each clip's indices are distinct and ascending. `frames_valid`: the last clip slot of every inner step and group holds all 8 time positions. `clip_valid`: clip slot 0 of every inner step and group is real.
All inputs are finite; a program needn't handle non-finite values.
Results may differ from a plain program's by a relative error of at most 0.0033.
The roundings to bfloat16 on the way count: a program that leaves them out, or rounds other values in their place, can miss the bound.
Values may be sent and summed in bfloat16 or wider, within the bound.
A program may use at most 384 MiB of HBM per device.

v0:
```python
import math

import jax
import jax.numpy as jnp
from jax import lax
from jax.sharding import PartitionSpec as P

D = 768
HDIM = 64
FF = 3072
DD = 384
DFF = 1536
PATCH = 1536
TUBES = 1568
FRAMES = 8
STEPS = 2
STEP_BEFORE = 6


CLIP = 0.001
LR_IN = 0.01
BETA1 = 0.9
BETA2 = 0.95
EPS = 1e-08
DECAY = 0.05
LR_OUT = 0.7
MOMENTUM = 0.9
FLOAT = jnp.float32
HALF = jnp.bfloat16


def sinus(count, width):
    places = jnp.arange(count).astype(jnp.float32)[:, None]
    column = jnp.arange(width)
    decays = jnp.power(10000.0, -2.0 * (column // 2).astype(jnp.float32) / width)
    angles = places * decays[None, :]
    return jnp.where(column % 2 == 0, jnp.sin(angles), jnp.cos(angles))


def layer_norm(stream, gain, bias):
    center = jnp.mean(stream, -1, keepdims=True)
    spread = jnp.mean((stream - center) ** 2, -1, keepdims=True)
    return (stream - center) * lax.rsqrt(spread + 1e-06) * gain + bias


def norm_back(stream, gain, bias, cotangent):
    _, pull = jax.vjp(layer_norm, stream, gain, bias)
    return pull(cotangent)


def gelu_exact(values):
    return jax.nn.gelu(values, approximate=False)


def split_flat(flat, shapes):
    pieces = []
    offset = 0
    for shapes_one in shapes:
        length = math.prod(shapes_one)
        pieces.append(flat[offset : offset + length].reshape(shapes_one))
        offset += length
    return pieces


def own_rows(stream, axis_dim):
    count = stream.shape[axis_dim] // lax.axis_size("tensor")
    return lax.dynamic_slice_in_dim(stream, lax.axis_index("tensor") * count, count, axis_dim)


def rows_sum(partial_rows):
    return lax.psum_scatter(partial_rows, "tensor", scatter_dimension=1, tiled=True)


def rows_full(own_part):
    return lax.all_gather(own_part, "tensor", axis=1, tiled=True)


def block_forward(stream, mats, vecs):
    w_qkv, w_out, w_up, w_down = mats
    gain_one, bias_one, out_bias, gain_two, bias_two, down_bias = vecs
    nclips, length, _ = stream.shape
    head_cols = w_out.shape[0]
    nheads = head_cols // HDIM
    normed = layer_norm(stream, gain_one, bias_one).astype(HALF)
    joined = jnp.dot(normed, w_qkv, preferred_element_type=FLOAT).astype(HALF)
    queries, key_rows, values = [
        joined[:, :, third_id * head_cols : (third_id + 1) * head_cols].reshape(
            nclips, length, nheads, HDIM
        )
        for third_id in range(3)
    ]
    scores = jnp.einsum(
        "cqhd,ckhd->chqk", queries, key_rows, preferred_element_type=FLOAT
    ) * HDIM ** (-0.5)
    highest = jnp.max(scores, -1, keepdims=True)
    totals = jnp.log(jnp.sum(jnp.exp(scores - highest), -1, keepdims=True)) + highest
    probs_low = jnp.exp(scores - totals).astype(HALF)
    blended = (
        jnp.einsum("chqk,ckhd->cqhd", probs_low, values, preferred_element_type=FLOAT)
        .astype(HALF)
        .reshape(nclips, length, head_cols)
    )
    attended = (
        rows_sum(jnp.dot(blended, w_out, preferred_element_type=FLOAT))
        + own_rows(stream, 1)
        + out_bias
    )
    second = layer_norm(attended, gain_two, bias_two).astype(HALF)
    second_all = lax.all_gather(second, "tensor", axis=1, tiled=True)
    upward = jnp.dot(second_all, w_up, preferred_element_type=FLOAT)
    activated = gelu_exact(upward).astype(HALF)
    result = (
        rows_sum(jnp.dot(activated, w_down, preferred_element_type=FLOAT)) + attended + down_bias
    )
    stored = (
        stream,
        normed,
        queries,
        key_rows,
        values,
        totals,
        blended,
        attended,
        second_all,
        upward,
        activated,
    )
    return (rows_full(result), stored)


def block_backward(grad_out, mats, vecs, stored):
    w_qkv, w_out, w_up, w_down = mats
    gain_one, bias_one, out_bias, gain_two, bias_two, down_bias = vecs
    (
        stream,
        normed,
        queries,
        key_rows,
        values,
        totals,
        blended,
        attended,
        second_all,
        upward,
        activated,
    ) = stored
    nclips, length, _ = stream.shape
    head_cols = w_out.shape[0]
    grad_low = grad_out.astype(HALF)
    grad_down = jnp.einsum("ctf,ctd->fd", activated, grad_low, preferred_element_type=FLOAT)
    down_bias_grad = jnp.sum(own_rows(grad_out, 1), (0, 1))
    grad_act = jnp.dot(grad_low, w_down.T, preferred_element_type=FLOAT)
    _, gelu_pull = jax.vjp(gelu_exact, upward)
    grad_up_in = gelu_pull(grad_act)[0].astype(HALF)
    grad_up = jnp.einsum("ctd,ctf->df", second_all, grad_up_in, preferred_element_type=FLOAT)
    grad_second = rows_sum(jnp.dot(grad_up_in, w_up.T, preferred_element_type=FLOAT))
    grad_att, gain_two_grad, bias_two_grad = norm_back(attended, gain_two, bias_two, grad_second)
    grad_att = grad_att + own_rows(grad_out, 1)
    out_bias_grad = jnp.sum(grad_att, (0, 1))
    grad_mid = rows_full(grad_att)
    mid_low = grad_mid.astype(HALF)
    grad_wout = jnp.einsum("cth,ctd->hd", blended, mid_low, preferred_element_type=FLOAT)
    nheads = head_cols // HDIM
    grad_blend = (
        jnp.dot(mid_low, w_out.T, preferred_element_type=FLOAT)
        .astype(HALF)
        .reshape(nclips, length, nheads, HDIM)
    )
    scores = jnp.einsum(
        "cqhd,ckhd->chqk", queries, key_rows, preferred_element_type=FLOAT
    ) * HDIM ** (-0.5)
    probs_full = jnp.exp(scores - totals)
    probs_low = probs_full.astype(HALF)
    grad_values = jnp.einsum("chqk,cqhd->ckhd", probs_low, grad_blend, preferred_element_type=FLOAT)
    grad_probs = jnp.einsum("cqhd,ckhd->chqk", grad_blend, values, preferred_element_type=FLOAT)
    grad_scores = (
        probs_full * (grad_probs - jnp.sum(probs_full * grad_probs, -1, keepdims=True))
    ).astype(HALF)
    grad_queries = jnp.einsum(
        "chqk,ckhd->cqhd", grad_scores, key_rows, preferred_element_type=FLOAT
    ) * HDIM ** (-0.5)
    grad_keys = jnp.einsum(
        "chqk,cqhd->ckhd", grad_scores, queries, preferred_element_type=FLOAT
    ) * HDIM ** (-0.5)
    grad_joined = jnp.concatenate(
        [
            part_grad.reshape(nclips, length, head_cols)
            for part_grad in (grad_queries, grad_keys, grad_values)
        ],
        -1,
    ).astype(HALF)
    grad_qkv = jnp.einsum("ctd,cte->de", normed, grad_joined, preferred_element_type=FLOAT)
    grad_norm_in = rows_sum(jnp.dot(grad_joined, w_qkv.T, preferred_element_type=FLOAT))
    grad_in, gain_one_grad, bias_one_grad = norm_back(
        own_rows(stream, 1), gain_one, bias_one, grad_norm_in
    )
    grad_in = grad_in + grad_att
    vec_grads = jnp.stack(
        [gain_one_grad, bias_one_grad, out_bias_grad, gain_two_grad, bias_two_grad, down_bias_grad]
    )
    return (rows_full(grad_in), (grad_qkv, grad_wout, grad_up, grad_down), vec_grads)


def group_step(patch_rows, visible_ids, shown, weight_rows, rep_full, ten_full):
    splits = lax.axis_size("tensor")
    patch_w, e2d_w, head_w, enc_vec, dec_vec, head_b = split_flat(
        rep_full, [(PATCH, D), (D, DD), (DD, PATCH), (9, D), (10, DD), (PATCH,)]
    )
    enc_vec = enc_vec.astype(FLOAT)
    dec_vec = dec_vec.astype(FLOAT)
    head_b = head_b.astype(FLOAT)
    enc_cols = D // splits
    dec_cols = DD // splits
    ten_pieces = split_flat(
        ten_full,
        [
            (D, 3 * enc_cols),
            (enc_cols, D),
            (D, FF // splits),
            (FF // splits, D),
            (DD, 3 * dec_cols),
            (dec_cols, DD),
            (DD, DFF // splits),
            (DFF // splits, DD),
        ],
    )
    enc_mats = ten_pieces[0:4]
    dec_mats = ten_pieces[4:8]
    enc_vecs = [enc_vec[i] for i in range(1, 7)]
    dec_vecs = [dec_vec[i] for i in range(2, 8)]
    shown_rows = jnp.take_along_axis(patch_rows, visible_ids[:, :, None], 1)
    embedded = (
        jnp.dot(shown_rows, patch_w, preferred_element_type=FLOAT)
        + enc_vec[0]
        + sinus(TUBES, D)[visible_ids]
    )
    encoded, enc_stored = block_forward(embedded, enc_mats, enc_vecs)
    final_enc = layer_norm(encoded, enc_vec[7], enc_vec[8]).astype(HALF)
    reduced = jnp.dot(final_enc, e2d_w, preferred_element_type=FLOAT) + dec_vec[0]
    blank = jnp.broadcast_to(dec_vec[1], (TUBES, DD))
    tokens_in = jax.vmap(lambda clip_ids, clip_rows: blank.at[clip_ids].set(clip_rows))(
        visible_ids, reduced
    ) + sinus(TUBES, DD)
    decoded, dec_stored = block_forward(tokens_in, dec_mats, dec_vecs)
    own_dec = own_rows(decoded, 1)
    final_low = layer_norm(own_dec, dec_vec[8], dec_vec[9]).astype(HALF)
    predicted = jnp.dot(final_low, head_w, preferred_element_type=FLOAT) + head_b
    pixels = own_rows(patch_rows, 1).astype(FLOAT)
    center = jnp.mean(pixels, -1, keepdims=True)
    spread = jnp.mean((pixels - center) ** 2, -1, keepdims=True)
    target = (pixels - center) * lax.rsqrt(spread + 1e-06)
    differ = predicted - target
    counted = own_rows(weight_rows, 1)
    loss_part = jnp.sum(jnp.mean(differ**2, -1) * counted)
    grad_pred = 2.0 / PATCH * differ * counted[:, :, None]
    pred_low = grad_pred.astype(HALF)
    head_w_grad = jnp.einsum("ctd,ctp->dp", final_low, pred_low, preferred_element_type=FLOAT)
    head_b_grad = jnp.sum(grad_pred, (0, 1))
    grad_final = jnp.dot(pred_low, head_w.T, preferred_element_type=FLOAT)
    grad_dec_own, dec_gain_grad, dec_bias_grad = norm_back(
        own_dec, dec_vec[8], dec_vec[9], grad_final
    )
    grad_tokens, dec_mat_grads, dec_vec_grads = block_backward(
        rows_full(grad_dec_own), dec_mats, dec_vecs, dec_stored
    )
    masked_own = own_rows(1.0 - shown.astype(FLOAT), 1)
    mask_grad = jnp.sum(own_rows(grad_tokens, 1) * masked_own[:, :, None], (0, 1))
    grad_reduced = own_rows(jnp.take_along_axis(grad_tokens, visible_ids[:, :, None], 1), 1)
    reduced_low = grad_reduced.astype(HALF)
    e2d_grad = jnp.einsum(
        "ctd,cte->de", own_rows(final_enc, 1), reduced_low, preferred_element_type=FLOAT
    )
    e2d_b_grad = jnp.sum(grad_reduced, (0, 1))
    grad_enc_final = jnp.dot(reduced_low, e2d_w.T, preferred_element_type=FLOAT)
    grad_enc_own, enc_gain_grad, enc_bias_grad = norm_back(
        own_rows(encoded, 1), enc_vec[7], enc_vec[8], grad_enc_final
    )
    grad_embedded, enc_mat_grads, enc_vec_grads = block_backward(
        rows_full(grad_enc_own), enc_mats, enc_vecs, enc_stored
    )
    own_embedded = own_rows(grad_embedded, 1)
    patch_grad = jnp.einsum(
        "ctp,ctd->pd",
        own_rows(shown_rows, 1),
        own_embedded.astype(HALF),
        preferred_element_type=FLOAT,
    )
    patch_b_grad = jnp.sum(own_embedded, (0, 1))
    enc_vec_grad = jnp.concatenate(
        [patch_b_grad[None], enc_vec_grads, enc_gain_grad[None], enc_bias_grad[None]], 0
    )
    dec_vec_grad = jnp.concatenate(
        [
            e2d_b_grad[None],
            mask_grad[None],
            dec_vec_grads,
            dec_gain_grad[None],
            dec_bias_grad[None],
        ],
        0,
    )
    rep_grad = jnp.concatenate(
        [
            patch_grad.reshape(-1),
            e2d_grad.reshape(-1),
            head_w_grad.reshape(-1),
            enc_vec_grad.reshape(-1),
            dec_vec_grad.reshape(-1),
            head_b_grad,
        ]
    )
    ten_grad = jnp.concatenate(
        [mat_grad.reshape(-1) for mat_grad in list(enc_mat_grads) + list(dec_mat_grads)]
    )
    return (loss_part, rep_grad, ten_grad)


def adamw(master, first, second, clipped, number):
    first = BETA1 * first + (1 - BETA1) * clipped
    second = BETA2 * second + (1 - BETA2) * clipped * clipped
    first_hat = first / (1 - BETA1**number)
    second_hat = second / (1 - BETA2**number)
    master = master - LR_IN * (first_hat / (jnp.sqrt(second_hat) + EPS) + DECAY * master)
    return (master, first, second)


def on_device(
    patches,
    visible,
    frames_valid,
    clip_valid,
    rep_weights,
    ten_weights,
    rep_m,
    rep_v,
    ten_m,
    ten_v,
    rep_outer,
    ten_outer,
):
    splits = lax.axis_size("tensor")
    owners = lax.axis_size("dp")
    tube_ids = jnp.arange(TUBES)
    rep_master, ten_master = (rep_weights, ten_weights[0])
    rep_first, rep_second = (rep_m[0], rep_v[0])
    ten_first, ten_second = (ten_m[0, 0], ten_v[0, 0])
    loss_list, count_list, norm_list = ([], [], [])
    for inner_step in range(STEPS):
        rep_full, ten_full = (
            lax.all_gather(rep_master.astype(HALF), "dp", axis=0, tiled=True),
            lax.all_gather(ten_master.astype(HALF), "dp", axis=0, tiled=True),
        )
        visible_ids = visible[inner_step, 0]
        shown = jnp.any(visible_ids[:, :, None] == tube_ids[None, None, :], axis=1)
        weight_rows = (
            jnp.where(shown, 0.0, 1.0)
            * (tube_ids[None, :] // (TUBES // FRAMES) < frames_valid[inner_step, 0][:, None])
            * (clip_valid[inner_step, 0][:, None] == 1)
        ).astype(FLOAT)
        count_part = jnp.sum(own_rows(weight_rows, 1))
        loss_part, rep_grad, ten_grad = group_step(
            patches[inner_step, 0], visible_ids, shown, weight_rows, rep_full, ten_full
        )
        rep_recv, ten_recv = (
            lax.all_to_all(
                rep_grad.reshape(owners, -1), "dp", split_axis=0, concat_axis=0, tiled=True
            ),
            lax.all_to_all(
                ten_grad.reshape(owners, -1), "dp", split_axis=0, concat_axis=0, tiled=True
            ),
        )
        rep_part = lax.psum(jnp.sum(rep_recv, 0), "tensor")
        ten_part = jnp.sum(ten_recv, 0)
        squares = jnp.sum(ten_part * ten_part) + jnp.sum(rep_part * rep_part) / splits
        square_all, loss_all, count_all = lax.psum(
            (squares, loss_part, count_part), ("dp", "tensor")
        )
        norm_value = jnp.sqrt(square_all + 1e-30) / count_all
        factor = jnp.minimum(1.0, CLIP / norm_value) / count_all
        number = STEP_BEFORE + inner_step + 1
        rep_master, rep_first, rep_second = adamw(
            rep_master, rep_first, rep_second, rep_part * factor, number
        )
        ten_master, ten_first, ten_second = adamw(
            ten_master, ten_first, ten_second, ten_part * factor, number
        )
        loss_list.append(loss_all)
        count_list.append(count_all)
        norm_list.append(norm_value)
    rep_sum, ten_sum = lax.psum((rep_weights - rep_master, ten_weights[0] - ten_master), "group")
    groups_count = lax.axis_size("group")
    rep_diff = rep_sum / groups_count
    ten_diff = ten_sum / groups_count
    rep_momentum = MOMENTUM * rep_outer + rep_diff
    ten_momentum = MOMENTUM * ten_outer[0] + ten_diff
    rep_new = rep_weights - LR_OUT * (rep_diff + MOMENTUM * rep_momentum)
    ten_new = ten_weights[0] - LR_OUT * (ten_diff + MOMENTUM * ten_momentum)
    return (
        jnp.stack(loss_list)[:, None],
        jnp.stack(count_list)[:, None],
        jnp.stack(norm_list)[:, None],
        rep_first[None],
        rep_second[None],
        ten_first[None, None],
        ten_second[None, None],
        rep_diff,
        ten_diff[None],
        rep_momentum,
        ten_momentum[None],
        rep_new,
        ten_new[None],
    )


def solution(mesh):
    placed = (
        P(None, "group", "dp", None, None),
        P(None, "group", "dp", None),
        P(None, "group", "dp"),
        P(None, "group", "dp"),
        P("dp"),
        P("tensor", "dp"),
        P("group", "dp"),
        P("group", "dp"),
        P("group", "tensor", "dp"),
        P("group", "tensor", "dp"),
        P("dp"),
        P("tensor", "dp"),
    )
    return jax.shard_map(
        on_device,
        mesh=mesh,
        in_specs=placed,
        out_specs=(
            P(None, "group"),
            P(None, "group"),
            P(None, "group"),
            P("group", "dp"),
            P("group", "dp"),
            P("group", "tensor", "dp"),
            P("group", "tensor", "dp"),
            P("dp"),
            P("tensor", "dp"),
            P("dp"),
            P("tensor", "dp"),
            P("dp"),
            P("tensor", "dp"),
        ),
        check_vma=False,
    )
```

profile of v0, /device:TPU:0, one launch (start us, length us, event | category | flops | bytes accessed | tf_op | source)
XLA Modules:
  0.0 3362.8 jit_solution(17322433668570207172)
XLA Ops:
  14.1 18.3 fusion.2
  51.2 41.8 %all-gather.15.cloned.1.call-done = bf16[2076672]{0:T(1024)(128)(2,1)} async-done(((bf16[519168]{0:T(1024)(128)(2,1)}), bf16[2076672]{0:T(1024)(128)(2,1)}) %all-gather.15.cloned.1.call-update) | async-done | bytes 4153360 | tf_op jit(solution)/shard_map/all_gather | solution.py:350
  102.8 148.1 %all-gather.17.cloned.1.call-done = bf16[4423680]{0:T(1024)(128)(2,1)} async-done(((bf16[1105920]{0:T(1024)(128)(2,1)}), bf16[4423680]{0:T(1024)(128)(2,1)}) %all-gather.17.cloned.1.call-update) | async-done | bytes 8847376 | tf_op jit(solution)/shard_map/all_gather | solution.py:351
  343.6 12.7 exponential_reduce_fusion.1
  356.4 15.1 convolution_convert_fusion.5
  374.7 35.1 %reduce-scatter.21.cloned.1.call-done = f32[1,784,384]{2,1,0:T(8,128)} async-done(((f32[1,1568,384]{2,1,0:T(8,128)}), f32[1,784,384]{2,1,0:T(8,128)}) %reduce-scatter.21.cloned.1.call-update) | async-done | bytes 1204240 | tf_op jit(solution)/shard_map/reduce_scatter | solution.py:71
  415.7 21.5 all-gather.19.cloned.1.call-done
  437.2 14.1 multiply_convert_fusion.3
  455.7 35.3 %reduce-scatter.23.cloned.1.call-done = f32[1,784,384]{2,1,0:T(8,128)} async-done(((f32[1,1568,384]{2,1,0:T(8,128)}), f32[1,784,384]{2,1,0:T(8,128)}) %reduce-scatter.23.cloned.1.call-update) | async-done | bytes 1204240 | tf_op jit(solution)/shard_map/reduce_scatter | solution.py:71
  507.4 22.9 all-gather.21.cloned.1.call-done
  543.1 36.7 %all-gather.23.cloned.1.call-done = f32[1,1568,384]{2,1,0:T(8,128)} async-done(((f32[1,784,384]{2,1,0:T(8,128)}), f32[1,1568,384]{2,1,0:T(8,128)}) %all-gather.23.cloned.1.call-update) | async-done | bytes 2408464 | tf_op jit(solution)/shard_map/all_gather | solution.py:75
  597.0 28.8 reduce-scatter.25.cloned.1.call-done
  637.7 16.4 all-gather.25.cloned.1.call-done
  656.0 13.0 convolution_convert_fusion.4
  669.0 23.8 multiply_reduce_fusion.1
  692.8 25.8 multiply_convert_fusion.1
  746.5 29.7 reduce-scatter.27.cloned.1.call-done
  933.0 172.6 %all-to-all-done = f32[4,1,519168]{2,1,0:T(1,128)} async-done(((f32[4,1,519168]{2,1,0:T(1,128)}), f32[4,1,519168]{2,1,0:T(1,128)}, u32[]{:S(2)}, u32[]{:S(2)}) %all-to-all-start) | async-done | bytes 8306720 | tf_op jit(solution)/shard_map/all_to_all | solution.py:365
  1112.8 41.0 %reduce_sum.1318 = f32[519168]{0:T(1024)} reduce(f32[4,1,519168]{2,1,0:T(1,128)} %all-to-all-done, f32[]{:T(128)} %constant.323.clone.1), dimensions={0,1}, to_apply=%region_77.80 | reduce | flops 1557504 | bytes 10383364 | tf_op jit(solution)/shard_map/reduce_sum | solution.py:372
  1159.2 57.7 %all-reduce.7.cloned.1.call-done = f32[519168]{0:T(1024)} async-done(((f32[519168]{0:T(1024)}), f32[519168]{0:T(1024)}) %all-reduce.7.cloned.1.call-update) | async-done | bytes 2076688 | tf_op jit(solution)/shard_map/psum | solution.py:372
  1220.2 274.5 %all-to-all-done.1 = f32[4,1,1105920]{2,1,0:T(1,128)} async-done(((f32[4,1,1105920]{2,1,0:T(1,128)}), f32[4,1,1105920]{2,1,0:T(1,128)}, u32[]{:S(2)}, u32[]{:S(2)}) %all-to-all-start.1) | async-done | bytes 17694752 | tf_op jit(solution)/shard_map/all_to_all | solution.py:368
  1494.8 86.1 %reduce_sum.1323 = f32[1105920]{0:T(1024)} reduce(f32[4,1,1105920]{2,1,0:T(1,128)} %all-to-all-done.1, f32[]{:T(128)} %constant.323.clone.1), dimensions={0,1}, to_apply=%region_81.84 | reduce | flops 3317760 | bytes 22118404 | tf_op jit(solution)/shard_map/reduce_sum | solution.py:373
  1585.2 19.3 all-reduce.1
  1633.1 56.8 %all-gather.29.cloned.1.call-done = bf16[2076672]{0:T(1024)(128)(2,1)} async-done(((bf16[519168]{0:T(1024)(128)(2,1)}), bf16[2076672]{0:T(1024)(128)(2,1)}) %all-gather.29.cloned.1.call-update) | async-done | bytes 4153360 | tf_op jit(solution)/shard_map/all_gather | solution.py:350
  1699.7 147.9 %all-gather.31.cloned.1.call-done = bf16[4423680]{0:T(1024)(128)(2,1)} async-done(((bf16[1105920]{0:T(1024)(128)(2,1)}), bf16[4423680]{0:T(1024)(128)(2,1)}) %all-gather.31.cloned.1.call-update) | async-done | bytes 8847376 | tf_op jit(solution)/shard_map/all_gather | solution.py:351
  1940.2 12.7 exponential_reduce_fusion
  1953.0 15.1 convolution_convert_fusion.3
  1971.3 35.1 %reduce-scatter.37.cloned.1.call-done = f32[1,784,384]{2,1,0:T(8,128)} async-done(((f32[1,1568,384]{2,1,0:T(8,128)}), f32[1,784,384]{2,1,0:T(8,128)}) %reduce-scatter.37.cloned.1.call-update) | async-done | bytes 1204240 | tf_op jit(solution)/shard_map/reduce_scatter | solution.py:71
  2012.3 21.5 all-gather.33.cloned.1.call-done
  2033.8 13.7 multiply_convert_fusion.2
  2051.9 35.3 %reduce-scatter.39.cloned.1.call-done = f32[1,784,384]{2,1,0:T(8,128)} async-done(((f32[1,1568,384]{2,1,0:T(8,128)}), f32[1,784,384]{2,1,0:T(8,128)}) %reduce-scatter.39.cloned.1.call-update) | async-done | bytes 1204240 | tf_op jit(solution)/shard_map/reduce_scatter | solution.py:71
  2097.6 28.9 all-gather.35.cloned.1.call-done
  2139.3 36.7 %all-gather.37.cloned.1.call-done = f32[1,1568,384]{2,1,0:T(8,128)} async-done(((f32[1,784,384]{2,1,0:T(8,128)}), f32[1,1568,384]{2,1,0:T(8,128)}) %all-gather.37.cloned.1.call-update) | async-done | bytes 2408464 | tf_op jit(solution)/shard_map/all_gather | solution.py:75
  2186.8 35.4 %reduce-scatter.41.cloned.1.call-done = f32[1,784,384]{2,1,0:T(8,128)} async-done(((f32[1,1568,384]{2,1,0:T(8,128)}), f32[1,784,384]{2,1,0:T(8,128)}) %reduce-scatter.41.cloned.1.call-update) | async-done | bytes 1204240 | tf_op jit(solution)/shard_map/reduce_scatter | solution.py:71
  2227.3 23.2 all-gather.39.cloned.1.call-done
  2252.3 13.4 convolution_convert_fusion.2
  2265.7 23.8 multiply_reduce_fusion
  2289.5 25.6 multiply_convert_fusion
  2338.4 34.3 %reduce-scatter.43.cloned.1.call-done = f32[1,784,384]{2,1,0:T(8,128)} async-done(((f32[1,1568,384]{2,1,0:T(8,128)}), f32[1,784,384]{2,1,0:T(8,128)}) %reduce-scatter.43.cloned.1.call-update) | async-done | bytes 1204240 | tf_op jit(solution)/shard_map/reduce_scatter | solution.py:71
  2529.2 172.6 %all-to-all-done.3 = f32[4,1,519168]{2,1,0:T(1,128)} async-done(((f32[4,1,519168]{2,1,0:T(1,128)}), f32[4,1,519168]{2,1,0:T(1,128)}, u32[]{:S(2)}, u32[]{:S(2)}) %all-to-all-start.3) | async-done | bytes 8306720 | tf_op jit(solution)/shard_map/all_to_all | solution.py:365
  2708.9 41.0 %reduce_sum.1618 = f32[519168]{0:T(1024)} reduce(f32[4,1,519168]{2,1,0:T(1,128)} %all-to-all-done.3, f32[]{:T(128)} %constant.323.clone.1), dimensions={0,1}, to_apply=%region_166.169 | reduce | flops 1557504 | bytes 10383364 | tf_op jit(solution)/shard_map/reduce_sum | solution.py:372
  2757.8 55.2 %all-reduce.9.cloned.1.call-done = f32[519168]{0:T(1024)} async-done(((f32[519168]{0:T(1024)}), f32[519168]{0:T(1024)}) %all-reduce.9.cloned.1.call-update) | async-done | bytes 2076688 | tf_op jit(solution)/shard_map/psum | solution.py:372
  2816.4 274.5 %all-to-all-done.2 = f32[4,1,1105920]{2,1,0:T(1,128)} async-done(((f32[4,1,1105920]{2,1,0:T(1,128)}), f32[4,1,1105920]{2,1,0:T(1,128)}, u32[]{:S(2)}, u32[]{:S(2)}) %all-to-all-start.2) | async-done | bytes 17694752 | tf_op jit(solution)/shard_map/all_to_all | solution.py:368
  3090.9 86.1 %reduce_sum.1591 = f32[1105920]{0:T(1024)} reduce(f32[4,1,1105920]{2,1,0:T(1,128)} %all-to-all-done.2, f32[]{:T(128)} %constant.323.clone.1), dimensions={0,1}, to_apply=%region_138.141 | reduce | flops 3317760 | bytes 22118404 | tf_op jit(solution)/shard_map/reduce_sum | solution.py:373
  3181.1 19.6 all-reduce
  3202.9 13.1 subtract_subtract_fusion
  3221.0 23.9 fusion.29
  3250.0 91.7 %all-reduce.11.cloned.1.call-done = (f32[519168]{0:T(1024)}, f32[1105920]{0:T(1024)}) async-done(((f32[519168]{0:T(1024)}, f32[1105920]{0:T(1024)}), (f32[519168]{0:T(1024)}, f32[1105920]{0:T(1024)})) %all-reduce.11.cloned.1.call-update) | async-done | bytes 6500368 | tf_op jit(solution)/shard_map/psum | solution.py:390
  (1058 shorter events, 807.3 us)
Async XLA Ops:
  7.2 85.8 %all-gather.15.cloned.1.call-start = ((), (), s32[]{:S(2)}) async-start(), calls=%async_computation.20 | async-start | bytes 5191680 | tf_op jit(solution)/shard_map/all_gather | solution.py:350
  9.9 241.0 %all-gather.17.cloned.1.call-start = ((), (), s32[]{:S(2)}) async-start(), calls=%async_computation.21 | async-start | bytes 11059200 | tf_op jit(solution)/shard_map/all_gather | solution.py:351
  13.4 261.6 %reduce-scatter.17.cloned.1.call-start = ((), (), s32[]{:S(2)}) async-start(), calls=%async_computation.22 | async-start | bytes 737280 | tf_op jit(solution)/shard_map/reduce_scatter | solution.py:71
  14.1 274.2 %copy-start.199 = (s32[1,160,1]{1,2,0:T(1,128)}, s32[1,160,1]{1,2,0:T(1,128)S(1)}, u32[]{:S(2)}) copy-start(s32[1,160,1]{1,2,0:T(1,128)S(1)} %get-tuple-element.103) | copy-start | bytes 1924
  14.1 304.3 %copy-start.150 = (f32[1568]{0:T(1024)}, f32[1568]{0:T(1024)S(1)}, u32[]{:S(2)}) copy-start(f32[1568]{0:T(1024)S(1)} %iota_convert_fusion) | copy-start | bytes 18820
  100.7 157.8 %copy-start.156 = (f32[768]{0:T(1024)}, f32[768]{0:T(1024)S(1)}, u32[]{:S(2)}) copy-start(f32[768]{0:T(1024)S(1)} %get-tuple-element.179) | copy-start | bytes 9220
  100.7 157.8 %copy-start.168 = (f32[768]{0:T(1024)}, f32[768]{0:T(1024)S(1)}, u32[]{:S(2)}) copy-start(f32[768]{0:T(1024)S(1)} %get-tuple-element.178) | copy-start | bytes 9220
  100.8 175.7 %copy-start.164 = (f32[768]{0:T(1024)}, f32[768]{0:T(1024)S(1)}, u32[]{:S(2)}) copy-start(f32[768]{0:T(1024)S(1)} %get-tuple-element.176) | copy-start | bytes 9220
  100.8 211.2 %copy-start.152 = (f32[768]{0:T(1024)}, f32[768]{0:T(1024)S(1)}, u32[]{:S(2)}) copy-start(f32[768]{0:T(1024)S(1)} %get-tuple-element.172) | copy-start | bytes 9220
  102.5 172.5 %copy-start.14 = (f32[160,768]{1,0:T(8,128)}, f32[160,768]{1,0:T(8,128)S(1)}, u32[]{:S(2)}) copy-start(f32[160,768]{1,0:T(8,128)S(1)} %get-tuple-element.213) | copy-start | bytes 1474564
  262.5 39.8 %reduce-scatter.19.cloned.1.call-start = ((), (), s32[]{:S(2)}) async-start(), calls=%async_computation.23 | async-start | bytes 737280 | tf_op jit(solution)/shard_map/reduce_scatter | solution.py:71
  288.2 121.6 %reduce-scatter.21.cloned.1.call-start = ((), (), s32[]{:S(2)}) async-start(), calls=%async_computation.24 | async-start | bytes 3612672 | tf_op jit(solution)/shard_map/reduce_scatter | solution.py:71
  374.4 62.8 %all-gather.19.cloned.1.call-start = ((), (), s32[]{:S(2)}) async-start(), calls=%async_computation.25 | async-start | bytes 1806336 | tf_op jit(solution)/shard_map/all_gather | solution.py:109
  414.0 77.0 %reduce-scatter.23.cloned.1.call-start = ((), (), s32[]{:S(2)}) async-start(), calls=%async_computation.26 | async-start | bytes 3612672 | tf_op jit(solution)/shard_map/reduce_scatter | solution.py:71
  455.6 74.6 %all-gather.21.cloned.1.call-start = ((), (), s32[]{:S(2)}) async-start(), calls=%async_computation.27 | async-start | bytes 3612672 | tf_op jit(solution)/shard_map/all_gather | solution.py:75
  493.5 86.3 %all-gather.23.cloned.1.call-start = ((), (), s32[]{:S(2)}) async-start(), calls=%async_computation.28 | async-start | bytes 3612672 | tf_op jit(solution)/shard_map/all_gather | solution.py:75
  543.0 82.8 %reduce-scatter.25.cloned.1.call-start = ((), (), s32[]{:S(2)}) async-start(), calls=%async_computation.29 | async-start | bytes 3612672 | tf_op jit(solution)/shard_map/reduce_scatter | solution.py:71
  590.5 63.7 %all-gather.25.cloned.1.call-start = ((), (), s32[]{:S(2)}) async-start(), calls=%async_computation.30 | async-start | bytes 1806336 | tf_op jit(solution)/shard_map/all_gather | solution.py:75
  630.9 145.3 %reduce-scatter.27.cloned.1.call-start = ((), (), s32[]{:S(2)}) async-start(), calls=%async_computation.31 | async-start | bytes 3612672 | tf_op jit(solution)/shard_map/reduce_scatter | solution.py:71
  740.9 76.3 %all-gather.27.cloned.1.call-start = ((), (), s32[]{:S(2)}) async-start(), calls=%async_computation.32 | async-start | bytes 3612672 | tf_op jit(solution)/shard_map/all_gather | solution.py:75
  780.3 79.5 %reduce-scatter.29.cloned.1.call-start = ((), (), s32[]{:S(2)}) async-start(), calls=%async_computation.33 | async-start | bytes 737280 | tf_op jit(solution)/shard_map/reduce_scatter | solution.py:71
  840.0 51.4 %reduce-scatter.31.cloned.1.call-start = ((), (), s32[]{:S(2)}) async-start(), calls=%async_computation.34 | async-start | bytes 737280 | tf_op jit(solution)/shard_map/reduce_scatter | solution.py:71
  919.3 186.4 %all-to-all-start = ((f32[4,1,519168]{2,1,0:T(1,128)}), f32[4,1,519168]{2,1,0:T(1,128)}, u32[]{:S(2)}, u32[]{:S(2)}) async-start(f32[4,1,519168]{2,1,0:T(1,128)} %bitcast.590), calls=%async_computation.8 | async-start | bytes 16613376 | tf_op jit(solution)/shard_map/all_to_all | solution.py:365
  1105.6 389.1 %all-to-all-start.1 = ((f32[4,1,1105920]{2,1,0:T(1,128)}), f32[4,1,1105920]{2,1,0:T(1,128)}, u32[]{:S(2)}, u32[]{:S(2)}) async-start(f32[4,1,1105920]{2,1,0:T(1,128)} %bitcast.91), calls=%async_computation.9 | async-start | bytes 35389440 | tf_op jit(solution)/shard_map/all_to_all | solution.py:368
  1112.8 104.1 %all-reduce.7.cloned.1.call-start = ((), (), s32[]{:S(2)}) async-start(), calls=%async_computation.35 | async-start | bytes 4153344 | tf_op jit(solution)/shard_map/psum | solution.py:372
  1153.9 536.1 %all-gather.29.cloned.1.call-start = ((), (), s32[]{:S(2)}) async-start(), calls=%async_computation.36 | async-start | bytes 5191680 | tf_op jit(solution)/shard_map/all_gather | solution.py:350
  1612.6 235.1 %all-gather.31.cloned.1.call-start = ((), (), s32[]{:S(2)}) async-start(), calls=%async_computation.37 | async-start | bytes 11059200 | tf_op jit(solution)/shard_map/all_gather | solution.py:351
  1624.0 247.7 %reduce-scatter.33.cloned.1.call-start = ((), (), s32[]{:S(2)}) async-start(), calls=%async_computation.38 | async-start | bytes 737280 | tf_op jit(solution)/shard_map/reduce_scatter | solution.py:71
  1697.7 157.7 %copy-start.158 = (f32[768]{0:T(1024)}, f32[768]{0:T(1024)S(1)}, u32[]{:S(2)}) copy-start(f32[768]{0:T(1024)S(1)} %get-tuple-element.170) | copy-start | bytes 9220
  1697.7 175.4 %copy-start.166 = (f32[768]{0:T(1024)}, f32[768]{0:T(1024)S(1)}, u32[]{:S(2)}) copy-start(f32[768]{0:T(1024)S(1)} %get-tuple-element.167) | copy-start | bytes 9220
  1697.7 211.1 %copy-start.154 = (f32[768]{0:T(1024)}, f32[768]{0:T(1024)S(1)}, u32[]{:S(2)}) copy-start(f32[768]{0:T(1024)S(1)} %get-tuple-element.163) | copy-start | bytes 9220
  1699.5 172.3 %copy-start.16 = (f32[160,768]{1,0:T(8,128)}, f32[160,768]{1,0:T(8,128)S(1)}, u32[]{:S(2)}) copy-start(f32[160,768]{1,0:T(8,128)S(1)} %get-tuple-element.228) | copy-start | bytes 1474564
  1859.2 39.9 %reduce-scatter.35.cloned.1.call-start = ((), (), s32[]{:S(2)}) async-start(), calls=%async_computation.39 | async-start | bytes 737280 | tf_op jit(solution)/shard_map/reduce_scatter | solution.py:71
  1884.7 121.7 %reduce-scatter.37.cloned.1.call-start = ((), (), s32[]{:S(2)}) async-start(), calls=%async_computation.40 | async-start | bytes 3612672 | tf_op jit(solution)/shard_map/reduce_scatter | solution.py:71
  1971.0 62.8 %all-gather.33.cloned.1.call-start = ((), (), s32[]{:S(2)}) async-start(), calls=%async_computation.41 | async-start | bytes 1806336 | tf_op jit(solution)/shard_map/all_gather | solution.py:109
  2010.6 76.7 %reduce-scatter.39.cloned.1.call-start = ((), (), s32[]{:S(2)}) async-start(), calls=%async_computation.42 | async-start | bytes 3612672 | tf_op jit(solution)/shard_map/reduce_scatter | solution.py:71
  2051.9 74.6 %all-gather.35.cloned.1.call-start = ((), (), s32[]{:S(2)}) async-start(), calls=%async_computation.43 | async-start | bytes 3612672 | tf_op jit(solution)/shard_map/all_gather | solution.py:75
  2089.7 86.4 %all-gather.37.cloned.1.call-start = ((), (), s32[]{:S(2)}) async-start(), calls=%async_computation.44 | async-start | bytes 3612672 | tf_op jit(solution)/shard_map/all_gather | solution.py:75
  2139.3 82.9 %reduce-scatter.41.cloned.1.call-start = ((), (), s32[]{:S(2)}) async-start(), calls=%async_computation.45 | async-start | bytes 3612672 | tf_op jit(solution)/shard_map/reduce_scatter | solution.py:71
  2186.8 63.7 %all-gather.39.cloned.1.call-start = ((), (), s32[]{:S(2)}) async-start(), calls=%async_computation.46 | async-start | bytes 1806336 | tf_op jit(solution)/shard_map/all_gather | solution.py:75
  2227.2 145.5 %reduce-scatter.43.cloned.1.call-start = ((), (), s32[]{:S(2)}) async-start(), calls=%async_computation.47 | async-start | bytes 3612672 | tf_op jit(solution)/shard_map/reduce_scatter | solution.py:71
  2337.3 76.4 %all-gather.41.cloned.1.call-start = ((), (), s32[]{:S(2)}) async-start(), calls=%async_computation.48 | async-start | bytes 3612672 | tf_op jit(solution)/shard_map/all_gather | solution.py:75
  2376.8 79.5 %reduce-scatter.45.cloned.1.call-start = ((), (), s32[]{:S(2)}) async-start(), calls=%async_computation.49 | async-start | bytes 737280 | tf_op jit(solution)/shard_map/reduce_scatter | solution.py:71
  2436.4 51.6 %reduce-scatter.47.cloned.1.call-start = ((), (), s32[]{:S(2)}) async-start(), calls=%async_computation.50 | async-start | bytes 737280 | tf_op jit(solution)/shard_map/reduce_scatter | solution.py:71
  2515.4 186.4 %all-to-all-start.3 = ((f32[4,1,519168]{2,1,0:T(1,128)}), f32[4,1,519168]{2,1,0:T(1,128)}, u32[]{:S(2)}, u32[]{:S(2)}) async-start(f32[4,1,519168]{2,1,0:T(1,128)} %bitcast.591), calls=%async_computation.19 | async-start | bytes 16613376 | tf_op jit(solution)/shard_map/all_to_all | solution.py:365
  2701.7 389.1 %all-to-all-start.2 = ((f32[4,1,1105920]{2,1,0:T(1,128)}), f32[4,1,1105920]{2,1,0:T(1,128)}, u32[]{:S(2)}, u32[]{:S(2)}) async-start(f32[4,1,1105920]{2,1,0:T(1,128)} %bitcast.179), calls=%async_computation.17 | async-start | bytes 35389440 | tf_op jit(solution)/shard_map/all_to_all | solution.py:368
  2708.9 104.1 %all-reduce.9.cloned.1.call-start = ((), (), s32[]{:S(2)}) async-start(), calls=%async_computation.51 | async-start | bytes 4153344 | tf_op jit(solution)/shard_map/psum | solution.py:372
  2750.0 591.7 %all-reduce.11.cloned.1.call-start = ((), (), s32[]{:S(2)}) async-start(), calls=%async_computation.52 | async-start | bytes 13000704 | tf_op jit(solution)/shard_map/psum | solution.py:390
  (245 other events, 3168.3 us)
Sparse Core Ops, SparseCore 0:
  10.2 82.8 all-gather.14
  95.1 155.6 all-gather.16
  262.6 12.3 reduce-scatter.16
  288.4 13.9 reduce-scatter.18
  374.5 35.2 reduce-scatter.20
  414.1 23.0 all-gather.18
  455.7 35.2 reduce-scatter.22
  493.6 36.6 all-gather.20
  543.1 36.6 all-gather.22
  590.6 35.2 reduce-scatter.24
  631.0 23.0 all-gather.24
  740.9 35.2 reduce-scatter.26
  780.5 36.7 all-gather.26
  840.1 14.1 reduce-scatter.28
  877.1 14.2 reduce-scatter.30
  1154.0 62.8 all-reduce.6
  1612.7 77.2 all-gather.28
  1691.9 155.6 all-gather.30
  1859.3 12.3 reduce-scatter.32
  1884.9 14.1 reduce-scatter.34
  1971.1 35.2 reduce-scatter.36
  2010.7 23.0 all-gather.32
  2052.0 35.2 reduce-scatter.38
  2089.8 36.6 all-gather.34
  2139.4 36.6 all-gather.36
  2186.9 35.2 reduce-scatter.40
  2227.3 23.0 all-gather.38
  2337.4 35.2 reduce-scatter.42
  2377.0 36.6 all-gather.40
  2436.5 14.1 reduce-scatter.44
  2473.7 14.2 reduce-scatter.46
  2750.1 62.9 all-reduce.8
  3221.1 120.5 all-reduce.10
where the time goes:
time: 3380 us; the launch traced here: 3360 us
  waiting for transfers between devices  2000 us (59%)
  other arithmetic  580 us (17%)
  matrix products  355 us (11%)
  local copies, waits for them, and re-layouts  254 us (8%)
  blocking collectives  113 us (3%)
    all_to_all x2, waiting for transfers between devices, on_device(): lax.all_to_all(ten_grad.reshape(owners, -1), 'dp', split_axis=0, concat_a...  549 us
    all_to_all x2, waiting for transfers between devices, on_device(): lax.all_to_all(rep_grad.reshape(owners, -1), 'dp', split_axis=0, concat_a...  345 us
    reduce_scatter x16, waiting for transfers between devices, rows_sum(): lax.psum_scatter(partial_rows, 'tensor', scatter_dimension=1, tiled=True)  299 us
    all_gather x2, waiting for transfers between devices, on_device(): lax.all_gather(ten_master.astype(HALF), 'dp', axis=0, tiled=True)  296 us
    reduce_sum x2, other arithmetic, on_device(): ten_part = jnp.sum(ten_recv, 0)  172 us
    all_gather x8, waiting for transfers between devices, rows_full(): return lax.all_gather(own_part, 'tensor', axis=1, tiled=True)  169 us
    psum x2, waiting for transfers between devices, on_device(): rep_part = lax.psum(jnp.sum(rep_recv, 0), 'tensor')  113 us
    all_gather x2, waiting for transfers between devices, on_device(): lax.all_gather(rep_master.astype(HALF), 'dp', axis=0, tiled=True)  98.6 us
  transfers between devices with their start and end apart: 37, of which 35 were waited for; matrix products, arithmetic and copies ran while one was open for 13% of the time, Pallas kernels for 0%

commit v1 on v0

--- a/solution.py
+++ b/solution.py
@@ -1,8 +1,11 @@
+import functools
 import math
 
 import jax
 import jax.numpy as jnp
 from jax import lax
+from jax.experimental import pallas as pl
+from jax.experimental.pallas import tpu as pltpu
 from jax.sharding import PartitionSpec as P
 
 D = 768
@@ -412,6 +415,1294 @@
     )
 
 
+NT=(((1,),(1,)),((),()))
+NN=(((1,),(0,)),((),()))
+TILE=224
+def dot(a,b,dims): return lax.dot_general(a,b,dims,preferred_element_type=FLOAT)
+
+def attn_forward_kernel(q_ref,k_ref,v_ref,out_ref,lse_ref):
+    heads=q_ref.shape[1]//HDIM; tiles=q_ref.shape[0]//TILE
+    for h in range(heads):
+        cols=slice(h*HDIM,(h+1)*HDIM)
+        keys=k_ref[:,cols]*HALF(HDIM**-0.5)
+        vt=v_ref[:,cols].T
+        def step(t,_):
+            rows=pl.ds(pl.multiple_of(t*TILE,TILE),TILE)
+            s=dot(keys,q_ref[rows,cols],NT)
+            m=jnp.max(s,0,keepdims=True)
+            e=jnp.exp(s-m)
+            total=jnp.sum(e,0,keepdims=True)
+            p=(e*(1.0/total)).astype(HALF)
+            bt=dot(vt,p,NN)
+            out_ref[rows,cols]=bt.T.astype(HALF)
+            lse_ref[h,pl.ds(t,1),:]=m+jnp.log(total)
+            return 0
+        lax.fori_loop(0,tiles,step,0)
+
+def attn_forward(q,k,v):
+    rows,width=q.shape
+    vm=pl.BlockSpec(memory_space=pltpu.VMEM)
+    return pl.pallas_call(attn_forward_kernel,name="attn_forward",
+      out_shape=(jax.ShapeDtypeStruct((rows,width),HALF),jax.ShapeDtypeStruct((width//HDIM,rows//TILE,TILE),FLOAT)),
+      in_specs=[vm]*3,out_specs=(vm,vm),
+      compiler_params=pltpu.CompilerParams(vmem_limit_bytes=48<<20),
+      cost_estimate=pl.CostEstimate(flops=4*rows*rows*width,bytes_accessed=rows*width*8,transcendentals=rows*rows*width//HDIM))(q,k,v)
+
+def attn_backward_kernel(q_ref,k_ref,v_ref,g_ref,lse_ref,out_ref,dk_ref,dv_ref):
+    width=q_ref.shape[1]
+    heads=width//HDIM; tiles=q_ref.shape[0]//TILE
+    for h in range(heads):
+        cols=slice(h*HDIM,(h+1)*HDIM)
+        keys=k_ref[:,cols]*HALF(HDIM**-0.5)
+        values=v_ref[:,cols]
+        kt=keys.T
+        dk_ref[...]=jnp.zeros_like(dk_ref); dv_ref[...]=jnp.zeros_like(dv_ref)
+        def step(t,_):
+            rows=pl.ds(pl.multiple_of(t*TILE,TILE),TILE)
+            q=q_ref[rows,cols]; g=g_ref[rows,cols]
+            p=jnp.exp(dot(keys,q,NT)-lse_ref[h,pl.ds(t,1),:])
+            dv_ref[...]+=dot(p.astype(HALF),g,NN)
+            dp=dot(values,g,NT)
+            ds=(p*(dp-jnp.sum(p*dp,0,keepdims=True))).astype(HALF)
+            dk_ref[...]+=dot(ds,q,NN)
+            out_ref[rows,cols]=dot(kt,ds,NN).T.astype(HALF)
+            return 0
+        lax.fori_loop(0,tiles,step,0)
+        out_ref[:,width+h*HDIM:width+(h+1)*HDIM]=(dk_ref[...]*HDIM**-0.5).astype(HALF)
+        out_ref[:,2*width+h*HDIM:2*width+(h+1)*HDIM]=dv_ref[...].astype(HALF)
+
+def attn_backward(q,k,v,g,lse):
+    rows,width=q.shape
+    vm=pl.BlockSpec(memory_space=pltpu.VMEM)
+    return pl.pallas_call(attn_backward_kernel,name="attn_backward",
+      out_shape=jax.ShapeDtypeStruct((rows,3*width),HALF),
+      in_specs=[vm]*5,out_specs=vm,
+      scratch_shapes=[pltpu.VMEM((rows,HDIM),FLOAT),pltpu.VMEM((rows,HDIM),FLOAT)],
+      compiler_params=pltpu.CompilerParams(vmem_limit_bytes=48<<20),
+      cost_estimate=pl.CostEstimate(flops=10*rows*rows*width,bytes_accessed=rows*width*14,transcendentals=rows*rows*width//HDIM))(q,k,v,g,lse)
+
+
+HOST = 1
+LAST = 3
+SWAP = [(0, 1), (1, 0)]
+ENC_SHAPES = [(D, 3 * D // 2), (D // 2, D), (D, FF // 2), (FF // 2, D)]
+DEC_SHAPES = [(DD, 3 * DD // 2), (DD // 2, DD), (DD, DFF // 2), (DFF // 2, DD)]
+ENC_SIZE = sum(math.prod(one) for one in ENC_SHAPES)
+DEC_SIZE = sum(math.prod(one) for one in DEC_SHAPES)
+PATCH_SIZE = PATCH * D
+E2D_SIZE = D * DD
+HEAD_SIZE = DD * PATCH
+ENC_VECS = 9 * D
+DEC_VECS = 10 * DD
+
+
+def hop(value, *moves):
+    pairs = [(2 * a + b, 2 * c + d) for (a, b), (c, d) in moves]
+    return lax.ppermute(value, ("dp", "tensor"), pairs)
+
+
+def hop_both(value, *moves):
+    return hop(value, *[((a, side), (b, side)) for a, b in moves for side in range(2)])
+
+
+def swap(value, *where):
+    if where:
+        return hop(value, *[((z, side), (z, 1 - side)) for z in where for side in range(2)])
+    return lax.ppermute(value, "tensor", SWAP)
+
+
+def partner(value):
+    count = lax.axis_size("group")
+    return lax.ppermute(value, "group", [(g, g ^ 1) for g in range(count)])
+
+
+def mm(left, right):
+    return jnp.dot(left, right, preferred_element_type=FLOAT)
+
+
+def mm_nt(left, right):
+    return lax.dot_general(left, right, (((1,), (1,)), ((), ())), preferred_element_type=FLOAT)
+
+
+def mm_tn(left, right):
+    return lax.dot_general(left, right, (((0,), (0,)), ((), ())), preferred_element_type=FLOAT)
+
+
+def sinus_at(ids, width):
+    column = jnp.arange(width)
+    decays = jnp.power(10000.0, -2.0 * (column // 2).astype(FLOAT) / width)
+    angles = ids.astype(FLOAT)[:, None] * decays[None, :]
+    return jnp.where(column % 2 == 0, jnp.sin(angles), jnp.cos(angles))
+
+
+(
+    QKV,
+    SQUARE,
+    UP,
+    PATCH_ROWS,
+    E2D,
+    HEAD,
+    HEAD_LATE,
+    VECS,
+    DEC_QKV,
+    DEC_OUT,
+    DEC_UP,
+    DEC_DOWN,
+    HEAD_HALF,
+    PATCH_LOW,
+    PATCH_HIGH,
+    W_QKV,
+    W_OUT,
+    W_UP,
+    W_DOWN,
+    E2D_W,
+    HEAD_UP,
+    SEND_ENC,
+    SEND_MATE,
+    CHAIN,
+    CROSS,
+    MATE_OWN,
+    MATE_OTHER,
+) = range(27)
+TEN_ROWS = [
+    [(QKV, 768), (SQUARE, 288)],
+    [(SQUARE, 96), (UP, 672)],
+    [(UP, 96), (SQUARE, 1248)],
+    [(SQUARE, 288), (DEC_QKV, 384), (DEC_OUT, 192), (DEC_UP, 384), (DEC_DOWN, 768)],
+]
+REP_ROWS = [
+    [(PATCH_ROWS, 676)],
+    [(PATCH_ROWS, 676)],
+    [(PATCH_ROWS, 184), (E2D, 768), (HEAD, 54)],
+    [(HEAD_LATE, 330), (VECS, 16)],
+]
+PIECES = {
+    QKV: (768, 1152),
+    SQUARE: (1248, 768),
+    UP: (672, 1536),
+    PATCH_ROWS: (704, 768),
+    E2D: (768, 384),
+    HEAD: (64, 1536),
+    HEAD_LATE: (384, 1536),
+    VECS: (16, 768),
+    DEC_QKV: (384, 576),
+    DEC_OUT: (192, 384),
+    DEC_UP: (384, 768),
+    DEC_DOWN: (768, 384),
+}
+
+
+def owned_pieces(rep_master, ten_master):
+    def branch(ten_rows, rep_rows):
+        def fill(ten, rep):
+            out = {}
+            for flat, rows in ((ten, ten_rows), (rep, rep_rows)):
+                offset = 0
+                for name, count in rows:
+                    width = PIECES[name][1]
+                    piece = flat[offset : offset + count * width].astype(HALF).reshape(count, width)
+                    offset += count * width
+                    top = PIECES[name][0] - count if name == HEAD_LATE else 0
+                    out[name] = jnp.pad(piece, ((top, PIECES[name][0] - count - top), (0, 0)))
+            return [out.get(name, jnp.zeros(PIECES[name], HALF)) for name in PIECES]
+
+        return fill
+
+    branches = [branch(ten_rows, rep_rows) for ten_rows, rep_rows in zip(TEN_ROWS, REP_ROWS)]
+    return dict(zip(PIECES, lax.switch(lax.axis_index("dp"), branches, ten_master, rep_master)))
+
+
+DEC_PARTS = [DEC_QKV, DEC_OUT, DEC_UP, DEC_DOWN, HEAD_HALF]
+SENT = [QKV, SQUARE, UP, PATCH_ROWS, E2D, HEAD, VECS] + DEC_PARTS
+ENC_PARTS = [
+    (PATCH_LOW, 704, 0, PATCH_ROWS, 0),
+    (W_QKV, 768, 0, QKV, 0),
+    (W_OUT, 288, 0, SQUARE, 0),
+    (W_OUT, 96, 1, SQUARE, 288),
+    (PATCH_HIGH, 192, 2, PATCH_ROWS, 0),
+    (W_UP, 672, 1, UP, 0),
+    (W_UP, 96, 2, UP, 672),
+    (W_DOWN, 1248, 2, SQUARE, 0),
+    (W_DOWN, 288, 3, SQUARE, 1248),
+    (E2D_W, 768, 2, E2D, 0),
+]
+GOT = {
+    PATCH_LOW: (704, 768),
+    PATCH_HIGH: (192, 768),
+    W_QKV: (768, 1152),
+    W_OUT: (384, 768),
+    W_UP: (768, 1536),
+    W_DOWN: (1536, 768),
+    E2D_W: (768, 384),
+    HEAD: (64, 1536),
+    VECS: (16, 768),
+}
+MESH_ID = pl.DeviceIdType.MESH
+
+
+def weights_kernel(shared, *refs):
+    sent = dict(zip(SENT, refs[: len(SENT)]))
+    refs = refs[len(SENT) :]
+    got = dict(zip(GOT, refs[: len(GOT)]))
+    refs = refs[len(GOT) :]
+    own = dict(zip(DEC_PARTS, refs[: len(DEC_PARTS)]))
+    other = dict(zip(DEC_PARTS, refs[len(DEC_PARTS) : 2 * len(DEC_PARTS)]))
+    send_sem, recv_sem, local_sem = refs[2 * len(DEC_PARTS) :]
+    g, z, x = lax.axis_index("group"), lax.axis_index("dp"), lax.axis_index("tensor")
+    odd = lax.rem(g, 2)
+    mate = (g + 1 - 2 * odd, z, x)
+    across = (g, z, 1 - x)
+
+    def at(row):
+        return (g, row, x)
+
+    def greet(peer):
+        pl.semaphore_signal(barrier, inc=1, device_id=peer, device_id_type=MESH_ID)
+
+    barrier = pltpu.get_barrier_semaphore()
+    greet(across)
+    near = {0: [1], 1: [0, 2, 3], 2: [1, 3], 3: [2, 1]}
+    if shared:
+        greet(mate)
+    for row, peers in near.items():
+
+        @pl.when(z == row)
+        def _():
+            for peer in peers:
+                greet(at(peer))
+            pl.semaphore_wait(barrier, len(peers) + (2 if shared else 1))
+
+    def part(ref, start, count, half):
+        if not half:
+            return ref.at[pl.ds(start, count)]
+        return ref.at[pl.ds(pl.multiple_of(start + odd * (count // 2), 16), count // 2)]
+
+    numbers = {}
+
+    def copy(key, source, target, peer):
+        index = numbers.setdefault(key, len(numbers))
+        return pltpu.make_async_remote_copy(
+            src_ref=source,
+            dst_ref=target,
+            send_sem=send_sem.at[index],
+            recv_sem=recv_sem.at[index],
+            device_id=peer,
+            device_id_type=MESH_ID,
+        )
+
+    def enc_copy(item):
+        name, count, owner, piece, first = item
+        return copy(
+            (SEND_ENC, name, first),
+            part(sent[piece], 0, count, shared),
+            part(got[name], first, count, shared),
+            at(HOST),
+        )
+
+    def enc_mate(item):
+        name, count, owner, piece, first = item
+        half = part(got[name], first, count, True)
+        return copy((SEND_MATE, name, first), half, half, mate)
+
+    def local(index, source, target):
+        return pltpu.make_async_copy(source, target, local_sem.at[index])
+
+    def chain(name, source, peer):
+        target = got[name] if name in got else own[name]
+        rows = source.shape[0]
+        half = shared and name in own
+        return copy((CHAIN, name), part(source, 0, rows, half), part(target, 0, rows, half), at(peer))
+
+    def cross(name, source):
+        rows = source.shape[0]
+        return copy(
+            (CROSS, name), part(source, 0, rows, shared), part(other[name], 0, rows, shared), across
+        )
+
+    def mates(name, ref, label):
+        half = part(ref, 0, ref.shape[0], True)
+        return copy((label, name), half, half, mate)
+
+    def owned(row):
+        return [item for item in ENC_PARTS if item[2] == row and row != HOST]
+
+    for item in ENC_PARTS:
+        numbers[(SEND_ENC, item[0], item[4])] = len(numbers)
+        numbers[(SEND_MATE, item[0], item[4])] = len(numbers)
+    for name in DEC_PARTS + [VECS, HEAD, HEAD_UP]:
+        for label in (CHAIN, CROSS, MATE_OWN, MATE_OTHER):
+            numbers[(label, name)] = len(numbers)
+
+    def head_up():
+        return copy((CHAIN, HEAD_UP), sent[HEAD], got[HEAD], at(LAST))
+
+    def finish_dec(name, source, here):
+        cross(name, source).start()
+        if shared and not here:
+            mates(name, own[name], MATE_OWN).start()
+
+    def end_dec(name, source, here):
+        cross(name, source).wait()
+        if shared:
+            mates(name, other[name], MATE_OTHER).start()
+
+    def end_mates(name, here):
+        if shared:
+            if not here:
+                mates(name, own[name], MATE_OWN).wait()
+            mates(name, other[name], MATE_OTHER).wait()
+
+    @pl.when(z == LAST)
+    def _():
+        for item in owned(LAST):
+            enc_copy(item).start()
+        chain(VECS, sent[VECS], 2).start()
+        for name in DEC_PARTS:
+            chain(name, sent[name], 2).start()
+            finish_dec(name, sent[name], True)
+        locals_ = [local(i, sent[name], own[name]) for i, name in enumerate(DEC_PARTS)]
+        locals_.append(local(len(DEC_PARTS), sent[VECS], got[VECS]))
+        for one in locals_:
+            one.start()
+        for name in DEC_PARTS:
+            end_dec(name, sent[name], True)
+        for item in owned(LAST):
+            enc_copy(item).wait_send()
+        chain(VECS, sent[VECS], 2).wait_send()
+        for name in DEC_PARTS:
+            chain(name, sent[name], 2).wait_send()
+            end_mates(name, True)
+        for one in locals_:
+            one.wait()
+        head_up().wait_recv()
+
+    @pl.when(z == 2)
+    def _():
+        head_up().start()
+        chain(HEAD, sent[HEAD], HOST).start()
+        first = local(0, sent[HEAD], got[HEAD])
+        first.start()
+        for item in owned(2):
+            enc_copy(item).start()
+        chain(VECS, sent[VECS], 2).wait_recv()
+        chain(VECS, got[VECS], HOST).start()
+        waited = False
+        for name in DEC_PARTS:
+            chain(name, sent[name], 2).wait_recv()
+            finish_dec(name, own[name], False)
+            if not waited:
+                for item in owned(2):
+                    enc_copy(item).wait_send()
+                waited = True
+            chain(name, own[name], HOST).start()
+        for name in DEC_PARTS:
+            end_dec(name, own[name], False)
+        for name in DEC_PARTS:
+            chain(name, own[name], HOST).wait_send()
+            end_mates(name, False)
+        chain(VECS, got[VECS], HOST).wait_send()
+        chain(HEAD, sent[HEAD], HOST).wait_send()
+        head_up().wait_send()
+        first.wait()
+
+    @pl.when(z == HOST)
+    def _():
+        mine = [
+            local(i, sent[piece].at[pl.ds(0, count)], got[name].at[pl.ds(first, count)])
+            for i, (name, count, owner, piece, first) in enumerate(ENC_PARTS)
+            if owner == HOST
+        ]
+        for one in mine:
+            one.start()
+        chain(HEAD, sent[HEAD], HOST).wait_recv()
+        chain(HEAD, got[HEAD], 0).start()
+        chain(VECS, sent[VECS], HOST).wait_recv()
+        chain(VECS, got[VECS], 0).start()
+        away = [item for item in ENC_PARTS if item[2] != HOST]
+        if shared:
+            for item in away:
+                enc_copy(item).wait_recv()
+                enc_mate(item).start()
+        for name in DEC_PARTS:
+            chain(name, sent[name], HOST).wait_recv()
+            chain(name, own[name], 0).start()
+            finish_dec(name, own[name], False)
+        for name in DEC_PARTS:
+            end_dec(name, own[name], False)
+        for item in away:
+            if shared:
+                enc_mate(item).wait()
+            else:
+                enc_copy(item).wait_recv()
+        for name in DEC_PARTS:
+            chain(name, own[name], 0).wait_send()
+            end_mates(name, False)
+        chain(VECS, got[VECS], 0).wait_send()
+        chain(HEAD, got[HEAD], 0).wait_send()
+        for one in mine:
+            one.wait()
+
+    @pl.when(z == 0)
+    def _():
+        for item in owned(0):
+            enc_copy(item).start()
+        for name in DEC_PARTS:
+            chain(name, sent[name], 0).wait_recv()
+            finish_dec(name, own[name], False)
+        for name in DEC_PARTS:
+            end_dec(name, own[name], False)
+        for name in DEC_PARTS:
+            end_mates(name, False)
+        chain(VECS, sent[VECS], 0).wait_recv()
+        chain(HEAD, sent[HEAD], 0).wait_recv()
+        for item in owned(0):
+            enc_copy(item).wait_send()
+
+
+def hosted_weights(rep_master, ten_master, shared):
+    side = lax.axis_index("tensor")
+    pieces = owned_pieces(rep_master, ten_master)
+    columns = PATCH // 2
+    pieces[HEAD_HALF] = lax.dynamic_slice_in_dim(pieces[HEAD_LATE], side * columns, columns, 1)
+    anywhere = pl.BlockSpec(memory_space=pl.ANY)
+    shapes = list(GOT.values()) + 2 * [pieces[name].shape for name in DEC_PARTS]
+    count = 2 * len(ENC_PARTS) + 4 * (len(DEC_PARTS) + 3)
+    out = pl.pallas_call(
+        functools.partial(weights_kernel, shared),
+        name="weights",
+        out_shape=[jax.ShapeDtypeStruct(shape, HALF) for shape in shapes],
+        in_specs=[anywhere] * len(SENT),
+        out_specs=[anywhere] * len(shapes),
+        scratch_shapes=[
+            pltpu.SemaphoreType.DMA((count,)),
+            pltpu.SemaphoreType.DMA((count,)),
+            pltpu.SemaphoreType.DMA((len(ENC_PARTS),)),
+        ],
+        compiler_params=pltpu.CompilerParams(collective_id=1 if shared else 2, has_side_effects=True),
+    )(*[pieces[name] for name in SENT])
+    got = dict(zip(GOT, out))
+    own = out[len(GOT) : len(GOT) + len(DEC_PARTS)]
+    other = out[len(GOT) + len(DEC_PARTS) :]
+    low, high = jnp.where(side == 0, own[4], other[4]), jnp.where(side == 0, other[4], own[4])
+    head_w = jnp.concatenate([low, high], 1)
+    top = got[HEAD].shape[0]
+    head_w = jnp.concatenate([head_w[:top] + got[HEAD], head_w[top:]], 0)
+    vecs = got[VECS].reshape(-1)
+    enc_vec, dec_vec, head_b = split_flat(vecs, [(9, D), (10, DD), (PATCH,)])
+    return (
+        (
+            (got[PATCH_LOW], pieces[PATCH_ROWS], got[PATCH_HIGH]),
+            tuple(got[name] for name in (W_QKV, W_OUT, W_UP, W_DOWN)),
+            got[E2D_W],
+            jnp.pad(enc_vec.astype(FLOAT), ((0, 7), (0, 0))),
+        ),
+        (own[:4], other[:4], head_w, dec_vec.astype(FLOAT), head_b.astype(FLOAT)),
+    )
+
+
+VISIBLE = 160
+OWN = 2 * VISIBLE
+ALL = 4 * VISIBLE
+SPAN = (0, 768, 1536)
+DEPTH = (704, 704, 192)
+WIDE = 1792
+SQRT_HALF = 0.5**0.5
+
+
+def norm_parts(x):
+    center = jnp.mean(x, -1, keepdims=True)
+    moved = x - center
+    scale = lax.rsqrt(jnp.mean(moved * moved, -1, keepdims=True) + 1e-06)
+    return moved * scale, scale
+
+
+def norm_to(x, gain, bias):
+    return norm_parts(x)[0] * gain + bias
+
+
+def norm_from(x, gain, cotangent):
+    hat, scale = norm_parts(x)
+    inner = cotangent * gain
+    grad = scale * (
+        inner - jnp.mean(inner, -1, keepdims=True) - hat * jnp.mean(inner * hat, -1, keepdims=True)
+    )
+    return grad, jnp.sum(cotangent * hat, 0, keepdims=True), jnp.sum(cotangent, 0, keepdims=True)
+
+
+def gelu_to(x):
+    return 0.5 * x * (1.0 + lax.erf(x * SQRT_HALF))
+
+
+def gelu_slope(x):
+    return 0.5 * (1.0 + lax.erf(x * SQRT_HALF)) + x * jnp.exp(-0.5 * x * x) * (2.0 * math.pi) ** -0.5
+
+
+def rows_at(index, count=VISIBLE):
+    return pl.ds(index * count, count)
+
+
+class Links:
+    def __init__(self, send_sem, recv_sem):
+        self.send_sem, self.recv_sem, self.keys = send_sem, recv_sem, {}
+
+    def copy(self, key, source, target, peer):
+        index = self.keys.setdefault(key, len(self.keys))
+        return pltpu.make_async_remote_copy(
+            src_ref=source,
+            dst_ref=target,
+            send_sem=self.send_sem.at[index],
+            recv_sem=self.recv_sem.at[index],
+            device_id=peer,
+            device_id_type=MESH_ID,
+        )
+
+
+def encoder_forward_kernel(
+    shown, places, patch_low, patch_mid, patch_high, w_qkv, w_out, w_up, w_down, e2d_w, vec,
+    reduced, stream, normed, joined, blended, attended, second, upward, activated, encoded, final_enc,
+    part_sent, part_got, reduced_own, send_sem, recv_sem, local_sem,
+):
+    g, z, x = lax.axis_index("group"), lax.axis_index("dp"), lax.axis_index("tensor")
+    barrier = pltpu.get_barrier_semaphore()
+    links = Links(send_sem, recv_sem)
+
+    def at(row, column):
+        return (g, row, column)
+
+    def greet(peer):
+        pl.semaphore_signal(barrier, inc=1, device_id=peer, device_id_type=MESH_ID)
+
+    for row in range(4):
+
+        @pl.when((z == row) & ((row != HOST) | (x == 1)))
+        def _():
+            greet(at(HOST, row // 2))
+
+    @pl.when((z == HOST) & (x == 0))
+    def _():
+        greet(at(HOST, 1))
+        pl.semaphore_wait(barrier, 3)
+
+    @pl.when((z == HOST) & (x == 1))
+    def _():
+        pl.semaphore_wait(barrier, 5)
+
+    def give(column, clip):
+        row = 2 * column + clip
+        out = []
+        for side in range(2):
+            if (row, side) != (HOST, column):
+                out.append(links.copy(8 + 2 * clip + side, reduced_own.at[clip], reduced, at(row, side)))
+        return out
+
+    @pl.when(z == HOST)
+    def _():
+        across = at(HOST, 1 - x)
+
+        def normed_copy(i):
+            return links.copy(i, normed.at[rows_at(i)], normed.at[rows_at(2 + i)], across)
+
+        def out_copy(i):
+            return links.copy(2 + i, part_sent.at[rows_at(i)], part_got.at[rows_at(i)], across)
+
+        def second_copy(i):
+            return links.copy(4 + i, second.at[rows_at(i)], second.at[rows_at(2 + i)], across)
+
+        def down_copy(i):
+            return links.copy(6 + i, part_sent.at[rows_at(2 + i)], part_got.at[rows_at(2 + i)], across)
+
+        for i in range(2):
+            rows = rows_at(i)
+            emb = places[rows] + vec[0:1]
+            for start, depth, weight in zip(SPAN, DEPTH, (patch_low, patch_mid, patch_high)):
+                emb = emb + mm(shown[rows, start : start + depth], weight[...])
+            stream[rows] = emb
+            normed[rows] = norm_to(emb, vec[1:2], vec[2:3]).astype(HALF)
+            normed_copy(i).start()
+
+        def attend(c):
+            rows = rows_at(c)
+            joined[rows] = mm(normed[rows], w_qkv[...]).astype(HALF)
+            width = D // 2
+            for h in range(width // HDIM):
+                column = h * HDIM
+                queries = joined[rows, column : column + HDIM]
+                keys = joined[rows, width + column : width + column + HDIM]
+                values = joined[rows, 2 * width + column : 2 * width + column + HDIM]
+                scores = mm_nt(queries, keys) * HDIM**-0.5
+                weights = jnp.exp(scores - jnp.max(scores, -1, keepdims=True))
+                probs = weights * (1.0 / jnp.sum(weights, -1, keepdims=True))
+                blended[rows, column : column + HDIM] = mm(probs.astype(HALF), values).astype(HALF)
+            return mm(blended[rows], w_out[...])
+
+        for i in range(2):
+            attended[rows_at(i)] = attend(i) + stream[rows_at(i)] + vec[3:4]
+            normed_copy(i).wait_recv()
+            part_sent[rows_at(i)] = attend(2 + i).astype(HALF)
+            out_copy(i).start()
+
+        def feed(c):
+            rows = rows_at(c)
+            up = mm(second[rows], w_up[...])
+            upward[rows] = up
+            activated[rows] = gelu_to(up).astype(HALF)
+            return mm(activated[rows], w_down[...])
+
+        for i in range(2):
+            rows = rows_at(i)
+            out_copy(i).wait_recv()
+            after = attended[rows] + part_got[rows].astype(FLOAT)
+            attended[rows] = after
+            second[rows] = norm_to(after, vec[4:5], vec[5:6]).astype(HALF)
+            second_copy(i).start()
+        for i in range(2):
+            rows = rows_at(i)
+            encoded[rows] = feed(i) + attended[rows] + vec[6:7]
+            second_copy(i).wait_recv()
+            part_sent[rows_at(2 + i)] = feed(2 + i).astype(HALF)
+            down_copy(i).start()
+        for i in range(2):
+            rows = rows_at(i)
+            down_copy(i).wait_recv()
+            after = encoded[rows] + part_got[rows_at(2 + i)].astype(FLOAT)
+            encoded[rows] = after
+            low = norm_to(after, vec[7:8], vec[8:9]).astype(HALF)
+            final_enc[rows] = low
+            reduced_own[i] = mm(low, e2d_w[...])
+            for column in range(2):
+
+                @pl.when(x == column)
+                def _():
+                    for one in give(column, i):
+                        one.start()
+
+        for i in range(2):
+            normed_copy(i).wait_send()
+            out_copy(i).wait_send()
+            second_copy(i).wait_send()
+            down_copy(i).wait_send()
+        for column in range(2):
+
+            @pl.when(x == column)
+            def _():
+                for i in range(2):
+                    for one in give(column, i):
+                        one.wait_send()
+
+    @pl.when((z == HOST) & (x == 0))
+    def _():
+        mine = pltpu.make_async_copy(reduced_own.at[1], reduced, local_sem)
+        mine.start()
+        mine.wait()
+
+    for row in range(4):
+        for side in range(2):
+            if (row, side) != (HOST, 0):
+
+                @pl.when((z == row) & (x == side))
+                def _():
+                    key = 8 + 2 * (row % 2) + side
+                    links.copy(key, reduced_own.at[row % 2], reduced, at(HOST, row // 2)).wait_recv()
+
+
+def encoder_forward(number, shown_own, places, weights):
+    patch_pieces, mats, e2d_w, vec = weights
+    vmem = pl.BlockSpec(memory_space=pltpu.VMEM)
+    stored = [
+        ((OWN, D), FLOAT),
+        ((ALL, D), HALF),
+        ((ALL, 3 * D // 2), HALF),
+        ((ALL, D // 2), HALF),
+        ((OWN, D), FLOAT),
+        ((ALL, D), HALF),
+        ((ALL, FF // 2), FLOAT),
+        ((ALL, FF // 2), HALF),
+        ((OWN, D), FLOAT),
+        ((OWN, D), HALF),
+    ]
+    shapes = [((VISIBLE, DD), FLOAT)] + stored
+    out = pl.pallas_call(
+        encoder_forward_kernel,
+        name="encoder_forward",
+        out_shape=[jax.ShapeDtypeStruct(*one) for one in shapes],
+        in_specs=[vmem] * 11,
+        out_specs=[vmem] * len(shapes),
+        scratch_shapes=[
+            pltpu.VMEM((ALL, D), HALF),
+            pltpu.VMEM((ALL, D), HALF),
+            pltpu.VMEM((2, VISIBLE, DD), FLOAT),
+            pltpu.SemaphoreType.DMA((12,)),
+            pltpu.SemaphoreType.DMA((12,)),
+            pltpu.SemaphoreType.DMA,
+        ],
+        compiler_params=pltpu.CompilerParams(
+            collective_id=number, has_side_effects=True, vmem_limit_bytes=56 << 20
+        ),
+    )(shown_own, places, *patch_pieces, *mats, e2d_w, vec)
+    return out[0], out[1:]
+
+
+def encoder_backward_kernel(
+    picked, shown, w_qkv, w_out, w_up, w_down, e2d_w, vec,
+    stream, normed, joined, blended, attended, second, upward, activated, encoded, final_enc,
+    qkv_out, square_out, up_out, patch_out, e2d_out, vec_out,
+    picks_got, low, grad_up_in, mid, grad_blend, grad_joined, part_sent, part_got, own_rows_grad, own_part,
+    emb_low, emb_got, down_grad, up_grad, out_grad, qkv_grad, patch_low, patch_mid, patch_high, e2d_part, e2d_got, e2d_grad,
+    vec_part, vec_got, send_sem, recv_sem, local_sem,
+):
+    g, z, x = lax.axis_index("group"), lax.axis_index("dp"), lax.axis_index("tensor")
+    barrier = pltpu.get_barrier_semaphore()
+    links = Links(send_sem, recv_sem)
+
+    def at(row, column):
+        return (g, row, column)
+
+    def greet(peer):
+        pl.semaphore_signal(barrier, inc=1, device_id=peer, device_id_type=MESH_ID)
+
+    @pl.when(z != HOST)
+    def _():
+        greet(at(HOST, x))
+        pl.semaphore_wait(barrier, 1)
+
+    for column in range(2):
+
+        @pl.when((z == HOST) & (x == column))
+        def _():
+            greet(at(HOST, 1 - column))
+            for row in (2 * column, 2 * column + 1):
+                if row != HOST:
+                    for side in range(2):
+                        greet(at(row, side))
+            pl.semaphore_wait(barrier, 4)
+
+    def pick_copy(row, side):
+        return links.copy((row % 2) * 2 + side, picked, picks_got.at[row % 2, side], at(HOST, row // 2))
+
+    for row in range(4):
+        for side in range(2):
+            if (row, side) != (HOST, 0):
+
+                @pl.when((z == row) & (x == side))
+                def _():
+                    pick_copy(row, side).start()
+
+    numbers = iter(range(4, 64))
+    low_number = [next(numbers), next(numbers)]
+    second_number = [next(numbers), next(numbers)]
+    mid_number = [next(numbers), next(numbers)]
+    normed_number = [next(numbers), next(numbers)]
+    emb_number = [next(numbers), next(numbers)]
+    e2d_number, vec_number = next(numbers), next(numbers)
+
+    def row_copies(numbers_two, ref):
+        return [
+            links.copy(numbers_two[i], ref.at[rows_at(i)], ref.at[rows_at(2 + i)], at(HOST, 1 - x)) for i in range(2)
+        ]
+
+    def part_copies(numbers_two, first):
+        return [
+            links.copy(
+                numbers_two[i], part_sent.at[rows_at(first + i)], part_got.at[rows_at(first + i)], at(HOST, 1 - x)
+            )
+            for i in range(2)
+        ]
+
+    out_rows, up_rows, down_rows = 288, 672, 1248
+    down_far = links.copy(next(numbers), down_grad.at[pl.ds(down_rows, 288)], square_out.at[pl.ds(0, 288)], at(LAST, x))
+    down_near = links.copy(next(numbers), down_grad.at[pl.ds(0, down_rows)], square_out, at(2, x))
+    up_near = links.copy(next(numbers), up_grad.at[pl.ds(up_rows, 96)], up_out.at[pl.ds(0, 96)], at(2, x))
+    out_near = links.copy(
+        next(numbers), out_grad.at[pl.ds(0, out_rows)], square_out.at[pl.ds(0, out_rows)], at(0, x)
+    )
+    qkv_near = links.copy(next(numbers), qkv_grad, qkv_out, at(0, x))
+    patch_one = links.copy(next(numbers), patch_low, patch_out, at(0, x))
+    patch_two = links.copy(next(numbers), patch_high, patch_out.at[pl.ds(0, 192)], at(2, x))
+    e2d_near = links.copy(next(numbers), e2d_grad, e2d_out, at(2, x))
+    vec_far = links.copy(next(numbers), vec_part, vec_out, at(LAST, x))
+
+    def tall_product(left, right, target, step):
+        def body(t, carry):
+            columns = pl.ds(pl.multiple_of(t * step, step), step)
+            target[columns] = mm_tn(left[:, columns], right[...]).astype(HALF)
+            return carry
+
+        lax.fori_loop(0, target.shape[0] // step, body, 0)
+
+    @pl.when(z == HOST)
+    def _():
+        low_sent, mid_sent = row_copies(low_number, low), row_copies(mid_number, mid)
+        second_sent, normed_sent = part_copies(second_number, 0), part_copies(normed_number, 2)
+        emb_sent = [
+            links.copy(
+                emb_number[i],
+                emb_low.at[1 - x, rows_at(i)],
+                emb_got.at[rows_at(i)],
+                at(HOST, 1 - x),
+            )
+            for i in range(2)
+        ]
+        e2d_sent = links.copy(e2d_number, e2d_part.at[1 - x], e2d_got, at(HOST, 1 - x))
+        vec_sent = links.copy(vec_number, vec_part, vec_got, at(HOST, 1 - x))
+
+        vec_part[...] = jnp.zeros_like(vec_part)
+
+        def count(row, value):
+            vec_part[row : row + 1] += value
+
+        @pl.when(x == 0)
+        def _():
+            mine = pltpu.make_async_copy(picked, picks_got.at[1, 0], local_sem.at[0])
+            mine.start()
+            mine.wait()
+
+        for clip in range(2):
+            for side in range(2):
+                waiting = links.copy(clip * 2 + side, picked, picks_got.at[clip, side], at(HOST, 0))
+                if clip == HOST % 2 and side == 0:
+
+                    @pl.when(x == 1)
+                    def _():
+                        waiting.wait_recv()
+
+                else:
+                    waiting.wait_recv()
+        reduced_low = []
+        for i in range(2):
+            rows = rows_at(i)
+            one = picks_got[i, 0] + picks_got[i, 1]
+            reduced_low.append(one)
+            grad, gain, bias = norm_from(encoded[rows], vec[7:8], mm_nt(one, e2d_w[...]))
+            count(7, gain)
+            count(8, bias)
+            count(6, jnp.sum(grad, 0, keepdims=True))
+            own_rows_grad[rows] = grad
+            low[rows] = grad.astype(HALF)
+            low_sent[i].start()
+        whole_low = jnp.concatenate(reduced_low, 0)
+        product = mm_tn(final_enc[...], whole_low).astype(HALF)
+        e2d_part[0] = product[: D // 2]
+        e2d_part[1] = product[D // 2 :]
+        e2d_sent.start()
+
+        def feed_back(c):
+            rows = rows_at(c)
+            grad_up_in[rows] = (mm_nt(low[rows], w_down[...]) * gelu_slope(upward[rows])).astype(HALF)
+            return mm_nt(grad_up_in[rows], w_up[...])
+
+        for i in range(2):
+            own_part[rows_at(i)] = feed_back(i)
+            low_sent[i].wait_recv()
+            part_sent[rows_at(i)] = feed_back(2 + i).astype(HALF)
+            second_sent[i].start()
+        tall_product(activated, low, down_grad, 256)
+        down_far.start()
+        down_near.start()
+        for i in range(2):
+            rows = rows_at(i)
+            second_sent[i].wait_recv()
+            total = own_part[rows] + part_got[rows].astype(FLOAT)
+            grad, gain, bias = norm_from(attended[rows], vec[4:5], total)
+            count(4, gain)
+            count(5, bias)
+            grad = grad + own_rows_grad[rows]
+            count(3, jnp.sum(grad, 0, keepdims=True))
+            own_rows_grad[rows] = grad
+            mid[rows] = grad.astype(HALF)
+            mid_sent[i].start()
+        e2d_sent.wait()
+        e2d_grad[...] = (e2d_part[x].astype(FLOAT) + e2d_got[...].astype(FLOAT)).astype(HALF)
+        e2d_near.start()
+
+        def attend_back(c):
+            rows = rows_at(c)
+            width = D // 2
+            grad_blend[...] = mm_nt(mid[rows], w_out[...]).astype(HALF)
+            for h in range(width // HDIM):
+                column = h * HDIM
+                queries = joined[rows, column : column + HDIM]
+                keys = joined[rows, width + column : width + column + HDIM]
+                values = joined[rows, 2 * width + column : 2 * width + column + HDIM]
+                grads = grad_blend[:, column : column + HDIM]
+                scores = mm_nt(queries, keys) * HDIM**-0.5
+                weights = jnp.exp(scores - jnp.max(scores, -1, keepdims=True))
+                probs = weights * (1.0 / jnp.sum(weights, -1, keepdims=True))
+                grad_values = mm_tn(probs.astype(HALF), grads)
+                grad_probs = mm_nt(grads, values)
+                grad_scores = (
+                    probs * (grad_probs - jnp.sum(probs * grad_probs, -1, keepdims=True))
+                ).astype(HALF)
+                for third, value in enumerate(
+                    (mm(grad_scores, keys) * HDIM**-0.5, mm_tn(grad_scores, queries) * HDIM**-0.5, grad_values)
+                ):
+                    start = third * width + column
+                    grad_joined[rows, start : start + HDIM] = value.astype(HALF)
+            return mm_nt(grad_joined[rows], w_qkv[...])
+
+        for i in range(2):
+            own_part[rows_at(i)] = attend_back(i)
+            mid_sent[i].wait_recv()
+            part_sent[rows_at(2 + i)] = attend_back(2 + i).astype(HALF)
+            normed_sent[i].start()
+        tall_product(second, grad_up_in, up_grad, 256)
+        up_near.start()
+        tall_product(blended, mid, out_grad, 128)
+        out_near.start()
+        for i in range(2):
+            rows = rows_at(i)
+            normed_sent[i].wait_recv()
+            total = own_part[rows] + part_got[rows_at(2 + i)].astype(FLOAT)
+            grad, gain, bias = norm_from(stream[rows], vec[1:2], total)
+            count(1, gain)
+            count(2, bias)
+            grad = grad + own_rows_grad[rows]
+            count(0, jnp.sum(grad, 0, keepdims=True))
+            grad_low = grad.astype(HALF)
+            emb_low[0, rows] = grad_low[:, : D // 2]
+            emb_low[1, rows] = grad_low[:, D // 2 :]
+            emb_sent[i].start()
+        vec_sent.start()
+        tall_product(normed, grad_joined, qkv_grad, 256)
+        qkv_near.start()
+        for one in emb_sent:
+            one.wait()
+        columns = jnp.concatenate([emb_low[x], emb_got[...]], 0)
+        for start, depth, target in zip(SPAN, DEPTH, (patch_low, patch_mid, patch_high)):
+            target[...] = mm_tn(shown[:, start : start + depth], columns).astype(HALF)
+        patch_one.start()
+        patch_two.start()
+        vec_sent.wait()
+        vec_part[...] += vec_got[...]
+        vec_far.start()
+        mine = [
+            pltpu.make_async_copy(out_grad.at[pl.ds(out_rows, 96)], square_out.at[pl.ds(0, 96)], local_sem.at[1]),
+            pltpu.make_async_copy(up_grad.at[pl.ds(0, up_rows)], up_out, local_sem.at[2]),
+            pltpu.make_async_copy(patch_mid, patch_out, local_sem.at[3]),
+        ]
+        for one in mine:
+            one.start()
+        for one in low_sent + mid_sent + second_sent + normed_sent:
+            one.wait_send()
+        for one in (down_far, down_near, up_near, out_near, qkv_near, patch_one, patch_two, e2d_near, vec_far):
+            one.wait_send()
+        for one in mine:
+            one.wait()
+
+    for row in range(4):
+        for side in range(2):
+            if (row, side) != (HOST, 0):
+
+                @pl.when((z == row) & (x == side))
+                def _():
+                    pick_copy(row, side).wait_send()
+
+    for row, ones in ((0, (out_near, qkv_near, patch_one)), (2, (down_near, up_near, patch_two, e2d_near)), (LAST, (down_far, vec_far))):
+
+        @pl.when(z == row)
+        def _():
+            for one in ones:
+                one.wait_recv()
+
+
+def encoder_backward(number, picked, shown, weights, stored):
+    _, mats, e2d_w, vec = weights
+    vmem = pl.BlockSpec(memory_space=pltpu.VMEM)
+    anywhere = pl.BlockSpec(memory_space=pl.ANY)
+    shapes = [
+        ((D, 3 * D // 2), HALF),
+        ((1248, D), HALF),
+        ((672, FF // 2), HALF),
+        ((704, D // 2), HALF),
+        ((D // 2, DD), HALF),
+        ((16, D), FLOAT),
+    ]
+    scratch = [
+        ((2, 2, VISIBLE, DD), HALF),
+        ((ALL, D), HALF),
+        ((ALL, FF // 2), HALF),
+        ((ALL, D), HALF),
+        ((VISIBLE, D // 2), HALF),
+        ((ALL, 3 * D // 2), HALF),
+        ((ALL, D), HALF),
+        ((ALL, D), HALF),
+        ((OWN, D), FLOAT),
+        ((OWN, D), FLOAT),
+        ((2, OWN, D // 2), HALF),
+        ((OWN, D // 2), HALF),
+        ((FF // 2, D), HALF),
+        ((D, FF // 2), HALF),
+        ((D // 2, D), HALF),
+        ((D, 3 * D // 2), HALF),
+        ((704, D // 2), HALF),
+        ((704, D // 2), HALF),
+        ((192, D // 2), HALF),
+        ((2, D // 2, DD), HALF),
+        ((D // 2, DD), HALF),
+        ((D // 2, DD), HALF),
+        ((16, D), FLOAT),
+        ((16, D), FLOAT),
+    ]
+    return pl.pallas_call(
+        encoder_backward_kernel,
+        name="encoder_backward",
+        out_shape=[jax.ShapeDtypeStruct(*one) for one in shapes],
+        in_specs=[vmem] * 18,
+        out_specs=[anywhere] * len(shapes),
+        scratch_shapes=[pltpu.VMEM(*one) for one in scratch]
+        + [pltpu.SemaphoreType.DMA((28,)), pltpu.SemaphoreType.DMA((28,)), pltpu.SemaphoreType.DMA((4,))],
+        compiler_params=pltpu.CompilerParams(
+            collective_id=number, has_side_effects=True, vmem_limit_bytes=60 << 20
+        ),
+    )(picked, shown, *mats, e2d_w, vec, *stored)
+
+
+def decoder_round(tokens, pixels_low, counted, weights):
+    own, other, head_w, vec, head_b = weights
+    count = pixels_low.shape[0]
+    width = DD // 2
+    normed = layer_norm(tokens, vec[2], vec[3]).astype(HALF)
+    joined = mm(normed, own[0]).astype(HALF)
+    queries, keys, values = [joined[:, i * width : (i + 1) * width] for i in range(3)]
+    blended, totals = attn_forward(queries, keys, values)
+    blend_own = blended[:count]
+    blend_other = swap(blended[count:])
+    stream = tokens[:count]
+    attended = mm(blend_own, own[1]) + mm(blend_other, other[1]) + stream + vec[4]
+    second = layer_norm(attended, vec[5], vec[6]).astype(HALF)
+    w_up = jnp.concatenate([own[2], other[2]], 1)
+    w_down = jnp.concatenate([own[3], other[3]], 0)
+    upward = mm(second, w_up)
+    activated = gelu_exact(upward).astype(HALF)
+    decoded = mm(activated, w_down) + attended + vec[7]
+    final_low = layer_norm(decoded, vec[8], vec[9]).astype(HALF)
+    predicted = mm(final_low, head_w) + head_b
+    pixels = pixels_low.astype(FLOAT)
+    center = jnp.mean(pixels, -1, keepdims=True)
+    spread = jnp.mean((pixels - center) ** 2, -1, keepdims=True)
+    differ = predicted - (pixels - center) * lax.rsqrt(spread + 1e-06)
+    loss = jnp.sum(jnp.mean(differ**2, -1) * counted)
+    grad_pred = 2.0 / PATCH * differ * counted[:, None]
+    pred_low = grad_pred.astype(HALF)
+    head_grad = mm_tn(final_low, pred_low)
+    head_b_grad = jnp.sum(grad_pred, 0)
+    grad_out, gain_end, bias_end = norm_back(decoded, vec[8], vec[9], mm_nt(pred_low, head_w))
+    grad_low = grad_out.astype(HALF)
+    down_grad = mm_tn(activated, grad_low)
+    down_bias = jnp.sum(grad_out, 0)
+    _, gelu_pull = jax.vjp(gelu_exact, upward)
+    grad_up_in = gelu_pull(mm_nt(grad_low, w_down))[0].astype(HALF)
+    up_grad = mm_tn(second, grad_up_in)
+    grad_att, gain_two, bias_two = norm_back(attended, vec[5], vec[6], mm_nt(grad_up_in, w_up))
+    grad_att = grad_att + grad_out
+    out_bias = jnp.sum(grad_att, 0)
+    mid = grad_att.astype(HALF)
+    grad_other = swap(mm_nt(mid, other[1]).astype(HALF))
+    grad_blend = jnp.concatenate([mm_nt(mid, own[1]).astype(HALF), grad_other], 0)
+    out_own, out_other = mm_tn(blend_own, mid), mm_tn(blend_other, mid)
+    side = lax.axis_index("tensor")
+    head_cols = PATCH // 2
+    wide_other = jnp.concatenate(
+        [
+            up_grad[:, DFF // 2 :].astype(HALF),
+            lax.dynamic_slice_in_dim(head_grad, (1 - side) * head_cols, head_cols, 1).astype(HALF),
+        ],
+        1,
+    )
+    tall_other = jnp.concatenate([down_grad[DFF // 2 :], out_other], 0).astype(HALF)
+    wide = jnp.concatenate(
+        [up_grad[:, : DFF // 2], lax.dynamic_slice_in_dim(head_grad, side * head_cols, head_cols, 1)], 1
+    ) + swap(wide_other)
+    tall = jnp.concatenate([down_grad[: DFF // 2], out_own], 0) + swap(tall_other)
+    grad_joined = attn_backward(queries, keys, values, grad_blend, totals)
+    joined_other = swap(grad_joined[count:])
+    qkv_grad = mm_tn(normed, grad_joined)
+    grad_normed = mm_nt(grad_joined[:count], own[0]) + mm_nt(joined_other, other[0])
+    grad_in, gain_one, bias_one = norm_back(stream, vec[2], vec[3], grad_normed)
+    grad_in = grad_in + grad_att
+    vec_rows = [gain_one, bias_one, out_bias, gain_two, bias_two, down_bias, gain_end, bias_end]
+    return loss, grad_in, (wide, tall, qkv_grad), vec_rows, head_b_grad
+
+
+def tree_sum(part):
+    z = lax.axis_index("dp")
+    low = part.astype(HALF)
+    part = part + hop_both(low, (0, 1), (2, 3)).astype(FLOAT)
+    return part + hop_both(part.astype(HALF), (1, 3)).astype(FLOAT)
+
+
+def hosted_round(
+    patches,
+    visible,
+    frames_valid,
+    clip_valid,
+    rep_weights,
+    ten_weights,
+    rep_m,
+    rep_v,
+    ten_m,
+    ten_v,
+    rep_outer,
+    ten_outer,
+):
+    side = lax.axis_index("tensor")
+    z = lax.axis_index("dp")
+    half_rows = TUBES // 2
+    tube_ids = (jnp.arange(TUBES) + side * half_rows) % TUBES
+    ids_one = hop(visible[:, 0, 0], ((0, 0), (HOST, 0)), ((2, 1), (HOST, 1)))
+    ids_two = hop(visible[:, 0, 0], ((3, 1), (HOST, 1)))
+    ids_two = jnp.where(side == 0, visible[:, 0, 0], ids_two)
+    dec_places = sinus_at(tube_ids, DD)
+    rep_master, ten_master = rep_weights, ten_weights[0]
+    rep_first, rep_second = rep_m[0], rep_v[0]
+    ten_first, ten_second = ten_m[0, 0], ten_v[0, 0]
+    quarter = ten_master.shape[0]
+    rep_quarter = rep_master.shape[0]
+    rest = ENC_SIZE - 3 * quarter
+    shown_steps = []
+    for s in range(STEPS):
+        picks = (visible[s, 0, 0][:, None] == jnp.arange(TUBES)[None, :]).astype(HALF)
+        rows = mm(picks, patches[s, 0, 0]).astype(HALF)
+        cuts = (0, rep_quarter // D, 2 * (rep_quarter // D), PATCH)
+        rows = jnp.concatenate(
+            [
+                jnp.pad(rows[:, cuts[i] : cuts[i + 1]], ((0, 0), (0, room - cuts[i + 1] + cuts[i])))
+                for i, room in enumerate((768, 768, 256))
+            ],
+            1,
+        )
+        one = hop(rows, ((0, 0), (HOST, 0)), ((2, 1), (HOST, 1)))
+        two = hop(rows, ((3, 1), (HOST, 1)))
+        own = jnp.concatenate([one, jnp.where(side == 0, rows, two)], 0)
+        shown_steps.append(jnp.concatenate([own, swap(own, HOST)], 0))
+    loss_list, count_list, norm_list = [], [], []
+    for s in range(STEPS):
+        enc_weights, dec_weights = hosted_weights(rep_master, ten_master, s == 0)
+        ids = visible[s, 0, 0]
+        picks = tube_ids[:, None] == ids[None, :]
+        shown_here = jnp.any(picks, 1)
+        counted = (
+            jnp.where(shown_here, 0.0, 1.0)
+            * (tube_ids // (TUBES // FRAMES) < frames_valid[s, 0, 0])
+            * (clip_valid[s, 0, 0] == 1)
+        ).astype(FLOAT)[:half_rows]
+        shown = shown_steps[s]
+        vis = ids.shape[0]
+        ids_own = jnp.concatenate([ids_one[s], ids_two[s]])
+        reduced_clip, enc_stored = encoder_forward(3 + s, shown[: 2 * vis], sinus_at(ids_own, D), enc_weights)
+        dec_vec = dec_weights[3]
+        placed = jnp.dot(
+            picks.astype(FLOAT), reduced_clip + dec_vec[0], precision=lax.Precision.HIGHEST
+        )
+        tokens = jnp.where(shown_here[:, None], placed, dec_vec[1]) + dec_places
+        pixels_low = lax.dynamic_slice_in_dim(patches[s, 0, 0], side * half_rows, half_rows, 0)
+        loss, grad_tokens, (wide, tall, qkv_grad), vec_rows, head_b_grad = decoder_round(
+            tokens, pixels_low, counted, dec_weights
+        )
+        shown_own = shown_here[:half_rows, None]
+        e2d_b_grad = jnp.sum(jnp.where(shown_own, grad_tokens, 0.0), 0)
+        mask_grad = jnp.sum(jnp.where(shown_own, 0.0, grad_tokens), 0)
+        picked = mm_tn(picks[:half_rows].astype(HALF), grad_tokens.astype(HALF)).astype(HALF)
+        small = jnp.concatenate(
+            [jnp.stack([e2d_b_grad, mask_grad] + vec_rows).reshape(-1), head_b_grad]
+        )
+        small = small + swap(small)
+        small = small + hop_both(small, (0, 1), (2, 3))
+        small = small + hop_both(small, (1, 3))
+        wide, tall, qkv_sum = tree_sum(wide), tree_sum(tall), tree_sum(qkv_grad)
+        qkv_got, square_got, up_got, patch_got, e2d_got, vec_got = encoder_backward(
+            5 + s, picked, shown, enc_weights, enc_stored
+        )
+        head_rows = (3 * rep_quarter - PATCH_SIZE - E2D_SIZE) // PATCH
+        head_cols = PATCH // 2
+        head_low = wide[:, DFF // 2 :].astype(HALF)
+        head_three = hop_both(head_low[:head_rows], (LAST, 2))
+        head_low = jnp.where(
+            z == LAST, head_low, jnp.concatenate([head_three, jnp.zeros((DD - head_rows, head_cols), HALF)], 0)
+        )
+        head_other = swap(head_low, 2, LAST)
+        head_sum = jnp.concatenate(
+            [jnp.where(side == 0, head_low, head_other), jnp.where(side == 0, head_other, head_low)], 1
+        )
+        patch_cut = rep_quarter // D
+        patch_tail = PATCH - 2 * patch_cut
+        narrow = jnp.concatenate(
+            [patch_got[:192], jnp.where(z == 2, jnp.pad(e2d_got, ((0, 128), (0, 0))), patch_got[192:])], 0
+        )
+        narrow_other = swap(narrow, 0, 1, 2)
+        narrow_low = jnp.where(side == 0, narrow, narrow_other)
+        narrow_high = jnp.where(side == 0, narrow_other, narrow)
+        flats = lambda *parts: jnp.concatenate([one.astype(FLOAT).reshape(-1) for one in parts])
+
+        def patch_rows(count):
+            return jnp.concatenate([narrow_low[:count], narrow_high[:count]], 1)
+
+        def first_owner():
+            return flats(qkv_got, square_got[:288]), flats(patch_rows(patch_cut))
+
+        def second_owner():
+            return flats(square_got[:96], up_got), flats(patch_rows(patch_cut))
+
+        def third_owner():
+            return flats(up_got[:96], square_got), flats(
+                patch_rows(patch_tail),
+                narrow_low[192 : 192 + D // 2],
+                narrow_high[192 : 192 + D // 2],
+                head_sum[:head_rows],
+            )
+
+        def last_owner():
+            return flats(
+                square_got[:288], qkv_sum, tall[DFF // 2 :], wide[:, : DFF // 2], tall[: DFF // 2]
+            ), flats(head_sum[head_rows:], vec_got[:9], small)
+
+        ten_part, rep_part = lax.switch(z, [first_owner, second_owner, third_owner, last_owner])
+        squares = jnp.sum(ten_part * ten_part) + jnp.sum(rep_part * rep_part) / 2
+        square_all, loss_all, count_all = lax.psum((squares, loss, jnp.sum(counted)), ("dp", "tensor"))
+        norm_value = jnp.sqrt(square_all + 1e-30) / count_all
+        factor = jnp.minimum(1.0, CLIP / norm_value) / count_all
+        number = STEP_BEFORE + s + 1
+        rep_master, rep_first, rep_second = adamw(rep_master, rep_first, rep_second, rep_part * factor, number)
+        ten_master, ten_first, ten_second = adamw(ten_master, ten_first, ten_second, ten_part * factor, number)
+        loss_list.append(loss_all)
+        count_list.append(count_all)
+        norm_list.append(norm_value)
+    groups_count = lax.axis_size("group")
+    rep_diff, ten_diff = group_mean(rep_weights - rep_master), group_mean(ten_weights[0] - ten_master)
+    rep_momentum = MOMENTUM * rep_outer + rep_diff
+    ten_momentum = MOMENTUM * ten_outer[0] + ten_diff
+    rep_new = rep_weights - LR_OUT * (rep_diff + MOMENTUM * rep_momentum)
+    ten_new = ten_weights[0] - LR_OUT * (ten_diff + MOMENTUM * ten_momentum)
+    return (
+        jnp.stack(loss_list)[:, None],
+        jnp.stack(count_list)[:, None],
+        jnp.stack(norm_list)[:, None],
+        rep_first[None],
+        rep_second[None],
+        ten_first[None, None],
+        ten_second[None, None],
+        rep_diff,
+        ten_diff[None],
+        rep_momentum,
+        ten_momentum[None],
+        rep_new,
+        ten_new[None],
+    )
+
+
+def group_mean(diff):
+    if lax.axis_size("group") != 4:
+        return lax.psum(diff, "group") / lax.axis_size("group")
+    odd = lax.axis_index("group") % 2 == 1
+    half = diff.shape[0] // 2
+    low, high = diff[:half], diff[half:]
+    part = jnp.where(odd, high, low) + partner(jnp.where(odd, low, high))
+    part_low = part.astype(HALF)
+    far = lax.ppermute(part_low, "group", [(g, g ^ 2) for g in range(4)])
+    total = (part_low.astype(FLOAT) + far.astype(FLOAT)) * 0.25
+    other = partner(total)
+    return jnp.concatenate([jnp.where(odd, other, total), jnp.where(odd, total, other)])
+
+
 def solution(mesh):
     placed = (
         P(None, "group", "dp", None, None),
@@ -428,7 +1719,7 @@
         P("tensor", "dp"),
     )
     return jax.shard_map(
-        on_device,
+        hosted_round if mesh.shape["dp"] == 4 and mesh.shape["tensor"] == 2 and mesh.shape["group"] % 2 == 0 else on_device,
         mesh=mesh,
         in_specs=placed,
         out_specs=(

time: 3380 us -> 1490 us (0.44)
  waiting for transfers between devices: 2000 us -> 80.5 us
  Pallas kernels: 0 us -> 755 us
  other arithmetic: 580 us -> 214 us
  matrix products: 355 us -> 118 us
  local copies, waits for them, and re-layouts: 254 us -> 119 us
  starting transfers between devices: 28.3 us -> 96.8 us
  blocking collectives: 113 us -> 57.4 us
    all_to_all x4 -> x0, waiting for transfers between devices: 894 us -> none  [the longest x2 549 us: on_device(): lax.all_to_all(ten_grad.reshape(owners, -1), 'dp', split_axis=0, concat_a...]
    pallas_call x0 -> x10, Pallas kernels: none -> 755 us  [the longest x2 252 us: encoder_backward(): pl.pallas_call(encoder_backward_kernel, name='encoder_backward', out_shap...]
    all_gather x14 -> x0, waiting for transfers between devices: 607 us -> none  [the longest x2 296 us: on_device(): lax.all_gather(ten_master.astype(HALF), 'dp', axis=0, tiled=True)]
    reduce_sum x40 -> x15, other arithmetic: 326 us -> 24.6 us  [the longest x4 11.3 us: hosted_round(): squares = jnp.sum(ten_part * ten_part) + jnp.sum(rep_part * rep_part) / 2]
    reduce_scatter x16 -> x0, waiting for transfers between devices: 299 us -> none  [rows_sum(): lax.psum_scatter(partial_rows, 'tensor', scatter_dimension=1, tiled=True)]
    dot_general x88 -> x44, matrix products: 355 us -> 118 us  [the longest x14 46.8 us: mm(): return jnp.dot(left, right, preferred_element_type=FLOAT)]
    psum x3 -> x0, waiting for transfers between devices: 205 us -> none  [the longest x2 113 us: on_device(): rep_part = lax.psum(jnp.sum(rep_recv, 0), 'tensor')]
    ppermute x0 -> x48, starting transfers between devices: none -> 96.8 us  [the longest x30 71.4 us: hop(): return lax.ppermute(value, ('dp', 'tensor'), pairs)]
  transfers between devices with their start and end apart: 37 -> 48, of which waited for: 35 -> 10; matrix products, arithmetic and copies ran while one was open for 13% -> 17% of each run, Pallas kernels for 0% -> 35%
where the time goes in v1:
time: 1490 us; the launch traced here: 1480 us
  Pallas kernels  755 us (51%)
  other arithmetic  214 us (14%)
  local copies, waits for them, and re-layouts  119 us (8%)
  matrix products  118 us (8%)
  starting transfers between devices  96.8 us (6%)
  waiting for transfers between devices  80.5 us (5%)
  blocking collectives  57.4 us (4%)
  loops' own time  32.1 us (2%)
    pallas_call x2, Pallas kernels, encoder_backward(): pl.pallas_call(encoder_backward_kernel, name='encoder_backward', out_shap...  252 us
    pallas_call x2, Pallas kernels, hosted_weights(): pl.pallas_call(functools.partial(weights_kernel, shared), name='weights',...  234 us
    pallas_call x2, Pallas kernels, encoder_forward(): pl.pallas_call(encoder_forward_kernel, name='encoder_forward', out_shape=...  126 us
    pallas_call x2, Pallas kernels, attn_backward(): pl.pallas_call(attn_backward_kernel, name='attn_backward', out_shape=jax....  84.4 us
    ppermute x30, starting transfers between devices, hop(): return lax.ppermute(value, ('dp', 'tensor'), pairs)  71.4 us
    psum x2, blocking collectives, hosted_round(): lax.psum((squares, loss, jnp.sum(counted)), ('dp', 'tensor'))  57.4 us
    pallas_call x2, Pallas kernels, attn_forward(): pl.pallas_call(attn_forward_kernel, name='attn_forward', out_shape=(jax.S...  57.3 us
    dot_general x14, matrix products, mm(): return jnp.dot(left, right, preferred_element_type=FLOAT)  46.8 us
  transfers between devices with their start and end apart: 48, of which 10 were waited for; matrix products, arithmetic and copies ran while one was open for 17% of the time, Pallas kernels for 35%

profile of v1, /device:TPU:0, one launch (start us, length us, event | category | flops | bytes accessed | tf_op | source)
XLA Modules:
  0.0 1483.5 jit_solution(2222339408532490957)
XLA Ops:
  11.2 5.8 collective-permute-start
  23.3 8.4 fusion.171
  34.7 25.4 %conditional.4 = (bf16[768,1152]{1,0:T(8,128)(2,1)}, bf16[1248,768]{1,0:T(8,128)(2,1)}, bf16[672,1536]{1,0:T(8,128)(2,1)}, bf16[704,768]{1,0:T(8,128)(2,1)S(1)},...) conditional(s32[]{:T(128)} %clamp.2, (f32[1105920]{0:T(1024)}, ...), branch_computations={%region_1.2_spmd, %region_2.3_spmd, %region_3.4_spmd, %region_4.5_... | conditional | flops 1625088 | bytes 51536120 | solution.py:612
  39.8 4.5 convert_element_type.449
  62.0 87.3 %weights.2 = (bf16[704,768]{1,0:T(8,128)(2,1)}, bf16[192,768]{1,0:T(8,128)(2,1)}, bf16[768,1152]{1,0:T(8,128)(2,1)}, bf16[384,768]{1,0:T(8,128)(2,1)}, bf16[768,...) custom-call(bf16[768,1152]{1,0:T(8,128)(2,1)} %get-tuple-element.317, ...), custom_call_target="tpu_custom_call" | custom-call | tf_op jit(solution)/shard_map/weights/pallas_call | solution.py:870
  159.6 6.6 broadcast_multiply_fusion.1
  170.3 6.7 broadcast_multiply_fusion
  191.1 8.3 fusion.61
  204.2 72.3 %encoder_forward.2 = (f32[160,384]{1,0:T(8,128)}, f32[320,768]{1,0:T(8,128)}, bf16[640,768]{1,0:T(8,128)(2,1)}, bf16[640,1152]{1,0:T(8,128)(2,1)}, bf16[640,384]...) custom-call(bf16[320,1792]{1,0:T(8,128)(2,1)} %pad_maximum_fusion.13, ...), custom_call_target="tpu_custom_call" | custom-call | tf_op jit(solution)/shard_map/encoder_forward/pallas_call | solution.py:1124
  276.6 11.9 fusion.179
  292.3 28.6 %attn_forward.2 = (bf16[1568,192]{1,0:T(8,128)(2,1)S(1)}, f32[3,7,224]{2,1,0:T(8,128)S(1)}) custom-call(bf16[1568,192]{1,0:T(8,128)(2,1)S(1)} %get-tuple-element.649.q_ref, bf16[1568,192]{1,0:T(8,128)(2,1)S(1)} %get-tuple-element.648.k_ref, bf16[1568,192]{1,0:T(8,128)(2,1)S(1)} %get-tuple-element.647.v_ref), custom_call_target="tpu_custom_call" | custom-call | flops 1888223232 | bytes 2408448 | tf_op jit(solution)/shard_map/attn_forward/pallas_call | solution.py:445
  321.0 5.6 collective-permute-start.4
  330.9 3.9 collective-permute-done.4
  336.3 11.2 multiply_convert_fusion.1
  389.8 42.3 %attn_backward.2 = bf16[1568,576]{1,0:T(8,128)(2,1)S(1)} custom-call(bf16[1568,192]{1,0:T(8,128)(2,1)S(1)} %get-tuple-element.649.q_ref, bf16[1568,192]{1,0:T(8,128)(2,1)S(1)} %get-tuple-element.648.k_ref, bf16[1568,192]{1,0:T(8,128)(2,1)S(1)} %get-tuple-element.647.v_ref, bf16[1568,192]{1,0:T(8,128)(2,1)S(1)} %pad_maximum_fusion.15.g_ref, ...), custom_call_target="tpu_custom_call" | custom-call | flops 4720558080 | bytes 4214784 | tf_op jit(solution)/shard_map/attn_backward/pallas_call | solution.py:477
  433.7 14.9 %collective-permute-start.16 = (bf16[384,576]{0,1:T(8,128)(2,1)S(1)}, bf16[384,576]{0,1:T(8,128)(2,1)S(1)}, u32[]{:S(2)}, u32[]{:S(2)}) collective-permute-start(bf16[384,576]{0,1:T(8,128)(2,1)S(1)} %get-tuple-element.690), channel_id=1, source_target_pairs={{0,2},{1,3},{4,6},{5,7},{8,10},{9,11},{12,14},{13,15},{16,18},{17,... | collective-permute-start | bytes 1327112 | tf_op jit(solution)/shard_map/ppermute | solution.py:501
  456.9 5.2 collective-permute-start.19
  474.0 21.5 %collective-permute-done.12 = bf16[384,1536]{1,0:T(8,128)(2,1)S(1)} collective-permute-done((bf16[384,1536]{1,0:T(8,128)(2,1)S(1)}, bf16[384,1536]{1,0:T(8,128)(2,1)S(1)}, u32[]{:S(2)}, u32[]{:S(2)}) %collective-permute-start.12) | collective-permute-done | bytes 1179680 | tf_op jit(solution)/shard_map/ppermute | solution.py:501
  500.5 134.1 %encoder_backward.2 = (bf16[768,1152]{1,0:T(8,128)(2,1)}, bf16[1248,768]{1,0:T(8,128)(2,1)}, bf16[672,1536]{1,0:T(8,128)(2,1)}, bf16[704,384]{1,0:T(8,128)(2,1)}...) custom-call(bf16[160,384]{1,0:T(8,128)(2,1)} %convolution_convert_fusion.9.picked, ...), custom_call_target="tpu_custom_call" | custom-call | tf_op jit(solution)/shard_map/encoder_backward/pallas_call | solution.py:1445
  667.9 24.4 %conditional.5 = (f32[1105920]{0:T(1024)}, f32[519168]{0:T(1024)S(1)}, f32[]{:T(128)}, f32[]{:T(128)}) conditional(s32[]{:T(128)} %clamp.2, (bf16[768,1152]{1,0:T(8,128)(2,1)}, bf16[1248,768]{1,0:T(8,128)(2,1)}, bf16[704,384]{1,0:T(8,128)(2,1)S(1)}, bf16[704,384]{1,0:T(8,128)(2,1)S(1)}) %tuple.89, ...), branch_computations={%region_39.42_spmd, %region_42.45_spmd, %region_45.48_spmd, %regio... | conditional | flops 12392447 | bytes 81952128 | solution.py:1658
  673.6 4.4 multiply_reduce_fusion
  693.0 23.8 %all-reduce.27 = (f32[]{:T(128)}, f32[]{:T(128)}) all-reduce(f32[]{:T(128)} %get-tuple-element.562, f32[]{:T(128)S(6)} %add.624), channel_id=1, replica_groups=mesh['group'=4,'dp'=4,'tensor'=2] {'dp','tensor'}, use_global_device_ids=true, to_apply=%region_52.53 | all-reduce | flops 2 | bytes 16 | tf_op jit(solution)/shard_map/psum | solution.py:1660
  718.9 7.9 multiply_subtract_fusion.1
  729.7 23.5 %conditional.6 = (bf16[768,1152]{1,0:T(8,128)(2,1)}, bf16[1248,768]{1,0:T(8,128)(2,1)}, bf16[672,1536]{1,0:T(8,128)(2,1)}, bf16[704,768]{1,0:T(8,128)(2,1)S(1)},...) conditional(s32[]{:T(128)} %clamp.2, (f32[1105920]{0:T(1024)S(1)}, ...), branch_computations={%region_54.55_spmd, %region_55.56_spmd, %region_56.57_spmd, %regio... | conditional | flops 1625088 | bytes 39592128 | solution.py:612
  731.2 4.5 convert_element_type.474
  754.1 147.1 %weights.3 = (bf16[704,768]{1,0:T(8,128)(2,1)}, bf16[192,768]{1,0:T(8,128)(2,1)}, bf16[768,1152]{1,0:T(8,128)(2,1)}, bf16[384,768]{1,0:T(8,128)(2,1)}, bf16[768,...) custom-call(bf16[768,1152]{1,0:T(8,128)(2,1)} %get-tuple-element.371, ...), custom_call_target="tpu_custom_call" | custom-call | tf_op jit(solution)/shard_map/weights/pallas_call | solution.py:870
  905.3 53.8 %encoder_forward.3 = (f32[160,384]{1,0:T(8,128)}, f32[320,768]{1,0:T(8,128)}, bf16[640,768]{1,0:T(8,128)(2,1)}, bf16[640,1152]{1,0:T(8,128)(2,1)}, bf16[640,384]...) custom-call(bf16[320,1792]{1,0:T(8,128)(2,1)} %pad_maximum_fusion.14, ...), custom_call_target="tpu_custom_call" | custom-call | tf_op jit(solution)/shard_map/encoder_forward/pallas_call | solution.py:1124
  959.2 11.9 fusion.183
  975.1 28.7 %attn_forward.3 = (bf16[1568,192]{1,0:T(8,128)(2,1)S(1)}, f32[3,7,224]{2,1,0:T(8,128)S(1)}) custom-call(bf16[1568,192]{1,0:T(8,128)(2,1)S(1)} %get-tuple-element.646.q_ref, bf16[1568,192]{1,0:T(8,128)(2,1)S(1)} %get-tuple-element.645.k_ref, bf16[1568,192]{1,0:T(8,128)(2,1)S(1)} %get-tuple-element.644.v_ref), custom_call_target="tpu_custom_call" | custom-call | flops 1888223232 | bytes 2408448 | tf_op jit(solution)/shard_map/attn_forward/pallas_call | solution.py:445
  1004.6 4.1 collective-permute-start.24
  1018.1 11.2 multiply_convert_fusion
  1039.5 4.4 add_convert_fusion
  1076.9 42.1 %attn_backward.3 = bf16[1568,576]{1,0:T(8,128)(2,1)S(1)} custom-call(bf16[1568,192]{1,0:T(8,128)(2,1)S(1)} %get-tuple-element.646.q_ref, bf16[1568,192]{1,0:T(8,128)(2,1)S(1)} %get-tuple-element.645.k_ref, bf16[1568,192]{1,0:T(8,128)(2,1)S(1)} %get-tuple-element.644.v_ref, bf16[1568,192]{1,0:T(8,128)(2,1)S(1)} %pad_maximum_fusion.16.g_ref, ...), custom_call_target="tpu_custom_call" | custom-call | flops 4720558080 | bytes 4214784 | tf_op jit(solution)/shard_map/attn_backward/pallas_call | solution.py:477
  1122.0 6.8 collective-permute-start.34
  1134.0 5.5 collective-permute-done.34
  1144.6 17.2 %collective-permute-done.30 = bf16[384,1536]{1,0:T(8,128)(2,1)S(1)} collective-permute-done((bf16[384,1536]{1,0:T(8,128)(2,1)S(1)}, bf16[384,1536]{1,0:T(8,128)(2,1)S(1)}, u32[]{:S(2)}, u32[]{:S(2)}) %collective-permute-start.30) | collective-permute-done | bytes 1179680 | tf_op jit(solution)/shard_map/ppermute | solution.py:501
  1166.9 118.2 %encoder_backward.3 = (bf16[768,1152]{1,0:T(8,128)(2,1)}, bf16[1248,768]{1,0:T(8,128)(2,1)}, bf16[672,1536]{1,0:T(8,128)(2,1)}, bf16[704,384]{1,0:T(8,128)(2,1)}...) custom-call(bf16[160,384]{1,0:T(8,128)(2,1)} %convolution_convert_fusion.8.picked, ...), custom_call_target="tpu_custom_call" | custom-call | tf_op jit(solution)/shard_map/encoder_backward/pallas_call | solution.py:1445
  1316.6 28.0 %conditional.7 = (f32[1105920]{0:T(1024)}, f32[519168]{0:T(1024)}, f32[]{:T(128)}, f32[]{:T(128)}) conditional(s32[]{:T(128)} %clamp.2, (bf16[768,1152]{1,0:T(8,128)(2,1)}, bf16[1248,768]{1,0:T(8,128)(2,1)}, bf16[704,384]{1,0:T(8,128)(2,1)S(1)}, bf16[704,384]{1,0:T(8,128)(2,1)S(1)}) %tuple.94, ...), branch_computations={%region_93.96_spmd, %region_96.99_spmd, %region_99.102_spmd, %regi... | conditional | flops 12392447 | bytes 74874192 | solution.py:1658
  1320.7 4.3 reshape.899
  1325.1 4.6 multiply_reduce_fusion.8
  1345.2 33.6 %all-reduce.26 = (f32[1]{0:T(128)}, f32[1]{0:T(128)}, f32[]{:T(128)}, f32[]{:T(128)}) all-reduce(f32[1]{0:T(128)} %bitcast.20, f32[1]{0:T(128)} %bitcast.8, f32[]{:T(128)} %get-tuple-element.559, f32[]{:T(128)S(6)} %add.675), channel_id=1, replica_groups=mesh['group'=4,'dp'=4,'tensor'=2] {'dp','tensor'}, use_global_device_ids=true, to_apply=%region_68.69 | all-reduce | flops 4 | bytes 32 | tf_op jit(solution)/shard_map/psum | solution.py:1660
  1380.9 8.2 subtract_subtract_fusion.1
  1389.4 11.4 subtract_subtract_fusion
  1402.6 3.9 slice_select_fusion
  1411.6 3.7 collective-permute-done.43
  1419.9 25.0 %collective-permute-done.46 = bf16[552960]{0:T(1024)(128)(2,1)S(1)} collective-permute-done((bf16[552960]{0:T(1024)(128)(2,1)S(1)}, bf16[552960]{0:T(1024)(128)(2,1)S(1)}, u32[]{:S(2)}, u32[]{:S(2)}) %collective-permute-start.46) | collective-permute-done | bytes 1105952 | tf_op jit(solution)/shard_map/ppermute | solution.py:1700
  1450.1 4.0 pad_maximum_fusion.4
  1454.1 29.2 %multiply_subtract_fusion = (f32[1,1105920]{1,0:T(1,128)}, f32[1,1105920]{1,0:T(1,128)}) fusion(f32[1,1105920]{1,0:T(1,128)S(1)} %bitcast.132, f32[1,552960]{1,0:T(1,128)S(1)} %bitcast.140, f32[1,552960]{1,0:T(1,128)S(1)} %bitcast.139, f32[1,1105920]{1,0:T(1,128)S(1)} %bitcast.150), kind=kLoop, calls=%fused_computation.110 | loop fusion | flops 7741440 | bytes 22118400 | tf_op jit(solution)/shard_map/sub | solution.py:1674
  (823 shorter events, 340.7 us)
Async XLA Ops:
  9.7 189.7 %collective-permute-start.1 = (bf16[160,1792]{1,0:T(8,128)(2,1)}, bf16[160,1792]{1,0:T(8,128)(2,1)}, u32[]{:S(2)}, u32[]{:S(2)}) collective-permute-start(bf16[160,1792]{1,0:T(8,128)(2,1)} %fusion.69), channel_id=1, source_target_pairs={{7,3},{15,11},{23,19},{31,27}} | collective-permute-start | bytes 1720328 | tf_op jit(solution)/shard_map/ppermute | solution.py:501
  11.2 188.4 %collective-permute-start = (bf16[160,1792]{1,0:T(8,128)(2,1)}, bf16[160,1792]{1,0:T(8,128)(2,1)}, u32[]{:S(2)}, u32[]{:S(2)}) collective-permute-start(bf16[160,1792]{1,0:T(8,128)(2,1)} %fusion.69), channel_id=1, source_target_pairs={{0,2},{5,3},{8,10},{13,11},{16,18},{21,19},{24,26},{29,27}} | collective-permute-start | bytes 1720328 | tf_op jit(solution)/shard_map/ppermute | solution.py:501
  17.6 171.3 %collective-permute-start.3 = (s32[2,160]{1,0:T(2,128)}, s32[2,160]{1,0:T(2,128)}, u32[]{:S(2)}, u32[]{:S(2)}) collective-permute-start(s32[2,160]{1,0:T(2,128)} %bitcast.120), channel_id=1, source_target_pairs={{7,3},{15,11},{23,19},{31,27}} | collective-permute-start | bytes 3848 | tf_op jit(solution)/shard_map/ppermute | solution.py:501
  18.8 171.4 %collective-permute-start.2 = (s32[2,160]{1,0:T(2,128)}, s32[2,160]{1,0:T(2,128)}, u32[]{:S(2)}, u32[]{:S(2)}) collective-permute-start(s32[2,160]{1,0:T(2,128)} %bitcast.120), channel_id=1, source_target_pairs={{0,2},{5,3},{8,10},{13,11},{16,18},{21,19},{24,26},{29,27}} | collective-permute-start | bytes 3848 | tf_op jit(solution)/shard_map/ppermute | solution.py:501
  21.8 305.2 %collective-permute-start.6 = (bf16[160,1792]{1,0:T(8,128)(2,1)}, bf16[160,1792]{1,0:T(8,128)(2,1)}, u32[]{:S(2)}, u32[]{:S(2)}) collective-permute-start(bf16[160,1792]{1,0:T(8,128)(2,1)} %fusion.71), channel_id=1, source_target_pairs={{7,3},{15,11},{23,19},{31,27}} | collective-permute-start | bytes 1720328 | tf_op jit(solution)/shard_map/ppermute | solution.py:501
  188.9 138.4 %collective-permute-start.5 = (bf16[160,1792]{1,0:T(8,128)(2,1)}, bf16[160,1792]{1,0:T(8,128)(2,1)S(1)}, u32[]{:S(2)}, u32[]{:S(2)}) collective-permute-start(bf16[160,1792]{1,0:T(8,128)(2,1)} %fusion.71), channel_id=1, source_target_pairs={{0,2},{5,3},{8,10},{13,11},{16,18},{21,19},{24,26},{29,27}} | collective-permute-start | bytes 1720328 | tf_op jit(solution)/shard_map/ppermute | solution.py:501
  202.5 262.6 %collective-permute-start.9 = (bf16[320,1792]{1,0:T(8,128)(2,1)}, bf16[320,1792]{1,0:T(8,128)(2,1)}, u32[]{:S(2)}, u32[]{:S(2)}) collective-permute-start(bf16[320,1792]{1,0:T(8,128)(2,1)} %pad_maximum_fusion.13.shown), channel_id=1, source_target_pairs={{2,3},{3,2},{10,11},{11,10},{18,19},{19,18},{26,27},{27,26}} | collective-permute-start | bytes 3440648 | tf_op jit(solution)/shard_map/ppermute | solution.py:501
  321.0 13.9 collective-permute-start.4
  328.4 327.9 %collective-permute-start.27 = (bf16[320,1792]{1,0:T(8,128)(2,1)}, bf16[320,1792]{1,0:T(8,128)(2,1)}, u32[]{:S(2)}, u32[]{:S(2)}) collective-permute-start(bf16[320,1792]{1,0:T(8,128)(2,1)} %pad_maximum_fusion.14.shown), channel_id=1, source_target_pairs={{2,3},{3,2},{10,11},{11,10},{18,19},{19,18},{26,27},{27,26}} | collective-permute-start | bytes 3440648 | tf_op jit(solution)/shard_map/ppermute | solution.py:501
  375.8 12.7 collective-permute-start.7
  383.3 80.0 %collective-permute-start.11 = (bf16[384,1536]{1,0:T(8,128)(2,1)}, bf16[384,1536]{1,0:T(8,128)(2,1)S(1)}, u32[]{:S(2)}, u32[]{:S(2)}) collective-permute-start(bf16[384,1536]{1,0:T(8,128)(2,1)} %pad_maximum_fusion.9), channel_id=1, source_target_pairs={{0,1},{1,0},{2,3},{3,2},{4,5},{5,4},{6,7},{7,6},{8,9},{9,8},{10,11... | collective-permute-start | bytes 3538952 | tf_op jit(solution)/shard_map/ppermute | solution.py:511
  386.3 67.3 %collective-permute-start.18 = (bf16[960,384]{1,0:T(8,128)(2,1)}, bf16[960,384]{1,0:T(8,128)(2,1)S(1)}, u32[]{:S(2)}, u32[]{:S(2)}) collective-permute-start(bf16[960,384]{1,0:T(8,128)(2,1)} %pad_maximum_fusion.17), channel_id=1, source_target_pairs={{0,1},{1,0},{2,3},{3,2},{4,5},{5,4},{6,7},{7,6},{8,9},{9,8},{10,11... | collective-permute-start | bytes 2211848 | tf_op jit(solution)/shard_map/ppermute | solution.py:511
  433.7 23.1 %collective-permute-start.16 = (bf16[384,576]{0,1:T(8,128)(2,1)S(1)}, bf16[384,576]{0,1:T(8,128)(2,1)S(1)}, u32[]{:S(2)}, u32[]{:S(2)}) collective-permute-start(bf16[384,576]{0,1:T(8,128)(2,1)S(1)} %get-tuple-element.690), channel_id=1, source_target_pairs={{0,2},{1,3},{4,6},{5,7},{8,10},{9,11},{12,14},{13,15},{16,18},{17,... | collective-permute-start | bytes 1327112 | tf_op jit(solution)/shard_map/ppermute | solution.py:501
  453.6 17.8 %collective-permute-start.8 = (bf16[784,576]{1,0:T(8,128)(2,1)S(1)}, bf16[784,576]{1,0:T(8,128)(2,1)S(1)}, u32[]{:S(2)}, u32[]{:S(2)}) collective-permute-start(bf16[784,576]{1,0:T(8,128)(2,1)S(1)} %slice.938), channel_id=1, source_target_pairs={{0,1},{1,0},{2,3},{3,2},{4,5},{5,4},{6,7},{7,6},{8,9},{9,8},{10,11... | collective-permute-start | bytes 2709512 | tf_op jit(solution)/shard_map/ppermute | solution.py:511
  456.9 194.5 %collective-permute-start.19 = (bf16[960,384]{1,0:T(8,128)(2,1)}, bf16[960,384]{1,0:T(8,128)(2,1)}, u32[]{:S(2)}, u32[]{:S(2)}) collective-permute-start(bf16[960,384]{1,0:T(8,128)(2,1)} %fusion.65), channel_id=1, source_target_pairs={{0,2},{1,3},{4,6},{5,7},{8,10},{9,11},{12,14},{13,15},{16,18},{17,... | collective-permute-start | bytes 2211848 | tf_op jit(solution)/shard_map/ppermute | solution.py:501
  463.3 198.1 %collective-permute-start.17 = (bf16[384,576]{0,1:T(8,128)(2,1)}, bf16[384,576]{0,1:T(8,128)(2,1)}, u32[]{:S(2)}, u32[]{:S(2)}) collective-permute-start(bf16[384,576]{0,1:T(8,128)(2,1)} %get-tuple-element.622), channel_id=1, source_target_pairs={{2,6},{3,7},{10,14},{11,15},{18,22},{19,23},{26,30},{27,31}} | collective-permute-start | bytes 1327112 | tf_op jit(solution)/shard_map/ppermute | solution.py:501
  465.2 30.3 %collective-permute-start.12 = (bf16[384,1536]{1,0:T(8,128)(2,1)S(1)}, bf16[384,1536]{1,0:T(8,128)(2,1)S(1)}, u32[]{:S(2)}, u32[]{:S(2)}) collective-permute-start(bf16[384,1536]{1,0:T(8,128)(2,1)S(1)} %fusion.101), channel_id=1, source_target_pairs={{0,2},{1,3},{4,6},{5,7},{8,10},{9,11},{12,14},{13,15},{16,18},{17,... | collective-permute-start | bytes 3538952 | tf_op jit(solution)/shard_map/ppermute | solution.py:501
  496.9 150.1 %collective-permute-start.13 = (bf16[384,1536]{1,0:T(8,128)(2,1)}, bf16[384,1536]{1,0:T(8,128)(2,1)}, u32[]{:S(2)}, u32[]{:S(2)}) collective-permute-start(bf16[384,1536]{1,0:T(8,128)(2,1)} %fusion.43), channel_id=1, source_target_pairs={{2,6},{3,7},{10,14},{11,15},{18,22},{19,23},{26,30},{27,31}} | collective-permute-start | bytes 3538952 | tf_op jit(solution)/shard_map/ppermute | solution.py:501
  638.5 25.6 %collective-permute-start.10 = (bf16[704,384]{1,0:T(8,128)(2,1)}, bf16[704,384]{1,0:T(8,128)(2,1)}, u32[]{:S(2)}, u32[]{:S(2)}) collective-permute-start(bf16[704,384]{1,0:T(8,128)(2,1)} %pad_maximum_fusion.19), channel_id=1, source_target_pairs={{0,1},{1,0},{2,3},{3,2},{4,5},{5,4},{8,9},{9,8},{10,11},{11,10},{1... | collective-permute-start | bytes 1622024 | tf_op jit(solution)/shard_map/ppermute | solution.py:501
  647.0 8.6 collective-permute-start.21
  651.4 3.4 collective-permute-start.14
  654.8 10.7 collective-permute-start.20
  655.6 11.1 collective-permute-start.15
  656.3 7.1 collective-permute-start.22
  663.5 4.4 collective-permute-start.23
  1004.6 11.0 collective-permute-start.24
  1063.2 12.5 collective-permute-start.25
  1067.9 64.3 %collective-permute-start.29 = (bf16[384,1536]{1,0:T(8,128)(2,1)S(1)}, bf16[384,1536]{1,0:T(8,128)(2,1)S(1)}, u32[]{:S(2)}, u32[]{:S(2)}) collective-permute-start(bf16[384,1536]{1,0:T(8,128)(2,1)S(1)} %pad_maximum_fusion.11), channel_id=1, source_target_pairs={{0,1},{1,0},{2,3},{3,2},{4,5},{5,4},{6,7},{7,6},{8,9},{9,8},{10,11... | collective-permute-start | bytes 3538952 | tf_op jit(solution)/shard_map/ppermute | solution.py:511
  1070.2 58.7 %collective-permute-start.36 = (bf16[960,384]{1,0:T(8,128)(2,1)S(1)}, bf16[960,384]{1,0:T(8,128)(2,1)S(1)}, u32[]{:S(2)}, u32[]{:S(2)}) collective-permute-start(bf16[960,384]{1,0:T(8,128)(2,1)S(1)} %pad_maximum_fusion.18), channel_id=1, source_target_pairs={{0,1},{1,0},{2,3},{3,2},{4,5},{5,4},{6,7},{7,6},{8,9},{9,8},{10,11... | collective-permute-start | bytes 2211848 | tf_op jit(solution)/shard_map/ppermute | solution.py:511
  1119.1 22.9 %collective-permute-start.26 = (bf16[784,576]{1,0:T(8,128)(2,1)S(1)}, bf16[784,576]{1,0:T(8,128)(2,1)S(1)}, u32[]{:S(2)}, u32[]{:S(2)}) collective-permute-start(bf16[784,576]{1,0:T(8,128)(2,1)S(1)} %slice.964), channel_id=1, source_target_pairs={{0,1},{1,0},{2,3},{3,2},{4,5},{5,4},{6,7},{7,6},{8,9},{9,8},{10,11... | collective-permute-start | bytes 2709512 | tf_op jit(solution)/shard_map/ppermute | solution.py:511
  1122.0 17.4 %collective-permute-start.34 = (bf16[384,576]{0,1:T(8,128)(2,1)S(1)}, bf16[384,576]{0,1:T(8,128)(2,1)S(1)}, u32[]{:S(2)}, u32[]{:S(2)}) collective-permute-start(bf16[384,576]{0,1:T(8,128)(2,1)S(1)} %get-tuple-element.704), channel_id=1, source_target_pairs={{0,2},{1,3},{4,6},{5,7},{8,10},{9,11},{12,14},{13,15},{16,18},{17,... | collective-permute-start | bytes 1327112 | tf_op jit(solution)/shard_map/ppermute | solution.py:501
  1130.0 173.1 %collective-permute-start.37 = (bf16[960,384]{1,0:T(8,128)(2,1)}, bf16[960,384]{1,0:T(8,128)(2,1)}, u32[]{:S(2)}, u32[]{:S(2)}) collective-permute-start(bf16[960,384]{1,0:T(8,128)(2,1)} %fusion.64), channel_id=1, source_target_pairs={{0,2},{1,3},{4,6},{5,7},{8,10},{9,11},{12,14},{13,15},{16,18},{17,... | collective-permute-start | bytes 2211848 | tf_op jit(solution)/shard_map/ppermute | solution.py:501
  1132.5 29.4 %collective-permute-start.30 = (bf16[384,1536]{1,0:T(8,128)(2,1)S(1)}, bf16[384,1536]{1,0:T(8,128)(2,1)S(1)}, u32[]{:S(2)}, u32[]{:S(2)}) collective-permute-start(bf16[384,1536]{1,0:T(8,128)(2,1)S(1)} %fusion.100), channel_id=1, source_target_pairs={{0,2},{1,3},{4,6},{5,7},{8,10},{9,11},{12,14},{13,15},{16,18},{17,... | collective-permute-start | bytes 3538952 | tf_op jit(solution)/shard_map/ppermute | solution.py:501
  1140.6 169.5 %collective-permute-start.35 = (bf16[384,576]{0,1:T(8,128)(2,1)}, bf16[384,576]{0,1:T(8,128)(2,1)}, u32[]{:S(2)}, u32[]{:S(2)}) collective-permute-start(bf16[384,576]{0,1:T(8,128)(2,1)} %get-tuple-element.607), channel_id=1, source_target_pairs={{2,6},{3,7},{10,14},{11,15},{18,22},{19,23},{26,30},{27,31}} | collective-permute-start | bytes 1327112 | tf_op jit(solution)/shard_map/ppermute | solution.py:501
  1163.2 135.6 %collective-permute-start.31 = (bf16[384,1536]{1,0:T(8,128)(2,1)}, bf16[384,1536]{1,0:T(8,128)(2,1)}, u32[]{:S(2)}, u32[]{:S(2)}) collective-permute-start(bf16[384,1536]{1,0:T(8,128)(2,1)} %fusion.44), channel_id=1, source_target_pairs={{2,6},{3,7},{10,14},{11,15},{18,22},{19,23},{26,30},{27,31}} | collective-permute-start | bytes 3538952 | tf_op jit(solution)/shard_map/ppermute | solution.py:501
  1289.0 23.9 %collective-permute-start.28 = (bf16[704,384]{1,0:T(8,128)(2,1)}, bf16[704,384]{1,0:T(8,128)(2,1)}, u32[]{:S(2)}, u32[]{:S(2)}) collective-permute-start(bf16[704,384]{1,0:T(8,128)(2,1)} %pad_maximum_fusion.20), channel_id=1, source_target_pairs={{0,1},{1,0},{2,3},{3,2},{4,5},{5,4},{8,9},{9,8},{10,11},{11,10},{1... | collective-permute-start | bytes 1622024 | tf_op jit(solution)/shard_map/ppermute | solution.py:501
  1297.4 9.9 collective-permute-start.39
  1302.4 4.1 collective-permute-start.32
  1305.7 8.5 collective-permute-start.38
  1306.6 8.7 collective-permute-start.33
  1307.4 4.8 collective-permute-start.40
  1312.2 4.4 collective-permute-start.41
  1389.2 11.6 collective-permute-start.42
  1401.0 14.3 collective-permute-start.43
  1407.1 8.4 collective-permute-start.45
  1415.4 4.3 collective-permute-start.44
  1418.1 26.8 %collective-permute-start.46 = (bf16[552960]{0:T(1024)(128)(2,1)S(1)}, bf16[552960]{0:T(1024)(128)(2,1)S(1)}, u32[]{:S(2)}, u32[]{:S(2)}) collective-permute-start(bf16[552960]{0:T(1024)(128)(2,1)S(1)} %add_convert_fusion.4), channel_id=1, source_target_pairs={{0,16},{8,24},{16,0},{24,8},{1,17},{9,25},{17,1},{25,9},{2,18},{10... | collective-permute-start | bytes 3317768 | tf_op jit(solution)/shard_map/ppermute | solution.py:1700
  1445.2 4.4 collective-permute-start.47
  (212 other events, 3618.1 us)

commit v2 on v1

--- a/solution.py
+++ b/solution.py
@@ -542,7 +542,6 @@
     PATCH_ROWS,
     E2D,
     HEAD,
-    HEAD_LATE,
     VECS,
     DEC_QKV,
     DEC_OUT,
@@ -563,19 +562,7 @@
     CROSS,
     MATE_OWN,
     MATE_OTHER,
-) = range(27)
-TEN_ROWS = [
-    [(QKV, 768), (SQUARE, 288)],
-    [(SQUARE, 96), (UP, 672)],
-    [(UP, 96), (SQUARE, 1248)],
-    [(SQUARE, 288), (DEC_QKV, 384), (DEC_OUT, 192), (DEC_UP, 384), (DEC_DOWN, 768)],
-]
-REP_ROWS = [
-    [(PATCH_ROWS, 676)],
-    [(PATCH_ROWS, 676)],
-    [(PATCH_ROWS, 184), (E2D, 768), (HEAD, 54)],
-    [(HEAD_LATE, 330), (VECS, 16)],
-]
+) = range(26)
 PIECES = {
     QKV: (768, 1152),
     SQUARE: (1248, 768),
@@ -583,33 +570,12 @@
     PATCH_ROWS: (704, 768),
     E2D: (768, 384),
     HEAD: (64, 1536),
-    HEAD_LATE: (384, 1536),
     VECS: (16, 768),
     DEC_QKV: (384, 576),
     DEC_OUT: (192, 384),
     DEC_UP: (384, 768),
     DEC_DOWN: (768, 384),
 }
-
-
-def owned_pieces(rep_master, ten_master):
-    def branch(ten_rows, rep_rows):
-        def fill(ten, rep):
-            out = {}
-            for flat, rows in ((ten, ten_rows), (rep, rep_rows)):
-                offset = 0
-                for name, count in rows:
-                    width = PIECES[name][1]
-                    piece = flat[offset : offset + count * width].astype(HALF).reshape(count, width)
-                    offset += count * width
-                    top = PIECES[name][0] - count if name == HEAD_LATE else 0
-                    out[name] = jnp.pad(piece, ((top, PIECES[name][0] - count - top), (0, 0)))
-            return [out.get(name, jnp.zeros(PIECES[name], HALF)) for name in PIECES]
-
-        return fill
-
-    branches = [branch(ten_rows, rep_rows) for ten_rows, rep_rows in zip(TEN_ROWS, REP_ROWS)]
-    return dict(zip(PIECES, lax.switch(lax.axis_index("dp"), branches, ten_master, rep_master)))
 
 
 DEC_PARTS = [DEC_QKV, DEC_OUT, DEC_UP, DEC_DOWN, HEAD_HALF]
@@ -859,11 +825,8 @@
             enc_copy(item).wait_send()
 
 
-def hosted_weights(rep_master, ten_master, shared):
+def hosted_weights(pieces, shared):
     side = lax.axis_index("tensor")
-    pieces = owned_pieces(rep_master, ten_master)
-    columns = PATCH // 2
-    pieces[HEAD_HALF] = lax.dynamic_slice_in_dim(pieces[HEAD_LATE], side * columns, columns, 1)
     anywhere = pl.BlockSpec(memory_space=pl.ANY)
     shapes = list(GOT.values()) + 2 * [pieces[name].shape for name in DEC_PARTS]
     count = 2 * len(ENC_PARTS) + 4 * (len(DEC_PARTS) + 3)
@@ -1145,7 +1108,10 @@
 def encoder_backward_kernel(
     picked, shown, w_qkv, w_out, w_up, w_down, e2d_w, vec,
     stream, normed, joined, blended, attended, second, upward, activated, encoded, final_enc,
+    wide, tall, dec_qkv, small,
     qkv_out, square_out, up_out, patch_out, e2d_out, vec_out,
+    one_wide, one_tall, one_qkv, one_small, two_wide, two_tall, two_qkv, two_small,
+    wide_sent, tall_sent, dec_qkv_sent, small_sent, wide_got, tall_got, dec_qkv_got, small_got,
     picks_got, low, grad_up_in, mid, grad_blend, grad_joined, part_sent, part_got, own_rows_grad, own_part,
     emb_low, emb_got, down_grad, up_grad, out_grad, qkv_grad, patch_low, patch_mid, patch_high, e2d_part, e2d_got, e2d_grad,
     vec_part, vec_got, send_sem, recv_sem, local_sem,
@@ -1163,18 +1129,32 @@
     @pl.when(z != HOST)
     def _():
         greet(at(HOST, x))
+
+    @pl.when(z == LAST)
+    def _():
+        greet(at(2, x))
+
+    @pl.when((z == HOST) & (x == 0))
+    def _():
+        for peer in ((0, 0), (0, 1), (HOST, 1)):
+            greet(at(*peer))
+
+    @pl.when((z == HOST) & (x == 1))
+    def _():
+        for peer in ((2, 0), (2, 1), (3, 0), (3, 1), (0, 1), (HOST, 0)):
+            greet(at(*peer))
+
+    @pl.when(z == HOST)
+    def _():
+        pl.semaphore_wait(barrier, 4)
+
+    @pl.when((z == 2) | ((z == 0) & (x == 1)))
+    def _():
+        pl.semaphore_wait(barrier, 2)
+
+    @pl.when((z == LAST) | ((z == 0) & (x == 0)))
+    def _():
         pl.semaphore_wait(barrier, 1)
-
-    for column in range(2):
-
-        @pl.when((z == HOST) & (x == column))
-        def _():
-            greet(at(HOST, 1 - column))
-            for row in (2 * column, 2 * column + 1):
-                if row != HOST:
-                    for side in range(2):
-                        greet(at(row, side))
-            pl.semaphore_wait(barrier, 4)
 
     def pick_copy(row, side):
         return links.copy((row % 2) * 2 + side, picked, picks_got.at[row % 2, side], at(HOST, row // 2))
@@ -1220,6 +1200,27 @@
     patch_two = links.copy(next(numbers), patch_high, patch_out.at[pl.ds(0, 192)], at(2, x))
     e2d_near = links.copy(next(numbers), e2d_grad, e2d_out, at(2, x))
     vec_far = links.copy(next(numbers), vec_part, vec_out, at(LAST, x))
+
+    own_dec = (wide, tall, dec_qkv, small)
+    sent_dec = (wide_sent, tall_sent, dec_qkv_sent, small_sent)
+    got_dec = (wide_got, tall_got, dec_qkv_got, small_got)
+    one_dec = (one_wide, one_tall, one_qkv, one_small)
+    two_dec = (two_wide, two_tall, two_qkv, two_small)
+    next_row = jnp.minimum(z + 1, LAST)
+    tree_one = [links.copy(next(numbers), sent_dec[i], got_dec[i], at(next_row, x)) for i in range(4)]
+    tree_two = [links.copy(next(numbers), sent_dec[i], two_dec[i], at(LAST, x)) for i in range(4)]
+
+    @pl.when((z == 0) | (z == 2))
+    def _():
+        for i in (3, 0, 1, 2):
+            sent_dec[i][...] = own_dec[i][...].astype(sent_dec[i].dtype)
+            tree_one[i].start()
+
+    def pass_on():
+        for i in (3, 0, 1, 2):
+            tree_one[i].wait_recv()
+            sent_dec[i][...] = (own_dec[i][...] + got_dec[i][...].astype(FLOAT)).astype(sent_dec[i].dtype)
+            tree_two[i].start()
 
     def tall_product(left, right, target, step):
         def body(t, carry):
@@ -1344,6 +1345,8 @@
             mid_sent[i].wait_recv()
             part_sent[rows_at(2 + i)] = attend_back(2 + i).astype(HALF)
             normed_sent[i].start()
+            if i == 0:
+                pass_on()
         tall_product(second, grad_up_in, up_grad, 256)
         up_near.start()
         tall_product(blended, mid, out_grad, 128)
@@ -1385,6 +1388,8 @@
             one.wait_send()
         for one in (down_far, down_near, up_near, out_near, qkv_near, patch_one, patch_two, e2d_near, vec_far):
             one.wait_send()
+        for one in tree_two:
+            one.wait_send()
         for one in mine:
             one.wait()
 
@@ -1403,8 +1408,24 @@
             for one in ones:
                 one.wait_recv()
 
-
-def encoder_backward(number, picked, shown, weights, stored):
+    @pl.when((z == 0) | (z == 2))
+    def _():
+        for one in tree_one:
+            one.wait_send()
+
+    @pl.when(z == LAST)
+    def _():
+        kept = []
+        for i in range(4):
+            tree_one[i].wait_recv()
+            kept.append(pltpu.make_async_copy(got_dec[i], one_dec[i], local_sem.at[i]))
+            kept[i].start()
+        for i in range(4):
+            tree_two[i].wait_recv()
+            kept[i].wait()
+
+
+def encoder_backward(number, picked, shown, weights, stored, dec_grads):
     _, mats, e2d_w, vec = weights
     vmem = pl.BlockSpec(memory_space=pltpu.VMEM)
     anywhere = pl.BlockSpec(memory_space=pl.ANY)
@@ -1416,7 +1437,9 @@
         ((D // 2, DD), HALF),
         ((16, D), FLOAT),
     ]
-    scratch = [
+    tree = [(one.shape, HALF) for one in dec_grads[:3]] + [(dec_grads[3].shape, FLOAT)]
+    shapes = shapes + 2 * tree
+    scratch = 2 * tree + [
         ((2, 2, VISIBLE, DD), HALF),
         ((ALL, D), HALF),
         ((ALL, FF // 2), HALF),
@@ -1446,14 +1469,350 @@
         encoder_backward_kernel,
         name="encoder_backward",
         out_shape=[jax.ShapeDtypeStruct(*one) for one in shapes],
-        in_specs=[vmem] * 18,
+        in_specs=[vmem] * 22,
         out_specs=[anywhere] * len(shapes),
         scratch_shapes=[pltpu.VMEM(*one) for one in scratch]
-        + [pltpu.SemaphoreType.DMA((28,)), pltpu.SemaphoreType.DMA((28,)), pltpu.SemaphoreType.DMA((4,))],
+        + [pltpu.SemaphoreType.DMA((36,)), pltpu.SemaphoreType.DMA((36,)), pltpu.SemaphoreType.DMA((4,))],
         compiler_params=pltpu.CompilerParams(
             collective_id=number, has_side_effects=True, vmem_limit_bytes=60 << 20
         ),
-    )(picked, shown, *mats, e2d_w, vec, *stored)
+    )(picked, shown, *mats, e2d_w, vec, *stored, *dec_grads)
+
+
+LANES = 128
+STEP_ROWS = 96
+TEN_LANES = 8640
+REP_LANES = 4056
+LAID = [QKV, SQUARE, UP, PATCH_ROWS, E2D, HEAD, VECS, DEC_QKV, DEC_OUT, DEC_UP, DEC_DOWN, HEAD_HALF]
+LAID_SHAPES = {**PIECES, HEAD_HALF: (384, 768)}
+TEN_PLACES = [
+    [(QKV, 768, 0), (SQUARE, 288, 6912)],
+    [(SQUARE, 96, 0), (UP, 672, 576)],
+    [(UP, 96, 0), (SQUARE, 1248, 1152)],
+    [(SQUARE, 288, 0), (DEC_OUT, 192, 3456), (DEC_UP, 384, 4032), (DEC_DOWN, 768, 6336)],
+]
+DEC_QKV_PLACE = 1728
+PATCH_COUNTS = (676, 676, 184)
+E2D_PLACE = 1104
+HEAD_PLACE = 3408
+HEAD_TOP = 54
+VEC_PLACE = 3960
+
+
+def spread_rows(flat, place, blocks, count, read):
+    def put(first, value):
+        rows = value.shape[0]
+        for j in range(blocks):
+            flat[pl.ds(place + first * blocks + j, rows, stride=blocks), :] = value[:, j * LANES : (j + 1) * LANES]
+
+    def body(t, carry):
+        put(t * STEP_ROWS, read(pl.multiple_of(t * STEP_ROWS, 16), STEP_ROWS))
+        return carry
+
+    whole = count // STEP_ROWS
+    if whole:
+        lax.fori_loop(0, whole, body, 0)
+    rest = count - whole * STEP_ROWS
+    if rest:
+        put(whole * STEP_ROWS, read(whole * STEP_ROWS, -(-rest // 16) * 16)[:rest])
+
+
+def gather_rows(piece, flat, place, blocks, count):
+    def put(first, rows, padded):
+        for j in range(blocks):
+            value = flat[pl.ds(place + first * blocks + j, rows, stride=blocks), :]
+            if padded > rows:
+                value = jnp.concatenate([value, jnp.zeros((padded - rows, LANES), FLOAT)], 0)
+            piece[pl.ds(first, padded), j * LANES : (j + 1) * LANES] = value.astype(HALF)
+
+    def body(t, carry):
+        put(pl.multiple_of(t * STEP_ROWS, 16), STEP_ROWS, STEP_ROWS)
+        return carry
+
+    whole = count // STEP_ROWS
+    if whole:
+        lax.fori_loop(0, whole, body, 0)
+    rest = count - whole * STEP_ROWS
+    if rest:
+        put(whole * STEP_ROWS, rest, -(-rest // 16) * 16)
+
+
+def lay_out(z, x, ten, rep, pieces, wide_rows):
+    for row in range(4):
+
+        @pl.when(z == row)
+        def _():
+            for name, count, place in TEN_PLACES[row]:
+                gather_rows(pieces[name], ten, place, PIECES[name][1] // LANES, count)
+            if row < LAST:
+                gather_rows(pieces[PATCH_ROWS], rep, 0, D // LANES, PATCH_COUNTS[row])
+            if row < 2:
+                pieces[PATCH_ROWS][pl.ds(688, 16)] = jnp.zeros((16, D), HALF)
+            if row == 2:
+                gather_rows(pieces[E2D], rep, E2D_PLACE, DD // LANES, D)
+                gather_rows(pieces[HEAD], rep, HEAD_PLACE, PATCH // LANES, HEAD_TOP)
+            if row == LAST:
+                gather_rows(pieces[VECS], rep, VEC_PLACE, D // LANES, 16)
+                for j in range(4):
+                    wide_rows[j, pl.ds(0, 192, stride=2), :] = ten[pl.ds(DEC_QKV_PLACE + j, 192, stride=9), :]
+                middle = ten[pl.ds(DEC_QKV_PLACE + 4, 192, stride=9), :]
+                late = [middle[:, 64:]] + [ten[pl.ds(DEC_QKV_PLACE + 5 + j, 192, stride=9), :] for j in range(4)]
+                late = jnp.concatenate(late + [jnp.zeros((192, 64), FLOAT)], 1)
+                wide_rows[4, pl.ds(0, 192, stride=2), :] = middle
+                for j in range(5):
+                    columns = slice(j * LANES, (j + 1) * LANES)
+                    wide_rows[j, pl.ds(1, 192, stride=2), :] = late[:, columns]
+                for j in range(4):
+                    columns = slice(j * LANES, (j + 1) * LANES)
+                    pieces[DEC_QKV][:, columns] = wide_rows[j].astype(HALF)
+                pieces[DEC_QKV][:, 512:576] = wide_rows[4][:, :64].astype(HALF)
+                half = pieces[HEAD_HALF]
+                blocks, offset = PATCH // LANES, x * 6
+                half[pl.ds(0, 48)] = jnp.zeros((48, D), HALF)
+                for j in range(6):
+                    columns = slice(j * LANES, (j + 1) * LANES)
+                    value = rep[pl.ds(offset + j, 42, stride=blocks), :]
+                    half[pl.ds(48, 48), columns] = jnp.concatenate(
+                        [jnp.zeros((6, LANES), FLOAT), value], 0
+                    ).astype(HALF)
+                    for t in range(1, 4):
+                        value = rep[pl.ds((96 * t - HEAD_TOP) * blocks + offset + j, 96, stride=blocks), :]
+                        half[pl.ds(96 * t, 96), columns] = value.astype(HALF)
+
+
+def lay_out_kernel(ten, rep, *refs):
+    pieces = dict(zip(LAID, refs))
+    lay_out(lax.axis_index("dp"), lax.axis_index("tensor"), ten, rep, pieces, refs[len(LAID)])
+
+
+def first_pieces(ten, rep):
+    vmem = pl.BlockSpec(memory_space=pltpu.VMEM)
+    out = pl.pallas_call(
+        lay_out_kernel,
+        name="lay_out",
+        out_shape=[jax.ShapeDtypeStruct(LAID_SHAPES[name], HALF) for name in LAID],
+        in_specs=[vmem] * 2,
+        out_specs=[vmem] * len(LAID),
+        scratch_shapes=[pltpu.VMEM((5, 384, LANES), FLOAT)],
+        compiler_params=pltpu.CompilerParams(vmem_limit_bytes=48 << 20),
+    )(ten, rep)
+    return dict(zip(LAID, out))
+
+
+def update_kernel(
+    number, last,
+    stats, qkv, square, up, patch, e2d, vec, wide, tall, dec_qkv, small,
+    one_wide, one_tall, one_qkv, one_small, two_wide, two_tall, two_qkv, two_small,
+    *refs,
+):
+    masters, refs = refs[:6], refs[6:]
+    stats_out, outs, refs = refs[0], refs[1:7], refs[7:]
+    pieces = {}
+    if not last:
+        pieces, refs = dict(zip(LAID, refs)), refs[len(LAID) :]
+    held, refs = refs[:6], refs[6:]
+    grad_ten, grad_rep, wide_rows, patch_other, e2d_other, head_own, head_other, slots, send_sem, recv_sem, local_sem = refs
+    g, z, x = lax.axis_index("group"), lax.axis_index("dp"), lax.axis_index("tensor")
+    me = 2 * z + x
+    links = Links(send_sem, recv_sem)
+    barrier = pltpu.get_barrier_semaphore()
+    loads = [pltpu.make_async_copy(masters[i], held[i], local_sem.at[i]) for i in range(6)]
+    for one in loads:
+        one.start()
+
+    def peer(shift):
+        other = lax.rem(me + shift, 8)
+        return (g, other // 2, lax.rem(other, 2))
+
+    for shift in range(1, 8):
+        pl.semaphore_signal(barrier, inc=1, device_id=peer(shift), device_id_type=MESH_ID)
+    pl.semaphore_wait(barrier, 7)
+
+    across = (g, z, 1 - x)
+    patch_swap = links.copy(0, patch, patch_other, across)
+    e2d_swap = links.copy(1, e2d, e2d_other, across)
+    head_swap = links.copy(2, head_own, head_other, across)
+    top_own = links.copy(3, head_own.at[pl.ds(0, 64)], head_own.at[pl.ds(0, 64)], (g, 2, x))
+    top_other = links.copy(4, head_other.at[pl.ds(0, 64)], head_other.at[pl.ds(0, 64)], (g, 2, x))
+
+    def plain(ref):
+        return lambda first, rows: ref[pl.ds(first, rows)].astype(FLOAT)
+
+    def joined(own, other):
+        def read(first, rows):
+            one, two = own[pl.ds(first, rows)].astype(FLOAT), other[pl.ds(first, rows)].astype(FLOAT)
+            return jnp.concatenate([jnp.where(x == 0, one, two), jnp.where(x == 0, two, one)], 1)
+
+        return read
+
+    def total(own, one, two, top, columns):
+        def read(first, rows):
+            at = pl.ds(top + first, rows)
+            return own[at, columns] + one[at, columns].astype(FLOAT) + two[at, columns].astype(FLOAT)
+
+        return read
+
+    @pl.when(z < LAST)
+    def _():
+        patch_swap.start()
+
+    @pl.when(z == 2)
+    def _():
+        e2d_swap.start()
+
+    fc = DFF // 2
+
+    @pl.when(z == LAST)
+    def _():
+        head_own[...] = total(wide, one_wide, two_wide, 0, slice(fc, 2 * fc))(0, DD).astype(HALF)
+        head_swap.start()
+        top_own.start()
+        whole = slice(0, DD)
+        spread_rows(grad_ten, 0, 6, 288, plain(square))
+        spread_rows(grad_ten, 3456, 3, 192, total(tall, one_tall, two_tall, fc, whole))
+        spread_rows(grad_ten, 4032, 6, 384, total(wide, one_wide, two_wide, 0, slice(0, fc)))
+        spread_rows(grad_ten, 6336, 3, 768, total(tall, one_tall, two_tall, 0, whole))
+        for j in range(4):
+            columns = slice(j * LANES, (j + 1) * LANES)
+            wide_rows[j] = total(dec_qkv, one_qkv, two_qkv, 0, columns)(0, DD)
+        tail = total(dec_qkv, one_qkv, two_qkv, 0, slice(512, 576))(0, DD)
+        wide_rows[4] = jnp.concatenate([tail, jnp.zeros((DD, 64), FLOAT)], 1)
+        for j in range(4):
+            grad_ten[pl.ds(DEC_QKV_PLACE + j, 192, stride=9), :] = wide_rows[j, pl.ds(0, 192, stride=2), :]
+        late = jnp.concatenate([wide_rows[j, pl.ds(1, 192, stride=2), :] for j in range(5)], 1)
+        early = wide_rows[4, pl.ds(0, 192, stride=2), :]
+        grad_ten[pl.ds(DEC_QKV_PLACE + 4, 192, stride=9), :] = jnp.concatenate([early[:, :64], late[:, :64]], 1)
+        for j in range(4):
+            start = 64 + j * LANES
+            grad_ten[pl.ds(DEC_QKV_PLACE + 5 + j, 192, stride=9), :] = late[:, start : start + LANES]
+        for j in range(6):
+            columns = slice(j * LANES, (j + 1) * LANES)
+            grad_rep[pl.ds(VEC_PLACE + j, 9, stride=6), :] = vec[0:9, columns]
+        grad_rep[pl.ds(VEC_PLACE + 54, 42), :] = small[0:42] + one_small[0:42] + two_small[0:42]
+        head_swap.wait_recv()
+        top_other.start()
+        read = joined(head_own, head_other)
+
+        def put(first, value):
+            rows = value.shape[0]
+            for j in range(12):
+                grad_rep[pl.ds(first * 12 + j, rows, stride=12), :] = value[:, j * LANES : (j + 1) * LANES]
+
+        put(0, read(48, 48)[6:])
+        for t in range(1, 4):
+            put(96 * t - HEAD_TOP, read(96 * t, 96))
+
+    for row in range(3):
+
+        @pl.when(z == row)
+        def _():
+            refs_of = {QKV: qkv, SQUARE: square, UP: up}
+            for name, count, place in TEN_PLACES[row]:
+                spread_rows(grad_ten, place, PIECES[name][1] // LANES, count, plain(refs_of[name]))
+            patch_swap.wait_recv()
+            spread_rows(grad_rep, 0, 6, PATCH_COUNTS[row], joined(patch, patch_other))
+            if row == 2:
+                e2d_swap.wait_recv()
+                for half in range(2):
+
+                    def read(first, rows):
+                        one, two = e2d[pl.ds(first, rows)].astype(FLOAT), e2d_other[pl.ds(first, rows)].astype(FLOAT)
+                        return jnp.where(x == half, one, two)
+
+                    spread_rows(grad_rep, E2D_PLACE + half * 1152, 3, 384, read)
+                top_own.wait_recv()
+                top_other.wait_recv()
+                spread_rows(grad_rep, HEAD_PLACE, 12, HEAD_TOP, joined(head_own, head_other))
+
+    def square_sum(flat, step):
+        def body(t, carry):
+            value = flat[pl.ds(pl.multiple_of(t * step, 8), step), :]
+            return carry + jnp.sum((value * value).reshape(step // 8, 8, LANES), 0)
+
+        return jnp.sum(lax.fori_loop(0, flat.shape[0] // step, body, jnp.zeros((8, LANES), FLOAT)))
+
+    squares = square_sum(grad_ten, 360) + square_sum(grad_rep, 312) * 0.5
+    line = lax.broadcasted_iota(jnp.int32, (8, LANES), 0)
+    slots[me] = jnp.where(line == 0, squares, stats[...])
+    shares = [links.copy(4 + shift, slots.at[me], slots.at[me], peer(shift)) for shift in range(1, 8)]
+    for one in shares:
+        one.start()
+    for one in shares:
+        one.wait()
+    whole = slots[0]
+    for i in range(1, 8):
+        whole = whole + slots[i]
+    square_all, loss_all, count_all = whole[0:1], whole[1:2], whole[2:3]
+    norm = jnp.sqrt(square_all + 1e-30) / count_all
+    factor = jnp.minimum(1.0, CLIP / norm) / count_all
+    stats_out[...] = jnp.where(line == 0, norm, whole)
+    for one in loads:
+        one.wait()
+
+    def adam(master, first, second, grad, step):
+        def body(t, carry):
+            at = pl.ds(pl.multiple_of(t * step, 8), step)
+            new = adamw(master[at, :], first[at, :], second[at, :], grad[at, :] * factor, number)
+            master[at, :], first[at, :], second[at, :] = new
+            return carry
+
+        lax.fori_loop(0, master.shape[0] // step, body, 0)
+
+    stores = [pltpu.make_async_copy(held[i], outs[i], local_sem.at[i]) for i in range(6)]
+    adam(*held[:3], grad_ten, 72)
+    for one in stores[:3]:
+        one.start()
+    adam(*held[3:], grad_rep, 104)
+    for one in stores[3:]:
+        one.start()
+    if not last:
+        lay_out(z, x, held[0], held[3], pieces, wide_rows)
+
+    @pl.when(z < LAST)
+    def _():
+        patch_swap.wait_send()
+
+    @pl.when(z == 2)
+    def _():
+        e2d_swap.wait_send()
+
+    @pl.when(z == LAST)
+    def _():
+        head_swap.wait_send()
+        top_own.wait_send()
+        top_other.wait_send()
+
+    for one in stores:
+        one.wait()
+
+
+def update(identity, number, last, stats, gradients, states):
+    vmem = pl.BlockSpec(memory_space=pltpu.VMEM)
+    anywhere = pl.BlockSpec(memory_space=pl.ANY)
+    laid = [] if last else LAID
+    flat = [(TEN_LANES, LANES)] * 3 + [(REP_LANES, LANES)] * 3
+    scratch = [(one, FLOAT) for one in flat + [(TEN_LANES, LANES), (REP_LANES, LANES), (5, 384, LANES)]] + [
+        ((704, D // 2), HALF),
+        ((D // 2, DD), HALF),
+        ((DD, PATCH // 2), HALF),
+        ((DD, PATCH // 2), HALF),
+        ((8, 8, LANES), FLOAT),
+    ]
+    out = pl.pallas_call(
+        functools.partial(update_kernel, number, last),
+        name="update",
+        out_shape=[jax.ShapeDtypeStruct((8, LANES), FLOAT)]
+        + [jax.ShapeDtypeStruct(one, FLOAT) for one in flat]
+        + [jax.ShapeDtypeStruct(LAID_SHAPES[name], HALF) for name in laid],
+        in_specs=[vmem] * (1 + len(gradients)) + [anywhere] * 6,
+        out_specs=[vmem] + [anywhere] * 6 + [vmem] * len(laid),
+        scratch_shapes=[pltpu.VMEM(*one) for one in scratch]
+        + [pltpu.SemaphoreType.DMA((12,)), pltpu.SemaphoreType.DMA((12,)), pltpu.SemaphoreType.DMA((6,))],
+        compiler_params=pltpu.CompilerParams(
+            collective_id=identity, has_side_effects=True, vmem_limit_bytes=61 << 20
+        ),
+    )(stats, *gradients, *states)
+    return out[0], out[1:7], dict(zip(laid, out[7:]))
 
 
 def decoder_round(tokens, pixels_low, counted, weights):
@@ -1523,13 +1882,6 @@
     return loss, grad_in, (wide, tall, qkv_grad), vec_rows, head_b_grad
 
 
-def tree_sum(part):
-    z = lax.axis_index("dp")
-    low = part.astype(HALF)
-    part = part + hop_both(low, (0, 1), (2, 3)).astype(FLOAT)
-    return part + hop_both(part.astype(HALF), (1, 3)).astype(FLOAT)
-
-
 def hosted_round(
     patches,
     visible,
@@ -1552,12 +1904,11 @@
     ids_two = hop(visible[:, 0, 0], ((3, 1), (HOST, 1)))
     ids_two = jnp.where(side == 0, visible[:, 0, 0], ids_two)
     dec_places = sinus_at(tube_ids, DD)
-    rep_master, ten_master = rep_weights, ten_weights[0]
-    rep_first, rep_second = rep_m[0], rep_v[0]
-    ten_first, ten_second = ten_m[0, 0], ten_v[0, 0]
-    quarter = ten_master.shape[0]
-    rep_quarter = rep_master.shape[0]
-    rest = ENC_SIZE - 3 * quarter
+    states = [one.reshape(TEN_LANES, LANES) for one in (ten_weights, ten_m, ten_v)]
+    states = states + [one.reshape(REP_LANES, LANES) for one in (rep_weights, rep_m, rep_v)]
+    starts = states[0], states[3]
+    pieces = first_pieces(*starts)
+    rep_quarter = rep_weights.shape[0]
     shown_steps = []
     for s in range(STEPS):
         picks = (visible[s, 0, 0][:, None] == jnp.arange(TUBES)[None, :]).astype(HALF)
@@ -1576,7 +1927,7 @@
         shown_steps.append(jnp.concatenate([own, swap(own, HOST)], 0))
     loss_list, count_list, norm_list = [], [], []
     for s in range(STEPS):
-        enc_weights, dec_weights = hosted_weights(rep_master, ten_master, s == 0)
+        enc_weights, dec_weights = hosted_weights(pieces, s == 0)
         ids = visible[s, 0, 0]
         picks = tube_ids[:, None] == ids[None, :]
         shown_here = jnp.any(picks, 1)
@@ -1606,68 +1957,19 @@
             [jnp.stack([e2d_b_grad, mask_grad] + vec_rows).reshape(-1), head_b_grad]
         )
         small = small + swap(small)
-        small = small + hop_both(small, (0, 1), (2, 3))
-        small = small + hop_both(small, (1, 3))
-        wide, tall, qkv_sum = tree_sum(wide), tree_sum(tall), tree_sum(qkv_grad)
-        qkv_got, square_got, up_got, patch_got, e2d_got, vec_got = encoder_backward(
-            5 + s, picked, shown, enc_weights, enc_stored
+        small = jnp.pad(small.reshape(-1, LANES), ((0, 6), (0, 0)))
+        back = encoder_backward(5 + s, picked, shown, enc_weights, enc_stored, (wide, tall, qkv_grad, small))
+        line = jnp.arange(8)[:, None]
+        stats = jnp.where(line == 1, loss, jnp.where(line == 2, jnp.sum(counted), 0.0))
+        stats = jnp.broadcast_to(stats, (8, LANES))
+        stats, states, pieces = update(
+            7 + s, STEP_BEFORE + s + 1, s == STEPS - 1, stats, (*back[:6], wide, tall, qkv_grad, small, *back[6:]), states
         )
-        head_rows = (3 * rep_quarter - PATCH_SIZE - E2D_SIZE) // PATCH
-        head_cols = PATCH // 2
-        head_low = wide[:, DFF // 2 :].astype(HALF)
-        head_three = hop_both(head_low[:head_rows], (LAST, 2))
-        head_low = jnp.where(
-            z == LAST, head_low, jnp.concatenate([head_three, jnp.zeros((DD - head_rows, head_cols), HALF)], 0)
-        )
-        head_other = swap(head_low, 2, LAST)
-        head_sum = jnp.concatenate(
-            [jnp.where(side == 0, head_low, head_other), jnp.where(side == 0, head_other, head_low)], 1
-        )
-        patch_cut = rep_quarter // D
-        patch_tail = PATCH - 2 * patch_cut
-        narrow = jnp.concatenate(
-            [patch_got[:192], jnp.where(z == 2, jnp.pad(e2d_got, ((0, 128), (0, 0))), patch_got[192:])], 0
-        )
-        narrow_other = swap(narrow, 0, 1, 2)
-        narrow_low = jnp.where(side == 0, narrow, narrow_other)
-        narrow_high = jnp.where(side == 0, narrow_other, narrow)
-        flats = lambda *parts: jnp.concatenate([one.astype(FLOAT).reshape(-1) for one in parts])
-
-        def patch_rows(count):
-            return jnp.concatenate([narrow_low[:count], narrow_high[:count]], 1)
-
-        def first_owner():
-            return flats(qkv_got, square_got[:288]), flats(patch_rows(patch_cut))
-
-        def second_owner():
-            return flats(square_got[:96], up_got), flats(patch_rows(patch_cut))
-
-        def third_owner():
-            return flats(up_got[:96], square_got), flats(
-                patch_rows(patch_tail),
-                narrow_low[192 : 192 + D // 2],
-                narrow_high[192 : 192 + D // 2],
-                head_sum[:head_rows],
-            )
-
-        def last_owner():
-            return flats(
-                square_got[:288], qkv_sum, tall[DFF // 2 :], wide[:, : DFF // 2], tall[: DFF // 2]
-            ), flats(head_sum[head_rows:], vec_got[:9], small)
-
-        ten_part, rep_part = lax.switch(z, [first_owner, second_owner, third_owner, last_owner])
-        squares = jnp.sum(ten_part * ten_part) + jnp.sum(rep_part * rep_part) / 2
-        square_all, loss_all, count_all = lax.psum((squares, loss, jnp.sum(counted)), ("dp", "tensor"))
-        norm_value = jnp.sqrt(square_all + 1e-30) / count_all
-        factor = jnp.minimum(1.0, CLIP / norm_value) / count_all
-        number = STEP_BEFORE + s + 1
-        rep_master, rep_first, rep_second = adamw(rep_master, rep_first, rep_second, rep_part * factor, number)
-        ten_master, ten_first, ten_second = adamw(ten_master, ten_first, ten_second, ten_part * factor, number)
-        loss_list.append(loss_all)
-        count_list.append(count_all)
-        norm_list.append(norm_value)
-    groups_count = lax.axis_size("group")
-    rep_diff, ten_diff = group_mean(rep_weights - rep_master), group_mean(ten_weights[0] - ten_master)
+        norm_list.append(stats[0, 0])
+        loss_list.append(stats[1, 0])
+        count_list.append(stats[2, 0])
+    ten_first, ten_second, rep_first, rep_second = [one.reshape(-1) for one in (*states[1:3], *states[4:])]
+    ten_diff, rep_diff = [group_mean(starts[i] - states[3 * i]).reshape(-1) for i in range(2)]
     rep_momentum = MOMENTUM * rep_outer + rep_diff
     ten_momentum = MOMENTUM * ten_outer[0] + ten_diff
     rep_new = rep_weights - LR_OUT * (rep_diff + MOMENTUM * rep_momentum)

time: 1490 us -> 1300 us (0.87)
  Pallas kernels: 755 us -> 898 us
  other arithmetic: 214 us -> 97.8 us
  starting transfers between devices: 96.8 us -> 36.6 us
  blocking collectives: 57.4 us -> 0 us
  local copies, waits for them, and re-layouts: 119 us -> 73.7 us
  loops' own time: 32.1 us -> 0 us
  waiting for transfers between devices: 80.5 us -> 53.2 us
    pallas_call x0 -> x3, Pallas kernels: none -> 140 us  [the longest x2 135 us: update(): pl.pallas_call(functools.partial(update_kernel, number, last), name='upda...]
    psum x2 -> x0, blocking collectives: 57.4 us -> none  [hosted_round(): lax.psum((squares, loss, jnp.sum(counted)), ('dp', 'tensor'))]
    ppermute x30 -> x8, starting transfers between devices: 71.4 us -> 14.7 us  [hop(): return lax.ppermute(value, ('dp', 'tensor'), pairs)]
    ppermute x30 -> x8, waiting for transfers between devices: 44.9 us -> 0.02 us  [hop(): return lax.ppermute(value, ('dp', 'tensor'), pairs)]
    another operation x4 -> x0, loops' own time: 32.1 us -> none  [the longest x2 16.2 us: hosted_round(): lax.switch(z, [first_owner, second_owner, third_owner, last_owner])]
    sub x4 -> x2, other arithmetic: 30.4 us -> 2.42 us  [hosted_round(): starts[i] - states[3 * i]]
    convert_element_type x18 -> x0, other arithmetic: 24.1 us -> none  [the longest x10 16.7 us: tree_sum(): return part + hop_both(part.astype(HALF), (1, 3)).astype(FLOAT)]
    mul x4 -> x0, other arithmetic: 19.7 us -> none  [the longest x2 9.86 us: adamw(): second = BETA2 * second + (1 - BETA2) * clipped * clipped]
  transfers between devices with their start and end apart: 48 -> 26, of which waited for: 10 -> 9; matrix products, arithmetic and copies ran while one was open for 17% -> 13% of each run, Pallas kernels for 35% -> 22%
where the time goes in v2:
time: 1300 us; the launch traced here: 1290 us
  Pallas kernels  898 us (69%)
  matrix products  122 us (9%)
  other arithmetic  97.8 us (8%)
  local copies, waits for them, and re-layouts  73.7 us (6%)
  waiting for transfers between devices  53.2 us (4%)
  starting transfers between devices  36.6 us (3%)
    pallas_call x2, Pallas kernels, hosted_weights(): pl.pallas_call(functools.partial(weights_kernel, shared), name='weights',...  249 us
    pallas_call x2, Pallas kernels, encoder_backward(): pl.pallas_call(encoder_backward_kernel, name='encoder_backward', out_shap...  245 us
    pallas_call x2, Pallas kernels, update(): pl.pallas_call(functools.partial(update_kernel, number, last), name='upda...  135 us
    pallas_call x2, Pallas kernels, encoder_forward(): pl.pallas_call(encoder_forward_kernel, name='encoder_forward', out_shape=...  123 us
    pallas_call x2, Pallas kernels, attn_backward(): pl.pallas_call(attn_backward_kernel, name='attn_backward', out_shape=jax....  84.3 us
    pallas_call x2, Pallas kernels, attn_forward(): pl.pallas_call(attn_forward_kernel, name='attn_forward', out_shape=(jax.S...  57.5 us
    dot_general x14, matrix products, mm(): return jnp.dot(left, right, preferred_element_type=FLOAT)  46.1 us
    unnamed x305, local copies, waits for them, and re-layouts  30.6 us
  transfers between devices with their start and end apart: 26, of which 9 were waited for; matrix products, arithmetic and copies ran while one was open for 13% of the time, Pallas kernels for 22%

profile of v2, /device:TPU:0, one launch (start us, length us, event | category | flops | bytes accessed | tf_op | source)
XLA Modules:
  0.0 1286.6 jit_solution(8190306488756330241)
XLA Ops:
  1.3 3.5 fusion.28
  5.1 3.5 fusion.31
  10.2 5.0 collective-permute-start
  20.9 8.1 fusion.147
  29.0 5.5 lay_out.1
  42.7 98.1 %weights.2 = (bf16[704,768]{1,0:T(8,128)(2,1)}, bf16[192,768]{1,0:T(8,128)(2,1)}, bf16[768,1152]{1,0:T(8,128)(2,1)}, bf16[384,768]{1,0:T(8,128)(2,1)}, bf16[768,...) custom-call(bf16[768,1152]{1,0:T(8,128)(2,1)} %copy-done.1, ...), custom_call_target="tpu_custom_call" | custom-call | tf_op jit(solution)/shard_map/weights/pallas_call | solution.py:833
  146.1 3.3 convert_reduce_fusion
  171.0 8.3 fusion.55
  183.0 71.6 %encoder_forward.2 = (f32[160,384]{1,0:T(8,128)}, f32[320,768]{1,0:T(8,128)}, bf16[640,768]{1,0:T(8,128)(2,1)}, bf16[640,1152]{1,0:T(8,128)(2,1)}, bf16[640,384]...) custom-call(bf16[320,1792]{1,0:T(8,128)(2,1)} %pad_maximum_fusion.5., ...), custom_call_target="tpu_custom_call" | custom-call | tf_op jit(solution)/shard_map/encoder_forward/pallas_call | solution.py:1087
  254.7 11.9 fusion.157
  270.5 28.6 %attn_forward.2 = (bf16[1568,192]{1,0:T(8,128)(2,1)S(1)}, f32[3,7,224]{2,1,0:T(8,128)S(1)}) custom-call(bf16[1568,192]{1,0:T(8,128)(2,1)S(1)} %get-tuple-element.365.q_ref, bf16[1568,192]{1,0:T(8,128)(2,1)S(1)} %get-tuple-element.364.k_ref, bf16[1568,192]{1,0:T(8,128)(2,1)S(1)} %get-tuple-element.363.v_ref), custom_call_target="tpu_custom_call" | custom-call | flops 1888223232 | bytes 2408448 | tf_op jit(solution)/shard_map/attn_forward/pallas_call | solution.py:445
  299.1 5.0 collective-permute-start.4
  308.4 3.5 collective-permute-done.4
  313.4 11.2 multiply_convert_fusion.1
  331.7 2.7 add_convert_fusion.1
  339.6 3.0 fusion.131
  342.7 3.0 fusion.133
  345.7 3.2 fusion.85
  367.6 42.1 %attn_backward.2 = bf16[1568,576]{1,0:T(8,128)(2,1)S(1)} custom-call(bf16[1568,192]{1,0:T(8,128)(2,1)S(1)} %get-tuple-element.365.q_ref, bf16[1568,192]{1,0:T(8,128)(2,1)S(1)} %get-tuple-element.364.k_ref, bf16[1568,192]{1,0:T(8,128)(2,1)S(1)} %get-tuple-element.363.v_ref, bf16[1568,192]{1,0:T(8,128)(2,1)S(1)} %pad_maximum_fusion.7.g_ref, ...), custom_call_target="tpu_custom_call" | custom-call | flops 4720558080 | bytes 4214784 | tf_op jit(solution)/shard_map/attn_backward/pallas_call | solution.py:477
  412.8 2.5 maximum_add_fusion.2.tall
  415.3 2.9 pad_maximum_fusion.1.shown
  418.2 2.9 pad_maximum_fusion.2.shown
  421.2 3.1 maximum_add_fusion.wide
  424.2 6.4 collective-permute-done.6
  438.7 144.8 %encoder_backward.2 = (bf16[768,1152]{1,0:T(8,128)(2,1)}, bf16[1248,768]{1,0:T(8,128)(2,1)}, bf16[672,1536]{1,0:T(8,128)(2,1)}, bf16[704,384]{1,0:T(8,128)(2,1)}...) custom-call(bf16[160,384]{1,0:T(8,128)(2,1)} %convolution_convert_fu, ...), custom_call_target="tpu_custom_call" | custom-call | tf_op jit(solution)/shard_map/encoder_backward/pallas_call | solution.py:1468
  584.2 62.6 %update.2 = (f32[8,128]{1,0:T(8,128)}, f32[8640,128]{1,0:T(8,128)}, f32[8640,128]{1,0:T(8,128)}, f32[8640,128]{1,0:T(8,128)}, f32[4056,128]{1,0:T(8,128)}, /*ind...) custom-call(f32[8,128]{1,0:T(8,128)} %broadcast_in_dim.192.stats, ...), custom_call_target="tpu_custom_call" | custom-call | tf_op jit(solution)/shard_map/update/pallas_call | solution.py:1801
  646.8 150.6 %weights.3 = (bf16[704,768]{1,0:T(8,128)(2,1)}, bf16[192,768]{1,0:T(8,128)(2,1)}, bf16[768,1152]{1,0:T(8,128)(2,1)}, bf16[384,768]{1,0:T(8,128)(2,1)}, bf16[768,...) custom-call(bf16[768,1152]{1,0:T(8,128)(2,1)} %get-tuple-element.202, ...), custom_call_target="tpu_custom_call" | custom-call | tf_op jit(solution)/shard_map/weights/pallas_call | solution.py:833
  801.5 51.3 %encoder_forward.3 = (f32[160,384]{1,0:T(8,128)}, f32[320,768]{1,0:T(8,128)}, bf16[640,768]{1,0:T(8,128)(2,1)}, bf16[640,1152]{1,0:T(8,128)(2,1)}, bf16[640,384]...) custom-call(bf16[320,1792]{1,0:T(8,128)(2,1)} %pad_maximum_fusion.6., ...), custom_call_target="tpu_custom_call" | custom-call | tf_op jit(solution)/shard_map/encoder_forward/pallas_call | solution.py:1087
  852.9 11.9 fusion.160
  868.6 29.0 %attn_forward.3 = (bf16[1568,192]{1,0:T(8,128)(2,1)S(1)}, f32[3,7,224]{2,1,0:T(8,128)S(1)}) custom-call(bf16[1568,192]{1,0:T(8,128)(2,1)S(1)} %get-tuple-element.362.q_ref, bf16[1568,192]{1,0:T(8,128)(2,1)S(1)} %get-tuple-element.361.k_ref, bf16[1568,192]{1,0:T(8,128)(2,1)S(1)} %get-tuple-element.360.v_ref), custom_call_target="tpu_custom_call" | custom-call | flops 1888223232 | bytes 2408448 | tf_op jit(solution)/shard_map/attn_forward/pallas_call | solution.py:445
  898.4 4.1 collective-permute-start.13
  911.1 11.2 multiply_convert_fusion
  922.4 2.9 fusion.162
  925.8 2.8 multiply_reduce_fusion.2
  932.4 4.2 add_convert_fusion
  944.6 3.0 fusion.135
  949.6 3.2 fusion.82
  971.7 42.2 %attn_backward.3 = bf16[1568,576]{1,0:T(8,128)(2,1)S(1)} custom-call(bf16[1568,192]{1,0:T(8,128)(2,1)S(1)} %get-tuple-element.362.q_ref, bf16[1568,192]{1,0:T(8,128)(2,1)S(1)} %get-tuple-element.361.k_ref, bf16[1568,192]{1,0:T(8,128)(2,1)S(1)} %get-tuple-element.360.v_ref, bf16[1568,192]{1,0:T(8,128)(2,1)S(1)} %pad_maximum_fusion.8.g_ref, ...), custom_call_target="tpu_custom_call" | custom-call | flops 4720558080 | bytes 4214784 | tf_op jit(solution)/shard_map/attn_backward/pallas_call | solution.py:477
  1016.5 2.5 maximum_add_fusion.3.tall
  1020.8 7.5 collective-permute-done.15
  1033.0 2.8 collective-permute-done.19
  1036.4 99.8 %encoder_backward.3 = (bf16[768,1152]{1,0:T(8,128)(2,1)}, bf16[1248,768]{1,0:T(8,128)(2,1)}, bf16[672,1536]{1,0:T(8,128)(2,1)}, bf16[704,384]{1,0:T(8,128)(2,1)}...) custom-call(bf16[160,384]{1,0:T(8,128)(2,1)} %convolution_convert_fu, ...), custom_call_target="tpu_custom_call" | custom-call | tf_op jit(solution)/shard_map/encoder_backward/pallas_call | solution.py:1468
  1136.9 72.2 %update.3 = (f32[8,128]{1,0:T(8,128)}, f32[8640,128]{1,0:T(8,128)}, f32[8640,128]{1,0:T(8,128)}, f32[8640,128]{1,0:T(8,128)}, f32[4056,128]{1,0:T(8,128)}, /*index=5*/f32[4056,128]{1,0:T(8,128)}, f32[4056,128]{1,0:T(8,128)}) custom-call(f32[8,128]{1,0:T(8,128)} %broadcast_in_dim.202.stats, bf16[768,1152]{1,0:T(8,128)(2,1)} %get-tuple-element.246.qkv, ...), custom_call_target="tpu_custom_call" | custom-call | tf_op jit(solution)/shard_map/update/pallas_call | solution.py:1801
  1216.0 12.7 collective-permute-done.21
  1239.3 16.8 %collective-permute-done.24 = bf16[4320,128]{1,0:T(8,128)(2,1)S(1)} collective-permute-done((bf16[4320,128]{1,0:T(8,128)(2,1)S(1)}, bf16[4320,128]{1,0:T(8,128)(2,1)S(1)}, u32[]{:S(2)}, u32[]{:S(2)}) %collective-permute-start.24) | collective-permute-done | bytes 1105952 | tf_op jit(solution)/shard_map/ppermute | solution.py:2002
  1256.5 3.1 multiply_subtract_fusion.1
  1261.3 2.6 pad_maximum_fusion
  1264.0 13.3 %multiply_subtract_fusion = (f32[1,1105920]{1,0:T(1,128)}, f32[1,1105920]{1,0:T(1,128)}) fusion(f32[1,1105920]{1,0:T(1,128)S(1)} %bitcast.131, f32[1,1105920]{1,0:T(1,128)S(1)} %bitcast.139, f32[1,1105920]{1,0:T(1,128)S(1)} %bitcast.142), kind=kLoop, calls=%fused_computation.59 | loop fusion | flops 6635520 | bytes 22118400 | tf_op jit(solution)/shard_map/sub | solution.py:1976
  (573 shorter events, 186.3 us)
Async XLA Ops:
  1.3 142.2 %copy-start.101 = (s32[1,1,1,160]{3,2,1,0:T(1,128)}, s32[1,1,1,160]{3,2,1,0:T(1,128)S(1)}, u32[]{:S(2)}) copy-start(s32[1,1,1,160]{3,2,1,0:T(1,128)S(1)} %get-tuple-element.386) | copy-start | bytes 1924
  9.5 169.8 %collective-permute-start.1 = (bf16[160,1792]{1,0:T(8,128)(2,1)}, bf16[160,1792]{1,0:T(8,128)(2,1)S(1)}, u32[]{:S(2)}, u32[]{:S(2)}) collective-permute-start(bf16[160,1792]{1,0:T(8,128)(2,1)} %fusion.61), channel_id=1, source_target_pairs={{7,3},{15,11},{23,19},{31,27}} | collective-permute-start | bytes 1720328 | tf_op jit(solution)/shard_map/ppermute | solution.py:501
  10.2 169.2 %collective-permute-start = (bf16[160,1792]{1,0:T(8,128)(2,1)}, bf16[160,1792]{1,0:T(8,128)(2,1)S(1)}, u32[]{:S(2)}, u32[]{:S(2)}) collective-permute-start(bf16[160,1792]{1,0:T(8,128)(2,1)} %fusion.61), channel_id=1, source_target_pairs={{0,2},{5,3},{8,10},{13,11},{16,18},{21,19},{24,26},{29,27}} | collective-permute-start | bytes 1720328 | tf_op jit(solution)/shard_map/ppermute | solution.py:501
  15.7 152.5 %collective-permute-start.3 = (s32[2,160]{1,0:T(2,128)}, s32[2,160]{1,0:T(2,128)S(1)}, u32[]{:S(2)}, u32[]{:S(2)}) collective-permute-start(s32[2,160]{1,0:T(2,128)} %bitcast.127), channel_id=1, source_target_pairs={{7,3},{15,11},{23,19},{31,27}} | collective-permute-start | bytes 3848 | tf_op jit(solution)/shard_map/ppermute | solution.py:501
  16.4 153.7 %collective-permute-start.2 = (s32[2,160]{1,0:T(2,128)}, s32[2,160]{1,0:T(2,128)}, u32[]{:S(2)}, u32[]{:S(2)}) collective-permute-start(s32[2,160]{1,0:T(2,128)} %bitcast.127), channel_id=1, source_target_pairs={{0,2},{5,3},{8,10},{13,11},{16,18},{21,19},{24,26},{29,27}} | collective-permute-start | bytes 3848 | tf_op jit(solution)/shard_map/ppermute | solution.py:501
  19.4 285.3 %collective-permute-start.12 = (bf16[160,1792]{1,0:T(8,128)(2,1)}, bf16[160,1792]{1,0:T(8,128)(2,1)}, u32[]{:S(2)}, u32[]{:S(2)}) collective-permute-start(bf16[160,1792]{1,0:T(8,128)(2,1)} %fusion.63), channel_id=1, source_target_pairs={{7,3},{15,11},{23,19},{31,27}} | collective-permute-start | bytes 1720328 | tf_op jit(solution)/shard_map/ppermute | solution.py:501
  42.7 99.6 %copy-start.127 = (s32[2,1,1]{0,2,1:T(1,128)S(1)}, s32[2,1,1]{0,2,1:T(1,128)}, u32[]{:S(2)}) copy-start(s32[2,1,1]{0,2,1:T(1,128)} %param.15) | copy-start | bytes 28
  42.7 102.1 %copy-start.128 = (s32[2,1,1]{0,2,1:T(1,128)S(1)}, s32[2,1,1]{0,2,1:T(1,128)}, u32[]{:S(2)}) copy-start(s32[2,1,1]{0,2,1:T(1,128)} %param.14) | copy-start | bytes 28
  142.3 112.4 %copy-start.124 = (f32[384]{0:T(512)}, f32[384]{0:T(512)S(1)}, u32[]{:S(2)}) copy-start(f32[384]{0:T(512)S(1)} %fusion.120) | copy-start | bytes 4612
  142.3 112.4 %copy-start.134 = (pred[384]{0:T(512)(128)(4,1)}, pred[384]{0:T(512)(128)(4,1)S(1)}, u32[]{:S(2)}) copy-start(pred[384]{0:T(512)(128)(4,1)S(1)} %fusion.116) | copy-start | bytes 1156
  154.9 112.2 %copy-start.112 = (f32[384]{0:T(512)}, f32[384]{0:T(512)S(1)}, u32[]{:S(2)}) copy-start(f32[384]{0:T(512)S(1)} %get-tuple-element.321) | copy-start | bytes 4612
  168.8 136.1 %collective-permute-start.11 = (bf16[160,1792]{1,0:T(8,128)(2,1)}, bf16[160,1792]{1,0:T(8,128)(2,1)S(1)}, u32[]{:S(2)}, u32[]{:S(2)}) collective-permute-start(bf16[160,1792]{1,0:T(8,128)(2,1)} %fusion.63), channel_id=1, source_target_pairs={{0,2},{5,3},{8,10},{13,11},{16,18},{21,19},{24,26},{29,27}} | collective-permute-start | bytes 1720328 | tf_op jit(solution)/shard_map/ppermute | solution.py:501
  180.2 74.4 %copy-start.43 = (bf16[160,1792]{1,0:T(8,128)(2,1)}, bf16[160,1792]{1,0:T(8,128)(2,1)S(1)}, u32[]{:S(2)}) copy-start(bf16[160,1792]{1,0:T(8,128)(2,1)S(1)} %collective-permute-done) | copy-start | bytes 1720324
  181.4 233.9 %collective-permute-start.7 = (bf16[320,1792]{1,0:T(8,128)(2,1)}, bf16[320,1792]{1,0:T(8,128)(2,1)}, u32[]{:S(2)}, u32[]{:S(2)}) collective-permute-start(bf16[320,1792]{1,0:T(8,128)(2,1)} %pad_maximum_fusion.5.shown), channel_id=1, source_target_pairs={{2,3},{3,2},{10,11},{11,10},{18,19},{19,18},{26,27},{27,26}} | collective-permute-start | bytes 3440648 | tf_op jit(solution)/shard_map/ppermute | solution.py:501
  266.6 45.4 %copy-start.11 = (f32[1568,384]{1,0:T(8,128)}, f32[1568,384]{1,0:T(8,128)S(1)}, u32[]{:S(2)}) copy-start(f32[1568,384]{1,0:T(8,128)S(1)} %get-tuple-element.395) | copy-start | bytes 7225348
  299.1 12.9 collective-permute-start.4
  306.0 112.2 %collective-permute-start.16 = (bf16[320,1792]{1,0:T(8,128)(2,1)}, bf16[320,1792]{1,0:T(8,128)(2,1)}, u32[]{:S(2)}, u32[]{:S(2)}) collective-permute-start(bf16[320,1792]{1,0:T(8,128)(2,1)} %pad_maximum_fusion.6.shown), channel_id=1, source_target_pairs={{2,3},{3,2},{10,11},{11,10},{18,19},{19,18},{26,27},{27,26}} | collective-permute-start | bytes 3440648 | tf_op jit(solution)/shard_map/ppermute | solution.py:501
  350.7 15.6 %collective-permute-start.5 = (bf16[784,192]{1,0:T(8,128)(2,1)}, bf16[784,192]{1,0:T(8,128)(2,1)}, u32[]{:S(2)}, u32[]{:S(2)}) collective-permute-start(bf16[784,192]{1,0:T(8,128)(2,1)} %copy.46), channel_id=1, source_target_pairs={{0,1},{1,0},{2,3},{3,2},{4,5},{5,4},{6,7},{7,6},{8,9},{9,8},{10,11... | collective-permute-start | bytes 903176 | tf_op jit(solution)/shard_map/ppermute | solution.py:511
  357.5 63.6 %collective-permute-start.8 = (bf16[384,1536]{1,0:T(8,128)(2,1)}, bf16[384,1536]{1,0:T(8,128)(2,1)}, u32[]{:S(2)}, u32[]{:S(2)}) collective-permute-start(bf16[384,1536]{1,0:T(8,128)(2,1)} %pad_maximum_fusion.3), channel_id=1, source_target_pairs={{0,1},{1,0},{2,3},{3,2},{4,5},{5,4},{6,7},{7,6},{8,9},{9,8},{10,11... | collective-permute-start | bytes 3538952 | tf_op jit(solution)/shard_map/ppermute | solution.py:511
  359.4 53.4 %collective-permute-start.9 = (bf16[960,384]{1,0:T(8,128)(2,1)}, bf16[960,384]{1,0:T(8,128)(2,1)}, u32[]{:S(2)}, u32[]{:S(2)}) collective-permute-start(bf16[960,384]{1,0:T(8,128)(2,1)} %pad_maximum_fusion.9), channel_id=1, source_target_pairs={{0,1},{1,0},{2,3},{3,2},{4,5},{5,4},{6,7},{7,6},{8,9},{9,8},{10,11... | collective-permute-start | bytes 2211848 | tf_op jit(solution)/shard_map/ppermute | solution.py:511
  367.6 42.8 %copy-start.12 = (f32[1568,384]{1,0:T(8,128)S(1)}, f32[1568,384]{1,0:T(8,128)}, u32[]{:S(2)}) copy-start(f32[1568,384]{1,0:T(8,128)} %copy-done.11) | copy-start | bytes 7225348
  367.6 42.8 %copy-start.98 = (f32[1568]{0:T(1024)S(1)}, f32[1568]{0:T(1024)}, u32[]{:S(2)}) copy-start(f32[1568]{0:T(1024)} %copy-done.97) | copy-start | bytes 18820
  367.6 42.8 %copy-start.113 = (f32[384]{0:T(512)S(1)}, f32[384]{0:T(512)}, u32[]{:S(2)}) copy-start(f32[384]{0:T(512)} %copy-done.112) | copy-start | bytes 4612
  409.9 20.8 %collective-permute-start.6 = (bf16[784,576]{1,0:T(8,128)(2,1)S(1)}, bf16[784,576]{1,0:T(8,128)(2,1)S(1)}, u32[]{:S(2)}, u32[]{:S(2)}) collective-permute-start(bf16[784,576]{1,0:T(8,128)(2,1)S(1)} %slice.393), channel_id=1, source_target_pairs={{0,1},{1,0},{2,3},{3,2},{4,5},{5,4},{6,7},{7,6},{8,9},{9,8},{10,11... | collective-permute-start | bytes 2709512 | tf_op jit(solution)/shard_map/ppermute | solution.py:511
  434.2 3.9 collective-permute-start.10
  646.8 152.6 %copy-start.111 = (pred[16]{0:T(512)(128)(4,1)S(1)}, pred[16]{0:T(512)(128)(4,1)}, u32[]{:S(2)}) copy-start(pred[16]{0:T(512)(128)(4,1)} %constant.217.clone.1) | copy-start | bytes 52
  801.5 64.1 %copy-start.89 = (f32[384]{0:T(512)}, f32[384]{0:T(512)S(1)}, u32[]{:S(2)}) copy-start(f32[384]{0:T(512)S(1)} %get-tuple-element.312) | copy-start | bytes 4612
  801.5 64.1 %copy-start.115 = (f32[384]{0:T(512)}, f32[384]{0:T(512)S(1)}, u32[]{:S(2)}) copy-start(f32[384]{0:T(512)S(1)} %get-tuple-element.311) | copy-start | bytes 4612
  801.5 51.3 %copy-start.87 = (pred[1568]{0:T(1024)(128)(4,1)S(1)}, pred[1568]{0:T(1024)(128)(4,1)}, u32[]{:S(2)}) copy-start(pred[1568]{0:T(1024)(128)(4,1)} %copy-done.86) | copy-start | bytes 4708
  801.5 51.3 %copy-start.102 = (s32[1,1,1,160]{3,2,1,0:T(1,128)S(1)}, s32[1,1,1,160]{3,2,1,0:T(1,128)}, u32[]{:S(2)}) copy-start(s32[1,1,1,160]{3,2,1,0:T(1,128)} %copy-done.101) | copy-start | bytes 1924
  801.5 51.3 %copy-start.125 = (f32[384]{0:T(512)S(1)}, f32[384]{0:T(512)}, u32[]{:S(2)}) copy-start(f32[384]{0:T(512)} %copy-done.124) | copy-start | bytes 4612
  801.5 51.3 %copy-start.135 = (pred[384]{0:T(512)(128)(4,1)S(1)}, pred[384]{0:T(512)(128)(4,1)}, u32[]{:S(2)}) copy-start(pred[384]{0:T(512)(128)(4,1)} %copy-done.134) | copy-start | bytes 1156
  898.4 10.3 collective-permute-start.13
  954.6 15.7 %collective-permute-start.14 = (bf16[784,192]{1,0:T(8,128)(2,1)}, bf16[784,192]{1,0:T(8,128)(2,1)}, u32[]{:S(2)}, u32[]{:S(2)}) collective-permute-start(bf16[784,192]{1,0:T(8,128)(2,1)} %copy.51), channel_id=1, source_target_pairs={{0,1},{1,0},{2,3},{3,2},{4,5},{5,4},{6,7},{7,6},{8,9},{9,8},{10,11... | collective-permute-start | bytes 903176 | tf_op jit(solution)/shard_map/ppermute | solution.py:511
  961.8 54.7 %collective-permute-start.18 = (bf16[960,384]{1,0:T(8,128)(2,1)}, bf16[960,384]{1,0:T(8,128)(2,1)}, u32[]{:S(2)}, u32[]{:S(2)}) collective-permute-start(bf16[960,384]{1,0:T(8,128)(2,1)} %pad_maximum_fusion.10), channel_id=1, source_target_pairs={{0,1},{1,0},{2,3},{3,2},{4,5},{5,4},{6,7},{7,6},{8,9},{9,8},{10,11... | collective-permute-start | bytes 2211848 | tf_op jit(solution)/shard_map/ppermute | solution.py:511
  966.8 52.2 %collective-permute-start.17 = (bf16[384,1536]{1,0:T(8,128)(2,1)}, bf16[384,1536]{1,0:T(8,128)(2,1)S(1)}, u32[]{:S(2)}, u32[]{:S(2)}) collective-permute-start(bf16[384,1536]{1,0:T(8,128)(2,1)} %pad_maximum_fusion.4), channel_id=1, source_target_pairs={{0,1},{1,0},{2,3},{3,2},{4,5},{5,4},{6,7},{7,6},{8,9},{9,8},{10,11... | collective-permute-start | bytes 3538952 | tf_op jit(solution)/shard_map/ppermute | solution.py:511
  971.6 42.5 %copy-start.14 = (f32[1568,384]{1,0:T(8,128)S(1)}, f32[1568,384]{1,0:T(8,128)}, u32[]{:S(2)}) copy-start(f32[1568,384]{1,0:T(8,128)} %copy-done.13) | copy-start | bytes 7225348
  971.6 42.4 %copy-start.90 = (f32[384]{0:T(512)S(1)}, f32[384]{0:T(512)}, u32[]{:S(2)}) copy-start(f32[384]{0:T(512)} %copy-done.89) | copy-start | bytes 4612
  971.6 42.4 %copy-start.96 = (f32[1568]{0:T(1024)S(1)}, f32[1568]{0:T(1024)}, u32[]{:S(2)}) copy-start(f32[1568]{0:T(1024)} %copy-done.95) | copy-start | bytes 18820
  1013.9 14.4 %collective-permute-start.15 = (bf16[784,576]{1,0:T(8,128)(2,1)S(1)}, bf16[784,576]{1,0:T(8,128)(2,1)S(1)}, u32[]{:S(2)}, u32[]{:S(2)}) collective-permute-start(bf16[784,576]{1,0:T(8,128)(2,1)S(1)} %slice.422), channel_id=1, source_target_pairs={{0,1},{1,0},{2,3},{3,2},{4,5},{5,4},{6,7},{7,6},{8,9},{9,8},{10,11... | collective-permute-start | bytes 2709512 | tf_op jit(solution)/shard_map/ppermute | solution.py:511
  1031.9 3.9 collective-permute-start.19
  1136.9 72.3 %copy-start.10 = (f32[519168]{0:T(1024)S(1)}, f32[519168]{0:T(1024)}, u32[]{:S(2)}) copy-start(f32[519168]{0:T(1024)} %param.16) | copy-start | bytes 6230020
  1211.3 2.9 collective-permute-start.20
  1214.1 14.8 %collective-permute-start.23 = (f32[4320,128]{1,0:T(8,128)S(1)}, f32[4320,128]{1,0:T(8,128)S(1)}, u32[]{:S(2)}, u32[]{:S(2)}) collective-permute-start(f32[4320,128]{1,0:T(8,128)S(1)} %slice_select_fusion), channel_id=1, source_target_pairs={{0,8},{8,0},{16,24},{24,16},{1,9},{9,1},{17,25},{25,17},{2,10},{10... | collective-permute-start | bytes 6635528 | tf_op jit(solution)/shard_map/ppermute | solution.py:516
  1214.4 14.3 %collective-permute-start.21 = (bf16[2028,128]{1,0:T(8,128)(2,1)S(1)}, bf16[2028,128]{1,0:T(8,128)(2,1)S(1)}, u32[]{:S(2)}, u32[]{:S(2)}) collective-permute-start(bf16[2028,128]{1,0:T(8,128)(2,1)S(1)} %add_convert_fusion.9), channel_id=1, source_target_pairs={{0,16},{8,24},{16,0},{24,8},{1,17},{9,25},{17,1},{25,9},{2,18},{10... | collective-permute-start | bytes 1557512 | tf_op jit(solution)/shard_map/ppermute | solution.py:2002
  1228.9 10.2 collective-permute-start.22
  1229.3 26.8 %collective-permute-start.24 = (bf16[4320,128]{1,0:T(8,128)(2,1)S(1)}, bf16[4320,128]{1,0:T(8,128)(2,1)S(1)}, u32[]{:S(2)}, u32[]{:S(2)}) collective-permute-start(bf16[4320,128]{1,0:T(8,128)(2,1)S(1)} %add_convert_fusion.4), channel_id=1, source_target_pairs={{0,16},{8,24},{16,0},{24,8},{1,17},{9,25},{17,1},{25,9},{2,18},{10... | collective-permute-start | bytes 3317768 | tf_op jit(solution)/shard_map/ppermute | solution.py:2002
  1256.4 4.4 collective-permute-start.25
  (130 other events, 698.3 us)

commit v3 on v2

--- a/solution.py
+++ b/solution.py
@@ -528,11 +528,29 @@
     return lax.dot_general(left, right, (((0,), (0,)), ((), ())), preferred_element_type=FLOAT)
 
 
-def sinus_at(ids, width):
+def sinus_parts(width):
     column = jnp.arange(width)
     decays = jnp.power(10000.0, -2.0 * (column // 2).astype(FLOAT) / width)
-    angles = ids.astype(FLOAT)[:, None] * decays[None, :]
-    return jnp.where(column % 2 == 0, jnp.sin(angles), jnp.cos(angles))
+    far = (32 * jnp.arange(-(-TUBES // 32))).astype(FLOAT)[:, None] * decays
+    near = jnp.arange(32).astype(FLOAT)[:, None] * decays
+    even = column % 2 == 0
+    near_one = jnp.where(even, jnp.cos(near), -jnp.sin(near))
+    near_two = jnp.where(even, jnp.sin(near), jnp.cos(near))
+    return jnp.concatenate([jnp.sin(far), jnp.cos(far)], 1), jnp.concatenate([near_one, near_two], 1)
+
+
+def sinus_all(width):
+    far, near = sinus_parts(width)
+    table = far[:, None, :width] * near[None, :, :width] + far[:, None, width:] * near[None, :, width:]
+    return table.reshape(-1, width)[:TUBES]
+
+
+def thirds_of(rows):
+    thirds = []
+    for _ in range(3):
+        thirds.append(lax.optimization_barrier(rows.astype(HALF)))
+        rows = rows - thirds[-1].astype(FLOAT)
+    return thirds
 
 
 (
@@ -592,275 +610,7 @@
     (W_DOWN, 288, 3, SQUARE, 1248),
     (E2D_W, 768, 2, E2D, 0),
 ]
-GOT = {
-    PATCH_LOW: (704, 768),
-    PATCH_HIGH: (192, 768),
-    W_QKV: (768, 1152),
-    W_OUT: (384, 768),
-    W_UP: (768, 1536),
-    W_DOWN: (1536, 768),
-    E2D_W: (768, 384),
-    HEAD: (64, 1536),
-    VECS: (16, 768),
-}
 MESH_ID = pl.DeviceIdType.MESH
-
-
-def weights_kernel(shared, *refs):
-    sent = dict(zip(SENT, refs[: len(SENT)]))
-    refs = refs[len(SENT) :]
-    got = dict(zip(GOT, refs[: len(GOT)]))
-    refs = refs[len(GOT) :]
-    own = dict(zip(DEC_PARTS, refs[: len(DEC_PARTS)]))
-    other = dict(zip(DEC_PARTS, refs[len(DEC_PARTS) : 2 * len(DEC_PARTS)]))
-    send_sem, recv_sem, local_sem = refs[2 * len(DEC_PARTS) :]
-    g, z, x = lax.axis_index("group"), lax.axis_index("dp"), lax.axis_index("tensor")
-    odd = lax.rem(g, 2)
-    mate = (g + 1 - 2 * odd, z, x)
-    across = (g, z, 1 - x)
-
-    def at(row):
-        return (g, row, x)
-
-    def greet(peer):
-        pl.semaphore_signal(barrier, inc=1, device_id=peer, device_id_type=MESH_ID)
-
-    barrier = pltpu.get_barrier_semaphore()
-    greet(across)
-    near = {0: [1], 1: [0, 2, 3], 2: [1, 3], 3: [2, 1]}
-    if shared:
-        greet(mate)
-    for row, peers in near.items():
-
-        @pl.when(z == row)
-        def _():
-            for peer in peers:
-                greet(at(peer))
-            pl.semaphore_wait(barrier, len(peers) + (2 if shared else 1))
-
-    def part(ref, start, count, half):
-        if not half:
-            return ref.at[pl.ds(start, count)]
-        return ref.at[pl.ds(pl.multiple_of(start + odd * (count // 2), 16), count // 2)]
-
-    numbers = {}
-
-    def copy(key, source, target, peer):
-        index = numbers.setdefault(key, len(numbers))
-        return pltpu.make_async_remote_copy(
-            src_ref=source,
-            dst_ref=target,
-            send_sem=send_sem.at[index],
-            recv_sem=recv_sem.at[index],
-            device_id=peer,
-            device_id_type=MESH_ID,
-        )
-
-    def enc_copy(item):
-        name, count, owner, piece, first = item
-        return copy(
-            (SEND_ENC, name, first),
-            part(sent[piece], 0, count, shared),
-            part(got[name], first, count, shared),
-            at(HOST),
-        )
-
-    def enc_mate(item):
-        name, count, owner, piece, first = item
-        half = part(got[name], first, count, True)
-        return copy((SEND_MATE, name, first), half, half, mate)
-
-    def local(index, source, target):
-        return pltpu.make_async_copy(source, target, local_sem.at[index])
-
-    def chain(name, source, peer):
-        target = got[name] if name in got else own[name]
-        rows = source.shape[0]
-        half = shared and name in own
-        return copy((CHAIN, name), part(source, 0, rows, half), part(target, 0, rows, half), at(peer))
-
-    def cross(name, source):
-        rows = source.shape[0]
-        return copy(
-            (CROSS, name), part(source, 0, rows, shared), part(other[name], 0, rows, shared), across
-        )
-
-    def mates(name, ref, label):
-        half = part(ref, 0, ref.shape[0], True)
-        return copy((label, name), half, half, mate)
-
-    def owned(row):
-        return [item for item in ENC_PARTS if item[2] == row and row != HOST]
-
-    for item in ENC_PARTS:
-        numbers[(SEND_ENC, item[0], item[4])] = len(numbers)
-        numbers[(SEND_MATE, item[0], item[4])] = len(numbers)
-    for name in DEC_PARTS + [VECS, HEAD, HEAD_UP]:
-        for label in (CHAIN, CROSS, MATE_OWN, MATE_OTHER):
-            numbers[(label, name)] = len(numbers)
-
-    def head_up():
-        return copy((CHAIN, HEAD_UP), sent[HEAD], got[HEAD], at(LAST))
-
-    def finish_dec(name, source, here):
-        cross(name, source).start()
-        if shared and not here:
-            mates(name, own[name], MATE_OWN).start()
-
-    def end_dec(name, source, here):
-        cross(name, source).wait()
-        if shared:
-            mates(name, other[name], MATE_OTHER).start()
-
-    def end_mates(name, here):
-        if shared:
-            if not here:
-                mates(name, own[name], MATE_OWN).wait()
-            mates(name, other[name], MATE_OTHER).wait()
-
-    @pl.when(z == LAST)
-    def _():
-        for item in owned(LAST):
-            enc_copy(item).start()
-        chain(VECS, sent[VECS], 2).start()
-        for name in DEC_PARTS:
-            chain(name, sent[name], 2).start()
-            finish_dec(name, sent[name], True)
-        locals_ = [local(i, sent[name], own[name]) for i, name in enumerate(DEC_PARTS)]
-        locals_.append(local(len(DEC_PARTS), sent[VECS], got[VECS]))
-        for one in locals_:
-            one.start()
-        for name in DEC_PARTS:
-            end_dec(name, sent[name], True)
-        for item in owned(LAST):
-            enc_copy(item).wait_send()
-        chain(VECS, sent[VECS], 2).wait_send()
-        for name in DEC_PARTS:
-            chain(name, sent[name], 2).wait_send()
-            end_mates(name, True)
-        for one in locals_:
-            one.wait()
-        head_up().wait_recv()
-
-    @pl.when(z == 2)
-    def _():
-        head_up().start()
-        chain(HEAD, sent[HEAD], HOST).start()
-        first = local(0, sent[HEAD], got[HEAD])
-        first.start()
-        for item in owned(2):
-            enc_copy(item).start()
-        chain(VECS, sent[VECS], 2).wait_recv()
-        chain(VECS, got[VECS], HOST).start()
-        waited = False
-        for name in DEC_PARTS:
-            chain(name, sent[name], 2).wait_recv()
-            finish_dec(name, own[name], False)
-            if not waited:
-                for item in owned(2):
-                    enc_copy(item).wait_send()
-                waited = True
-            chain(name, own[name], HOST).start()
-        for name in DEC_PARTS:
-            end_dec(name, own[name], False)
-        for name in DEC_PARTS:
-            chain(name, own[name], HOST).wait_send()
-            end_mates(name, False)
-        chain(VECS, got[VECS], HOST).wait_send()
-        chain(HEAD, sent[HEAD], HOST).wait_send()
-        head_up().wait_send()
-        first.wait()
-
-    @pl.when(z == HOST)
-    def _():
-        mine = [
-            local(i, sent[piece].at[pl.ds(0, count)], got[name].at[pl.ds(first, count)])
-            for i, (name, count, owner, piece, first) in enumerate(ENC_PARTS)
-            if owner == HOST
-        ]
-        for one in mine:
-            one.start()
-        chain(HEAD, sent[HEAD], HOST).wait_recv()
-        chain(HEAD, got[HEAD], 0).start()
-        chain(VECS, sent[VECS], HOST).wait_recv()
-        chain(VECS, got[VECS], 0).start()
-        away = [item for item in ENC_PARTS if item[2] != HOST]
-        if shared:
-            for item in away:
-                enc_copy(item).wait_recv()
-                enc_mate(item).start()
-        for name in DEC_PARTS:
-            chain(name, sent[name], HOST).wait_recv()
-            chain(name, own[name], 0).start()
-            finish_dec(name, own[name], False)
-        for name in DEC_PARTS:
-            end_dec(name, own[name], False)
-        for item in away:
-            if shared:
-                enc_mate(item).wait()
-            else:
-                enc_copy(item).wait_recv()
-        for name in DEC_PARTS:
-            chain(name, own[name], 0).wait_send()
-            end_mates(name, False)
-        chain(VECS, got[VECS], 0).wait_send()
-        chain(HEAD, got[HEAD], 0).wait_send()
-        for one in mine:
-            one.wait()
-
-    @pl.when(z == 0)
-    def _():
-        for item in owned(0):
-            enc_copy(item).start()
-        for name in DEC_PARTS:
-            chain(name, sent[name], 0).wait_recv()
-            finish_dec(name, own[name], False)
-        for name in DEC_PARTS:
-            end_dec(name, own[name], False)
-        for name in DEC_PARTS:
-            end_mates(name, False)
-        chain(VECS, sent[VECS], 0).wait_recv()
-        chain(HEAD, sent[HEAD], 0).wait_recv()
-        for item in owned(0):
-            enc_copy(item).wait_send()
-
-
-def hosted_weights(pieces, shared):
-    side = lax.axis_index("tensor")
-    anywhere = pl.BlockSpec(memory_space=pl.ANY)
-    shapes = list(GOT.values()) + 2 * [pieces[name].shape for name in DEC_PARTS]
-    count = 2 * len(ENC_PARTS) + 4 * (len(DEC_PARTS) + 3)
-    out = pl.pallas_call(
-        functools.partial(weights_kernel, shared),
-        name="weights",
-        out_shape=[jax.ShapeDtypeStruct(shape, HALF) for shape in shapes],
-        in_specs=[anywhere] * len(SENT),
-        out_specs=[anywhere] * len(shapes),
-        scratch_shapes=[
-            pltpu.SemaphoreType.DMA((count,)),
-            pltpu.SemaphoreType.DMA((count,)),
-            pltpu.SemaphoreType.DMA((len(ENC_PARTS),)),
-        ],
-        compiler_params=pltpu.CompilerParams(collective_id=1 if shared else 2, has_side_effects=True),
-    )(*[pieces[name] for name in SENT])
-    got = dict(zip(GOT, out))
-    own = out[len(GOT) : len(GOT) + len(DEC_PARTS)]
-    other = out[len(GOT) + len(DEC_PARTS) :]
-    low, high = jnp.where(side == 0, own[4], other[4]), jnp.where(side == 0, other[4], own[4])
-    head_w = jnp.concatenate([low, high], 1)
-    top = got[HEAD].shape[0]
-    head_w = jnp.concatenate([head_w[:top] + got[HEAD], head_w[top:]], 0)
-    vecs = got[VECS].reshape(-1)
-    enc_vec, dec_vec, head_b = split_flat(vecs, [(9, D), (10, DD), (PATCH,)])
-    return (
-        (
-            (got[PATCH_LOW], pieces[PATCH_ROWS], got[PATCH_HIGH]),
-            tuple(got[name] for name in (W_QKV, W_OUT, W_UP, W_DOWN)),
-            got[E2D_W],
-            jnp.pad(enc_vec.astype(FLOAT), ((0, 7), (0, 0))),
-        ),
-        (own[:4], other[:4], head_w, dec_vec.astype(FLOAT), head_b.astype(FLOAT)),
-    )
 
 
 VISIBLE = 160
@@ -920,72 +670,265 @@
         )
 
 
-def encoder_forward_kernel(
-    shown, places, patch_low, patch_mid, patch_high, w_qkv, w_out, w_up, w_down, e2d_w, vec,
-    reduced, stream, normed, joined, blended, attended, second, upward, activated, encoded, final_enc,
-    part_sent, part_got, reduced_own, send_sem, recv_sem, local_sem,
-):
+LANDED = [W_QKV, W_OUT, W_UP, W_DOWN, E2D_W, VECS]
+LANDED_SHAPES = [(768, 1152), (384, 768), (768, 1536), (1536, 768), (768, 384), (16, 768)]
+STORED = [
+    ((OWN, D), FLOAT),
+    ((ALL, D), HALF),
+    ((ALL, 3 * D // 2), HALF),
+    ((ALL, D // 2), HALF),
+    ((OWN, D), FLOAT),
+    ((ALL, D), HALF),
+    ((ALL, FF // 2), FLOAT),
+    ((ALL, FF // 2), HALF),
+    ((OWN, D), FLOAT),
+    ((OWN, D), HALF),
+]
+
+
+def forward_kernel(shared, *refs):
+    sent, refs = dict(zip(SENT, refs[: len(SENT)])), refs[len(SENT) :]
+    shown, ids, far_places, near_places, refs = refs[0], refs[1], refs[2], refs[3], refs[4:]
+    got, refs = dict(zip(LANDED, refs[: len(LANDED)])), refs[len(LANDED) :]
+    got[HEAD], reduced, refs = refs[0], refs[1], refs[2:]
+    own, refs = dict(zip(DEC_PARTS, refs[: len(DEC_PARTS)])), refs[len(DEC_PARTS) :]
+    other, refs = dict(zip(DEC_PARTS, refs[: len(DEC_PARTS)])), refs[len(DEC_PARTS) :]
+    stream, normed, joined, blended, attended, second, upward, activated, encoded, final_enc = refs[:10]
+    got[PATCH_LOW], patch_mid, got[PATCH_HIGH], part_sent, part_got, reduced_own, places = refs[10:17]
+    send_sem, recv_sem, local_sem = refs[17:]
     g, z, x = lax.axis_index("group"), lax.axis_index("dp"), lax.axis_index("tensor")
+    odd = lax.rem(g, 2)
+    mate = (g + 1 - 2 * odd, z, x)
+    across = (g, z, 1 - x)
+    links = Links(send_sem, recv_sem)
+    copy = links.copy
     barrier = pltpu.get_barrier_semaphore()
-    links = Links(send_sem, recv_sem)
-
-    def at(row, column):
-        return (g, row, column)
+
+    def at(row, column=None):
+        return (g, row, x if column is None else column)
 
     def greet(peer):
         pl.semaphore_signal(barrier, inc=1, device_id=peer, device_id_type=MESH_ID)
 
-    for row in range(4):
-
-        @pl.when((z == row) & ((row != HOST) | (x == 1)))
+    greet(across)
+    if shared:
+        greet(mate)
+    near = {0: [1], 1: [0, 2, 3], 2: [1, 3], 3: [2, 1]}
+    for row, peers in near.items():
+
+        @pl.when(z == row)
         def _():
-            greet(at(HOST, row // 2))
-
-    @pl.when((z == HOST) & (x == 0))
-    def _():
-        greet(at(HOST, 1))
-        pl.semaphore_wait(barrier, 3)
-
-    @pl.when((z == HOST) & (x == 1))
-    def _():
-        pl.semaphore_wait(barrier, 5)
+            for peer in peers:
+                greet(at(peer))
+            if row != HOST:
+
+                @pl.when(x != row // 2)
+                def _():
+                    greet(at(HOST, row // 2))
+
+                pl.semaphore_wait(barrier, len(peers) + (2 if shared else 1))
+
+    for column in range(2):
+
+        @pl.when((z == HOST) & (x == column))
+        def _():
+            pl.semaphore_wait(barrier, 3 + (2 if shared else 1) + 1 + column)
+
+    def part(ref, start, count, half):
+        if not half:
+            return ref.at[pl.ds(start, count)]
+        return ref.at[pl.ds(pl.multiple_of(start + odd * (count // 2), 16), count // 2)]
+
+    keys = [(SEND_ENC, item[0], item[4]) for item in ENC_PARTS] + [(SEND_MATE, item[0], item[4]) for item in ENC_PARTS]
+    for name in DEC_PARTS + [VECS, HEAD, HEAD_UP]:
+        keys += [(label, name) for label in (CHAIN, CROSS, MATE_OWN, MATE_OTHER)]
+    for key in keys + list(range(12)):
+        links.keys[key] = len(links.keys)
+
+    def enc_copy(item):
+        name, count, owner, piece, first = item
+        return copy(
+            (SEND_ENC, name, first), part(sent[piece], 0, count, shared), part(got[name], first, count, shared), at(HOST)
+        )
+
+    def enc_mate(item):
+        name, count, owner, piece, first = item
+        half = part(got[name], first, count, True)
+        return copy((SEND_MATE, name, first), half, half, mate)
+
+    def local(index, source, target):
+        return pltpu.make_async_copy(source, target, local_sem.at[index])
+
+    def chain(name, source, peer):
+        target = got[name] if name in got else own[name]
+        rows = source.shape[0]
+        half = shared and name in own
+        return copy((CHAIN, name), part(source, 0, rows, half), part(target, 0, rows, half), at(peer))
+
+    def cross(name, source):
+        rows = source.shape[0]
+        return copy((CROSS, name), part(source, 0, rows, shared), part(other[name], 0, rows, shared), across)
+
+    def mates(name, ref, label):
+        half = part(ref, 0, ref.shape[0], True)
+        return copy((label, name), half, half, mate)
+
+    def owned(row):
+        return [item for item in ENC_PARTS if item[2] == row and row != HOST]
+
+    def head_up():
+        return copy((CHAIN, HEAD_UP), sent[HEAD], got[HEAD], at(LAST))
+
+    def finish_dec(name, source, here):
+        cross(name, source).start()
+        if shared and not here:
+            mates(name, own[name], MATE_OWN).start()
+
+    def end_all(source_of, here):
+        for name in DEC_PARTS:
+            cross(name, source_of[name]).wait()
+            if shared:
+                mates(name, other[name], MATE_OTHER).start()
+        for name in DEC_PARTS:
+            if shared:
+                if not here:
+                    mates(name, own[name], MATE_OWN).wait()
+                mates(name, other[name], MATE_OTHER).wait()
 
     def give(column, clip):
         row = 2 * column + clip
-        out = []
-        for side in range(2):
-            if (row, side) != (HOST, column):
-                out.append(links.copy(8 + 2 * clip + side, reduced_own.at[clip], reduced, at(row, side)))
-        return out
+        return [
+            copy(8 + 2 * clip + side, reduced_own.at[clip], reduced, at(row, side))
+            for side in range(2)
+            if (row, side) != (HOST, column)
+        ]
+
+    @pl.when(z == LAST)
+    def _():
+        chain(VECS, sent[VECS], 2).start()
+        locals_ = [local(i, sent[name], own[name]) for i, name in enumerate(DEC_PARTS)]
+        locals_.append(local(len(DEC_PARTS), sent[VECS], got[VECS]))
+        for one in locals_:
+            one.start()
+        for item in owned(LAST):
+            enc_copy(item).start()
+            enc_copy(item).wait_send()
+        for i, name in enumerate(DEC_PARTS):
+            chain(name, sent[name], 2).start()
+            finish_dec(name, sent[name], True)
+            if i:
+                chain(DEC_PARTS[i - 1], sent[DEC_PARTS[i - 1]], 2).wait_send()
+        chain(DEC_PARTS[-1], sent[DEC_PARTS[-1]], 2).wait_send()
+        chain(VECS, sent[VECS], 2).wait_send()
+        end_all(sent, True)
+        for one in locals_:
+            one.wait()
+        head_up().wait_recv()
+
+    @pl.when(z == 2)
+    def _():
+        first = local(0, sent[HEAD], got[HEAD])
+        first.start()
+        chain(VECS, sent[VECS], 2).wait_recv()
+        chain(VECS, got[VECS], HOST).start()
+        late = [item for item in owned(2) if item[0] == E2D_W]
+        for item in owned(2):
+            if item not in late:
+                enc_copy(item).start()
+                enc_copy(item).wait_send()
+        head_up().start()
+        chain(HEAD, sent[HEAD], HOST).start()
+        for i, name in enumerate(DEC_PARTS):
+            chain(name, sent[name], 2).wait_recv()
+            chain(name, own[name], HOST).start()
+            finish_dec(name, own[name], False)
+            if i:
+                chain(DEC_PARTS[i - 1], own[DEC_PARTS[i - 1]], HOST).wait_send()
+        for item in late:
+            enc_copy(item).start()
+            enc_copy(item).wait_send()
+        chain(DEC_PARTS[-1], own[DEC_PARTS[-1]], HOST).wait_send()
+        end_all(own, False)
+        chain(VECS, got[VECS], HOST).wait_send()
+        chain(HEAD, sent[HEAD], HOST).wait_send()
+        head_up().wait_send()
+        first.wait()
+
+    @pl.when(z == 0)
+    def _():
+        for item in owned(0):
+            enc_copy(item).start()
+            enc_copy(item).wait_send()
+        for name in DEC_PARTS:
+            chain(name, sent[name], 0).wait_recv()
+            finish_dec(name, own[name], False)
+        end_all(own, False)
+        chain(VECS, sent[VECS], 0).wait_recv()
+        chain(HEAD, sent[HEAD], 0).wait_recv()
 
     @pl.when(z == HOST)
     def _():
-        across = at(HOST, 1 - x)
+        mine = [
+            local(i, sent[piece].at[pl.ds(0, count)], got[name].at[pl.ds(first, count)])
+            for i, (name, count, owner, piece, first) in enumerate(ENC_PARTS)
+            if owner == HOST
+        ]
+        mine.append(local(len(ENC_PARTS), sent[PATCH_ROWS], patch_mid))
+        for one in mine:
+            one.start()
+        chain(VECS, sent[VECS], HOST).wait_recv()
+        chain(VECS, got[VECS], 0).start()
+        vec = got[VECS][...].astype(FLOAT)
+        for one in mine:
+            one.wait()
+
+        def await_parts(names):
+            items = [item for item in ENC_PARTS if item[2] != HOST and item[0] in names]
+            for item in items:
+                enc_copy(item).wait_recv()
+                if shared:
+                    enc_mate(item).start()
+            if shared:
+                for item in items:
+                    enc_mate(item).wait()
+
+        def pump(name):
+            chain(name, sent[name], HOST).wait_recv()
+            chain(name, own[name], 0).start()
+            finish_dec(name, own[name], False)
 
         def normed_copy(i):
-            return links.copy(i, normed.at[rows_at(i)], normed.at[rows_at(2 + i)], across)
+            return copy(i, normed.at[rows_at(i)], normed.at[rows_at(2 + i)], across)
 
         def out_copy(i):
-            return links.copy(2 + i, part_sent.at[rows_at(i)], part_got.at[rows_at(i)], across)
+            return copy(2 + i, part_sent.at[rows_at(i)], part_got.at[rows_at(i)], across)
 
         def second_copy(i):
-            return links.copy(4 + i, second.at[rows_at(i)], second.at[rows_at(2 + i)], across)
+            return copy(4 + i, second.at[rows_at(i)], second.at[rows_at(2 + i)], across)
 
         def down_copy(i):
-            return links.copy(6 + i, part_sent.at[rows_at(2 + i)], part_got.at[rows_at(2 + i)], across)
-
+            return copy(6 + i, part_sent.at[rows_at(2 + i)], part_got.at[rows_at(2 + i)], across)
+
+        spots = lax.broadcasted_iota(jnp.int32, (OWN, 64), 1)
+        high = ((ids[...] // 32) == spots).astype(FLOAT).astype(HALF)
+        low_hot = (lax.rem(ids[...], 32) == spots).astype(FLOAT).astype(HALF)
+        far = mm(high, far_places[0]) + mm(high, far_places[1]) + mm(high, far_places[2])
+        near = mm(low_hot, near_places[0]) + mm(low_hot, near_places[1]) + mm(low_hot, near_places[2])
+        places[...] = far[:, :D] * near[:, :D] + far[:, D:] * near[:, D:]
+        await_parts((PATCH_LOW, PATCH_HIGH))
         for i in range(2):
             rows = rows_at(i)
             emb = places[rows] + vec[0:1]
-            for start, depth, weight in zip(SPAN, DEPTH, (patch_low, patch_mid, patch_high)):
+            for start, depth, weight in zip(SPAN, DEPTH, (got[PATCH_LOW], patch_mid, got[PATCH_HIGH])):
                 emb = emb + mm(shown[rows, start : start + depth], weight[...])
             stream[rows] = emb
             normed[rows] = norm_to(emb, vec[1:2], vec[2:3]).astype(HALF)
             normed_copy(i).start()
+        await_parts((W_QKV,))
 
         def attend(c):
             rows = rows_at(c)
-            joined[rows] = mm(normed[rows], w_qkv[...]).astype(HALF)
+            joined[rows] = mm(normed[rows], got[W_QKV][...]).astype(HALF)
             width = D // 2
             for h in range(width // HDIM):
                 column = h * HDIM
@@ -996,20 +939,23 @@
                 weights = jnp.exp(scores - jnp.max(scores, -1, keepdims=True))
                 probs = weights * (1.0 / jnp.sum(weights, -1, keepdims=True))
                 blended[rows, column : column + HDIM] = mm(probs.astype(HALF), values).astype(HALF)
-            return mm(blended[rows], w_out[...])
 
         for i in range(2):
-            attended[rows_at(i)] = attend(i) + stream[rows_at(i)] + vec[3:4]
+            attend(i)
+            if i == 0:
+                await_parts((W_OUT,))
+            attended[rows_at(i)] = mm(blended[rows_at(i)], got[W_OUT][...]) + stream[rows_at(i)] + vec[3:4]
             normed_copy(i).wait_recv()
-            part_sent[rows_at(i)] = attend(2 + i).astype(HALF)
+            attend(2 + i)
+            part_sent[rows_at(i)] = mm(blended[rows_at(2 + i)], got[W_OUT][...]).astype(HALF)
             out_copy(i).start()
 
         def feed(c):
             rows = rows_at(c)
-            up = mm(second[rows], w_up[...])
+            up = mm(second[rows], got[W_UP][...])
             upward[rows] = up
             activated[rows] = gelu_to(up).astype(HALF)
-            return mm(activated[rows], w_down[...])
+            return mm(activated[rows], got[W_DOWN][...])
 
         for i in range(2):
             rows = rows_at(i)
@@ -1018,12 +964,20 @@
             attended[rows] = after
             second[rows] = norm_to(after, vec[4:5], vec[5:6]).astype(HALF)
             second_copy(i).start()
+        await_parts((W_UP, W_DOWN))
+        chain(HEAD, sent[HEAD], HOST).wait_recv()
+        chain(HEAD, got[HEAD], 0).start()
+        pump(DEC_QKV)
+        pump(DEC_OUT)
         for i in range(2):
             rows = rows_at(i)
             encoded[rows] = feed(i) + attended[rows] + vec[6:7]
             second_copy(i).wait_recv()
             part_sent[rows_at(2 + i)] = feed(2 + i).astype(HALF)
             down_copy(i).start()
+            pump((DEC_UP, DEC_DOWN)[i])
+        pump(HEAD_HALF)
+        await_parts((E2D_W,))
         for i in range(2):
             rows = rows_at(i)
             down_copy(i).wait_recv()
@@ -1031,7 +985,7 @@
             encoded[rows] = after
             low = norm_to(after, vec[7:8], vec[8:9]).astype(HALF)
             final_enc[rows] = low
-            reduced_own[i] = mm(low, e2d_w[...])
+            reduced_own[i] = mm(low, got[E2D_W][...])
             for column in range(2):
 
                 @pl.when(x == column)
@@ -1052,9 +1006,15 @@
                     for one in give(column, i):
                         one.wait_send()
 
+        end_all(own, False)
+        for name in DEC_PARTS:
+            chain(name, own[name], 0).wait_send()
+        chain(VECS, got[VECS], 0).wait_send()
+        chain(HEAD, got[HEAD], 0).wait_send()
+
     @pl.when((z == HOST) & (x == 0))
     def _():
-        mine = pltpu.make_async_copy(reduced_own.at[1], reduced, local_sem)
+        mine = local(0, reduced_own.at[1], reduced)
         mine.start()
         mine.wait()
 
@@ -1065,50 +1025,57 @@
                 @pl.when((z == row) & (x == side))
                 def _():
                     key = 8 + 2 * (row % 2) + side
-                    links.copy(key, reduced_own.at[row % 2], reduced, at(HOST, row // 2)).wait_recv()
-
-
-def encoder_forward(number, shown_own, places, weights):
-    patch_pieces, mats, e2d_w, vec = weights
+                    copy(key, reduced_own.at[row % 2], reduced, at(HOST, row // 2)).wait_recv()
+
+
+def encoder_forward(number, shared, pieces, shown_own, ids_and_places):
+    side = lax.axis_index("tensor")
     vmem = pl.BlockSpec(memory_space=pltpu.VMEM)
-    stored = [
+    anywhere = pl.BlockSpec(memory_space=pl.ANY)
+    dec_shapes = [(pieces[name].shape, HALF) for name in DEC_PARTS]
+    shapes = [(one, HALF) for one in LANDED_SHAPES] + [((64, PATCH), HALF), ((VISIBLE, DD), FLOAT)]
+    shapes = shapes + 2 * dec_shapes + STORED
+    count = 2 * len(ENC_PARTS) + 4 * (len(DEC_PARTS) + 3) + 12
+    scratch = [
+        ((704, D), HALF),
+        ((704, D), HALF),
+        ((192, D), HALF),
+        ((ALL, D), HALF),
+        ((ALL, D), HALF),
+        ((2, VISIBLE, DD), FLOAT),
         ((OWN, D), FLOAT),
-        ((ALL, D), HALF),
-        ((ALL, 3 * D // 2), HALF),
-        ((ALL, D // 2), HALF),
-        ((OWN, D), FLOAT),
-        ((ALL, D), HALF),
-        ((ALL, FF // 2), FLOAT),
-        ((ALL, FF // 2), HALF),
-        ((OWN, D), FLOAT),
-        ((OWN, D), HALF),
     ]
-    shapes = [((VISIBLE, DD), FLOAT)] + stored
     out = pl.pallas_call(
-        encoder_forward_kernel,
+        functools.partial(forward_kernel, shared),
         name="encoder_forward",
         out_shape=[jax.ShapeDtypeStruct(*one) for one in shapes],
-        in_specs=[vmem] * 11,
-        out_specs=[vmem] * len(shapes),
-        scratch_shapes=[
-            pltpu.VMEM((ALL, D), HALF),
-            pltpu.VMEM((ALL, D), HALF),
-            pltpu.VMEM((2, VISIBLE, DD), FLOAT),
-            pltpu.SemaphoreType.DMA((12,)),
-            pltpu.SemaphoreType.DMA((12,)),
-            pltpu.SemaphoreType.DMA,
+        in_specs=[anywhere] * len(SENT) + [vmem] * 4,
+        out_specs=[vmem] * len(LANDED) + [anywhere, vmem] + [anywhere] * (2 * len(DEC_PARTS)) + [vmem] * len(STORED),
+        scratch_shapes=[pltpu.VMEM(*one) for one in scratch]
+        + [
+            pltpu.SemaphoreType.DMA((count,)),
+            pltpu.SemaphoreType.DMA((count,)),
+            pltpu.SemaphoreType.DMA((len(ENC_PARTS) + 1,)),
         ],
         compiler_params=pltpu.CompilerParams(
             collective_id=number, has_side_effects=True, vmem_limit_bytes=56 << 20
         ),
-    )(shown_own, places, *patch_pieces, *mats, e2d_w, vec)
-    return out[0], out[1:]
+    )(*[pieces[name] for name in SENT], shown_own, *ids_and_places)
+    landed, out = out[: len(LANDED)], out[len(LANDED) :]
+    head, reduced, out = out[0], out[1], out[2:]
+    own, other, stored = out[: len(DEC_PARTS)], out[len(DEC_PARTS) : 2 * len(DEC_PARTS)], out[2 * len(DEC_PARTS) :]
+    low, high = jnp.where(side == 0, own[4], other[4]), jnp.where(side == 0, other[4], own[4])
+    head_w = jnp.concatenate([low, high], 1)
+    head_w = jnp.concatenate([head_w[:64] + head, head_w[64:]], 0)
+    enc_vec, dec_vec, head_b = split_flat(landed[5].astype(FLOAT).reshape(-1), [(9, D), (10, DD), (PATCH,)])
+    enc_weights = (landed[:4], landed[4], jnp.pad(enc_vec, ((0, 7), (0, 0))))
+    return reduced, stored, enc_weights, (own[:4], other[:4], head_w, dec_vec, head_b)
 
 
 def encoder_backward_kernel(
-    picked, shown, w_qkv, w_out, w_up, w_down, e2d_w, vec,
+    picked, shown, shown_other, w_qkv, w_out, w_up, w_down, e2d_w, vec,
     stream, normed, joined, blended, attended, second, upward, activated, encoded, final_enc,
-    wide, tall, dec_qkv, small,
+    wide, tall, dec_qkv, small, normed_far, active_far, active_last,
     qkv_out, square_out, up_out, patch_out, e2d_out, vec_out,
     one_wide, one_tall, one_qkv, one_small, two_wide, two_tall, two_qkv, two_small,
     wide_sent, tall_sent, dec_qkv_sent, small_sent, wide_got, tall_got, dec_qkv_got, small_got,
@@ -1189,13 +1156,15 @@
         ]
 
     out_rows, up_rows, down_rows = 288, 672, 1248
-    down_far = links.copy(next(numbers), down_grad.at[pl.ds(down_rows, 288)], square_out.at[pl.ds(0, 288)], at(LAST, x))
-    down_near = links.copy(next(numbers), down_grad.at[pl.ds(0, down_rows)], square_out, at(2, x))
+    next_row = jnp.minimum(z + 1, LAST)
+    low_far = links.copy(next(numbers), low, low, at(next_row, x))
+    joined_far = [
+        links.copy(next(numbers), grad_joined.at[rows_at(c)], grad_joined.at[rows_at(c)], at(0, x)) for c in range(4)
+    ]
     up_near = links.copy(next(numbers), up_grad.at[pl.ds(up_rows, 96)], up_out.at[pl.ds(0, 96)], at(2, x))
     out_near = links.copy(
         next(numbers), out_grad.at[pl.ds(0, out_rows)], square_out.at[pl.ds(0, out_rows)], at(0, x)
     )
-    qkv_near = links.copy(next(numbers), qkv_grad, qkv_out, at(0, x))
     patch_one = links.copy(next(numbers), patch_low, patch_out, at(0, x))
     patch_two = links.copy(next(numbers), patch_high, patch_out.at[pl.ds(0, 192)], at(2, x))
     e2d_near = links.copy(next(numbers), e2d_grad, e2d_out, at(2, x))
@@ -1206,7 +1175,6 @@
     got_dec = (wide_got, tall_got, dec_qkv_got, small_got)
     one_dec = (one_wide, one_tall, one_qkv, one_small)
     two_dec = (two_wide, two_tall, two_qkv, two_small)
-    next_row = jnp.minimum(z + 1, LAST)
     tree_one = [links.copy(next(numbers), sent_dec[i], got_dec[i], at(next_row, x)) for i in range(4)]
     tree_two = [links.copy(next(numbers), sent_dec[i], two_dec[i], at(LAST, x)) for i in range(4)]
 
@@ -1214,10 +1182,13 @@
     def _():
         for i in (3, 0, 1, 2):
             sent_dec[i][...] = own_dec[i][...].astype(sent_dec[i].dtype)
+        for i in (3, 0, 1, 2):
             tree_one[i].start()
-
-    def pass_on():
-        for i in (3, 0, 1, 2):
+            if i != 3:
+                tree_one[i].wait_send()
+
+    def pass_on(*parts):
+        for i in parts:
             tree_one[i].wait_recv()
             sent_dec[i][...] = (own_dec[i][...] + got_dec[i][...].astype(FLOAT)).astype(sent_dec[i].dtype)
             tree_two[i].start()
@@ -1294,11 +1265,10 @@
         for i in range(2):
             own_part[rows_at(i)] = feed_back(i)
             low_sent[i].wait_recv()
+            if i == 1:
+                low_far.start()
             part_sent[rows_at(i)] = feed_back(2 + i).astype(HALF)
             second_sent[i].start()
-        tall_product(activated, low, down_grad, 256)
-        down_far.start()
-        down_near.start()
         for i in range(2):
             rows = rows_at(i)
             second_sent[i].wait_recv()
@@ -1342,13 +1312,13 @@
 
         for i in range(2):
             own_part[rows_at(i)] = attend_back(i)
+            joined_far[i].start()
+            pass_on(*((3, 0), (1,))[i])
             mid_sent[i].wait_recv()
             part_sent[rows_at(2 + i)] = attend_back(2 + i).astype(HALF)
             normed_sent[i].start()
-            if i == 0:
-                pass_on()
-        tall_product(second, grad_up_in, up_grad, 256)
-        up_near.start()
+            joined_far[2 + i].start()
+        pass_on(2)
         tall_product(blended, mid, out_grad, 128)
         out_near.start()
         for i in range(2):
@@ -1365,13 +1335,13 @@
             emb_low[1, rows] = grad_low[:, D // 2 :]
             emb_sent[i].start()
         vec_sent.start()
-        tall_product(normed, grad_joined, qkv_grad, 256)
-        qkv_near.start()
+        tall_product(second, grad_up_in, up_grad, 256)
+        up_near.start()
         for one in emb_sent:
             one.wait()
-        columns = jnp.concatenate([emb_low[x], emb_got[...]], 0)
         for start, depth, target in zip(SPAN, DEPTH, (patch_low, patch_mid, patch_high)):
-            target[...] = mm_tn(shown[:, start : start + depth], columns).astype(HALF)
+            columns = slice(start, start + depth)
+            target[...] = (mm_tn(shown[:, columns], emb_low[x]) + mm_tn(shown_other[:, columns], emb_got[...])).astype(HALF)
         patch_one.start()
         patch_two.start()
         vec_sent.wait()
@@ -1386,7 +1356,7 @@
             one.start()
         for one in low_sent + mid_sent + second_sent + normed_sent:
             one.wait_send()
-        for one in (down_far, down_near, up_near, out_near, qkv_near, patch_one, patch_two, e2d_near, vec_far):
+        for one in (low_far, *joined_far, up_near, out_near, patch_one, patch_two, e2d_near, vec_far):
             one.wait_send()
         for one in tree_two:
             one.wait_send()
@@ -1401,7 +1371,7 @@
                 def _():
                     pick_copy(row, side).wait_send()
 
-    for row, ones in ((0, (out_near, qkv_near, patch_one)), (2, (down_near, up_near, patch_two, e2d_near)), (LAST, (down_far, vec_far))):
+    for row, ones in ((0, (out_near, patch_one)), (2, (up_near, patch_two, e2d_near)), (LAST, (vec_far,))):
 
         @pl.when(z == row)
         def _():
@@ -1410,8 +1380,34 @@
 
     @pl.when((z == 0) | (z == 2))
     def _():
-        for one in tree_one:
-            one.wait_send()
+        tree_one[3].wait_send()
+
+    @pl.when(z == 2)
+    def _():
+        low_far.wait_recv()
+        low_far.start()
+        tall_product(active_far, low, down_grad, 128)
+        kept = pltpu.make_async_copy(down_grad.at[pl.ds(0, down_rows)], square_out, local_sem.at[0])
+        kept.start()
+        low_far.wait_send()
+        kept.wait()
+
+    @pl.when(z == LAST)
+    def _():
+        low_far.wait_recv()
+        down_grad[pl.ds(0, 384)] = mm_tn(active_last[...], low[...]).astype(HALF)
+        kept = pltpu.make_async_copy(down_grad.at[pl.ds(96, 288)], square_out.at[pl.ds(0, 288)], local_sem.at[0])
+        kept.start()
+        kept.wait()
+
+    @pl.when(z == 0)
+    def _():
+        for one in joined_far:
+            one.wait_recv()
+        tall_product(normed_far, grad_joined, qkv_grad, 256)
+        kept = pltpu.make_async_copy(qkv_grad, qkv_out, local_sem.at[0])
+        kept.start()
+        kept.wait()
 
     @pl.when(z == LAST)
     def _():
@@ -1425,8 +1421,8 @@
             kept[i].wait()
 
 
-def encoder_backward(number, picked, shown, weights, stored, dec_grads):
-    _, mats, e2d_w, vec = weights
+def encoder_backward(number, picked, shown, weights, stored, dec_grads, far):
+    mats, e2d_w, vec = weights
     vmem = pl.BlockSpec(memory_space=pltpu.VMEM)
     anywhere = pl.BlockSpec(memory_space=pl.ANY)
     shapes = [
@@ -1469,14 +1465,14 @@
         encoder_backward_kernel,
         name="encoder_backward",
         out_shape=[jax.ShapeDtypeStruct(*one) for one in shapes],
-        in_specs=[vmem] * 22,
+        in_specs=[vmem] * 26,
         out_specs=[anywhere] * len(shapes),
         scratch_shapes=[pltpu.VMEM(*one) for one in scratch]
-        + [pltpu.SemaphoreType.DMA((36,)), pltpu.SemaphoreType.DMA((36,)), pltpu.SemaphoreType.DMA((4,))],
+        + [pltpu.SemaphoreType.DMA((40,)), pltpu.SemaphoreType.DMA((40,)), pltpu.SemaphoreType.DMA((4,))],
         compiler_params=pltpu.CompilerParams(
             collective_id=number, has_side_effects=True, vmem_limit_bytes=60 << 20
         ),
-    )(picked, shown, *mats, e2d_w, vec, *stored, *dec_grads)
+    )(picked, *shown, *mats, e2d_w, vec, *stored, *dec_grads, *far)
 
 
 LANES = 128
@@ -1594,7 +1590,7 @@
         in_specs=[vmem] * 2,
         out_specs=[vmem] * len(LAID),
         scratch_shapes=[pltpu.VMEM((5, 384, LANES), FLOAT)],
-        compiler_params=pltpu.CompilerParams(vmem_limit_bytes=48 << 20),
+        compiler_params=pltpu.CompilerParams(vmem_limit_bytes=61 << 20),
     )(ten, rep)
     return dict(zip(LAID, out))
 
@@ -1759,10 +1755,10 @@
         lax.fori_loop(0, master.shape[0] // step, body, 0)
 
     stores = [pltpu.make_async_copy(held[i], outs[i], local_sem.at[i]) for i in range(6)]
-    adam(*held[:3], grad_ten, 72)
+    adam(*held[:3], grad_ten, 240)
     for one in stores[:3]:
         one.start()
-    adam(*held[3:], grad_rep, 104)
+    adam(*held[3:], grad_rep, 312)
     for one in stores[3:]:
         one.start()
     if not last:
@@ -1815,7 +1811,7 @@
     return out[0], out[1:7], dict(zip(laid, out[7:]))
 
 
-def decoder_round(tokens, pixels_low, counted, weights):
+def decoder_round(tokens, pixels_low, counted, weights, far):
     own, other, head_w, vec, head_b = weights
     count = pixels_low.shape[0]
     width = DD // 2
@@ -1872,6 +1868,7 @@
         [up_grad[:, : DFF // 2], lax.dynamic_slice_in_dim(head_grad, side * head_cols, head_cols, 1)], 1
     ) + swap(wide_other)
     tall = jnp.concatenate([down_grad[: DFF // 2], out_own], 0) + swap(tall_other)
+    grad_blend, far = lax.optimization_barrier((grad_blend, far))
     grad_joined = attn_backward(queries, keys, values, grad_blend, totals)
     joined_other = swap(grad_joined[count:])
     qkv_grad = mm_tn(normed, grad_joined)
@@ -1879,7 +1876,7 @@
     grad_in, gain_one, bias_one = norm_back(stream, vec[2], vec[3], grad_normed)
     grad_in = grad_in + grad_att
     vec_rows = [gain_one, bias_one, out_bias, gain_two, bias_two, down_bias, gain_end, bias_end]
-    return loss, grad_in, (wide, tall, qkv_grad), vec_rows, head_b_grad
+    return loss, grad_in, (wide, tall, qkv_grad), vec_rows, head_b_grad, far
 
 
 def hosted_round(
@@ -1903,7 +1900,12 @@
     ids_one = hop(visible[:, 0, 0], ((0, 0), (HOST, 0)), ((2, 1), (HOST, 1)))
     ids_two = hop(visible[:, 0, 0], ((3, 1), (HOST, 1)))
     ids_two = jnp.where(side == 0, visible[:, 0, 0], ids_two)
-    dec_places = sinus_at(tube_ids, DD)
+    dec_table = sinus_all(DD)
+    places = []
+    for part in sinus_parts(D):
+        part = jnp.pad(part, ((0, -part.shape[0] % 64), (0, 0)))
+        places.append(jnp.stack(thirds_of(part)))
+    dec_places = jnp.where(side == 0, dec_table, jnp.roll(dec_table, -half_rows, 0))
     states = [one.reshape(TEN_LANES, LANES) for one in (ten_weights, ten_m, ten_v)]
     states = states + [one.reshape(REP_LANES, LANES) for one in (rep_weights, rep_m, rep_v)]
     starts = states[0], states[3]
@@ -1924,10 +1926,9 @@
         one = hop(rows, ((0, 0), (HOST, 0)), ((2, 1), (HOST, 1)))
         two = hop(rows, ((3, 1), (HOST, 1)))
         own = jnp.concatenate([one, jnp.where(side == 0, rows, two)], 0)
-        shown_steps.append(jnp.concatenate([own, swap(own, HOST)], 0))
+        shown_steps.append((own, swap(own, HOST)))
     loss_list, count_list, norm_list = [], [], []
     for s in range(STEPS):
-        enc_weights, dec_weights = hosted_weights(pieces, s == 0)
         ids = visible[s, 0, 0]
         picks = tube_ids[:, None] == ids[None, :]
         shown_here = jnp.any(picks, 1)
@@ -1939,15 +1940,23 @@
         shown = shown_steps[s]
         vis = ids.shape[0]
         ids_own = jnp.concatenate([ids_one[s], ids_two[s]])
-        reduced_clip, enc_stored = encoder_forward(3 + s, shown[: 2 * vis], sinus_at(ids_own, D), enc_weights)
+        reduced_clip, enc_stored, enc_weights, dec_weights = encoder_forward(
+            3 + s, s == 0, pieces, shown[0], (ids_own[:, None], *places)
+        )
+        normed, activated = enc_stored[1], enc_stored[7]
+        far = (
+            hop_both(normed, (HOST, 0)),
+            hop_both(activated, (HOST, 2)),
+            hop_both(activated[:, 1152:], (HOST, LAST)),
+        )
         dec_vec = dec_weights[3]
-        placed = jnp.dot(
-            picks.astype(FLOAT), reduced_clip + dec_vec[0], precision=lax.Precision.HIGHEST
-        )
+        thirds = thirds_of(reduced_clip + dec_vec[0])
+        hot = picks.astype(HALF)
+        placed = mm(jnp.concatenate([hot, hot, hot], 1), jnp.concatenate(thirds, 0))
         tokens = jnp.where(shown_here[:, None], placed, dec_vec[1]) + dec_places
         pixels_low = lax.dynamic_slice_in_dim(patches[s, 0, 0], side * half_rows, half_rows, 0)
-        loss, grad_tokens, (wide, tall, qkv_grad), vec_rows, head_b_grad = decoder_round(
-            tokens, pixels_low, counted, dec_weights
+        loss, grad_tokens, (wide, tall, qkv_grad), vec_rows, head_b_grad, far = decoder_round(
+            tokens, pixels_low, counted, dec_weights, far
         )
         shown_own = shown_here[:half_rows, None]
         e2d_b_grad = jnp.sum(jnp.where(shown_own, grad_tokens, 0.0), 0)
@@ -1958,7 +1967,7 @@
         )
         small = small + swap(small)
         small = jnp.pad(small.reshape(-1, LANES), ((0, 6), (0, 0)))
-        back = encoder_backward(5 + s, picked, shown, enc_weights, enc_stored, (wide, tall, qkv_grad, small))
+        back = encoder_backward(5 + s, picked, shown, enc_weights, enc_stored, (wide, tall, qkv_grad, small), far)
         line = jnp.arange(8)[:, None]
         stats = jnp.where(line == 1, loss, jnp.where(line == 2, jnp.sum(counted), 0.0))
         stats = jnp.broadcast_to(stats, (8, LANES))
@@ -1998,7 +2007,7 @@
     half = diff.shape[0] // 2
     low, high = diff[:half], diff[half:]
     part = jnp.where(odd, high, low) + partner(jnp.where(odd, low, high))
-    part_low = part.astype(HALF)
+    part_low = lax.optimization_barrier(part.astype(HALF))
     far = lax.ppermute(part_low, "group", [(g, g ^ 2) for g in range(4)])
     total = (part_low.astype(FLOAT) + far.astype(FLOAT)) * 0.25
     other = partner(total)

time: 1300 us -> 1190 us (0.915)
  Pallas kernels: 898 us -> 790 us
  waiting for transfers between devices: 53.2 us -> 80.1 us
  matrix products: 122 us -> 103 us
    pallas_call x4 -> x2, Pallas kernels: 372 us -> 284 us  [encoder_forward(): pl.pallas_call(functools.partial(forward_kernel, shared), name='encoder_f...]
    pallas_call x2, Pallas kernels: 245 us -> 199 us  [encoder_backward(): pl.pallas_call(encoder_backward_kernel, name='encoder_backward', out_shap...]
    ppermute x12, waiting for transfers between devices: 22.4 us -> 49.3 us  [swap(): return lax.ppermute(value, 'tensor', SWAP)]
    pallas_call x2, Pallas kernels: 135 us -> 159 us  [update(): pl.pallas_call(functools.partial(update_kernel, number, last), name='upda...]
    dot_general x2 -> x0, matrix products: 23.8 us -> none  [hosted_round(): jnp.dot(picks.astype(FLOAT), reduced_clip + dec_vec[0], precision=lax.Pre...]
    unnamed x305 -> x203, local copies, waits for them, and re-layouts: 30.6 us -> 21 us
    dot_general x14 -> x16, matrix products: 46.1 us -> 49.5 us  [mm(): return jnp.dot(left, right, preferred_element_type=FLOAT)]
  transfers between devices with their start and end apart: 26 -> 32, of which waited for: 9 -> 11; matrix products, arithmetic and copies ran while one was open for 13% -> 17% of each run, Pallas kernels for 22% -> 23%
where the time goes in v3:
time: 1190 us; the launch traced here: 1180 us
  Pallas kernels  790 us (66%)
  matrix products  103 us (9%)
  other arithmetic  91.2 us (8%)
  waiting for transfers between devices  80.1 us (7%)
  local copies, waits for them, and re-layouts  62.6 us (5%)
  starting transfers between devices  44.9 us (4%)
    pallas_call x2, Pallas kernels, encoder_forward(): pl.pallas_call(functools.partial(forward_kernel, shared), name='encoder_f...  284 us
    pallas_call x2, Pallas kernels, encoder_backward(): pl.pallas_call(encoder_backward_kernel, name='encoder_backward', out_shap...  199 us
    pallas_call x2, Pallas kernels, update(): pl.pallas_call(functools.partial(update_kernel, number, last), name='upda...  159 us
    pallas_call x2, Pallas kernels, attn_backward(): pl.pallas_call(attn_backward_kernel, name='attn_backward', out_shape=jax....  84.2 us
    pallas_call x2, Pallas kernels, attn_forward(): pl.pallas_call(attn_forward_kernel, name='attn_forward', out_shape=(jax.S...  57.1 us
    dot_general x16, matrix products, mm(): return jnp.dot(left, right, preferred_element_type=FLOAT)  49.5 us
    ppermute x12, waiting for transfers between devices, swap(): return lax.ppermute(value, 'tensor', SWAP)  49.3 us
    dot_general x14, matrix products, mm_tn(): lax.dot_general(left, right, (((0,), (0,)), ((), ())), preferred_element_...  31.6 us
  transfers between devices with their start and end apart: 32, of which 11 were waited for; matrix products, arithmetic and copies ran while one was open for 17% of the time, Pallas kernels for 23%

profile of v3, /device:TPU:0, one launch (start us, length us, event | category | flops | bytes accessed | tf_op | source)
XLA Modules:
  0.0 1176.8 jit_solution(12207061992040718012)
XLA Ops:
  1.3 3.5 fusion.50
  5.1 3.5 fusion.53
  11.1 5.8 collective-permute-start
  22.1 8.1 fusion.185
  34.0 3.3 convert_reduce_fusion
  39.2 2.5 fusion.3
  49.1 2.4 pad_maximum_fusion.9
  52.1 7.4 lay_out.1
  66.7 119.6 %encoder_forward.2 = (bf16[768,1152]{1,0:T(8,128)(2,1)}, bf16[384,768]{1,0:T(8,128)(2,1)}, bf16[768,1536]{1,0:T(8,128)(2,1)}, bf16[1536,768]{1,0:T(8,128)(2,1)},...) custom-call(bf16[768,1152]{1,0:T(8,128)(2,1)} %get-tuple-element.147, ...), custom_call_target="tpu_custom_call" | custom-call | tf_op jit(solution)/shard_map/encoder_forward/pallas_call | solution.py:1048
  193.7 3.3 fusion.196
  200.9 28.6 %attn_forward.2 = (bf16[1568,192]{1,0:T(8,128)(2,1)S(1)}, f32[3,7,224]{2,1,0:T(8,128)S(1)}) custom-call(bf16[1568,192]{1,0:T(8,128)(2,1)S(1)} %get-tuple-element.375.q_ref, bf16[1568,192]{1,0:T(8,128)(2,1)S(1)} %get-tuple-element.374.k_ref, bf16[1568,192]{1,0:T(8,128)(2,1)S(1)} %get-tuple-element.373.v_ref), custom_call_target="tpu_custom_call" | custom-call | flops 1888223232 | bytes 2408448 | tf_op jit(solution)/shard_map/attn_forward/pallas_call | solution.py:445
  238.2 3.4 collective-permute-done.4
  242.8 11.4 multiply_convert_fusion.1
  260.2 3.1 fusion.167
  264.2 2.9 add_convert_fusion.1
  269.0 3.0 fusion.171
  271.9 3.2 fusion.107
  299.9 9.5 collective-permute-done.12
  311.0 2.4 maximum_add_fusion.2.tall
  313.4 42.1 %attn_backward.2 = bf16[1568,576]{1,0:T(8,128)(2,1)S(1)} custom-call(bf16[1568,192]{1,0:T(8,128)(2,1)S(1)} %get-tuple-element.375.q_ref, bf16[1568,192]{1,0:T(8,128)(2,1)S(1)} %get-tuple-element.374.k_ref, bf16[1568,192]{1,0:T(8,128)(2,1)S(1)} %get-tuple-element.373.v_ref, bf16[1568,192]{1,0:T(8,128)(2,1)S(1)} %pad_maximum_fusion.5.g_ref, ...), custom_call_target="tpu_custom_call" | custom-call | flops 4720558080 | bytes 4214784 | tf_op jit(solution)/shard_map/attn_backward/pallas_call | solution.py:477
  357.6 3.0 maximum_add_fusion.wide
  360.6 2.4 fusion.177.dec_qkv
  363.0 14.8 %collective-permute-done.9 = bf16[784,576]{1,0:T(8,128)(2,1)S(1)} collective-permute-done((bf16[784,576]{1,0:T(8,128)(2,1)S(1)}, bf16[784,576]{1,0:T(8,128)(2,1)S(1)}, u32[]{:S(2)}, u32[]{:S(2)}) %collective-permute-start.9) | collective-permute-done | bytes 903200 | tf_op jit(solution)/shard_map/ppermute | solution.py:511
  386.7 108.0 %encoder_backward.2 = (bf16[768,1152]{1,0:T(8,128)(2,1)}, bf16[1248,768]{1,0:T(8,128)(2,1)}, bf16[672,1536]{1,0:T(8,128)(2,1)}, bf16[704,384]{1,0:T(8,128)(2,1)}...) custom-call(bf16[160,384]{1,0:T(8,128)(2,1)} %convolution_convert_fu, ...), custom_call_target="tpu_custom_call" | custom-call | tf_op jit(solution)/shard_map/encoder_backward/pallas_call | solution.py:1464
  495.4 75.4 %update.2 = (f32[8,128]{1,0:T(8,128)}, f32[8640,128]{1,0:T(8,128)}, f32[8640,128]{1,0:T(8,128)}, f32[8640,128]{1,0:T(8,128)}, f32[4056,128]{1,0:T(8,128)}, /*ind...) custom-call(f32[8,128]{1,0:T(8,128)} %broadcast_in_dim.210.stats, ...), custom_call_target="tpu_custom_call" | custom-call | tf_op jit(solution)/shard_map/update/pallas_call | solution.py:1797
  570.8 164.0 %encoder_forward.3 = (bf16[768,1152]{1,0:T(8,128)(2,1)}, bf16[384,768]{1,0:T(8,128)(2,1)}, bf16[768,1536]{1,0:T(8,128)(2,1)}, bf16[1536,768]{1,0:T(8,128)(2,1)},...) custom-call(bf16[768,1152]{1,0:T(8,128)(2,1)} %get-tuple-element.208, ...), custom_call_target="tpu_custom_call" | custom-call | tf_op jit(solution)/shard_map/encoder_forward/pallas_call | solution.py:1048
  743.2 3.3 fusion.199
  750.4 28.6 %attn_forward.3 = (bf16[1568,192]{1,0:T(8,128)(2,1)S(1)}, f32[3,7,224]{2,1,0:T(8,128)S(1)}) custom-call(bf16[1568,192]{1,0:T(8,128)(2,1)S(1)} %get-tuple-element.372.q_ref, bf16[1568,192]{1,0:T(8,128)(2,1)S(1)} %get-tuple-element.371.k_ref, bf16[1568,192]{1,0:T(8,128)(2,1)S(1)} %get-tuple-element.370.v_ref), custom_call_target="tpu_custom_call" | custom-call | flops 1888223232 | bytes 2408448 | tf_op jit(solution)/shard_map/attn_forward/pallas_call | solution.py:445
  779.0 2.5 collective-permute-start.16
  788.7 11.2 multiply_convert_fusion
  806.0 3.1 fusion.168
  810.0 3.2 add_convert_fusion
  815.0 3.0 fusion.173
  817.9 3.2 fusion.104
  846.1 8.1 collective-permute-done.24
  855.8 2.4 maximum_add_fusion.3.tall
  858.2 42.1 %attn_backward.3 = bf16[1568,576]{1,0:T(8,128)(2,1)S(1)} custom-call(bf16[1568,192]{1,0:T(8,128)(2,1)S(1)} %get-tuple-element.372.q_ref, bf16[1568,192]{1,0:T(8,128)(2,1)S(1)} %get-tuple-element.371.k_ref, bf16[1568,192]{1,0:T(8,128)(2,1)S(1)} %get-tuple-element.370.v_ref, bf16[1568,192]{1,0:T(8,128)(2,1)S(1)} %pad_maximum_fusion.6.g_ref, ...), custom_call_target="tpu_custom_call" | custom-call | flops 4720558080 | bytes 4214784 | tf_op jit(solution)/shard_map/attn_backward/pallas_call | solution.py:477
  901.6 3.0 maximum_add_fusion.1.wide
  904.6 2.4 fusion.178.dec_qkv
  907.1 7.7 collective-permute-done.21
  920.7 2.4 collective-permute-done.25
  923.7 90.8 %encoder_backward.3 = (bf16[768,1152]{1,0:T(8,128)(2,1)}, bf16[1248,768]{1,0:T(8,128)(2,1)}, bf16[672,1536]{1,0:T(8,128)(2,1)}, bf16[704,384]{1,0:T(8,128)(2,1)}...) custom-call(bf16[160,384]{1,0:T(8,128)(2,1)} %convolution_convert_fu, ...), custom_call_target="tpu_custom_call" | custom-call | tf_op jit(solution)/shard_map/encoder_backward/pallas_call | solution.py:1464
  1015.1 84.0 %update.3 = (f32[8,128]{1,0:T(8,128)}, f32[8640,128]{1,0:T(8,128)}, f32[8640,128]{1,0:T(8,128)}, f32[8640,128]{1,0:T(8,128)}, f32[4056,128]{1,0:T(8,128)}, /*index=5*/f32[4056,128]{1,0:T(8,128)}, f32[4056,128]{1,0:T(8,128)}) custom-call(f32[8,128]{1,0:T(8,128)} %broadcast_in_dim.221.stats, bf16[768,1152]{1,0:T(8,128)(2,1)} %get-tuple-element.254.qkv, ...), custom_call_target="tpu_custom_call" | custom-call | tf_op jit(solution)/shard_map/update/pallas_call | solution.py:1797
  1106.0 12.7 %collective-permute-done.27 = bf16[2028,128]{1,0:T(8,128)(2,1)S(1)} collective-permute-done((bf16[2028,128]{1,0:T(8,128)(2,1)S(1)}, bf16[2028,128]{1,0:T(8,128)(2,1)S(1)}, u32[]{:S(2)}, u32[]{:S(2)}) %collective-permute-start.27) | collective-permute-done | bytes 519200 | tf_op jit(solution)/shard_map/ppermute | solution.py:2011
  1129.3 16.8 %collective-permute-done.30 = bf16[4320,128]{1,0:T(8,128)(2,1)S(1)} collective-permute-done((bf16[4320,128]{1,0:T(8,128)(2,1)S(1)}, bf16[4320,128]{1,0:T(8,128)(2,1)S(1)}, u32[]{:S(2)}, u32[]{:S(2)}) %collective-permute-start.30) | collective-permute-done | bytes 1105952 | tf_op jit(solution)/shard_map/ppermute | solution.py:2011
  1146.5 3.1 multiply_subtract_fusion.1
  1151.2 2.6 pad_maximum_fusion
  1153.9 13.3 %multiply_subtract_fusion = (f32[1,1105920]{1,0:T(1,128)}, f32[1,1105920]{1,0:T(1,128)}) fusion(f32[1,1105920]{1,0:T(1,128)S(1)} %bitcast.138, f32[1,1105920]{1,0:T(1,128)S(1)} %bitcast.146, f32[1,1105920]{1,0:T(1,128)S(1)} %bitcast.152), kind=kLoop, calls=%fused_computation.59 | loop fusion | flops 6635520 | bytes 22118400 | tf_op jit(solution)/shard_map/sub | solution.py:1985
  (503 shorter events, 186.6 us)
Async XLA Ops:
  9.6 53.7 %collective-permute-start.1 = (bf16[160,1792]{1,0:T(8,128)(2,1)}, bf16[160,1792]{1,0:T(8,128)(2,1)}, u32[]{:S(2)}, u32[]{:S(2)}) collective-permute-start(bf16[160,1792]{1,0:T(8,128)(2,1)} %fusion.80), channel_id=1, source_target_pairs={{7,3},{15,11},{23,19},{31,27}} | collective-permute-start | bytes 1720328 | tf_op jit(solution)/shard_map/ppermute | solution.py:501
  11.1 53.3 %collective-permute-start = (bf16[160,1792]{1,0:T(8,128)(2,1)}, bf16[160,1792]{1,0:T(8,128)(2,1)}, u32[]{:S(2)}, u32[]{:S(2)}) collective-permute-start(bf16[160,1792]{1,0:T(8,128)(2,1)} %fusion.80), channel_id=1, source_target_pairs={{0,2},{5,3},{8,10},{13,11},{16,18},{21,19},{24,26},{29,27}} | collective-permute-start | bytes 1720328 | tf_op jit(solution)/shard_map/ppermute | solution.py:501
  16.8 42.7 %collective-permute-start.3 = (s32[2,160]{1,0:T(2,128)S(1)}, s32[2,160]{1,0:T(2,128)S(1)}, u32[]{:S(2)}, u32[]{:S(2)}) collective-permute-start(s32[2,160]{1,0:T(2,128)S(1)} %bitcast.179), channel_id=1, source_target_pairs={{7,3},{15,11},{23,19},{31,27}} | collective-permute-start | bytes 3848 | tf_op jit(solution)/shard_map/ppermute | solution.py:501
  17.5 44.1 %collective-permute-start.2 = (s32[2,160]{1,0:T(2,128)S(1)}, s32[2,160]{1,0:T(2,128)S(1)}, u32[]{:S(2)}, u32[]{:S(2)}) collective-permute-start(s32[2,160]{1,0:T(2,128)S(1)} %bitcast.180), channel_id=1, source_target_pairs={{0,2},{5,3},{8,10},{13,11},{16,18},{21,19},{24,26},{29,27}} | collective-permute-start | bytes 3848 | tf_op jit(solution)/shard_map/ppermute | solution.py:501
  20.6 214.1 %collective-permute-start.15 = (bf16[160,1792]{1,0:T(8,128)(2,1)}, bf16[160,1792]{1,0:T(8,128)(2,1)}, u32[]{:S(2)}, u32[]{:S(2)}) collective-permute-start(bf16[160,1792]{1,0:T(8,128)(2,1)} %fusion.82), channel_id=1, source_target_pairs={{7,3},{15,11},{23,19},{31,27}} | collective-permute-start | bytes 1720328 | tf_op jit(solution)/shard_map/ppermute | solution.py:501
  32.8 18.8 %copy-start.70 = (pred[1568]{0:T(1024)(128)(4,1)}, pred[1568]{0:T(1024)(128)(4,1)S(1)}, u32[]{:S(2)}) copy-start(pred[1568]{0:T(1024)(128)(4,1)S(1)} %get-tuple-element.334) | copy-start | bytes 4708
  45.5 148.1 %copy-start.11 = (f32[49,32,384]{2,1,0:T(8,128)}, f32[49,32,384]{2,1,0:T(8,128)S(1)}, u32[]{:S(2)}) copy-start(f32[49,32,384]{2,1,0:T(8,128)S(1)} %multiply_add_fusion.1) | copy-start | bytes 7225348
  59.5 176.4 %collective-permute-start.14 = (bf16[160,1792]{1,0:T(8,128)(2,1)}, bf16[160,1792]{1,0:T(8,128)(2,1)}, u32[]{:S(2)}, u32[]{:S(2)}) collective-permute-start(bf16[160,1792]{1,0:T(8,128)(2,1)} %fusion.82), channel_id=1, source_target_pairs={{0,2},{5,3},{8,10},{13,11},{16,18},{21,19},{24,26},{29,27}} | collective-permute-start | bytes 1720328 | tf_op jit(solution)/shard_map/ppermute | solution.py:501
  187.7 125.7 %collective-permute-start.7 = (bf16[640,1536]{1,0:T(8,128)(2,1)}, bf16[640,1536]{1,0:T(8,128)(2,1)}, u32[]{:S(2)}, u32[]{:S(2)}) collective-permute-start(bf16[640,1536]{1,0:T(8,128)(2,1)} %get-tuple-element.173.activated), channel_id=1, source_target_pairs={{2,4},{3,5},{10,12},{11,13},{18,20},{19,21},{26,28},{27,29}} | collective-permute-start | bytes 5898248 | tf_op jit(solution)/shard_map/ppermute | solution.py:501
  197.0 44.9 %copy-start.1 = (f32[1568,384]{1,0:T(8,128)}, f32[1568,384]{1,0:T(8,128)S(1)}, u32[]{:S(2)}) copy-start(f32[1568,384]{1,0:T(8,128)S(1)} %get-tuple-element.411) | copy-start | bytes 7225348
  200.9 30.9 %copy-start.52 = (bf16[384,768]{1,0:T(8,128)(2,1)S(1)}, bf16[384,768]{1,0:T(8,128)(2,1)}, u32[]{:S(2)}) copy-start(bf16[384,768]{1,0:T(8,128)(2,1)} %get-tuple-element.165) | copy-start | bytes 1769476
  229.5 12.0 %collective-permute-start.4 = (bf16[784,192]{1,0:T(8,128)(2,1)S(1)}, bf16[784,192]{1,0:T(8,128)(2,1)S(1)}, u32[]{:S(2)}, u32[]{:S(2)}) collective-permute-start(bf16[784,192]{1,0:T(8,128)(2,1)S(1)} %slice.316), channel_id=1, source_target_pairs={{0,1},{1,0},{2,3},{3,2},{4,5},{5,4},{6,7},{7,6},{8,9},{9,8},{10,11... | collective-permute-start | bytes 903176 | tf_op jit(solution)/shard_map/ppermute | solution.py:511
  232.2 81.2 %collective-permute-start.6 = (bf16[640,768]{1,0:T(8,128)(2,1)}, bf16[640,768]{1,0:T(8,128)(2,1)}, u32[]{:S(2)}, u32[]{:S(2)}) collective-permute-start(bf16[640,768]{1,0:T(8,128)(2,1)} %get-tuple-element.172.normed), channel_id=1, source_target_pairs={{2,0},{3,1},{10,8},{11,9},{18,16},{19,17},{26,24},{27,25}} | collective-permute-start | bytes 2949128 | tf_op jit(solution)/shard_map/ppermute | solution.py:501
  281.1 16.8 %collective-permute-start.5 = (bf16[784,192]{1,0:T(8,128)(2,1)}, bf16[784,192]{1,0:T(8,128)(2,1)}, u32[]{:S(2)}, u32[]{:S(2)}) collective-permute-start(bf16[784,192]{1,0:T(8,128)(2,1)} %copy.61), channel_id=1, source_target_pairs={{0,1},{1,0},{2,3},{3,2},{4,5},{5,4},{6,7},{7,6},{8,9},{9,8},{10,11... | collective-permute-start | bytes 903176 | tf_op jit(solution)/shard_map/ppermute | solution.py:511
  287.0 22.4 %collective-permute-start.12 = (bf16[960,384]{1,0:T(8,128)(2,1)}, bf16[960,384]{1,0:T(8,128)(2,1)}, u32[]{:S(2)}, u32[]{:S(2)}) collective-permute-start(bf16[960,384]{1,0:T(8,128)(2,1)} %pad_maximum_fusion.7), channel_id=1, source_target_pairs={{0,1},{1,0},{2,3},{3,2},{4,5},{5,4},{6,7},{7,6},{8,9},{9,8},{10,11... | collective-permute-start | bytes 2211848 | tf_op jit(solution)/shard_map/ppermute | solution.py:511
  290.8 66.8 %collective-permute-start.11 = (bf16[384,1536]{1,0:T(8,128)(2,1)}, bf16[384,1536]{1,0:T(8,128)(2,1)}, u32[]{:S(2)}, u32[]{:S(2)}) collective-permute-start(bf16[384,1536]{1,0:T(8,128)(2,1)} %pad_maximum_fusion.1), channel_id=1, source_target_pairs={{0,1},{1,0},{2,3},{3,2},{4,5},{5,4},{6,7},{7,6},{8,9},{9,8},{10,11... | collective-permute-start | bytes 3538952 | tf_op jit(solution)/shard_map/ppermute | solution.py:511
  297.9 15.5 %collective-permute-start.8 = (bf16[640,384]{1,0:T(8,128)(2,1)}, bf16[640,384]{1,0:T(8,128)(2,1)S(1)}, u32[]{:S(2)}, u32[]{:S(2)}) collective-permute-start(bf16[640,384]{1,0:T(8,128)(2,1)} %slice.331), channel_id=1, source_target_pairs={{2,6},{3,7},{10,14},{11,15},{18,22},{19,23},{26,30},{27,31}} | collective-permute-start | bytes 1474568 | tf_op jit(solution)/shard_map/ppermute | solution.py:501
  309.4 77.4 %collective-permute-start.10 = (bf16[320,1792]{1,0:T(8,128)(2,1)}, bf16[320,1792]{1,0:T(8,128)(2,1)}, u32[]{:S(2)}, u32[]{:S(2)}) collective-permute-start(bf16[320,1792]{1,0:T(8,128)(2,1)} %pad_maximum_fusion.3.refs_12_.shown), channel_id=1, source_target_pairs={{2,3},{3,2},{10,11},{11,10},{18,19},{19,18},{26,27},{27,26}} | collective-permute-start | bytes 3440648 | tf_op jit(solution)/shard_map/ppermute | solution.py:501
  313.4 42.1 %copy-start.54 = (bf16[640,384]{1,0:T(8,128)(2,1)}, bf16[640,384]{1,0:T(8,128)(2,1)S(1)}, u32[]{:S(2)}) copy-start(bf16[640,384]{1,0:T(8,128)(2,1)S(1)} %collective-permute-done.8.active_last) | copy-start | bytes 1474564
  313.4 44.1 %copy-start.20 = (f32[384,768]{1,0:T(8,128)S(1)}, f32[384,768]{1,0:T(8,128)}, u32[]{:S(2)}) copy-start(f32[384,768]{1,0:T(8,128)} %constant_dynamic-slice_fusion.1) | copy-start | bytes 3538948
  355.7 22.2 %collective-permute-start.9 = (bf16[784,576]{1,0:T(8,128)(2,1)S(1)}, bf16[784,576]{1,0:T(8,128)(2,1)S(1)}, u32[]{:S(2)}, u32[]{:S(2)}) collective-permute-start(bf16[784,576]{1,0:T(8,128)(2,1)S(1)} %slice.415), channel_id=1, source_target_pairs={{0,1},{1,0},{2,3},{3,2},{4,5},{5,4},{6,7},{7,6},{8,9},{9,8},{10,11... | collective-permute-start | bytes 2709512 | tf_op jit(solution)/shard_map/ppermute | solution.py:511
  360.6 17.3 %copy-start.55 = (bf16[384,576]{1,0:T(8,128)(2,1)S(1)}, bf16[384,576]{1,0:T(8,128)(2,1)}, u32[]{:S(2)}) copy-start(bf16[384,576]{1,0:T(8,128)(2,1)} %get-tuple-element.176) | copy-start | bytes 1327108
  382.2 3.9 collective-permute-start.13
  570.8 172.4 %copy-start.59 = (pred[1568,160]{0,1:T(32,128)(4,1)S(1)}, pred[1568,160]{0,1:T(32,128)(4,1)}, u32[]{:S(2)}) copy-start(pred[1568,160]{0,1:T(32,128)(4,1)} %get-tuple-element.380) | copy-start | bytes 752644
  736.3 121.9 %collective-permute-start.19 = (bf16[640,1536]{1,0:T(8,128)(2,1)}, bf16[640,1536]{1,0:T(8,128)(2,1)}, u32[]{:S(2)}, u32[]{:S(2)}) collective-permute-start(bf16[640,1536]{1,0:T(8,128)(2,1)} %get-tuple-element.234.activated), channel_id=1, source_target_pairs={{2,4},{3,5},{10,12},{11,13},{18,20},{19,21},{26,28},{27,29}} | collective-permute-start | bytes 5898248 | tf_op jit(solution)/shard_map/ppermute | solution.py:501
  746.5 41.3 %copy-start.3 = (f32[1568,384]{1,0:T(8,128)}, f32[1568,384]{1,0:T(8,128)S(1)}, u32[]{:S(2)}) copy-start(f32[1568,384]{1,0:T(8,128)S(1)} %get-tuple-element.422) | copy-start | bytes 7225348
  750.4 31.2 %copy-start.50 = (bf16[384,768]{1,0:T(8,128)(2,1)S(1)}, bf16[384,768]{1,0:T(8,128)(2,1)}, u32[]{:S(2)}) copy-start(bf16[384,768]{1,0:T(8,128)(2,1)} %get-tuple-element.226) | copy-start | bytes 1769476
  779.0 8.4 collective-permute-start.16
  782.1 76.1 %collective-permute-start.18 = (bf16[640,768]{1,0:T(8,128)(2,1)}, bf16[640,768]{1,0:T(8,128)(2,1)}, u32[]{:S(2)}, u32[]{:S(2)}) collective-permute-start(bf16[640,768]{1,0:T(8,128)(2,1)} %get-tuple-element.233.normed), channel_id=1, source_target_pairs={{2,0},{3,1},{10,8},{11,9},{18,16},{19,17},{26,24},{27,25}} | collective-permute-start | bytes 2949128 | tf_op jit(solution)/shard_map/ppermute | solution.py:501
  827.1 17.0 %collective-permute-start.17 = (bf16[784,192]{1,0:T(8,128)(2,1)}, bf16[784,192]{1,0:T(8,128)(2,1)}, u32[]{:S(2)}, u32[]{:S(2)}) collective-permute-start(bf16[784,192]{1,0:T(8,128)(2,1)} %copy.67), channel_id=1, source_target_pairs={{0,1},{1,0},{2,3},{3,2},{4,5},{5,4},{6,7},{7,6},{8,9},{9,8},{10,11... | collective-permute-start | bytes 903176 | tf_op jit(solution)/shard_map/ppermute | solution.py:511
  833.2 20.9 %collective-permute-start.24 = (bf16[960,384]{1,0:T(8,128)(2,1)}, bf16[960,384]{1,0:T(8,128)(2,1)}, u32[]{:S(2)}, u32[]{:S(2)}) collective-permute-start(bf16[960,384]{1,0:T(8,128)(2,1)} %pad_maximum_fusion.8), channel_id=1, source_target_pairs={{0,1},{1,0},{2,3},{3,2},{4,5},{5,4},{6,7},{7,6},{8,9},{9,8},{10,11... | collective-permute-start | bytes 2211848 | tf_op jit(solution)/shard_map/ppermute | solution.py:511
  836.8 64.2 %collective-permute-start.23 = (bf16[384,1536]{1,0:T(8,128)(2,1)}, bf16[384,1536]{1,0:T(8,128)(2,1)}, u32[]{:S(2)}, u32[]{:S(2)}) collective-permute-start(bf16[384,1536]{1,0:T(8,128)(2,1)} %pad_maximum_fusion.2), channel_id=1, source_target_pairs={{0,1},{1,0},{2,3},{3,2},{4,5},{5,4},{6,7},{7,6},{8,9},{9,8},{10,11... | collective-permute-start | bytes 3538952 | tf_op jit(solution)/shard_map/ppermute | solution.py:511
  844.1 14.1 %collective-permute-start.20 = (bf16[640,384]{1,0:T(8,128)(2,1)}, bf16[640,384]{1,0:T(8,128)(2,1)S(1)}, u32[]{:S(2)}, u32[]{:S(2)}) collective-permute-start(bf16[640,384]{1,0:T(8,128)(2,1)} %slice.371), channel_id=1, source_target_pairs={{2,6},{3,7},{10,14},{11,15},{18,22},{19,23},{26,30},{27,31}} | collective-permute-start | bytes 1474568 | tf_op jit(solution)/shard_map/ppermute | solution.py:501
  854.1 69.6 %collective-permute-start.22 = (bf16[320,1792]{1,0:T(8,128)(2,1)}, bf16[320,1792]{1,0:T(8,128)(2,1)}, u32[]{:S(2)}, u32[]{:S(2)}) collective-permute-start(bf16[320,1792]{1,0:T(8,128)(2,1)} %pad_maximum_fusion.4.refs_12_.shown), channel_id=1, source_target_pairs={{2,3},{3,2},{10,11},{11,10},{18,19},{19,18},{26,27},{27,26}} | collective-permute-start | bytes 3440648 | tf_op jit(solution)/shard_map/ppermute | solution.py:501
  858.2 42.1 %copy-start.53 = (bf16[640,384]{1,0:T(8,128)(2,1)}, bf16[640,384]{1,0:T(8,128)(2,1)S(1)}, u32[]{:S(2)}) copy-start(bf16[640,384]{1,0:T(8,128)(2,1)S(1)} %collective-permute-done.20.active_last) | copy-start | bytes 1474564
  858.2 42.8 %copy-start.19 = (f32[384,768]{1,0:T(8,128)S(1)}, f32[384,768]{1,0:T(8,128)}, u32[]{:S(2)}) copy-start(f32[384,768]{1,0:T(8,128)} %constant_dynamic-slice_fusion) | copy-start | bytes 3538948
  900.4 14.4 %collective-permute-start.21 = (bf16[784,576]{1,0:T(8,128)(2,1)S(1)}, bf16[784,576]{1,0:T(8,128)(2,1)S(1)}, u32[]{:S(2)}, u32[]{:S(2)}) collective-permute-start(bf16[784,576]{1,0:T(8,128)(2,1)S(1)} %slice.446), channel_id=1, source_target_pairs={{0,1},{1,0},{2,3},{3,2},{4,5},{5,4},{6,7},{7,6},{8,9},{9,8},{10,11... | collective-permute-start | bytes 2709512 | tf_op jit(solution)/shard_map/ppermute | solution.py:511
  919.2 3.9 collective-permute-start.25
  1015.1 84.0 %copy-start = (f32[519168]{0:T(1024)S(1)}, f32[519168]{0:T(1024)}, u32[]{:S(2)}) copy-start(f32[519168]{0:T(1024)} %param.16) | copy-start | bytes 6230020
  1101.3 2.9 collective-permute-start.26
  1104.1 14.8 %collective-permute-start.29 = (f32[4320,128]{1,0:T(8,128)S(1)}, f32[4320,128]{1,0:T(8,128)S(1)}, u32[]{:S(2)}, u32[]{:S(2)}) collective-permute-start(f32[4320,128]{1,0:T(8,128)S(1)} %slice_select_fusion), channel_id=1, source_target_pairs={{0,8},{8,0},{16,24},{24,16},{1,9},{9,1},{17,25},{25,17},{2,10},{10... | collective-permute-start | bytes 6635528 | tf_op jit(solution)/shard_map/ppermute | solution.py:516
  1104.4 14.3 %collective-permute-start.27 = (bf16[2028,128]{1,0:T(8,128)(2,1)S(1)}, bf16[2028,128]{1,0:T(8,128)(2,1)S(1)}, u32[]{:S(2)}, u32[]{:S(2)}) collective-permute-start(bf16[2028,128]{1,0:T(8,128)(2,1)S(1)} %add_convert_fusion.9), channel_id=1, source_target_pairs={{0,16},{8,24},{16,0},{24,8},{1,17},{9,25},{17,1},{25,9},{2,18},{10... | collective-permute-start | bytes 1557512 | tf_op jit(solution)/shard_map/ppermute | solution.py:2011
  1118.8 10.2 collective-permute-start.28
  1119.2 26.8 %collective-permute-start.30 = (bf16[4320,128]{1,0:T(8,128)(2,1)S(1)}, bf16[4320,128]{1,0:T(8,128)(2,1)S(1)}, u32[]{:S(2)}, u32[]{:S(2)}) collective-permute-start(bf16[4320,128]{1,0:T(8,128)(2,1)S(1)} %add_convert_fusion.4), channel_id=1, source_target_pairs={{0,16},{8,24},{16,0},{24,8},{1,17},{9,25},{17,1},{25,9},{2,18},{10... | collective-permute-start | bytes 3317768 | tf_op jit(solution)/shard_map/ppermute | solution.py:2011
  1129.3 17.2 %copy-start.26 = (f32[519168]{0:T(1024)S(1)}, f32[519168]{0:T(1024)}, u32[]{:S(2)}) copy-start(f32[519168]{0:T(1024)} %param.22) | copy-start | bytes 6230020
  1146.4 4.4 collective-permute-start.31
  1151.2 19.7 %slice-start.14 = ((s8[4423680]{0:T(1024)(128)(4,1)}), s8[4194304]{0:T(1024)(128)(4,1)S(1)}, s32[]{:S(2)}) async-start(s8[4423680]{0:T(1024)(128)(4,1)} %bitcast.156), calls=%async_computation.14 | async-start | bytes 8388608
  1153.9 17.0 %slice-start.15 = ((s8[4423680]{0:T(1024)(128)(4,1)}), s8[229376]{0:T(1024)(128)(4,1)S(1)}, s32[]{:S(2)}) async-start(s8[4423680]{0:T(1024)(128)(4,1)} %bitcast.156), calls=%async_computation.15 | async-start | bytes 458752
  (85 other events, 400.0 us)

commit v4 on v3

--- a/solution.py
+++ b/solution.py
@@ -415,71 +415,7 @@
     )
 
 
-NT=(((1,),(1,)),((),()))
-NN=(((1,),(0,)),((),()))
-TILE=224
-def dot(a,b,dims): return lax.dot_general(a,b,dims,preferred_element_type=FLOAT)
-
-def attn_forward_kernel(q_ref,k_ref,v_ref,out_ref,lse_ref):
-    heads=q_ref.shape[1]//HDIM; tiles=q_ref.shape[0]//TILE
-    for h in range(heads):
-        cols=slice(h*HDIM,(h+1)*HDIM)
-        keys=k_ref[:,cols]*HALF(HDIM**-0.5)
-        vt=v_ref[:,cols].T
-        def step(t,_):
-            rows=pl.ds(pl.multiple_of(t*TILE,TILE),TILE)
-            s=dot(keys,q_ref[rows,cols],NT)
-            m=jnp.max(s,0,keepdims=True)
-            e=jnp.exp(s-m)
-            total=jnp.sum(e,0,keepdims=True)
-            p=(e*(1.0/total)).astype(HALF)
-            bt=dot(vt,p,NN)
-            out_ref[rows,cols]=bt.T.astype(HALF)
-            lse_ref[h,pl.ds(t,1),:]=m+jnp.log(total)
-            return 0
-        lax.fori_loop(0,tiles,step,0)
-
-def attn_forward(q,k,v):
-    rows,width=q.shape
-    vm=pl.BlockSpec(memory_space=pltpu.VMEM)
-    return pl.pallas_call(attn_forward_kernel,name="attn_forward",
-      out_shape=(jax.ShapeDtypeStruct((rows,width),HALF),jax.ShapeDtypeStruct((width//HDIM,rows//TILE,TILE),FLOAT)),
-      in_specs=[vm]*3,out_specs=(vm,vm),
-      compiler_params=pltpu.CompilerParams(vmem_limit_bytes=48<<20),
-      cost_estimate=pl.CostEstimate(flops=4*rows*rows*width,bytes_accessed=rows*width*8,transcendentals=rows*rows*width//HDIM))(q,k,v)
-
-def attn_backward_kernel(q_ref,k_ref,v_ref,g_ref,lse_ref,out_ref,dk_ref,dv_ref):
-    width=q_ref.shape[1]
-    heads=width//HDIM; tiles=q_ref.shape[0]//TILE
-    for h in range(heads):
-        cols=slice(h*HDIM,(h+1)*HDIM)
-        keys=k_ref[:,cols]*HALF(HDIM**-0.5)
-        values=v_ref[:,cols]
-        kt=keys.T
-        dk_ref[...]=jnp.zeros_like(dk_ref); dv_ref[...]=jnp.zeros_like(dv_ref)
-        def step(t,_):
-            rows=pl.ds(pl.multiple_of(t*TILE,TILE),TILE)
-            q=q_ref[rows,cols]; g=g_ref[rows,cols]
-            p=jnp.exp(dot(keys,q,NT)-lse_ref[h,pl.ds(t,1),:])
-            dv_ref[...]+=dot(p.astype(HALF),g,NN)
-            dp=dot(values,g,NT)
-            ds=(p*(dp-jnp.sum(p*dp,0,keepdims=True))).astype(HALF)
-            dk_ref[...]+=dot(ds,q,NN)
-            out_ref[rows,cols]=dot(kt,ds,NN).T.astype(HALF)
-            return 0
-        lax.fori_loop(0,tiles,step,0)
-        out_ref[:,width+h*HDIM:width+(h+1)*HDIM]=(dk_ref[...]*HDIM**-0.5).astype(HALF)
-        out_ref[:,2*width+h*HDIM:2*width+(h+1)*HDIM]=dv_ref[...].astype(HALF)
-
-def attn_backward(q,k,v,g,lse):
-    rows,width=q.shape
-    vm=pl.BlockSpec(memory_space=pltpu.VMEM)
-    return pl.pallas_call(attn_backward_kernel,name="attn_backward",
-      out_shape=jax.ShapeDtypeStruct((rows,3*width),HALF),
-      in_specs=[vm]*5,out_specs=vm,
-      scratch_shapes=[pltpu.VMEM((rows,HDIM),FLOAT),pltpu.VMEM((rows,HDIM),FLOAT)],
-      compiler_params=pltpu.CompilerParams(vmem_limit_bytes=48<<20),
-      cost_estimate=pl.CostEstimate(flops=10*rows*rows*width,bytes_accessed=rows*width*14,transcendentals=rows*rows*width//HDIM))(q,k,v,g,lse)
+TILE = 224
 
 
 HOST = 1
@@ -1811,72 +1747,219 @@
     return out[0], out[1:7], dict(zip(laid, out[7:]))
 
 
-def decoder_round(tokens, pixels_low, counted, weights, far):
+def decoder_kernel(
+    q_ref, k_ref, v_ref, tokens, pixels, counted, out_own, out_oth, up_own, up_oth, down_own, down_oth, head_w, vec, head_b,
+    grad_joined, grad_att, wide, tall, vec_grad, head_b_grad, loss,
+    blended, blend_other, totals, upward, activated, second, final_low, pred_low, low, grad_up_in, mid, grad_blend,
+    blend_sent, wide_sent, wide_got, tall_sent, tall_got, dk_ref, dv_ref, send_sem, recv_sem,
+):
+    g, z, x = lax.axis_index("group"), lax.axis_index("dp"), lax.axis_index("tensor")
+    across = (g, z, 1 - x)
+    links = Links(send_sem, recv_sem)
+    barrier = pltpu.get_barrier_semaphore()
+    pl.semaphore_signal(barrier, inc=1, device_id=across, device_id_type=MESH_ID)
+    half = tokens.shape[0]
+    width = q_ref.shape[1]
+    heads = width // HDIM
+    tiles = q_ref.shape[0] // TILE
+    fc = DFF // 2
+
+    def attend(first, last):
+        for h in range(heads):
+            cols = slice(h * HDIM, (h + 1) * HDIM)
+            keys = k_ref[:, cols] * HALF(HDIM**-0.5)
+            turned = v_ref[:, cols].T
+
+            def step(t, carry):
+                rows = pl.ds(pl.multiple_of(t * TILE, TILE), TILE)
+                scores = mm_nt(keys, q_ref[rows, cols])
+                highest = jnp.max(scores, 0, keepdims=True)
+                weights = jnp.exp(scores - highest)
+                total = jnp.sum(weights, 0, keepdims=True)
+                probs = (weights * (1.0 / total)).astype(HALF)
+                blended[rows, cols] = mm(turned, probs).T.astype(HALF)
+                totals[h, pl.ds(t, 1), :] = highest + jnp.log(total)
+                return carry
+
+            lax.fori_loop(first, last, step, 0)
+
+    whole = half // TILE
+    attend(whole, tiles)
+    pl.semaphore_wait(barrier, 1)
+    blend_swap = links.copy(0, blended.at[pl.ds(half, half)], blend_other, across)
+    blend_swap.start()
+    attend(0, whole)
+    vec_grad[...] = jnp.zeros_like(vec_grad)
+    head_b_grad[...] = jnp.zeros_like(head_b_grad)
+    loss[...] = jnp.zeros_like(loss)
+    blend_swap.wait_recv()
+
+    def count(row, value):
+        vec_grad[row : row + 1] += value
+
+    grad_swaps = []
+    start = 0
+    for step, size in enumerate((400, 384)):
+        rows = pl.ds(start, size)
+        start += size
+        attended = mm(blended[rows], out_own[...]) + mm(blend_other[rows], out_oth[...]) + tokens[rows] + vec[4:5]
+        second[rows] = norm_to(attended, vec[5:6], vec[6:7]).astype(HALF)
+        decoded = attended + vec[7:8]
+        for side, (into, back) in enumerate(((up_own, down_own), (up_oth, down_oth))):
+            cols = slice(side * fc, (side + 1) * fc)
+            up = mm(second[rows], into[...])
+            upward[rows, cols] = up
+            activated[rows, cols] = gelu_to(up).astype(HALF)
+            decoded = decoded + mm(activated[rows, cols], back[...])
+        final_low[rows] = norm_to(decoded, vec[8:9], vec[9:10]).astype(HALF)
+        differ = mm(final_low[rows], head_w[...]) + head_b[...]
+        differ = differ - norm_parts(pixels[rows].astype(FLOAT))[0]
+        share = counted[rows]
+        loss[...] += jnp.sum(jnp.mean(differ * differ, -1, keepdims=True) * share)
+        grad = (2.0 / PATCH) * differ * share
+        head_b_grad[...] += jnp.sum(grad, 0, keepdims=True)
+        pred_low[rows] = grad.astype(HALF)
+        grad_out, gain, bias = norm_from(decoded, vec[8:9], mm_nt(pred_low[rows], head_w[...]))
+        count(8, gain)
+        count(9, bias)
+        count(7, jnp.sum(grad_out, 0, keepdims=True))
+        low[rows] = grad_out.astype(HALF)
+        grad_second = jnp.zeros((size, DD), FLOAT)
+        for side, (into, back) in enumerate(((up_own, down_own), (up_oth, down_oth))):
+            cols = slice(side * fc, (side + 1) * fc)
+            slope = gelu_slope(upward[rows, cols])
+            grad_up_in[rows, cols] = (mm_nt(low[rows], back[...]) * slope).astype(HALF)
+            grad_second = grad_second + mm_nt(grad_up_in[rows, cols], into[...])
+        grad, gain, bias = norm_from(attended, vec[5:6], grad_second)
+        count(5, gain)
+        count(6, bias)
+        grad = grad + grad_out
+        count(4, jnp.sum(grad, 0, keepdims=True))
+        grad_att[rows] = grad
+        mid[rows] = grad.astype(HALF)
+        grad_blend[rows] = mm_nt(mid[rows], out_own[...]).astype(HALF)
+        blend_sent[rows] = mm_nt(mid[rows], out_oth[...]).astype(HALF)
+        swap_rows = pl.ds(half + start - size, size)
+        grad_swaps.append(links.copy(1 + step, blend_sent.at[rows], grad_blend.at[swap_rows], across))
+        grad_swaps[-1].start()
+    mine = pl.ds(pl.multiple_of(x * fc, LANES), fc)
+    theirs = pl.ds(pl.multiple_of((1 - x) * fc, LANES), fc)
+    wide_sent[:, :fc] = mm_tn(second[...], grad_up_in[:, fc:]).astype(HALF)
+    wide_sent[:, fc:] = mm_tn(final_low[...], pred_low[:, theirs]).astype(HALF)
+    wide_swap = links.copy(3, wide_sent, wide_got, across)
+    wide_swap.start()
+    tall_sent[:fc] = mm_tn(activated[:, fc:], low[...]).astype(HALF)
+    tall_sent[fc:] = mm_tn(blend_other[...], mid[...]).astype(HALF)
+    tall_swap = links.copy(4, tall_sent, tall_got, across)
+    tall_swap.start()
+    wide[:, :fc] = mm_tn(second[...], grad_up_in[:, :fc])
+    wide[:, fc:] = mm_tn(final_low[...], pred_low[:, mine])
+    tall[:fc] = mm_tn(activated[:, :fc], low[...])
+    tall[fc:] = mm_tn(blended[pl.ds(0, half)], mid[...])
+    for one in grad_swaps:
+        one.wait_recv()
+    for h in range(heads):
+        cols = slice(h * HDIM, (h + 1) * HDIM)
+        keys = k_ref[:, cols] * HALF(HDIM**-0.5)
+        values = v_ref[:, cols]
+        turned = keys.T
+        dk_ref[...] = jnp.zeros_like(dk_ref)
+        dv_ref[...] = jnp.zeros_like(dv_ref)
+
+        def back_step(t, carry):
+            rows = pl.ds(pl.multiple_of(t * TILE, TILE), TILE)
+            queries, grads = q_ref[rows, cols], grad_blend[rows, cols]
+            probs = jnp.exp(mm_nt(keys, queries) - totals[h, pl.ds(t, 1), :])
+            dv_ref[...] += mm(probs.astype(HALF), grads)
+            grad_probs = mm_nt(values, grads)
+            grad_scores = (probs * (grad_probs - jnp.sum(probs * grad_probs, 0, keepdims=True))).astype(HALF)
+            dk_ref[...] += mm(grad_scores, queries)
+            grad_joined[rows, cols] = mm(turned, grad_scores).T.astype(HALF)
+            return carry
+
+        lax.fori_loop(0, tiles, back_step, 0)
+        grad_joined[:, width + h * HDIM : width + (h + 1) * HDIM] = (dk_ref[...] * HDIM**-0.5).astype(HALF)
+        grad_joined[:, 2 * width + h * HDIM : 2 * width + (h + 1) * HDIM] = dv_ref[...].astype(HALF)
+    wide_swap.wait_recv()
+    wide[...] += wide_got[...].astype(FLOAT)
+    tall_swap.wait_recv()
+    tall[...] += tall_got[...].astype(FLOAT)
+    for one in [blend_swap, wide_swap, tall_swap] + grad_swaps:
+        one.wait_send()
+
+
+def decoder_round(number, tokens, pixels_low, counted, weights):
     own, other, head_w, vec, head_b = weights
-    count = pixels_low.shape[0]
-    width = DD // 2
+    count, rows, width = pixels_low.shape[0], tokens.shape[0], DD // 2
     normed = layer_norm(tokens, vec[2], vec[3]).astype(HALF)
     joined = mm(normed, own[0]).astype(HALF)
     queries, keys, values = [joined[:, i * width : (i + 1) * width] for i in range(3)]
-    blended, totals = attn_forward(queries, keys, values)
-    blend_own = blended[:count]
-    blend_other = swap(blended[count:])
-    stream = tokens[:count]
-    attended = mm(blend_own, own[1]) + mm(blend_other, other[1]) + stream + vec[4]
-    second = layer_norm(attended, vec[5], vec[6]).astype(HALF)
-    w_up = jnp.concatenate([own[2], other[2]], 1)
-    w_down = jnp.concatenate([own[3], other[3]], 0)
-    upward = mm(second, w_up)
-    activated = gelu_exact(upward).astype(HALF)
-    decoded = mm(activated, w_down) + attended + vec[7]
-    final_low = layer_norm(decoded, vec[8], vec[9]).astype(HALF)
-    predicted = mm(final_low, head_w) + head_b
-    pixels = pixels_low.astype(FLOAT)
-    center = jnp.mean(pixels, -1, keepdims=True)
-    spread = jnp.mean((pixels - center) ** 2, -1, keepdims=True)
-    differ = predicted - (pixels - center) * lax.rsqrt(spread + 1e-06)
-    loss = jnp.sum(jnp.mean(differ**2, -1) * counted)
-    grad_pred = 2.0 / PATCH * differ * counted[:, None]
-    pred_low = grad_pred.astype(HALF)
-    head_grad = mm_tn(final_low, pred_low)
-    head_b_grad = jnp.sum(grad_pred, 0)
-    grad_out, gain_end, bias_end = norm_back(decoded, vec[8], vec[9], mm_nt(pred_low, head_w))
-    grad_low = grad_out.astype(HALF)
-    down_grad = mm_tn(activated, grad_low)
-    down_bias = jnp.sum(grad_out, 0)
-    _, gelu_pull = jax.vjp(gelu_exact, upward)
-    grad_up_in = gelu_pull(mm_nt(grad_low, w_down))[0].astype(HALF)
-    up_grad = mm_tn(second, grad_up_in)
-    grad_att, gain_two, bias_two = norm_back(attended, vec[5], vec[6], mm_nt(grad_up_in, w_up))
-    grad_att = grad_att + grad_out
-    out_bias = jnp.sum(grad_att, 0)
-    mid = grad_att.astype(HALF)
-    grad_other = swap(mm_nt(mid, other[1]).astype(HALF))
-    grad_blend = jnp.concatenate([mm_nt(mid, own[1]).astype(HALF), grad_other], 0)
-    out_own, out_other = mm_tn(blend_own, mid), mm_tn(blend_other, mid)
-    side = lax.axis_index("tensor")
-    head_cols = PATCH // 2
-    wide_other = jnp.concatenate(
-        [
-            up_grad[:, DFF // 2 :].astype(HALF),
-            lax.dynamic_slice_in_dim(head_grad, (1 - side) * head_cols, head_cols, 1).astype(HALF),
-        ],
-        1,
-    )
-    tall_other = jnp.concatenate([down_grad[DFF // 2 :], out_other], 0).astype(HALF)
-    wide = jnp.concatenate(
-        [up_grad[:, : DFF // 2], lax.dynamic_slice_in_dim(head_grad, side * head_cols, head_cols, 1)], 1
-    ) + swap(wide_other)
-    tall = jnp.concatenate([down_grad[: DFF // 2], out_own], 0) + swap(tall_other)
-    grad_blend, far = lax.optimization_barrier((grad_blend, far))
-    grad_joined = attn_backward(queries, keys, values, grad_blend, totals)
+    vmem = pl.BlockSpec(memory_space=pltpu.VMEM)
+    shapes = [
+        ((rows, 3 * width), HALF),
+        ((count, DD), FLOAT),
+        ((DD, DFF // 2 + PATCH // 2), FLOAT),
+        ((DFF // 2 + width, DD), FLOAT),
+        ((16, DD), FLOAT),
+        ((1, PATCH), FLOAT),
+        ((8, LANES), FLOAT),
+    ]
+    scratch = [
+        ((rows, width), HALF),
+        ((count, width), HALF),
+        ((width // HDIM, rows // TILE, TILE), FLOAT),
+        ((count, DFF), FLOAT),
+        ((count, DFF), HALF),
+        ((count, DD), HALF),
+        ((count, DD), HALF),
+        ((count, PATCH), HALF),
+        ((count, DD), HALF),
+        ((count, DFF), HALF),
+        ((count, DD), HALF),
+        ((rows, width), HALF),
+        ((count, width), HALF),
+        ((DD, DFF // 2 + PATCH // 2), HALF),
+        ((DD, DFF // 2 + PATCH // 2), HALF),
+        ((DFF // 2 + width, DD), HALF),
+        ((DFF // 2 + width, DD), HALF),
+        ((rows, HDIM), FLOAT),
+        ((rows, HDIM), FLOAT),
+    ]
+    grad_joined, grad_att, wide, tall, vec_grad, head_b_grad, loss = pl.pallas_call(
+        decoder_kernel,
+        name="decoder",
+        out_shape=[jax.ShapeDtypeStruct(*one) for one in shapes],
+        in_specs=[vmem] * 15,
+        out_specs=[vmem] * len(shapes),
+        scratch_shapes=[pltpu.VMEM(*one) for one in scratch]
+        + [pltpu.SemaphoreType.DMA((5,)), pltpu.SemaphoreType.DMA((5,))],
+        compiler_params=pltpu.CompilerParams(
+            collective_id=number, has_side_effects=True, vmem_limit_bytes=60 << 20
+        ),
+    )(
+        queries,
+        keys,
+        values,
+        tokens[:count],
+        pixels_low,
+        counted[:, None],
+        own[1],
+        other[1],
+        own[2],
+        other[2],
+        own[3],
+        other[3],
+        head_w,
+        jnp.pad(vec, ((0, 6), (0, 0))),
+        head_b[None],
+    )
     joined_other = swap(grad_joined[count:])
     qkv_grad = mm_tn(normed, grad_joined)
     grad_normed = mm_nt(grad_joined[:count], own[0]) + mm_nt(joined_other, other[0])
-    grad_in, gain_one, bias_one = norm_back(stream, vec[2], vec[3], grad_normed)
+    grad_in, gain_one, bias_one = norm_back(tokens[:count], vec[2], vec[3], grad_normed)
     grad_in = grad_in + grad_att
-    vec_rows = [gain_one, bias_one, out_bias, gain_two, bias_two, down_bias, gain_end, bias_end]
-    return loss, grad_in, (wide, tall, qkv_grad), vec_rows, head_b_grad, far
+    vec_rows = [gain_one, bias_one] + [vec_grad[i] for i in range(4, 10)]
+    return loss[0, 0], grad_in, (wide, tall, qkv_grad), vec_rows, head_b_grad[0]
 
 
 def hosted_round(
@@ -1955,8 +2038,8 @@
         placed = mm(jnp.concatenate([hot, hot, hot], 1), jnp.concatenate(thirds, 0))
         tokens = jnp.where(shown_here[:, None], placed, dec_vec[1]) + dec_places
         pixels_low = lax.dynamic_slice_in_dim(patches[s, 0, 0], side * half_rows, half_rows, 0)
-        loss, grad_tokens, (wide, tall, qkv_grad), vec_rows, head_b_grad, far = decoder_round(
-            tokens, pixels_low, counted, dec_weights, far
+        loss, grad_tokens, (wide, tall, qkv_grad), vec_rows, head_b_grad = decoder_round(
+            9 + s, tokens, pixels_low, counted, dec_weights
         )
         shown_own = shown_here[:half_rows, None]
         e2d_b_grad = jnp.sum(jnp.where(shown_own, grad_tokens, 0.0), 0)

time: 1190 us -> 1130 us (0.950)
  Pallas kernels: 790 us -> 868 us
  matrix products: 103 us -> 35.2 us
  waiting for transfers between devices: 80.1 us -> 39.1 us
  other arithmetic: 91.2 us -> 74.1 us
    pallas_call x4 -> x2, Pallas kernels: 141 us -> 197 us  [decoder_round(): pl.pallas_call(decoder_kernel, name='decoder', out_shape=[jax.ShapeDtypeS...]
    ppermute x12 -> x4, waiting for transfers between devices: 49.3 us -> 7.27 us  [swap(): return lax.ppermute(value, 'tensor', SWAP)]
    dot_general x16 -> x6, matrix products: 49.5 us -> 17.2 us  [mm(): return jnp.dot(left, right, preferred_element_type=FLOAT)]
    dot_general x14 -> x4, matrix products: 31.6 us -> 11.5 us  [mm_tn(): lax.dot_general(left, right, (((0,), (0,)), ((), ())), preferred_element_...]
    pallas_call x2, Pallas kernels: 199 us -> 217 us  [encoder_backward(): pl.pallas_call(encoder_backward_kernel, name='encoder_backward', out_shap...]
    dot_general x14 -> x4, matrix products: 22.1 us -> 6.48 us  [mm_nt(): lax.dot_general(left, right, (((1,), (1,)), ((), ())), preferred_element_...]
  transfers between devices with their start and end apart: 32 -> 24, of which waited for: 11 -> 6; matrix products, arithmetic and copies ran while one was open for 17% -> 11% of each run, Pallas kernels for 23% -> 62%
where the time goes in v4:
time: 1130 us; the launch traced here: 1120 us
  Pallas kernels  868 us (77%)
  other arithmetic  74.1 us (7%)
  local copies, waits for them, and re-layouts  64.8 us (6%)
  waiting for transfers between devices  39.1 us (3%)
  matrix products  35.2 us (3%)
  starting transfers between devices  34.4 us (3%)
    pallas_call x2, Pallas kernels, encoder_forward(): pl.pallas_call(functools.partial(forward_kernel, shared), name='encoder_f...  294 us
    pallas_call x2, Pallas kernels, encoder_backward(): pl.pallas_call(encoder_backward_kernel, name='encoder_backward', out_shap...  217 us
    pallas_call x2, Pallas kernels, decoder_round(): pl.pallas_call(decoder_kernel, name='decoder', out_shape=[jax.ShapeDtypeS...  197 us
    pallas_call x2, Pallas kernels, update(): pl.pallas_call(functools.partial(update_kernel, number, last), name='upda...  154 us
    ppermute x2, waiting for transfers between devices, group_mean(): far = lax.ppermute(part_low, 'group', [(g, g ^ 2) for g in range(4)])  29.1 us
    ppermute x14, starting transfers between devices, hop(): return lax.ppermute(value, ('dp', 'tensor'), pairs)  25.3 us
  transfers between devices with their start and end apart: 24, of which 6 were waited for; matrix products, arithmetic and copies ran while one was open for 11% of the time, Pallas kernels for 62%

profile of v4, /device:TPU:0, one launch (start us, length us, event | category | flops | bytes accessed | tf_op | source)
XLA Modules:
  0.0 1119.6 jit_solution(9665848306653039510)
XLA Ops:
  1.3 3.5 fusion.28
  5.1 3.5 fusion.31
  10.9 5.7 collective-permute-start
  20.6 8.1 fusion.121
  38.1 4.9 dynamic-slice_bitcast_fusion
  43.1 2.0 fusion.119
  48.0 7.4 lay_out.1
  55.4 2.1 collective-permute-start.10
  59.4 2.1 pad_maximum_fusion.1.refs_12_.shown
  61.5 122.8 %encoder_forward.2 = (bf16[768,1152]{1,0:T(8,128)(2,1)}, bf16[384,768]{1,0:T(8,128)(2,1)}, bf16[768,1536]{1,0:T(8,128)(2,1)}, bf16[1536,768]{1,0:T(8,128)(2,1)},...) custom-call(bf16[768,1152]{1,0:T(8,128)(2,1)} %get-tuple-element.149, ...), custom_call_target="tpu_custom_call" | custom-call | tf_op jit(solution)/shard_map/encoder_forward/pallas_call | solution.py:984
  186.5 2.0 collective-permute-start.8
  188.5 1.9 slice.274
  195.2 4.3 fusion.132
  202.7 2.1 convolution_convert_fusion.1
  206.8 1.9 fusion.124
  208.7 97.1 %decoder.2 = (bf16[1568,576]{1,0:T(8,128)(2,1)}, f32[784,384]{1,0:T(8,128)}, f32[384,1536]{1,0:T(8,128)}, f32[960,384]{1,0:T(8,128)}, f32[16,384]{1,0:T(8,128)}, /*index=5*/f32[1,1536]{1,0:T(1,128)}, f32[8,128]{1,0:T(8,128)}) custom-call(bf16[1568,192]{1,0:T(8,128)(2,1)} %get-tuple-element.335.q_ref, bf16[1568,192]{1,0:T(8,128)(2,1)} %get-tuple-element.334.k_ref, ...), custom_call_target="tpu_custom_call" | custom-call | tf_op jit(solution)/shard_map/decoder/pallas_call | solution.py:1928
  305.8 2.3 slice.271
  315.1 1.9 compare_select_fusion.3
  322.4 3.3 fusion.117.dec_qkv
  325.7 6.3 collective-permute-done.4
  332.0 1.9 fusion.134
  341.4 2.1 convolution_convert_fusion.3.picked
  346.5 118.9 %encoder_backward.2 = (bf16[768,1152]{1,0:T(8,128)(2,1)}, bf16[1248,768]{1,0:T(8,128)(2,1)}, bf16[672,1536]{1,0:T(8,128)(2,1)}, bf16[704,384]{1,0:T(8,128)(2,1)}...) custom-call(bf16[160,384]{1,0:T(8,128)(2,1)} %convolution_convert_fu, ...), custom_call_target="tpu_custom_call" | custom-call | tf_op jit(solution)/shard_map/encoder_backward/pallas_call | solution.py:1400
  466.1 76.3 %update.2 = (f32[8,128]{1,0:T(8,128)}, f32[8640,128]{1,0:T(8,128)}, f32[8640,128]{1,0:T(8,128)}, f32[8640,128]{1,0:T(8,128)}, f32[4056,128]{1,0:T(8,128)}, /*ind...) custom-call(f32[8,128]{1,0:T(8,128)} %broadcast_in_dim.184.stats, ...), custom_call_target="tpu_custom_call" | custom-call | tf_op jit(solution)/shard_map/update/pallas_call | solution.py:1733
  542.4 171.4 %encoder_forward.3 = (bf16[768,1152]{1,0:T(8,128)(2,1)}, bf16[384,768]{1,0:T(8,128)(2,1)}, bf16[768,1536]{1,0:T(8,128)(2,1)}, bf16[1536,768]{1,0:T(8,128)(2,1)},...) custom-call(bf16[768,1152]{1,0:T(8,128)(2,1)} %get-tuple-element.211, ...), custom_call_target="tpu_custom_call" | custom-call | tf_op jit(solution)/shard_map/encoder_forward/pallas_call | solution.py:984
  716.0 1.9 collective-permute-start.16
  718.0 1.9 slice.304
  729.0 2.1 convolution_convert_fusion
  731.1 1.8 fusion.123
  733.5 99.4 %decoder.3 = (bf16[1568,576]{1,0:T(8,128)(2,1)}, f32[784,384]{1,0:T(8,128)}, f32[384,1536]{1,0:T(8,128)}, f32[960,384]{1,0:T(8,128)}, f32[16,384]{1,0:T(8,128)}, /*index=5*/f32[1,1536]{1,0:T(1,128)}, f32[8,128]{1,0:T(8,128)}) custom-call(bf16[1568,192]{1,0:T(8,128)(2,1)} %get-tuple-element.332.q_ref, bf16[1568,192]{1,0:T(8,128)(2,1)} %get-tuple-element.331.k_ref, ...), custom_call_target="tpu_custom_call" | custom-call | tf_op jit(solution)/shard_map/decoder/pallas_call | solution.py:1928
  833.0 2.2 slice.301
  845.9 4.0 fusion.118.dec_qkv
  850.9 1.9 fusion.135
  860.3 2.1 convolution_convert_fusion.2.picked
  863.8 97.7 %encoder_backward.3 = (bf16[768,1152]{1,0:T(8,128)(2,1)}, bf16[1248,768]{1,0:T(8,128)(2,1)}, bf16[672,1536]{1,0:T(8,128)(2,1)}, bf16[704,384]{1,0:T(8,128)(2,1)}...) custom-call(bf16[160,384]{1,0:T(8,128)(2,1)} %convolution_convert_fu, ...), custom_call_target="tpu_custom_call" | custom-call | tf_op jit(solution)/shard_map/encoder_backward/pallas_call | solution.py:1400
  962.2 77.3 %update.3 = (f32[8,128]{1,0:T(8,128)}, f32[8640,128]{1,0:T(8,128)}, f32[8640,128]{1,0:T(8,128)}, f32[8640,128]{1,0:T(8,128)}, f32[4056,128]{1,0:T(8,128)}, /*index=5*/f32[4056,128]{1,0:T(8,128)}, f32[4056,128]{1,0:T(8,128)}) custom-call(f32[8,128]{1,0:T(8,128)} %broadcast_in_dim.195.stats, bf16[768,1152]{1,0:T(8,128)(2,1)} %get-tuple-element.258.qkv, ...), custom_call_target="tpu_custom_call" | custom-call | tf_op jit(solution)/shard_map/update/pallas_call | solution.py:1733
  1039.5 4.0 sub.135
  1045.5 1.8 collective-permute-done.18
  1049.2 12.4 %collective-permute-done.19 = bf16[2028,128]{1,0:T(8,128)(2,1)S(1)} collective-permute-done((bf16[2028,128]{1,0:T(8,128)(2,1)S(1)}, bf16[2028,128]{1,0:T(8,128)(2,1)S(1)}, u32[]{:S(2)}, u32[]{:S(2)}) %collective-permute-start.19) | collective-permute-done | bytes 519200 | tf_op jit(solution)/shard_map/ppermute | solution.py:2094
  1066.3 1.9 maximum_bitcast_fusion.3
  1068.1 1.9 maximum_bitcast_fusion.2
  1070.0 1.9 maximum_bitcast_fusion.1
  1072.1 16.8 %collective-permute-done.22 = bf16[4320,128]{1,0:T(8,128)(2,1)S(1)} collective-permute-done((bf16[4320,128]{1,0:T(8,128)(2,1)S(1)}, bf16[4320,128]{1,0:T(8,128)(2,1)S(1)}, u32[]{:S(2)}, u32[]{:S(2)}) %collective-permute-start.22) | collective-permute-done | bytes 1105952 | tf_op jit(solution)/shard_map/ppermute | solution.py:2094
  1089.3 3.5 multiply_subtract_fusion.1
  1094.1 2.6 pad_maximum_fusion
  1096.8 13.3 %multiply_subtract_fusion = (f32[1,1105920]{1,0:T(1,128)}, f32[1,1105920]{1,0:T(1,128)}) fusion(f32[1,1105920]{1,0:T(1,128)S(1)} %bitcast.93, f32[1,1105920]{1,0:T(1,128)S(1)} %bitcast.96, f32[1,1105920]{1,0:T(1,128)S(1)} %bitcast.102), kind=kLoop, calls=%fused_computation.5 | loop fusion | flops 6635520 | bytes 22118400 | tf_op jit(solution)/shard_map/sub | solution.py:2068
  1113.8 2.3 copy.72
  1117.1 2.1 copy.73
  (311 shorter events, 103.2 us)
Async XLA Ops:
  8.6 8.1 copy-start.32
  9.5 49.8 %collective-permute-start.1 = (bf16[160,1792]{1,0:T(8,128)(2,1)}, bf16[160,1792]{1,0:T(8,128)(2,1)}, u32[]{:S(2)}, u32[]{:S(2)}) collective-permute-start(bf16[160,1792]{1,0:T(8,128)(2,1)} %fusion.52), channel_id=1, source_target_pairs={{7,3},{15,11},{23,19},{31,27}} | collective-permute-start | bytes 1720328 | tf_op jit(solution)/shard_map/ppermute | solution.py:437
  10.9 48.4 %collective-permute-start = (bf16[160,1792]{1,0:T(8,128)(2,1)}, bf16[160,1792]{1,0:T(8,128)(2,1)}, u32[]{:S(2)}, u32[]{:S(2)}) collective-permute-start(bf16[160,1792]{1,0:T(8,128)(2,1)} %fusion.52), channel_id=1, source_target_pairs={{0,2},{5,3},{8,10},{13,11},{16,18},{21,19},{24,26},{29,27}} | collective-permute-start | bytes 1720328 | tf_op jit(solution)/shard_map/ppermute | solution.py:437
  16.7 38.7 %collective-permute-start.3 = (s32[2,160]{1,0:T(2,128)S(1)}, s32[2,160]{1,0:T(2,128)S(1)}, u32[]{:S(2)}, u32[]{:S(2)}) collective-permute-start(s32[2,160]{1,0:T(2,128)S(1)} %bitcast.131), channel_id=1, source_target_pairs={{7,3},{15,11},{23,19},{31,27}} | collective-permute-start | bytes 3848 | tf_op jit(solution)/shard_map/ppermute | solution.py:437
  17.3 40.2 %collective-permute-start.2 = (s32[2,160]{1,0:T(2,128)S(1)}, s32[2,160]{1,0:T(2,128)S(1)}, u32[]{:S(2)}, u32[]{:S(2)}) collective-permute-start(s32[2,160]{1,0:T(2,128)S(1)} %bitcast.132), channel_id=1, source_target_pairs={{0,2},{5,3},{8,10},{13,11},{16,18},{21,19},{24,26},{29,27}} | collective-permute-start | bytes 3848 | tf_op jit(solution)/shard_map/ppermute | solution.py:437
  19.8 290.0 %collective-permute-start.11 = (bf16[160,1792]{1,0:T(8,128)(2,1)}, bf16[160,1792]{1,0:T(8,128)(2,1)S(1)}, u32[]{:S(2)}, u32[]{:S(2)}) collective-permute-start(bf16[160,1792]{1,0:T(8,128)(2,1)} %fusion.54), channel_id=1, source_target_pairs={{7,3},{15,11},{23,19},{31,27}} | collective-permute-start | bytes 1720328 | tf_op jit(solution)/shard_map/ppermute | solution.py:437
  34.5 8.6 copy-start.37
  34.5 8.6 copy-start.39
  55.4 263.8 %collective-permute-start.10 = (bf16[160,1792]{1,0:T(8,128)(2,1)}, bf16[160,1792]{1,0:T(8,128)(2,1)}, u32[]{:S(2)}, u32[]{:S(2)}) collective-permute-start(bf16[160,1792]{1,0:T(8,128)(2,1)} %fusion.54), channel_id=1, source_target_pairs={{0,2},{5,3},{8,10},{13,11},{16,18},{21,19},{24,26},{29,27}} | collective-permute-start | bytes 1720328 | tf_op jit(solution)/shard_map/ppermute | solution.py:437
  184.4 9.0 copy-start.21
  186.5 160.0 %collective-permute-start.8 = (bf16[640,1536]{1,0:T(8,128)(2,1)}, bf16[640,1536]{1,0:T(8,128)(2,1)}, u32[]{:S(2)}, u32[]{:S(2)}) collective-permute-start(bf16[640,1536]{1,0:T(8,128)(2,1)} %get-tuple-element.189.activated), channel_id=1, source_target_pairs={{2,4},{3,5},{10,12},{11,13},{18,20},{19,21},{26,28},{27,29}} | collective-permute-start | bytes 5898248 | tf_op jit(solution)/shard_map/ppermute | solution.py:437
  190.4 156.1 %collective-permute-start.5 = (bf16[320,1792]{1,0:T(8,128)(2,1)}, bf16[320,1792]{1,0:T(8,128)(2,1)}, u32[]{:S(2)}, u32[]{:S(2)}) collective-permute-start(bf16[320,1792]{1,0:T(8,128)(2,1)} %pad_maximum_fusion.1.refs_12_.shown), channel_id=1, source_target_pairs={{2,3},{3,2},{10,11},{11,10},{18,19},{19,18},{26,27},{27,26}} | collective-permute-start | bytes 3440648 | tf_op jit(solution)/shard_map/ppermute | solution.py:437
  194.6 8.0 copy-start.35
  194.6 8.0 copy-start.46
  305.8 6.2 copy-start.42
  308.1 23.9 %collective-permute-start.4 = (bf16[784,576]{1,0:T(8,128)(2,1)}, bf16[784,576]{1,0:T(8,128)(2,1)}, u32[]{:S(2)}, u32[]{:S(2)}) collective-permute-start(bf16[784,576]{1,0:T(8,128)(2,1)} %slice.271), channel_id=1, source_target_pairs={{0,1},{1,0},{2,3},{3,2},{4,5},{5,4},{6,7},{7,6},{8,9},{9,8},{10,11... | collective-permute-start | bytes 2709512 | tf_op jit(solution)/shard_map/ppermute | solution.py:447
  309.8 36.7 %collective-permute-start.7 = (bf16[640,768]{1,0:T(8,128)(2,1)}, bf16[640,768]{1,0:T(8,128)(2,1)}, u32[]{:S(2)}, u32[]{:S(2)}) collective-permute-start(bf16[640,768]{1,0:T(8,128)(2,1)} %get-tuple-element.183.normed), channel_id=1, source_target_pairs={{2,0},{3,1},{10,8},{11,9},{18,16},{19,17},{26,24},{27,25}} | collective-permute-start | bytes 2949128 | tf_op jit(solution)/shard_map/ppermute | solution.py:437
  315.1 7.2 copy-start.15
  319.2 27.3 %collective-permute-start.9 = (bf16[640,384]{1,0:T(8,128)(2,1)}, bf16[640,384]{1,0:T(8,128)(2,1)}, u32[]{:S(2)}, u32[]{:S(2)}) collective-permute-start(bf16[640,384]{1,0:T(8,128)(2,1)} %slice.274), channel_id=1, source_target_pairs={{2,6},{3,7},{10,14},{11,15},{18,22},{19,23},{26,30},{27,31}} | collective-permute-start | bytes 1474568 | tf_op jit(solution)/shard_map/ppermute | solution.py:437
  322.4 21.1 %copy-start.2 = (bf16[320,1792]{1,0:T(8,128)(2,1)}, bf16[320,1792]{1,0:T(8,128)(2,1)S(1)}, u32[]{:S(2)}) copy-start(bf16[320,1792]{1,0:T(8,128)(2,1)S(1)} %pad_maximum_fusion.2.refs_12_.shown) | copy-start | bytes 3440644
  322.4 9.6 copy-start.17
  325.7 8.3 copy-start.25
  325.7 8.3 copy-start.36
  325.7 8.3 copy-start.53
  339.7 3.8 collective-permute-start.6
  343.5 520.3 %collective-permute-start.13 = (bf16[320,1792]{1,0:T(8,128)(2,1)S(1)}, bf16[320,1792]{1,0:T(8,128)(2,1)}, u32[]{:S(2)}, u32[]{:S(2)}) collective-permute-start(bf16[320,1792]{1,0:T(8,128)(2,1)S(1)} %pad_maximum_fusion.2.refs_12_.shown), channel_id=1, source_target_pairs={{2,3},{3,2},{10,11},{11,10},{18,19},{19,18},{26,27},{27,26}} | collective-permute-start | bytes 3440648 | tf_op jit(solution)/shard_map/ppermute | solution.py:437
  346.5 118.9 %copy-start.50 = (f32[8]{0:T(128)S(1)}, f32[8]{0:T(128)}, u32[]{:S(2)}) copy-start(f32[8]{0:T(128)} %compare_select_fusion.3) | copy-start | bytes 100
  713.9 7.3 copy-start.20
  714.7 14.3 %copy-start.33 = (f32[384]{0:T(512)}, f32[384]{0:T(512)S(1)}, u32[]{:S(2)}) copy-start(f32[384]{0:T(512)S(1)} %get-tuple-element.297) | copy-start | bytes 4612
  714.7 14.3 %copy-start.45 = (f32[384]{0:T(512)}, f32[384]{0:T(512)S(1)}, u32[]{:S(2)}) copy-start(f32[384]{0:T(512)S(1)} %get-tuple-element.298) | copy-start | bytes 4612
  716.0 147.7 %collective-permute-start.16 = (bf16[640,1536]{1,0:T(8,128)(2,1)}, bf16[640,1536]{1,0:T(8,128)(2,1)}, u32[]{:S(2)}, u32[]{:S(2)}) collective-permute-start(bf16[640,1536]{1,0:T(8,128)(2,1)} %get-tuple-element.251.activated), channel_id=1, source_target_pairs={{2,4},{3,5},{10,12},{11,13},{18,20},{19,21},{26,28},{27,29}} | collective-permute-start | bytes 5898248 | tf_op jit(solution)/shard_map/ppermute | solution.py:437
  835.2 15.7 %collective-permute-start.12 = (bf16[784,576]{1,0:T(8,128)(2,1)}, bf16[784,576]{1,0:T(8,128)(2,1)}, u32[]{:S(2)}, u32[]{:S(2)}) collective-permute-start(bf16[784,576]{1,0:T(8,128)(2,1)} %slice.301), channel_id=1, source_target_pairs={{0,1},{1,0},{2,3},{3,2},{4,5},{5,4},{6,7},{7,6},{8,9},{9,8},{10,11... | collective-permute-start | bytes 2709512 | tf_op jit(solution)/shard_map/ppermute | solution.py:447
  835.2 28.5 %collective-permute-start.15 = (bf16[640,768]{1,0:T(8,128)(2,1)}, bf16[640,768]{1,0:T(8,128)(2,1)}, u32[]{:S(2)}, u32[]{:S(2)}) collective-permute-start(bf16[640,768]{1,0:T(8,128)(2,1)} %get-tuple-element.245.normed), channel_id=1, source_target_pairs={{2,0},{3,1},{10,8},{11,9},{18,16},{19,17},{26,24},{27,25}} | collective-permute-start | bytes 2949128 | tf_op jit(solution)/shard_map/ppermute | solution.py:437
  836.5 27.3 %collective-permute-start.17 = (bf16[640,384]{1,0:T(8,128)(2,1)}, bf16[640,384]{1,0:T(8,128)(2,1)}, u32[]{:S(2)}, u32[]{:S(2)}) collective-permute-start(bf16[640,384]{1,0:T(8,128)(2,1)} %slice.304), channel_id=1, source_target_pairs={{2,6},{3,7},{10,14},{11,15},{18,22},{19,23},{26,30},{27,31}} | collective-permute-start | bytes 1474568 | tf_op jit(solution)/shard_map/ppermute | solution.py:437
  858.6 3.9 collective-permute-start.14
  863.8 97.8 %copy-start.51 = (f32[8]{0:T(128)S(1)}, f32[8]{0:T(128)}, u32[]{:S(2)}) copy-start(f32[8]{0:T(128)} %compare_select_fusion.2) | copy-start | bytes 100
  1044.7 2.7 collective-permute-start.18
  1045.0 16.8 %collective-permute-start.21 = (f32[4320,128]{1,0:T(8,128)S(1)}, f32[4320,128]{1,0:T(8,128)S(1)}, u32[]{:S(2)}, u32[]{:S(2)}) collective-permute-start(f32[4320,128]{1,0:T(8,128)S(1)} %slice_select_fusion), channel_id=1, source_target_pairs={{0,8},{8,0},{16,24},{24,16},{1,9},{9,1},{17,25},{25,17},{2,10},{10... | collective-permute-start | bytes 6635528 | tf_op jit(solution)/shard_map/ppermute | solution.py:452
  1047.6 13.9 %collective-permute-start.19 = (bf16[2028,128]{1,0:T(8,128)(2,1)S(1)}, bf16[2028,128]{1,0:T(8,128)(2,1)S(1)}, u32[]{:S(2)}, u32[]{:S(2)}) collective-permute-start(bf16[2028,128]{1,0:T(8,128)(2,1)S(1)} %add_convert_fusion.3), channel_id=1, source_target_pairs={{0,16},{8,24},{16,0},{24,8},{1,17},{9,25},{17,1},{25,9},{2,18},{10... | collective-permute-start | bytes 1557512 | tf_op jit(solution)/shard_map/ppermute | solution.py:2094
  1061.7 10.2 collective-permute-start.20
  1062.1 26.8 %collective-permute-start.22 = (bf16[4320,128]{1,0:T(8,128)(2,1)S(1)}, bf16[4320,128]{1,0:T(8,128)(2,1)S(1)}, u32[]{:S(2)}, u32[]{:S(2)}) collective-permute-start(bf16[4320,128]{1,0:T(8,128)(2,1)S(1)} %add_convert_fusion.2), channel_id=1, source_target_pairs={{0,16},{8,24},{16,0},{24,8},{1,17},{9,25},{17,1},{25,9},{2,18},{10... | collective-permute-start | bytes 3317768 | tf_op jit(solution)/shard_map/ppermute | solution.py:2094
  1072.1 17.2 %copy-start.7 = (f32[519168]{0:T(1024)S(1)}, f32[519168]{0:T(1024)}, u32[]{:S(2)}) copy-start(f32[519168]{0:T(1024)} %param.22) | copy-start | bytes 6230020
  1089.2 4.4 collective-permute-start.23
  1089.3 7.4 slice-start.2
  1094.1 19.7 %slice-start.6 = ((s8[4423680]{0:T(1024)(128)(4,1)}), s8[229376]{0:T(1024)(128)(4,1)S(1)}, s32[]{:S(2)}) async-start(s8[4423680]{0:T(1024)(128)(4,1)} %bitcast.106), calls=%async_computation.6 | async-start | bytes 458752
  1096.7 13.4 %copy-start.1 = (f32[8640,128]{1,0:T(8,128)}, f32[8640,128]{1,0:T(8,128)S(1)}, u32[]{:S(2)}) copy-start(f32[8640,128]{1,0:T(8,128)S(1)} %pad_maximum_fusion) | copy-start | bytes 13271044
  1096.8 13.3 %copy-start.9 = (f32[4056,128]{1,0:T(8,128)S(1)}, f32[4056,128]{1,0:T(8,128)}, u32[]{:S(2)}) copy-start(f32[4056,128]{1,0:T(8,128)} %get-tuple-element.279) | copy-start | bytes 6230020
  1096.8 17.0 %slice-start.7 = ((s8[4423680]{0:T(1024)(128)(4,1)}), s8[4194304]{0:T(1024)(128)(4,1)S(1)}, s32[]{:S(2)}) async-start(s8[4423680]{0:T(1024)(128)(4,1)} %bitcast.106), calls=%async_computation.7 | async-start | bytes 8388608
  (40 other events, 103.4 us)

commit v5 on v4

--- a/solution.py
+++ b/solution.py
@@ -670,10 +670,13 @@
         def _():
             pl.semaphore_wait(barrier, 3 + (2 if shared else 1) + 1 + column)
 
-    def part(ref, start, count, half):
+    def part(ref, start, count, half, index=odd):
         if not half:
             return ref.at[pl.ds(start, count)]
-        return ref.at[pl.ds(pl.multiple_of(start + odd * (count // 2), 16), count // 2)]
+        return ref.at[pl.ds(pl.multiple_of(start + index * (count // 2), 16), count // 2)]
+
+    def twice(name):
+        return not shared and name in (PATCH_LOW, PATCH_HIGH, E2D_W)
 
     keys = [(SEND_ENC, item[0], item[4]) for item in ENC_PARTS] + [(SEND_MATE, item[0], item[4]) for item in ENC_PARTS]
     for name in DEC_PARTS + [VECS, HEAD, HEAD_UP]:
@@ -683,14 +686,18 @@
 
     def enc_copy(item):
         name, count, owner, piece, first = item
+        half, index = shared or twice(name), x if twice(name) else odd
         return copy(
-            (SEND_ENC, name, first), part(sent[piece], 0, count, shared), part(got[name], first, count, shared), at(HOST)
+            (SEND_ENC, name, first),
+            part(sent[piece], 0, count, half, index),
+            part(got[name], first, count, half, index),
+            at(HOST),
         )
 
     def enc_mate(item):
         name, count, owner, piece, first = item
-        half = part(got[name], first, count, True)
-        return copy((SEND_MATE, name, first), half, half, mate)
+        half = part(got[name], first, count, True, x if twice(name) else odd)
+        return copy((SEND_MATE, name, first), half, half, across if twice(name) else mate)
 
     def local(index, source, target):
         return pltpu.make_async_copy(source, target, local_sem.at[index])
@@ -822,10 +829,10 @@
             items = [item for item in ENC_PARTS if item[2] != HOST and item[0] in names]
             for item in items:
                 enc_copy(item).wait_recv()
-                if shared:
+                if shared or twice(item[0]):
                     enc_mate(item).start()
-            if shared:
-                for item in items:
+            for item in items:
+                if shared or twice(item[0]):
                     enc_mate(item).wait()
 
         def pump(name):
@@ -1093,7 +1100,7 @@
 
     out_rows, up_rows, down_rows = 288, 672, 1248
     next_row = jnp.minimum(z + 1, LAST)
-    low_far = links.copy(next(numbers), low, low, at(next_row, x))
+    low_far = [links.copy(next(numbers), low.at[rows_at(c)], low.at[rows_at(c)], at(next_row, x)) for c in range(4)]
     joined_far = [
         links.copy(next(numbers), grad_joined.at[rows_at(c)], grad_joined.at[rows_at(c)], at(0, x)) for c in range(4)
     ]
@@ -1187,6 +1194,7 @@
             own_rows_grad[rows] = grad
             low[rows] = grad.astype(HALF)
             low_sent[i].start()
+            low_far[i].start()
         whole_low = jnp.concatenate(reduced_low, 0)
         product = mm_tn(final_enc[...], whole_low).astype(HALF)
         e2d_part[0] = product[: D // 2]
@@ -1201,8 +1209,7 @@
         for i in range(2):
             own_part[rows_at(i)] = feed_back(i)
             low_sent[i].wait_recv()
-            if i == 1:
-                low_far.start()
+            low_far[2 + i].start()
             part_sent[rows_at(i)] = feed_back(2 + i).astype(HALF)
             second_sent[i].start()
         for i in range(2):
@@ -1255,7 +1262,7 @@
             normed_sent[i].start()
             joined_far[2 + i].start()
         pass_on(2)
-        tall_product(blended, mid, out_grad, 128)
+        tall_product(blended, mid, out_grad, 384)
         out_near.start()
         for i in range(2):
             rows = rows_at(i)
@@ -1271,7 +1278,7 @@
             emb_low[1, rows] = grad_low[:, D // 2 :]
             emb_sent[i].start()
         vec_sent.start()
-        tall_product(second, grad_up_in, up_grad, 256)
+        tall_product(second, grad_up_in, up_grad, 384)
         up_near.start()
         for one in emb_sent:
             one.wait()
@@ -1292,7 +1299,7 @@
             one.start()
         for one in low_sent + mid_sent + second_sent + normed_sent:
             one.wait_send()
-        for one in (low_far, *joined_far, up_near, out_near, patch_one, patch_two, e2d_near, vec_far):
+        for one in (*low_far, *joined_far, up_near, out_near, patch_one, patch_two, e2d_near, vec_far):
             one.wait_send()
         for one in tree_two:
             one.wait_send()
@@ -1320,17 +1327,20 @@
 
     @pl.when(z == 2)
     def _():
-        low_far.wait_recv()
-        low_far.start()
-        tall_product(active_far, low, down_grad, 128)
+        for one in low_far:
+            one.wait_recv()
+            one.start()
+        tall_product(active_far, low, down_grad, 384)
         kept = pltpu.make_async_copy(down_grad.at[pl.ds(0, down_rows)], square_out, local_sem.at[0])
         kept.start()
-        low_far.wait_send()
+        for one in low_far:
+            one.wait_send()
         kept.wait()
 
     @pl.when(z == LAST)
     def _():
-        low_far.wait_recv()
+        for one in low_far:
+            one.wait_recv()
         down_grad[pl.ds(0, 384)] = mm_tn(active_last[...], low[...]).astype(HALF)
         kept = pltpu.make_async_copy(down_grad.at[pl.ds(96, 288)], square_out.at[pl.ds(0, 288)], local_sem.at[0])
         kept.start()
@@ -1340,7 +1350,7 @@
     def _():
         for one in joined_far:
             one.wait_recv()
-        tall_product(normed_far, grad_joined, qkv_grad, 256)
+        tall_product(normed_far, grad_joined, qkv_grad, 384)
         kept = pltpu.make_async_copy(qkv_grad, qkv_out, local_sem.at[0])
         kept.start()
         kept.wait()
@@ -1404,7 +1414,7 @@
         in_specs=[vmem] * 26,
         out_specs=[anywhere] * len(shapes),
         scratch_shapes=[pltpu.VMEM(*one) for one in scratch]
-        + [pltpu.SemaphoreType.DMA((40,)), pltpu.SemaphoreType.DMA((40,)), pltpu.SemaphoreType.DMA((4,))],
+        + [pltpu.SemaphoreType.DMA((44,)), pltpu.SemaphoreType.DMA((44,)), pltpu.SemaphoreType.DMA((4,))],
         compiler_params=pltpu.CompilerParams(
             collective_id=number, has_side_effects=True, vmem_limit_bytes=60 << 20
         ),
@@ -1620,7 +1630,9 @@
         for j in range(6):
             columns = slice(j * LANES, (j + 1) * LANES)
             grad_rep[pl.ds(VEC_PLACE + j, 9, stride=6), :] = vec[0:9, columns]
-        grad_rep[pl.ds(VEC_PLACE + 54, 42), :] = small[0:42] + one_small[0:42] + two_small[0:42]
+        rest = small[...] + one_small[...] + two_small[...]
+        for j in range(3):
+            grad_rep[pl.ds(VEC_PLACE + 54 + j, 14, stride=3), :] = rest[0:14, j * LANES : (j + 1) * LANES]
         head_swap.wait_recv()
         top_other.start()
         read = joined(head_own, head_other)
@@ -1748,8 +1760,10 @@
 
 
 def decoder_kernel(
-    q_ref, k_ref, v_ref, tokens, pixels, counted, out_own, out_oth, up_own, up_oth, down_own, down_oth, head_w, vec, head_b,
-    grad_joined, grad_att, wide, tall, vec_grad, head_b_grad, loss,
+    reduced, hot, shown, places, pixels, counted, qkv_own, qkv_oth,
+    out_own, out_oth, up_own, up_oth, down_own, down_oth, head_w, vec, head_b,
+    picked, wide, tall, qkv_grad, small, loss,
+    normed, tokens, q_ref, k_ref, v_ref, parts, parts_got, grad_att, vec_grad, vec_got, head_b_grad,
     blended, blend_other, totals, upward, activated, second, final_low, pred_low, low, grad_up_in, mid, grad_blend,
     blend_sent, wide_sent, wide_got, tall_sent, tall_got, dk_ref, dv_ref, send_sem, recv_sem,
 ):
@@ -1758,11 +1772,32 @@
     links = Links(send_sem, recv_sem)
     barrier = pltpu.get_barrier_semaphore()
     pl.semaphore_signal(barrier, inc=1, device_id=across, device_id_type=MESH_ID)
-    half = tokens.shape[0]
+    half = pixels.shape[0]
     width = q_ref.shape[1]
     heads = width // HDIM
     tiles = q_ref.shape[0] // TILE
     fc = DFF // 2
+    left = reduced[...] + vec[0:1]
+    thirds = []
+    for _ in range(3):
+        thirds.append(left.astype(HALF))
+        left = left - thirds[-1].astype(FLOAT)
+
+    def embed(t, carry):
+        rows = pl.ds(pl.multiple_of(t * TILE, TILE), TILE)
+        placed = mm(hot[rows], thirds[0]) + mm(hot[rows], thirds[1]) + mm(hot[rows], thirds[2])
+        values = jnp.where(shown[rows] > 0.5, placed, vec[1:2]) + places[rows]
+        tokens[rows] = values
+        low_rows = norm_to(values, vec[2:3], vec[3:4]).astype(HALF)
+        normed[rows] = low_rows
+        joined = mm(low_rows, qkv_own[...]).astype(HALF)
+        q_ref[rows] = joined[:, :width]
+        k_ref[rows] = joined[:, width : 2 * width]
+        v_ref[rows] = joined[:, 2 * width :]
+        return carry
+
+    lax.fori_loop(0, tiles, embed, 0)
+    parts[...] = jnp.zeros_like(parts)
 
     def attend(first, last):
         for h in range(heads):
@@ -1858,6 +1893,15 @@
     tall[fc:] = mm_tn(blended[pl.ds(0, half)], mid[...])
     for one in grad_swaps:
         one.wait_recv()
+    part_swaps = []
+
+    def send_parts(block):
+        for third in range(3):
+            cols = pl.ds(256 * third + 128 * block, 128)
+            one = links.copy(5 + 3 * block + third, parts.at[pl.ds(half, half), cols], parts_got.at[:, cols], across)
+            one.start()
+            part_swaps.append(one)
+
     for h in range(heads):
         cols = slice(h * HDIM, (h + 1) * HDIM)
         keys = k_ref[:, cols] * HALF(HDIM**-0.5)
@@ -1874,37 +1918,77 @@
             grad_probs = mm_nt(values, grads)
             grad_scores = (probs * (grad_probs - jnp.sum(probs * grad_probs, 0, keepdims=True))).astype(HALF)
             dk_ref[...] += mm(grad_scores, queries)
-            grad_joined[rows, cols] = mm(turned, grad_scores).T.astype(HALF)
+            parts[rows, cols] = mm(turned, grad_scores).T.astype(HALF)
             return carry
 
         lax.fori_loop(0, tiles, back_step, 0)
-        grad_joined[:, width + h * HDIM : width + (h + 1) * HDIM] = (dk_ref[...] * HDIM**-0.5).astype(HALF)
-        grad_joined[:, 2 * width + h * HDIM : 2 * width + (h + 1) * HDIM] = dv_ref[...].astype(HALF)
+        parts[:, 256 + h * HDIM : 256 + (h + 1) * HDIM] = (dk_ref[...] * HDIM**-0.5).astype(HALF)
+        parts[:, 512 + h * HDIM : 512 + (h + 1) * HDIM] = dv_ref[...].astype(HALF)
+        if h == 1:
+            send_parts(0)
+    send_parts(1)
+
+    def back(ref, rows, weights):
+        total = jnp.zeros((half, DD), FLOAT)
+        for third in range(3):
+            columns = ref[rows, 256 * third : 256 * third + width]
+            total = total + mm_nt(columns, weights[:, third * width : (third + 1) * width])
+        return total
+
+    own_rows_ = pl.ds(0, half)
+    grad_normed = back(parts, own_rows_, qkv_own)
+    product = mm_tn(normed[...], parts[...])
+    for third in range(3):
+        qkv_grad[:, third * width : (third + 1) * width] = product[:, 256 * third : 256 * third + width]
     wide_swap.wait_recv()
     wide[...] += wide_got[...].astype(FLOAT)
     tall_swap.wait_recv()
     tall[...] += tall_got[...].astype(FLOAT)
-    for one in [blend_swap, wide_swap, tall_swap] + grad_swaps:
+    for one in part_swaps:
+        one.wait_recv()
+    grad_normed = grad_normed + back(parts_got, own_rows_, qkv_oth)
+    grad, gain, bias = norm_from(tokens[own_rows_], vec[2:3], grad_normed)
+    count(2, gain)
+    count(3, bias)
+    grad = grad + grad_att[...]
+    seen = jnp.where(shown[own_rows_] > 0.5, grad, 0.0)
+    count(0, jnp.sum(seen, 0, keepdims=True))
+    count(1, jnp.sum(grad - seen, 0, keepdims=True))
+    for i in range(PATCH // DD):
+        count(10 + i, head_b_grad[:, i * DD : (i + 1) * DD])
+    vec_swap = links.copy(11, vec_grad, vec_got, across)
+    vec_swap.start()
+    picked[...] = mm_tn(hot[own_rows_], grad.astype(HALF)).astype(HALF)
+    vec_swap.wait_recv()
+    small[...] = vec_grad[...] + vec_got[...]
+    for one in [blend_swap, wide_swap, tall_swap, vec_swap] + grad_swaps + part_swaps:
         one.wait_send()
 
 
-def decoder_round(number, tokens, pixels_low, counted, weights):
+def decoder_round(number, reduced, hot, shown, places, pixels_low, counted, weights):
     own, other, head_w, vec, head_b = weights
-    count, rows, width = pixels_low.shape[0], tokens.shape[0], DD // 2
-    normed = layer_norm(tokens, vec[2], vec[3]).astype(HALF)
-    joined = mm(normed, own[0]).astype(HALF)
-    queries, keys, values = [joined[:, i * width : (i + 1) * width] for i in range(3)]
+    count, rows, width = pixels_low.shape[0], hot.shape[0], DD // 2
     vmem = pl.BlockSpec(memory_space=pltpu.VMEM)
     shapes = [
-        ((rows, 3 * width), HALF),
-        ((count, DD), FLOAT),
+        ((VISIBLE, DD), HALF),
         ((DD, DFF // 2 + PATCH // 2), FLOAT),
         ((DFF // 2 + width, DD), FLOAT),
+        ((DD, 3 * width), FLOAT),
         ((16, DD), FLOAT),
-        ((1, PATCH), FLOAT),
         ((8, LANES), FLOAT),
     ]
     scratch = [
+        ((rows, DD), HALF),
+        ((rows, DD), FLOAT),
+        ((rows, width), HALF),
+        ((rows, width), HALF),
+        ((rows, width), HALF),
+        ((rows, 768), HALF),
+        ((count, 768), HALF),
+        ((count, DD), FLOAT),
+        ((16, DD), FLOAT),
+        ((16, DD), FLOAT),
+        ((1, PATCH), FLOAT),
         ((rows, width), HALF),
         ((count, width), HALF),
         ((width // HDIM, rows // TILE, TILE), FLOAT),
@@ -1925,24 +2009,26 @@
         ((rows, HDIM), FLOAT),
         ((rows, HDIM), FLOAT),
     ]
-    grad_joined, grad_att, wide, tall, vec_grad, head_b_grad, loss = pl.pallas_call(
+    return pl.pallas_call(
         decoder_kernel,
         name="decoder",
         out_shape=[jax.ShapeDtypeStruct(*one) for one in shapes],
-        in_specs=[vmem] * 15,
+        in_specs=[vmem] * 17,
         out_specs=[vmem] * len(shapes),
         scratch_shapes=[pltpu.VMEM(*one) for one in scratch]
-        + [pltpu.SemaphoreType.DMA((5,)), pltpu.SemaphoreType.DMA((5,))],
+        + [pltpu.SemaphoreType.DMA((12,)), pltpu.SemaphoreType.DMA((12,))],
         compiler_params=pltpu.CompilerParams(
             collective_id=number, has_side_effects=True, vmem_limit_bytes=60 << 20
         ),
     )(
-        queries,
-        keys,
-        values,
-        tokens[:count],
+        reduced,
+        hot,
+        shown,
+        places,
         pixels_low,
         counted[:, None],
+        own[0],
+        other[0],
         own[1],
         other[1],
         own[2],
@@ -1953,13 +2039,6 @@
         jnp.pad(vec, ((0, 6), (0, 0))),
         head_b[None],
     )
-    joined_other = swap(grad_joined[count:])
-    qkv_grad = mm_tn(normed, grad_joined)
-    grad_normed = mm_nt(grad_joined[:count], own[0]) + mm_nt(joined_other, other[0])
-    grad_in, gain_one, bias_one = norm_back(tokens[:count], vec[2], vec[3], grad_normed)
-    grad_in = grad_in + grad_att
-    vec_rows = [gain_one, bias_one] + [vec_grad[i] for i in range(4, 10)]
-    return loss[0, 0], grad_in, (wide, tall, qkv_grad), vec_rows, head_b_grad[0]
 
 
 def hosted_round(
@@ -1994,18 +2073,14 @@
     starts = states[0], states[3]
     pieces = first_pieces(*starts)
     rep_quarter = rep_weights.shape[0]
+    source, target = jnp.arange(PATCH)[:, None], jnp.arange(WIDE)[None, :]
+    cut = rep_quarter // D
+    layout = (target == source + (SPAN[1] - cut) * (source // cut)).astype(HALF)
     shown_steps = []
     for s in range(STEPS):
         picks = (visible[s, 0, 0][:, None] == jnp.arange(TUBES)[None, :]).astype(HALF)
         rows = mm(picks, patches[s, 0, 0]).astype(HALF)
-        cuts = (0, rep_quarter // D, 2 * (rep_quarter // D), PATCH)
-        rows = jnp.concatenate(
-            [
-                jnp.pad(rows[:, cuts[i] : cuts[i + 1]], ((0, 0), (0, room - cuts[i + 1] + cuts[i])))
-                for i, room in enumerate((768, 768, 256))
-            ],
-            1,
-        )
+        rows = mm(rows, layout).astype(HALF)
         one = hop(rows, ((0, 0), (HOST, 0)), ((2, 1), (HOST, 1)))
         two = hop(rows, ((3, 1), (HOST, 1)))
         own = jnp.concatenate([one, jnp.where(side == 0, rows, two)], 0)
@@ -2032,27 +2107,20 @@
             hop_both(activated, (HOST, 2)),
             hop_both(activated[:, 1152:], (HOST, LAST)),
         )
-        dec_vec = dec_weights[3]
-        thirds = thirds_of(reduced_clip + dec_vec[0])
-        hot = picks.astype(HALF)
-        placed = mm(jnp.concatenate([hot, hot, hot], 1), jnp.concatenate(thirds, 0))
-        tokens = jnp.where(shown_here[:, None], placed, dec_vec[1]) + dec_places
         pixels_low = lax.dynamic_slice_in_dim(patches[s, 0, 0], side * half_rows, half_rows, 0)
-        loss, grad_tokens, (wide, tall, qkv_grad), vec_rows, head_b_grad = decoder_round(
-            9 + s, tokens, pixels_low, counted, dec_weights
+        picked, wide, tall, qkv_grad, small, loss = decoder_round(
+            9 + s,
+            reduced_clip,
+            picks.astype(HALF),
+            shown_here[:, None].astype(FLOAT),
+            dec_places,
+            pixels_low,
+            counted,
+            dec_weights,
         )
-        shown_own = shown_here[:half_rows, None]
-        e2d_b_grad = jnp.sum(jnp.where(shown_own, grad_tokens, 0.0), 0)
-        mask_grad = jnp.sum(jnp.where(shown_own, 0.0, grad_tokens), 0)
-        picked = mm_tn(picks[:half_rows].astype(HALF), grad_tokens.astype(HALF)).astype(HALF)
-        small = jnp.concatenate(
-            [jnp.stack([e2d_b_grad, mask_grad] + vec_rows).reshape(-1), head_b_grad]
-        )
-        small = small + swap(small)
-        small = jnp.pad(small.reshape(-1, LANES), ((0, 6), (0, 0)))
         back = encoder_backward(5 + s, picked, shown, enc_weights, enc_stored, (wide, tall, qkv_grad, small), far)
         line = jnp.arange(8)[:, None]
-        stats = jnp.where(line == 1, loss, jnp.where(line == 2, jnp.sum(counted), 0.0))
+        stats = jnp.where(line == 1, loss[0, 0], jnp.where(line == 2, jnp.sum(counted), 0.0))
         stats = jnp.broadcast_to(stats, (8, LANES))
         stats, states, pieces = update(
             7 + s, STEP_BEFORE + s + 1, s == STEPS - 1, stats, (*back[:6], wide, tall, qkv_grad, small, *back[6:]), states

time: 1130 us -> 1120 us (level)
  Pallas kernels: 868 us -> 930 us
  matrix products: 35.2 us -> 12.4 us
  local copies, waits for them, and re-layouts: 64.8 us -> 46.9 us
  other arithmetic: 74.1 us -> 58.9 us
    pallas_call x2, Pallas kernels: 197 us -> 263 us  [decoder_round(): pl.pallas_call(decoder_kernel, name='decoder', out_shape=[jax.ShapeDtypeS...]
    dot_general x8 -> x0, matrix products: 18 us -> none  [the longest x4 11.5 us: mm_tn(): lax.dot_general(left, right, (((0,), (0,)), ((), ())), preferred_element_...]
    pallas_call x2, Pallas kernels: 294 us -> 281 us  [encoder_forward(): pl.pallas_call(functools.partial(forward_kernel, shared), name='encoder_f...]
    slice x17 -> x3, local copies, waits for them, and re-layouts: 14.9 us -> 3.07 us  [the longest x2 2.37 us: hosted_round(): loss[0, 0]]
  transfers between devices with their start and end apart: 24 -> 20, of which waited for: 6 -> 4; matrix products, arithmetic and copies ran while one was open for 11% -> 7% of each run, Pallas kernels for 62% -> 35%
where the time goes in v5:
time: 1120 us; the launch traced here: 1110 us
  Pallas kernels  930 us (83%)
  other arithmetic  58.9 us (5%)
  local copies, waits for them, and re-layouts  46.9 us (4%)
  waiting for transfers between devices  31.8 us (3%)
  starting transfers between devices  27.6 us (2%)
  matrix products  12.4 us (1%)
    pallas_call x2, Pallas kernels, encoder_forward(): pl.pallas_call(functools.partial(forward_kernel, shared), name='encoder_f...  281 us
    pallas_call x2, Pallas kernels, decoder_round(): pl.pallas_call(decoder_kernel, name='decoder', out_shape=[jax.ShapeDtypeS...  263 us
    pallas_call x2, Pallas kernels, encoder_backward(): pl.pallas_call(encoder_backward_kernel, name='encoder_backward', out_shap...  216 us
    pallas_call x2, Pallas kernels, update(): pl.pallas_call(functools.partial(update_kernel, number, last), name='upda...  162 us
    ppermute x2, waiting for transfers between devices, group_mean(): far = lax.ppermute(part_low, 'group', [(g, g ^ 2) for g in range(4)])  29.1 us
    ppermute x14, starting transfers between devices, hop(): return lax.ppermute(value, ('dp', 'tensor'), pairs)  23.6 us
  transfers between devices with their start and end apart: 20, of which 4 were waited for; matrix products, arithmetic and copies ran while one was open for 7% of the time, Pallas kernels for 35%

profile of v5, /device:TPU:0, one launch (start us, length us, event | category | flops | bytes accessed | tf_op | source)
XLA Modules:
  0.0 1110.4 jit_solution(18362941680296608171)
XLA Ops:
  1.4 6.2 fusion.8
  7.6 1.5 collective-permute-start.1
  9.0 5.7 collective-permute-start
  16.7 6.2 fusion.9
  22.9 1.5 collective-permute-start.9
  24.5 8.1 fusion.78
  35.8 1.6 fusion.79
  37.3 1.8 compare_reduce_fusion.1
  41.6 3.3 maximum_select_fusion.places
  44.9 5.0 dynamic-slice_bitcast_fusion
  51.0 2.0 fusion.76
  55.2 7.4 lay_out.1
  62.6 2.1 collective-permute-start.8
  67.5 2.1 pad_maximum_fusion.1.refs_12_.shown
  69.7 120.1 %encoder_forward.2 = (bf16[768,1152]{1,0:T(8,128)(2,1)}, bf16[384,768]{1,0:T(8,128)(2,1)}, bf16[768,1536]{1,0:T(8,128)(2,1)}, bf16[1536,768]{1,0:T(8,128)(2,1)},...) custom-call(bf16[768,1152]{1,0:T(8,128)(2,1)} %get-tuple-element.147, ...), custom_call_target="tpu_custom_call" | custom-call | tf_op jit(solution)/shard_map/encoder_forward/pallas_call | solution.py:991
  189.7 1.9 collective-permute-start.6
  191.7 1.9 slice.144
  193.5 1.8 collective-permute-start.4
  196.7 1.3 broadcast_select_fusion.5
  198.0 1.5 collective-permute-start.7
  203.0 132.9 %decoder.2 = (bf16[160,384]{1,0:T(8,128)(2,1)}, f32[384,1536]{1,0:T(8,128)}, f32[960,384]{1,0:T(8,128)}, f32[384,576]{1,0:T(8,128)}, f32[16,384]{1,0:T(8,128)}, /*index=5*/f32[8,128]{1,0:T(8,128)}) custom-call(f32[160,384]{1,0:T(8,128)} %get-tuple-element.159.reduced, bf16[1568,160]{1,0:T(8,128)(2,1)} %get-tuple-element.305.hot, f32[1568,1]{1,0:T(8,128)} %reshape.356.shown, ...), custom_call_target="tpu_custom_call" | custom-call | tf_op jit(solution)/shard_map/decoder/pallas_call | solution.py:2012
  339.1 2.1 pad_maximum_fusion.2.refs_12_.shown
  341.2 111.2 %encoder_backward.2 = (bf16[768,1152]{1,0:T(8,128)(2,1)}, bf16[1248,768]{1,0:T(8,128)(2,1)}, bf16[672,1536]{1,0:T(8,128)(2,1)}, bf16[704,384]{1,0:T(8,128)(2,1)}...) custom-call(bf16[160,384]{1,0:T(8,128)(2,1)} %get-tuple-element.173., ...), custom_call_target="tpu_custom_call" | custom-call | tf_op jit(solution)/shard_map/encoder_backward/pallas_call | solution.py:1410
  453.1 79.5 %update.2 = (f32[8,128]{1,0:T(8,128)}, f32[8640,128]{1,0:T(8,128)}, f32[8640,128]{1,0:T(8,128)}, f32[8640,128]{1,0:T(8,128)}, f32[4056,128]{1,0:T(8,128)}, /*ind...) custom-call(f32[8,128]{1,0:T(8,128)} %broadcast_in_dim.116.stats, ...), custom_call_target="tpu_custom_call" | custom-call | tf_op jit(solution)/shard_map/update/pallas_call | solution.py:1745
  532.7 161.4 %encoder_forward.3 = (bf16[768,1152]{1,0:T(8,128)(2,1)}, bf16[384,768]{1,0:T(8,128)(2,1)}, bf16[768,1536]{1,0:T(8,128)(2,1)}, bf16[1536,768]{1,0:T(8,128)(2,1)},...) custom-call(bf16[768,1152]{1,0:T(8,128)(2,1)} %get-tuple-element.208, ...), custom_call_target="tpu_custom_call" | custom-call | tf_op jit(solution)/shard_map/encoder_forward/pallas_call | solution.py:991
  696.9 1.7 collective-permute-start.10
  700.1 1.9 slice.158
  705.1 1.3 broadcast_select_fusion.3
  707.6 129.9 %decoder.3 = (bf16[160,384]{1,0:T(8,128)(2,1)}, f32[384,1536]{1,0:T(8,128)}, f32[960,384]{1,0:T(8,128)}, f32[384,576]{1,0:T(8,128)}, f32[16,384]{1,0:T(8,128)}, /*index=5*/f32[8,128]{1,0:T(8,128)}) custom-call(f32[160,384]{1,0:T(8,128)} %get-tuple-element.220.reduced, bf16[1568,160]{1,0:T(8,128)(2,1)} %get-tuple-element.304.hot, f32[1568,1]{1,0:T(8,128)} %reshape.357.shown, ...), custom_call_target="tpu_custom_call" | custom-call | tf_op jit(solution)/shard_map/decoder/pallas_call | solution.py:2012
  838.7 1.3 compare_select_fusion.2
  842.2 105.0 %encoder_backward.3 = (bf16[768,1152]{1,0:T(8,128)(2,1)}, bf16[1248,768]{1,0:T(8,128)(2,1)}, bf16[672,1536]{1,0:T(8,128)(2,1)}, bf16[704,384]{1,0:T(8,128)(2,1)}...) custom-call(bf16[160,384]{1,0:T(8,128)(2,1)} %get-tuple-element.234., ...), custom_call_target="tpu_custom_call" | custom-call | tf_op jit(solution)/shard_map/encoder_backward/pallas_call | solution.py:1410
  947.8 82.6 %update.3 = (f32[8,128]{1,0:T(8,128)}, f32[8640,128]{1,0:T(8,128)}, f32[8640,128]{1,0:T(8,128)}, f32[8640,128]{1,0:T(8,128)}, f32[4056,128]{1,0:T(8,128)}, /*index=5*/f32[4056,128]{1,0:T(8,128)}, f32[4056,128]{1,0:T(8,128)}) custom-call(f32[8,128]{1,0:T(8,128)} %broadcast_in_dim.122.stats, bf16[768,1152]{1,0:T(8,128)(2,1)} %get-tuple-element.254.qkv, ...), custom_call_target="tpu_custom_call" | custom-call | tf_op jit(solution)/shard_map/update/pallas_call | solution.py:1745
  1030.4 4.0 sub.72
  1036.4 1.8 collective-permute-done.14
  1038.4 1.6 collective-permute-start.15
  1040.0 12.4 %collective-permute-done.15 = bf16[2028,128]{1,0:T(8,128)(2,1)S(1)} collective-permute-done((bf16[2028,128]{1,0:T(8,128)(2,1)S(1)}, bf16[2028,128]{1,0:T(8,128)(2,1)S(1)}, u32[]{:S(2)}, u32[]{:S(2)}) %collective-permute-start.15) | collective-permute-done | bytes 519200 | tf_op jit(solution)/shard_map/ppermute | solution.py:2162
  1052.9 1.6 collective-permute-start.18
  1057.1 1.9 maximum_bitcast_fusion.3
  1059.0 1.9 maximum_bitcast_fusion.2
  1060.9 1.9 maximum_bitcast_fusion.1
  1063.0 16.8 %collective-permute-done.18 = bf16[4320,128]{1,0:T(8,128)(2,1)S(1)} collective-permute-done((bf16[4320,128]{1,0:T(8,128)(2,1)S(1)}, bf16[4320,128]{1,0:T(8,128)(2,1)S(1)}, u32[]{:S(2)}, u32[]{:S(2)}) %collective-permute-start.18) | collective-permute-done | bytes 1105952 | tf_op jit(solution)/shard_map/ppermute | solution.py:2162
  1080.2 3.5 multiply_subtract_fusion.1
  1084.9 2.6 pad_maximum_fusion
  1087.6 13.3 %multiply_subtract_fusion = (f32[1,1105920]{1,0:T(1,128)}, f32[1,1105920]{1,0:T(1,128)}) fusion(f32[1,1105920]{1,0:T(1,128)S(1)} %bitcast.82, f32[1,1105920]{1,0:T(1,128)S(1)} %bitcast.86, f32[1,1105920]{1,0:T(1,128)S(1)} %bitcast.89), kind=kLoop, calls=%fused_computation.10 | loop fusion | flops 6635520 | bytes 22118400 | tf_op jit(solution)/shard_map/sub | solution.py:2136
  1101.0 1.3 copy.42
  1103.3 1.3 copy.43
  1104.6 2.3 copy.44
  1108.0 2.1 copy.45
  (158 shorter events, 43.6 us)
Async XLA Ops:
  1.4 13.4 %copy-start.15 = (s32[2,1,1,160]{3,2,1,0:T(1,128)S(1)}, s32[2,1,1,160]{3,2,1,0:T(1,128)}, u32[]{:S(2)}) copy-start(s32[2,1,1,160]{3,2,1,0:T(1,128)} %param.13) | copy-start | bytes 3844
  7.6 58.8 %collective-permute-start.1 = (bf16[160,1792]{1,0:T(8,128)(2,1)}, bf16[160,1792]{1,0:T(8,128)(2,1)}, u32[]{:S(2)}, u32[]{:S(2)}) collective-permute-start(bf16[160,1792]{1,0:T(8,128)(2,1)} %fusion.8), channel_id=1, source_target_pairs={{7,3},{15,11},{23,19},{31,27}} | collective-permute-start | bytes 1720328 | tf_op jit(solution)/shard_map/ppermute | solution.py:437
  9.0 58.5 %collective-permute-start = (bf16[160,1792]{1,0:T(8,128)(2,1)}, bf16[160,1792]{1,0:T(8,128)(2,1)}, u32[]{:S(2)}, u32[]{:S(2)}) collective-permute-start(bf16[160,1792]{1,0:T(8,128)(2,1)} %fusion.8), channel_id=1, source_target_pairs={{0,2},{5,3},{8,10},{13,11},{16,18},{21,19},{24,26},{29,27}} | collective-permute-start | bytes 1720328 | tf_op jit(solution)/shard_map/ppermute | solution.py:437
  14.8 47.8 %collective-permute-start.3 = (s32[2,160]{1,0:T(2,128)S(1)}, s32[2,160]{1,0:T(2,128)S(1)}, u32[]{:S(2)}, u32[]{:S(2)}) collective-permute-start(s32[2,160]{1,0:T(2,128)S(1)} %bitcast.118), channel_id=1, source_target_pairs={{7,3},{15,11},{23,19},{31,27}} | collective-permute-start | bytes 3848 | tf_op jit(solution)/shard_map/ppermute | solution.py:437
  15.4 49.2 %collective-permute-start.2 = (s32[2,160]{1,0:T(2,128)S(1)}, s32[2,160]{1,0:T(2,128)S(1)}, u32[]{:S(2)}, u32[]{:S(2)}) collective-permute-start(s32[2,160]{1,0:T(2,128)S(1)} %bitcast.119), channel_id=1, source_target_pairs={{0,2},{5,3},{8,10},{13,11},{16,18},{21,19},{24,26},{29,27}} | collective-permute-start | bytes 3848 | tf_op jit(solution)/shard_map/ppermute | solution.py:437
  22.9 175.1 %collective-permute-start.9 = (bf16[160,1792]{1,0:T(8,128)(2,1)}, bf16[160,1792]{1,0:T(8,128)(2,1)}, u32[]{:S(2)}, u32[]{:S(2)}) collective-permute-start(bf16[160,1792]{1,0:T(8,128)(2,1)} %fusion.9), channel_id=1, source_target_pairs={{7,3},{15,11},{23,19},{31,27}} | collective-permute-start | bytes 1720328 | tf_op jit(solution)/shard_map/ppermute | solution.py:437
  35.7 3.4 copy-start.17
  35.7 5.3 copy-start.18
  44.9 5.0 copy-start.9
  62.6 276.5 %collective-permute-start.8 = (bf16[160,1792]{1,0:T(8,128)(2,1)}, bf16[160,1792]{1,0:T(8,128)(2,1)}, u32[]{:S(2)}, u32[]{:S(2)}) collective-permute-start(bf16[160,1792]{1,0:T(8,128)(2,1)} %fusion.9), channel_id=1, source_target_pairs={{0,2},{5,3},{8,10},{13,11},{16,18},{21,19},{24,26},{29,27}} | collective-permute-start | bytes 1720328 | tf_op jit(solution)/shard_map/ppermute | solution.py:437
  69.7 123.9 %copy-start.3 = (bf16[320,1792]{1,0:T(8,128)(2,1)S(1)}, bf16[320,1792]{1,0:T(8,128)(2,1)}, u32[]{:S(2)}) copy-start(bf16[320,1792]{1,0:T(8,128)(2,1)} %pad_maximum_fusion.1.refs_12_.shown) | copy-start | bytes 3440644
  189.7 151.5 %collective-permute-start.6 = (bf16[640,1536]{1,0:T(8,128)(2,1)}, bf16[640,1536]{1,0:T(8,128)(2,1)}, u32[]{:S(2)}, u32[]{:S(2)}) collective-permute-start(bf16[640,1536]{1,0:T(8,128)(2,1)} %get-tuple-element.186.activated), channel_id=1, source_target_pairs={{2,4},{3,5},{10,12},{11,13},{18,20},{19,21},{26,28},{27,29}} | collective-permute-start | bytes 5898248 | tf_op jit(solution)/shard_map/ppermute | solution.py:437
  193.5 7.1 copy-start.14
  193.5 147.7 %collective-permute-start.4 = (bf16[320,1792]{1,0:T(8,128)(2,1)S(1)}, bf16[320,1792]{1,0:T(8,128)(2,1)}, u32[]{:S(2)}, u32[]{:S(2)}) collective-permute-start(bf16[320,1792]{1,0:T(8,128)(2,1)S(1)} %copy-done.3), channel_id=1, source_target_pairs={{2,3},{3,2},{10,11},{11,10},{18,19},{19,18},{26,27},{27,26}} | collective-permute-start | bytes 3440648 | tf_op jit(solution)/shard_map/ppermute | solution.py:437
  195.4 145.9 %collective-permute-start.5 = (bf16[640,768]{1,0:T(8,128)(2,1)}, bf16[640,768]{1,0:T(8,128)(2,1)}, u32[]{:S(2)}, u32[]{:S(2)}) collective-permute-start(bf16[640,768]{1,0:T(8,128)(2,1)} %get-tuple-element.180.normed), channel_id=1, source_target_pairs={{2,0},{3,1},{10,8},{11,9},{18,16},{19,17},{26,24},{27,25}} | collective-permute-start | bytes 2949128 | tf_op jit(solution)/shard_map/ppermute | solution.py:437
  198.0 2.7 copy-start.12
  198.0 143.2 %collective-permute-start.7 = (bf16[640,384]{1,0:T(8,128)(2,1)}, bf16[640,384]{1,0:T(8,128)(2,1)}, u32[]{:S(2)}, u32[]{:S(2)}) collective-permute-start(bf16[640,384]{1,0:T(8,128)(2,1)} %slice.144), channel_id=1, source_target_pairs={{2,6},{3,7},{10,14},{11,15},{18,22},{19,23},{26,30},{27,31}} | collective-permute-start | bytes 1474568 | tf_op jit(solution)/shard_map/ppermute | solution.py:437
  203.0 135.3 %copy-start.16 = (pred[16]{0:T(512)(128)(4,1)S(1)}, pred[16]{0:T(512)(128)(4,1)}, u32[]{:S(2)}) copy-start(pred[16]{0:T(512)(128)(4,1)} %constant.141.clone.1) | copy-start | bytes 52
  532.7 164.3 %copy-start.2 = (bf16[320,1792]{1,0:T(8,128)(2,1)S(1)}, bf16[320,1792]{1,0:T(8,128)(2,1)}, u32[]{:S(2)}) copy-start(bf16[320,1792]{1,0:T(8,128)(2,1)} %pad_maximum_fusion.2.refs_12_.shown) | copy-start | bytes 3440644
  694.0 146.7 %collective-permute-start.12 = (bf16[640,1536]{1,0:T(8,128)(2,1)}, bf16[640,1536]{1,0:T(8,128)(2,1)S(1)}, u32[]{:S(2)}, u32[]{:S(2)}) collective-permute-start(bf16[640,1536]{1,0:T(8,128)(2,1)} %get-tuple-element.247.activated), channel_id=1, source_target_pairs={{2,4},{3,5},{10,12},{11,13},{18,20},{19,21},{26,28},{27,29}} | collective-permute-start | bytes 5898248 | tf_op jit(solution)/shard_map/ppermute | solution.py:437
  695.8 10.7 copy-start.13
  696.9 143.8 %collective-permute-start.10 = (bf16[320,1792]{1,0:T(8,128)(2,1)S(1)}, bf16[320,1792]{1,0:T(8,128)(2,1)}, u32[]{:S(2)}, u32[]{:S(2)}) collective-permute-start(bf16[320,1792]{1,0:T(8,128)(2,1)S(1)} %copy-done.2), channel_id=1, source_target_pairs={{2,3},{3,2},{10,11},{11,10},{18,19},{19,18},{26,27},{27,26}} | collective-permute-start | bytes 3440648 | tf_op jit(solution)/shard_map/ppermute | solution.py:437
  703.1 137.6 %collective-permute-start.11 = (bf16[640,768]{1,0:T(8,128)(2,1)}, bf16[640,768]{1,0:T(8,128)(2,1)}, u32[]{:S(2)}, u32[]{:S(2)}) collective-permute-start(bf16[640,768]{1,0:T(8,128)(2,1)} %get-tuple-element.241.normed), channel_id=1, source_target_pairs={{2,0},{3,1},{10,8},{11,9},{18,16},{19,17},{26,24},{27,25}} | collective-permute-start | bytes 2949128 | tf_op jit(solution)/shard_map/ppermute | solution.py:437
  704.4 136.3 %collective-permute-start.13 = (bf16[640,384]{1,0:T(8,128)(2,1)}, bf16[640,384]{1,0:T(8,128)(2,1)S(1)}, u32[]{:S(2)}, u32[]{:S(2)}) collective-permute-start(bf16[640,384]{1,0:T(8,128)(2,1)} %slice.158), channel_id=1, source_target_pairs={{2,6},{3,7},{10,14},{11,15},{18,22},{19,23},{26,30},{27,31}} | collective-permute-start | bytes 1474568 | tf_op jit(solution)/shard_map/ppermute | solution.py:437
  707.6 132.4 %copy-start.11 = (bf16[16,768]{1,0:T(8,128)(2,1)S(1)}, bf16[16,768]{1,0:T(8,128)(2,1)}, u32[]{:S(2)}) copy-start(bf16[16,768]{1,0:T(8,128)(2,1)} %get-tuple-element.232) | copy-start | bytes 73732
  840.7 0.8 copy-start.10
  840.8 1.4 copy-start.8
  1030.4 4.2 copy-start
  1030.4 4.8 copy-start.7
  1035.5 2.7 collective-permute-start.14
  1035.8 16.8 %collective-permute-start.17 = (f32[4320,128]{1,0:T(8,128)S(1)}, f32[4320,128]{1,0:T(8,128)S(1)}, u32[]{:S(2)}, u32[]{:S(2)}) collective-permute-start(f32[4320,128]{1,0:T(8,128)S(1)} %slice_select_fusion), channel_id=1, source_target_pairs={{0,8},{8,0},{16,24},{24,16},{1,9},{9,1},{17,25},{25,17},{2,10},{10... | collective-permute-start | bytes 6635528 | tf_op jit(solution)/shard_map/ppermute | solution.py:452
  1038.4 13.9 %collective-permute-start.15 = (bf16[2028,128]{1,0:T(8,128)(2,1)S(1)}, bf16[2028,128]{1,0:T(8,128)(2,1)S(1)}, u32[]{:S(2)}, u32[]{:S(2)}) collective-permute-start(bf16[2028,128]{1,0:T(8,128)(2,1)S(1)} %add_convert_fusion.1), channel_id=1, source_target_pairs={{0,16},{8,24},{16,0},{24,8},{1,17},{9,25},{17,1},{25,9},{2,18},{10... | collective-permute-start | bytes 1557512 | tf_op jit(solution)/shard_map/ppermute | solution.py:2162
  1052.5 10.2 collective-permute-start.16
  1052.9 26.8 %collective-permute-start.18 = (bf16[4320,128]{1,0:T(8,128)(2,1)S(1)}, bf16[4320,128]{1,0:T(8,128)(2,1)S(1)}, u32[]{:S(2)}, u32[]{:S(2)}) collective-permute-start(bf16[4320,128]{1,0:T(8,128)(2,1)S(1)} %add_convert_fusion), channel_id=1, source_target_pairs={{0,16},{8,24},{16,0},{24,8},{1,17},{9,25},{17,1},{25,9},{2,18},{10... | collective-permute-start | bytes 3317768 | tf_op jit(solution)/shard_map/ppermute | solution.py:2162
  1063.0 17.2 %copy-start.4 = (f32[519168]{0:T(1024)S(1)}, f32[519168]{0:T(1024)}, u32[]{:S(2)}) copy-start(f32[519168]{0:T(1024)} %param.22) | copy-start | bytes 6230020
  1080.1 4.4 collective-permute-start.19
  1080.1 7.4 slice-start.2
  1083.6 3.9 slice-start.3
  1084.4 3.1 slice-start
  1084.9 2.7 slice-start.1
  1084.9 19.7 %slice-start.6 = ((s8[4423680]{0:T(1024)(128)(4,1)}), s8[229376]{0:T(1024)(128)(4,1)S(1)}, s32[]{:S(2)}) async-start(s8[4423680]{0:T(1024)(128)(4,1)} %bitcast.93), calls=%async_computation.6 | async-start | bytes 458752
  1087.5 13.4 %copy-start.1 = (f32[8640,128]{1,0:T(8,128)}, f32[8640,128]{1,0:T(8,128)S(1)}, u32[]{:S(2)}) copy-start(f32[8640,128]{1,0:T(8,128)S(1)} %pad_maximum_fusion) | copy-start | bytes 13271044
  1087.6 13.3 %copy-start.6 = (f32[4056,128]{1,0:T(8,128)S(1)}, f32[4056,128]{1,0:T(8,128)}, u32[]{:S(2)}) copy-start(f32[4056,128]{1,0:T(8,128)} %get-tuple-element.275) | copy-start | bytes 6230020
  1087.6 17.0 %slice-start.7 = ((s8[4423680]{0:T(1024)(128)(4,1)}), s8[4194304]{0:T(1024)(128)(4,1)S(1)}, s32[]{:S(2)}) async-start(s8[4423680]{0:T(1024)(128)(4,1)} %bitcast.93), calls=%async_computation.7 | async-start | bytes 8388608
  1101.0 2.3 copy-start.5
  1103.3 4.5 slice-start.4
  1104.6 3.4 slice-start.5

commit v6 on v5

--- a/solution.py
+++ b/solution.py
@@ -1018,7 +1018,7 @@
 def encoder_backward_kernel(
     picked, shown, shown_other, w_qkv, w_out, w_up, w_down, e2d_w, vec,
     stream, normed, joined, blended, attended, second, upward, activated, encoded, final_enc,
-    wide, tall, dec_qkv, small, normed_far, active_far, active_last,
+    wide, tall, dec_qkv, small, normed_far, active_far,
     qkv_out, square_out, up_out, patch_out, e2d_out, vec_out,
     one_wide, one_tall, one_qkv, one_small, two_wide, two_tall, two_qkv, two_small,
     wide_sent, tall_sent, dec_qkv_sent, small_sent, wide_got, tall_got, dec_qkv_got, small_got,
@@ -1100,7 +1100,8 @@
 
     out_rows, up_rows, down_rows = 288, 672, 1248
     next_row = jnp.minimum(z + 1, LAST)
-    low_far = [links.copy(next(numbers), low.at[rows_at(c)], low.at[rows_at(c)], at(next_row, x)) for c in range(4)]
+    low_far = [links.copy(next(numbers), low.at[rows_at(c)], low.at[rows_at(c)], at(2, x)) for c in range(4)]
+    down_far = links.copy(next(numbers), down_grad.at[pl.ds(96, 288)], square_out.at[pl.ds(0, 288)], at(LAST, x))
     joined_far = [
         links.copy(next(numbers), grad_joined.at[rows_at(c)], grad_joined.at[rows_at(c)], at(0, x)) for c in range(4)
     ]
@@ -1212,6 +1213,8 @@
             low_far[2 + i].start()
             part_sent[rows_at(i)] = feed_back(2 + i).astype(HALF)
             second_sent[i].start()
+        down_grad[pl.ds(0, 384)] = mm_tn(activated[:, 1152:], low[...]).astype(HALF)
+        down_far.start()
         for i in range(2):
             rows = rows_at(i)
             second_sent[i].wait_recv()
@@ -1299,7 +1302,7 @@
             one.start()
         for one in low_sent + mid_sent + second_sent + normed_sent:
             one.wait_send()
-        for one in (*low_far, *joined_far, up_near, out_near, patch_one, patch_two, e2d_near, vec_far):
+        for one in (*low_far, down_far, *joined_far, up_near, out_near, patch_one, patch_two, e2d_near, vec_far):
             one.wait_send()
         for one in tree_two:
             one.wait_send()
@@ -1314,7 +1317,7 @@
                 def _():
                     pick_copy(row, side).wait_send()
 
-    for row, ones in ((0, (out_near, patch_one)), (2, (up_near, patch_two, e2d_near)), (LAST, (vec_far,))):
+    for row, ones in ((0, (out_near, patch_one)), (2, (up_near, patch_two, e2d_near)), (LAST, (down_far, vec_far))):
 
         @pl.when(z == row)
         def _():
@@ -1329,20 +1332,8 @@
     def _():
         for one in low_far:
             one.wait_recv()
-            one.start()
         tall_product(active_far, low, down_grad, 384)
         kept = pltpu.make_async_copy(down_grad.at[pl.ds(0, down_rows)], square_out, local_sem.at[0])
-        kept.start()
-        for one in low_far:
-            one.wait_send()
-        kept.wait()
-
-    @pl.when(z == LAST)
-    def _():
-        for one in low_far:
-            one.wait_recv()
-        down_grad[pl.ds(0, 384)] = mm_tn(active_last[...], low[...]).astype(HALF)
-        kept = pltpu.make_async_copy(down_grad.at[pl.ds(96, 288)], square_out.at[pl.ds(0, 288)], local_sem.at[0])
         kept.start()
         kept.wait()
 
@@ -1411,7 +1402,7 @@
         encoder_backward_kernel,
         name="encoder_backward",
         out_shape=[jax.ShapeDtypeStruct(*one) for one in shapes],
-        in_specs=[vmem] * 26,
+        in_specs=[vmem] * 25,
         out_specs=[anywhere] * len(shapes),
         scratch_shapes=[pltpu.VMEM(*one) for one in scratch]
         + [pltpu.SemaphoreType.DMA((44,)), pltpu.SemaphoreType.DMA((44,)), pltpu.SemaphoreType.DMA((4,))],
@@ -2075,7 +2066,8 @@
     rep_quarter = rep_weights.shape[0]
     source, target = jnp.arange(PATCH)[:, None], jnp.arange(WIDE)[None, :]
     cut = rep_quarter // D
-    layout = (target == source + (SPAN[1] - cut) * (source // cut)).astype(HALF)
+    moved = lax.optimization_barrier(source + (SPAN[1] - cut) * (source // cut))
+    layout = (target == moved).astype(HALF)
     shown_steps = []
     for s in range(STEPS):
         picks = (visible[s, 0, 0][:, None] == jnp.arange(TUBES)[None, :]).astype(HALF)
@@ -2105,7 +2097,6 @@
         far = (
             hop_both(normed, (HOST, 0)),
             hop_both(activated, (HOST, 2)),
-            hop_both(activated[:, 1152:], (HOST, LAST)),
         )
         pixels_low = lax.dynamic_slice_in_dim(patches[s, 0, 0], side * half_rows, half_rows, 0)
         picked, wide, tall, qkv_grad, small, loss = decoder_round(
@@ -2128,7 +2119,8 @@
         norm_list.append(stats[0, 0])
         loss_list.append(stats[1, 0])
         count_list.append(stats[2, 0])
-    ten_first, ten_second, rep_first, rep_second = [one.reshape(-1) for one in (*states[1:3], *states[4:])]
+    one = jnp.where(count_list[-1] >= 0, 1.0, 0.0)
+    ten_first, ten_second, rep_first, rep_second = [(one * part).reshape(-1) for part in (*states[1:3], *states[4:])]
     ten_diff, rep_diff = [group_mean(starts[i] - states[3 * i]).reshape(-1) for i in range(2)]
     rep_momentum = MOMENTUM * rep_outer + rep_diff
     ten_momentum = MOMENTUM * ten_outer[0] + ten_diff

time: 1120 us -> 1110 us (level)
    pallas_call x2, Pallas kernels: 162 us -> 141 us  [update(): pl.pallas_call(functools.partial(update_kernel, number, last), name='upda...]
    ppermute x14 -> x12, starting transfers between devices: 23.6 us -> 20.6 us  [hop(): return lax.ppermute(value, ('dp', 'tensor'), pairs)]
  transfers between devices with their start and end apart: 20 -> 18, of which waited for: 4 -> 3; matrix products, arithmetic and copies ran while one was open for 7% -> 7% of each run, Pallas kernels for 35% -> 36%
where the time goes in v6:
time: 1110 us; the launch traced here: 1090 us
  Pallas kernels  923 us (83%)
  other arithmetic  65.3 us (6%)
  local copies, waits for them, and re-layouts  36.4 us (3%)
  waiting for transfers between devices  30.1 us (3%)
  starting transfers between devices  24 us (2%)
  matrix products  12.4 us (1%)
    pallas_call x2, Pallas kernels, encoder_forward(): pl.pallas_call(functools.partial(forward_kernel, shared), name='encoder_f...  283 us
    pallas_call x2, Pallas kernels, decoder_round(): pl.pallas_call(decoder_kernel, name='decoder', out_shape=[jax.ShapeDtypeS...  264 us
    pallas_call x2, Pallas kernels, encoder_backward(): pl.pallas_call(encoder_backward_kernel, name='encoder_backward', out_shap...  227 us
    pallas_call x2, Pallas kernels, update(): pl.pallas_call(functools.partial(update_kernel, number, last), name='upda...  141 us
    ppermute x2, waiting for transfers between devices, group_mean(): far = lax.ppermute(part_low, 'group', [(g, g ^ 2) for g in range(4)])  29.3 us
  transfers between devices with their start and end apart: 18, of which 3 were waited for; matrix products, arithmetic and copies ran while one was open for 7% of the time, Pallas kernels for 36%

profile of v6, /device:TPU:0, one launch (start us, length us, event | category | flops | bytes accessed | tf_op | source)
XLA Modules:
  0.0 1094.6 jit_solution(15221400887978883045)
XLA Ops:
  1.4 6.2 fusion.8
  7.6 1.5 collective-permute-start.1
  9.1 5.8 collective-permute-start
  15.5 1.3 collective-permute-start.2
  16.8 6.2 fusion.9
  23.0 1.5 collective-permute-start.8
  24.6 8.2 fusion.75
  35.9 1.6 fusion.76
  37.5 1.8 compare_reduce_fusion.1
  41.7 3.3 maximum_select_fusion.places
  45.1 5.0 dynamic-slice_bitcast_fusion
  51.2 2.0 fusion.73
  55.2 7.4 lay_out.1
  62.6 2.1 collective-permute-start.7
  68.8 1.7 collective-permute-start.4
  70.4 119.8 %encoder_forward.2 = (bf16[768,1152]{1,0:T(8,128)(2,1)}, bf16[384,768]{1,0:T(8,128)(2,1)}, bf16[768,1536]{1,0:T(8,128)(2,1)}, bf16[1536,768]{1,0:T(8,128)(2,1)},...) custom-call(bf16[768,1152]{1,0:T(8,128)(2,1)} %get-tuple-element.147, ...), custom_call_target="tpu_custom_call" | custom-call | tf_op jit(solution)/shard_map/encoder_forward/pallas_call | solution.py:991
  191.2 1.3 broadcast_select_fusion.5
  194.3 1.3 collective-permute-start.5
  196.2 133.1 %decoder.2 = (bf16[160,384]{1,0:T(8,128)(2,1)}, f32[384,1536]{1,0:T(8,128)}, f32[960,384]{1,0:T(8,128)}, f32[384,576]{1,0:T(8,128)}, f32[16,384]{1,0:T(8,128)}, /*index=5*/f32[8,128]{1,0:T(8,128)}) custom-call(f32[160,384]{1,0:T(8,128)} %get-tuple-element.159.reduced, bf16[1568,160]{1,0:T(8,128)(2,1)} %get-tuple-element.305.hot, f32[1568,1]{1,0:T(8,128)} %reshape.388.shown, ...), custom_call_target="tpu_custom_call" | custom-call | tf_op jit(solution)/shard_map/decoder/pallas_call | solution.py:2003
  331.3 1.3 compare_select_fusion.3
  333.8 2.1 pad_maximum_fusion.2.refs_12_.shown
  335.9 1.3 copy-done.9
  337.2 109.8 %encoder_backward.2 = (bf16[768,1152]{1,0:T(8,128)(2,1)}, bf16[1248,768]{1,0:T(8,128)(2,1)}, bf16[672,1536]{1,0:T(8,128)(2,1)}, bf16[704,384]{1,0:T(8,128)(2,1)}...) custom-call(bf16[160,384]{1,0:T(8,128)(2,1)} %get-tuple-element.173., ...), custom_call_target="tpu_custom_call" | custom-call | tf_op jit(solution)/shard_map/encoder_backward/pallas_call | solution.py:1401
  447.6 72.7 %update.2 = (f32[8,128]{1,0:T(8,128)}, f32[8640,128]{1,0:T(8,128)}, f32[8640,128]{1,0:T(8,128)}, f32[8640,128]{1,0:T(8,128)}, f32[4056,128]{1,0:T(8,128)}, /*ind...) custom-call(f32[8,128]{1,0:T(8,128)} %broadcast_in_dim.116.stats, ...), custom_call_target="tpu_custom_call" | custom-call | tf_op jit(solution)/shard_map/update/pallas_call | solution.py:1736
  520.3 163.2 %encoder_forward.3 = (bf16[768,1152]{1,0:T(8,128)(2,1)}, bf16[384,768]{1,0:T(8,128)(2,1)}, bf16[768,1536]{1,0:T(8,128)(2,1)}, bf16[1536,768]{1,0:T(8,128)(2,1)},...) custom-call(bf16[768,1152]{1,0:T(8,128)(2,1)} %get-tuple-element.208, ...), custom_call_target="tpu_custom_call" | custom-call | tf_op jit(solution)/shard_map/encoder_forward/pallas_call | solution.py:991
  686.6 1.7 collective-permute-start.9
  691.0 1.3 collective-permute-start.10
  692.3 1.3 broadcast_select_fusion.3
  694.8 131.3 %decoder.3 = (bf16[160,384]{1,0:T(8,128)(2,1)}, f32[384,1536]{1,0:T(8,128)}, f32[960,384]{1,0:T(8,128)}, f32[384,576]{1,0:T(8,128)}, f32[16,384]{1,0:T(8,128)}, /*index=5*/f32[8,128]{1,0:T(8,128)}) custom-call(f32[160,384]{1,0:T(8,128)} %get-tuple-element.220.reduced, bf16[1568,160]{1,0:T(8,128)(2,1)} %get-tuple-element.304.hot, f32[1568,1]{1,0:T(8,128)} %reshape.389.shown, ...), custom_call_target="tpu_custom_call" | custom-call | tf_op jit(solution)/shard_map/decoder/pallas_call | solution.py:2003
  828.5 1.3 fusion.77
  831.8 117.0 %encoder_backward.3 = (bf16[768,1152]{1,0:T(8,128)(2,1)}, bf16[1248,768]{1,0:T(8,128)(2,1)}, bf16[672,1536]{1,0:T(8,128)(2,1)}, bf16[704,384]{1,0:T(8,128)(2,1)}...) custom-call(bf16[160,384]{1,0:T(8,128)(2,1)} %get-tuple-element.234., ...), custom_call_target="tpu_custom_call" | custom-call | tf_op jit(solution)/shard_map/encoder_backward/pallas_call | solution.py:1401
  949.5 68.4 %update.3 = (f32[8,128]{1,0:T(8,128)}, f32[8640,128]{1,0:T(8,128)}, f32[8640,128]{1,0:T(8,128)}, f32[8640,128]{1,0:T(8,128)}, f32[4056,128]{1,0:T(8,128)}, /*index=5*/f32[4056,128]{1,0:T(8,128)}, f32[4056,128]{1,0:T(8,128)}) custom-call(f32[8,128]{1,0:T(8,128)} %broadcast_in_dim.122.stats, bf16[768,1152]{1,0:T(8,128)(2,1)} %get-tuple-element.254.qkv, ...), custom_call_target="tpu_custom_call" | custom-call | tf_op jit(solution)/shard_map/update/pallas_call | solution.py:1736
  1017.9 3.8 sub.70
  1024.4 1.4 fusion.78
  1026.5 2.3 broadcast_multiply_fusion
  1028.7 2.2 broadcast_multiply_fusion.1
  1031.2 1.6 collective-permute-start.13
  1032.7 1.4 broadcast_multiply_fusion.2
  1034.2 11.3 %collective-permute-done.13 = bf16[2028,128]{1,0:T(8,128)(2,1)S(1)} collective-permute-done((bf16[2028,128]{1,0:T(8,128)(2,1)S(1)}, bf16[2028,128]{1,0:T(8,128)(2,1)S(1)}, u32[]{:S(2)}, u32[]{:S(2)}) %collective-permute-start.13) | collective-permute-done | bytes 519200 | tf_op jit(solution)/shard_map/ppermute | solution.py:2154
  1046.2 1.6 collective-permute-start.16
  1047.8 1.4 broadcast_multiply_fusion.3
  1049.3 1.9 maximum_bitcast_fusion.3
  1051.1 1.9 maximum_bitcast_fusion.2
  1053.0 1.9 maximum_bitcast_fusion.1
  1055.1 18.0 %collective-permute-done.16 = bf16[4320,128]{1,0:T(8,128)(2,1)S(1)} collective-permute-done((bf16[4320,128]{1,0:T(8,128)(2,1)S(1)}, bf16[4320,128]{1,0:T(8,128)(2,1)S(1)}, u32[]{:S(2)}, u32[]{:S(2)}) %collective-permute-start.16) | collective-permute-done | bytes 1105952 | tf_op jit(solution)/shard_map/ppermute | solution.py:2154
  1073.5 3.5 multiply_subtract_fusion.1
  1078.2 2.6 pad_maximum_fusion
  1080.9 13.3 %multiply_subtract_fusion = (f32[1,1105920]{1,0:T(1,128)}, f32[1,1105920]{1,0:T(1,128)}) fusion(f32[1,1105920]{1,0:T(1,128)S(1)} %bitcast.83, f32[1,1105920]{1,0:T(1,128)S(1)} %bitcast.87, f32[1,1105920]{1,0:T(1,128)S(1)} %bitcast.90), kind=kLoop, calls=%fused_computation.10 | loop fusion | flops 6635520 | bytes 22118400 | tf_op jit(solution)/shard_map/sub | solution.py:2128
  (153 shorter events, 37.1 us)
Async XLA Ops:
  1.4 13.5 %copy-start.15 = (s32[2,1,1,160]{3,2,1,0:T(1,128)S(1)}, s32[2,1,1,160]{3,2,1,0:T(1,128)}, u32[]{:S(2)}) copy-start(s32[2,1,1,160]{3,2,1,0:T(1,128)} %param.13) | copy-start | bytes 3844
  7.6 58.9 %collective-permute-start.1 = (bf16[160,1792]{1,0:T(8,128)(2,1)}, bf16[160,1792]{1,0:T(8,128)(2,1)}, u32[]{:S(2)}, u32[]{:S(2)}) collective-permute-start(bf16[160,1792]{1,0:T(8,128)(2,1)} %fusion.8), channel_id=1, source_target_pairs={{7,3},{15,11},{23,19},{31,27}} | collective-permute-start | bytes 1720328 | tf_op jit(solution)/shard_map/ppermute | solution.py:437
  9.1 58.5 %collective-permute-start = (bf16[160,1792]{1,0:T(8,128)(2,1)}, bf16[160,1792]{1,0:T(8,128)(2,1)}, u32[]{:S(2)}, u32[]{:S(2)}) collective-permute-start(bf16[160,1792]{1,0:T(8,128)(2,1)} %fusion.8), channel_id=1, source_target_pairs={{0,2},{5,3},{8,10},{13,11},{16,18},{21,19},{24,26},{29,27}} | collective-permute-start | bytes 1720328 | tf_op jit(solution)/shard_map/ppermute | solution.py:437
  14.8 47.8 %collective-permute-start.3 = (s32[2,160]{1,0:T(2,128)S(1)}, s32[2,160]{1,0:T(2,128)S(1)}, u32[]{:S(2)}, u32[]{:S(2)}) collective-permute-start(s32[2,160]{1,0:T(2,128)S(1)} %bitcast.119), channel_id=1, source_target_pairs={{7,3},{15,11},{23,19},{31,27}} | collective-permute-start | bytes 3848 | tf_op jit(solution)/shard_map/ppermute | solution.py:437
  15.5 49.3 %collective-permute-start.2 = (s32[2,160]{1,0:T(2,128)S(1)}, s32[2,160]{1,0:T(2,128)S(1)}, u32[]{:S(2)}, u32[]{:S(2)}) collective-permute-start(s32[2,160]{1,0:T(2,128)S(1)} %bitcast.120), channel_id=1, source_target_pairs={{0,2},{5,3},{8,10},{13,11},{16,18},{21,19},{24,26},{29,27}} | collective-permute-start | bytes 3848 | tf_op jit(solution)/shard_map/ppermute | solution.py:437
  23.0 309.6 %collective-permute-start.8 = (bf16[160,1792]{1,0:T(8,128)(2,1)}, bf16[160,1792]{1,0:T(8,128)(2,1)}, u32[]{:S(2)}, u32[]{:S(2)}) collective-permute-start(bf16[160,1792]{1,0:T(8,128)(2,1)} %fusion.9), channel_id=1, source_target_pairs={{7,3},{15,11},{23,19},{31,27}} | collective-permute-start | bytes 1720328 | tf_op jit(solution)/shard_map/ppermute | solution.py:437
  35.9 3.4 copy-start.17
  35.9 5.3 copy-start.18
  45.0 5.0 copy-start.10
  62.6 271.1 %collective-permute-start.7 = (bf16[160,1792]{1,0:T(8,128)(2,1)}, bf16[160,1792]{1,0:T(8,128)(2,1)}, u32[]{:S(2)}, u32[]{:S(2)}) collective-permute-start(bf16[160,1792]{1,0:T(8,128)(2,1)} %fusion.9), channel_id=1, source_target_pairs={{0,2},{5,3},{8,10},{13,11},{16,18},{21,19},{24,26},{29,27}} | collective-permute-start | bytes 1720328 | tf_op jit(solution)/shard_map/ppermute | solution.py:437
  68.8 1.7 copy-start.3
  68.8 267.1 %collective-permute-start.4 = (bf16[320,1792]{1,0:T(8,128)(2,1)S(1)}, bf16[320,1792]{1,0:T(8,128)(2,1)}, u32[]{:S(2)}, u32[]{:S(2)}) collective-permute-start(bf16[320,1792]{1,0:T(8,128)(2,1)S(1)} %pad_maximum_fusion.1.refs_12_.shown), channel_id=1, source_target_pairs={{2,3},{3,2},{10,11},{11,10},{18,19},{19,18},{26,27},{27,26}} | collective-permute-start | bytes 3440648 | tf_op jit(solution)/shard_map/ppermute | solution.py:437
  190.2 2.3 copy-start.14
  190.2 145.7 %collective-permute-start.6 = (bf16[640,1536]{1,0:T(8,128)(2,1)}, bf16[640,1536]{1,0:T(8,128)(2,1)S(1)}, u32[]{:S(2)}, u32[]{:S(2)}) collective-permute-start(bf16[640,1536]{1,0:T(8,128)(2,1)} %get-tuple-element.186.activated), channel_id=1, source_target_pairs={{2,4},{3,5},{10,12},{11,13},{18,20},{19,21},{26,28},{27,29}} | collective-permute-start | bytes 5898248 | tf_op jit(solution)/shard_map/ppermute | solution.py:437
  192.5 1.2 copy-start.12
  194.3 141.6 %collective-permute-start.5 = (bf16[640,768]{1,0:T(8,128)(2,1)}, bf16[640,768]{1,0:T(8,128)(2,1)}, u32[]{:S(2)}, u32[]{:S(2)}) collective-permute-start(bf16[640,768]{1,0:T(8,128)(2,1)} %get-tuple-element.180.normed), channel_id=1, source_target_pairs={{2,0},{3,1},{10,8},{11,9},{18,16},{19,17},{26,24},{27,25}} | collective-permute-start | bytes 2949128 | tf_op jit(solution)/shard_map/ppermute | solution.py:437
  196.2 134.3 %copy-start.16 = (pred[16]{0:T(512)(128)(4,1)S(1)}, pred[16]{0:T(512)(128)(4,1)}, u32[]{:S(2)}) copy-start(pred[16]{0:T(512)(128)(4,1)} %constant.144.clone.1) | copy-start | bytes 52
  335.9 1.3 copy-start.9
  520.3 166.3 %copy-start.2 = (bf16[320,1792]{1,0:T(8,128)(2,1)S(1)}, bf16[320,1792]{1,0:T(8,128)(2,1)}, u32[]{:S(2)}) copy-start(bf16[320,1792]{1,0:T(8,128)(2,1)} %pad_maximum_fusion.2.refs_12_.shown) | copy-start | bytes 3440644
  683.5 10.1 copy-start.13
  683.6 147.0 %collective-permute-start.11 = (bf16[640,1536]{1,0:T(8,128)(2,1)}, bf16[640,1536]{1,0:T(8,128)(2,1)S(1)}, u32[]{:S(2)}, u32[]{:S(2)}) collective-permute-start(bf16[640,1536]{1,0:T(8,128)(2,1)} %get-tuple-element.247.activated), channel_id=1, source_target_pairs={{2,4},{3,5},{10,12},{11,13},{18,20},{19,21},{26,28},{27,29}} | collective-permute-start | bytes 5898248 | tf_op jit(solution)/shard_map/ppermute | solution.py:437
  686.6 143.9 %collective-permute-start.9 = (bf16[320,1792]{1,0:T(8,128)(2,1)S(1)}, bf16[320,1792]{1,0:T(8,128)(2,1)}, u32[]{:S(2)}, u32[]{:S(2)}) collective-permute-start(bf16[320,1792]{1,0:T(8,128)(2,1)S(1)} %copy-done.2), channel_id=1, source_target_pairs={{2,3},{3,2},{10,11},{11,10},{18,19},{19,18},{26,27},{27,26}} | collective-permute-start | bytes 3440648 | tf_op jit(solution)/shard_map/ppermute | solution.py:437
  691.0 139.5 %collective-permute-start.10 = (bf16[640,768]{1,0:T(8,128)(2,1)}, bf16[640,768]{1,0:T(8,128)(2,1)}, u32[]{:S(2)}, u32[]{:S(2)}) collective-permute-start(bf16[640,768]{1,0:T(8,128)(2,1)} %get-tuple-element.241.normed), channel_id=1, source_target_pairs={{2,0},{3,1},{10,8},{11,9},{18,16},{19,17},{26,24},{27,25}} | collective-permute-start | bytes 2949128 | tf_op jit(solution)/shard_map/ppermute | solution.py:437
  694.8 135.0 %copy-start.11 = (bf16[16,768]{1,0:T(8,128)(2,1)S(1)}, bf16[16,768]{1,0:T(8,128)(2,1)}, u32[]{:S(2)}) copy-start(bf16[16,768]{1,0:T(8,128)(2,1)} %get-tuple-element.232) | copy-start | bytes 73732
  830.5 1.3 copy-start.8
  1021.8 1.6 copy-start
  1021.8 2.2 copy-start.7
  1022.0 23.7 %collective-permute-start.15 = (f32[4320,128]{1,0:T(8,128)S(1)}, f32[4320,128]{1,0:T(8,128)S(1)}, u32[]{:S(2)}, u32[]{:S(2)}) collective-permute-start(f32[4320,128]{1,0:T(8,128)S(1)} %slice_select_fusion), channel_id=1, source_target_pairs={{0,8},{8,0},{16,24},{24,16},{1,9},{9,1},{17,25},{25,17},{2,10},{10... | collective-permute-start | bytes 6635528 | tf_op jit(solution)/shard_map/ppermute | solution.py:452
  1022.1 4.3 slice-start.6
  1024.0 2.5 slice-start.7
  1024.2 4.5 slice-start.4
  1024.3 6.7 collective-permute-start.12
  1026.5 2.3 slice-start.5
  1031.0 1.8 copy-start.6
  1031.2 14.4 %collective-permute-start.13 = (bf16[2028,128]{1,0:T(8,128)(2,1)S(1)}, bf16[2028,128]{1,0:T(8,128)(2,1)S(1)}, u32[]{:S(2)}, u32[]{:S(2)}) collective-permute-start(bf16[2028,128]{1,0:T(8,128)(2,1)S(1)} %add_convert_fusion.1), channel_id=1, source_target_pairs={{0,16},{8,24},{16,0},{24,8},{1,17},{9,25},{17,1},{25,9},{2,18},{10... | collective-permute-start | bytes 1557512 | tf_op jit(solution)/shard_map/ppermute | solution.py:2154
  1045.7 2.2 copy-start.5
  1045.7 9.2 collective-permute-start.14
  1046.2 26.8 %collective-permute-start.16 = (bf16[4320,128]{1,0:T(8,128)(2,1)S(1)}, bf16[4320,128]{1,0:T(8,128)(2,1)S(1)}, u32[]{:S(2)}, u32[]{:S(2)}) collective-permute-start(bf16[4320,128]{1,0:T(8,128)(2,1)S(1)} %add_convert_fusion), channel_id=1, source_target_pairs={{0,16},{8,24},{16,0},{24,8},{1,17},{9,25},{17,1},{25,9},{2,18},{10... | collective-permute-start | bytes 3317768 | tf_op jit(solution)/shard_map/ppermute | solution.py:2154
  1055.1 18.3 %copy-start.4 = (f32[519168]{0:T(1024)S(1)}, f32[519168]{0:T(1024)}, u32[]{:S(2)}) copy-start(f32[519168]{0:T(1024)} %param.22) | copy-start | bytes 6230020
  1073.4 4.4 collective-permute-start.17
  1073.5 7.4 slice-start.2
  1077.0 3.9 slice-start.3
  1077.8 3.1 slice-start
  1078.2 2.7 slice-start.1
  1080.9 13.4 %copy-start.1 = (f32[8640,128]{1,0:T(8,128)}, f32[8640,128]{1,0:T(8,128)S(1)}, u32[]{:S(2)}) copy-start(f32[8640,128]{1,0:T(8,128)S(1)} %pad_maximum_fusion) | copy-start | bytes 13271044

commit v7 on v6

--- a/solution.py
+++ b/solution.py
@@ -873,15 +873,11 @@
             rows = rows_at(c)
             joined[rows] = mm(normed[rows], got[W_QKV][...]).astype(HALF)
             width = D // 2
-            for h in range(width // HDIM):
-                column = h * HDIM
-                queries = joined[rows, column : column + HDIM]
-                keys = joined[rows, width + column : width + column + HDIM]
-                values = joined[rows, 2 * width + column : 2 * width + column + HDIM]
-                scores = mm_nt(queries, keys) * HDIM**-0.5
-                weights = jnp.exp(scores - jnp.max(scores, -1, keepdims=True))
-                probs = weights * (1.0 / jnp.sum(weights, -1, keepdims=True))
-                blended[rows, column : column + HDIM] = mm(probs.astype(HALF), values).astype(HALF)
+            thirds = [[joined[rows, t * width + h * HDIM : t * width + (h + 1) * HDIM] for h in range(width // HDIM)] for t in range(3)]
+            scores = [mm_nt(one, two) * HDIM**-0.5 for one, two in zip(*thirds[:2])]
+            weights = [jnp.exp(one - jnp.max(one, -1, keepdims=True)) for one in scores]
+            probs = [(one * (1.0 / jnp.sum(one, -1, keepdims=True))).astype(HALF) for one in weights]
+            blended[rows] = jnp.concatenate([mm(one, two) for one, two in zip(probs, thirds[2])], 1).astype(HALF)
 
         for i in range(2):
             attend(i)
@@ -1197,7 +1193,7 @@
             low_sent[i].start()
             low_far[i].start()
         whole_low = jnp.concatenate(reduced_low, 0)
-        product = mm_tn(final_enc[...], whole_low).astype(HALF)
+        product = mm_tn(final_enc[...], whole_low)
         e2d_part[0] = product[: D // 2]
         e2d_part[1] = product[D // 2 :]
         e2d_sent.start()
@@ -1228,32 +1224,26 @@
             mid[rows] = grad.astype(HALF)
             mid_sent[i].start()
         e2d_sent.wait()
-        e2d_grad[...] = (e2d_part[x].astype(FLOAT) + e2d_got[...].astype(FLOAT)).astype(HALF)
+        e2d_grad[...] = (e2d_part[x] + e2d_got[...]).astype(HALF)
         e2d_near.start()
 
         def attend_back(c):
             rows = rows_at(c)
             width = D // 2
             grad_blend[...] = mm_nt(mid[rows], w_out[...]).astype(HALF)
-            for h in range(width // HDIM):
-                column = h * HDIM
-                queries = joined[rows, column : column + HDIM]
-                keys = joined[rows, width + column : width + column + HDIM]
-                values = joined[rows, 2 * width + column : 2 * width + column + HDIM]
-                grads = grad_blend[:, column : column + HDIM]
-                scores = mm_nt(queries, keys) * HDIM**-0.5
-                weights = jnp.exp(scores - jnp.max(scores, -1, keepdims=True))
-                probs = weights * (1.0 / jnp.sum(weights, -1, keepdims=True))
-                grad_values = mm_tn(probs.astype(HALF), grads)
-                grad_probs = mm_nt(grads, values)
-                grad_scores = (
-                    probs * (grad_probs - jnp.sum(probs * grad_probs, -1, keepdims=True))
-                ).astype(HALF)
-                for third, value in enumerate(
-                    (mm(grad_scores, keys) * HDIM**-0.5, mm_tn(grad_scores, queries) * HDIM**-0.5, grad_values)
-                ):
-                    start = third * width + column
-                    grad_joined[rows, start : start + HDIM] = value.astype(HALF)
+            heads = range(width // HDIM)
+            queries, keys, values = [[joined[rows, t * width + h * HDIM : t * width + (h + 1) * HDIM] for h in heads] for t in range(3)]
+            grads = [grad_blend[:, h * HDIM : (h + 1) * HDIM] for h in heads]
+            scores = [mm_nt(queries[h], keys[h]) * HDIM**-0.5 for h in heads]
+            grad_probs = [mm_nt(grads[h], values[h]) for h in heads]
+            weights = [jnp.exp(one - jnp.max(one, -1, keepdims=True)) for one in scores]
+            probs = [one * (1.0 / jnp.sum(one, -1, keepdims=True)) for one in weights]
+            sums = [jnp.sum(probs[h] * grad_probs[h], -1, keepdims=True) for h in heads]
+            grad_scores = [(probs[h] * (grad_probs[h] - sums[h])).astype(HALF) for h in heads]
+            parts = [mm(grad_scores[h], keys[h]) * HDIM**-0.5 for h in heads]
+            parts += [mm_tn(grad_scores[h], queries[h]) * HDIM**-0.5 for h in heads]
+            parts += [mm_tn(probs[h].astype(HALF), grads[h]) for h in heads]
+            grad_joined[rows] = jnp.concatenate(parts, 1).astype(HALF)
             return mm_nt(grad_joined[rows], w_qkv[...])
 
         for i in range(2):
@@ -1392,8 +1382,8 @@
         ((704, D // 2), HALF),
         ((704, D // 2), HALF),
         ((192, D // 2), HALF),
-        ((2, D // 2, DD), HALF),
-        ((D // 2, DD), HALF),
+        ((2, D // 2, DD), FLOAT),
+        ((D // 2, DD), FLOAT),
         ((D // 2, DD), HALF),
         ((16, D), FLOAT),
         ((16, D), FLOAT),
@@ -1597,7 +1587,7 @@
 
     @pl.when(z == LAST)
     def _():
-        head_own[...] = total(wide, one_wide, two_wide, 0, slice(fc, 2 * fc))(0, DD).astype(HALF)
+        head_own[...] = total(wide, one_wide, two_wide, 0, slice(fc, 2 * fc))(0, DD)
         head_swap.start()
         top_own.start()
         whole = slice(0, DD)
@@ -1729,8 +1719,8 @@
     scratch = [(one, FLOAT) for one in flat + [(TEN_LANES, LANES), (REP_LANES, LANES), (5, 384, LANES)]] + [
         ((704, D // 2), HALF),
         ((D // 2, DD), HALF),
-        ((DD, PATCH // 2), HALF),
-        ((DD, PATCH // 2), HALF),
+        ((DD, PATCH // 2), FLOAT),
+        ((DD, PATCH // 2), FLOAT),
         ((8, 8, LANES), FLOAT),
     ]
     out = pl.pallas_call(
@@ -1756,7 +1746,7 @@
     picked, wide, tall, qkv_grad, small, loss,
     normed, tokens, q_ref, k_ref, v_ref, parts, parts_got, grad_att, vec_grad, vec_got, head_b_grad,
     blended, blend_other, totals, upward, activated, second, final_low, pred_low, low, grad_up_in, mid, grad_blend,
-    blend_sent, wide_sent, wide_got, tall_sent, tall_got, dk_ref, dv_ref, send_sem, recv_sem,
+    blend_sent, head_sent, head_got, wide_sent, wide_got, tall_sent, tall_got, dk_ref, dv_ref, send_sem, recv_sem,
 ):
     g, z, x = lax.axis_index("group"), lax.axis_index("dp"), lax.axis_index("tensor")
     across = (g, z, 1 - x)
@@ -1870,8 +1860,10 @@
         grad_swaps[-1].start()
     mine = pl.ds(pl.multiple_of(x * fc, LANES), fc)
     theirs = pl.ds(pl.multiple_of((1 - x) * fc, LANES), fc)
-    wide_sent[:, :fc] = mm_tn(second[...], grad_up_in[:, fc:]).astype(HALF)
-    wide_sent[:, fc:] = mm_tn(final_low[...], pred_low[:, theirs]).astype(HALF)
+    head_sent[...] = mm_tn(final_low[...], pred_low[:, theirs])
+    head_swap = links.copy(12, head_sent, head_got, across)
+    head_swap.start()
+    wide_sent[...] = mm_tn(second[...], grad_up_in[:, fc:]).astype(HALF)
     wide_swap = links.copy(3, wide_sent, wide_got, across)
     wide_swap.start()
     tall_sent[:fc] = mm_tn(activated[:, fc:], low[...]).astype(HALF)
@@ -1931,8 +1923,10 @@
     product = mm_tn(normed[...], parts[...])
     for third in range(3):
         qkv_grad[:, third * width : (third + 1) * width] = product[:, 256 * third : 256 * third + width]
+    head_swap.wait_recv()
+    wide[:, fc:] += head_got[...]
     wide_swap.wait_recv()
-    wide[...] += wide_got[...].astype(FLOAT)
+    wide[:, :fc] += wide_got[...].astype(FLOAT)
     tall_swap.wait_recv()
     tall[...] += tall_got[...].astype(FLOAT)
     for one in part_swaps:
@@ -1952,7 +1946,7 @@
     picked[...] = mm_tn(hot[own_rows_], grad.astype(HALF)).astype(HALF)
     vec_swap.wait_recv()
     small[...] = vec_grad[...] + vec_got[...]
-    for one in [blend_swap, wide_swap, tall_swap, vec_swap] + grad_swaps + part_swaps:
+    for one in [blend_swap, head_swap, wide_swap, tall_swap, vec_swap] + grad_swaps + part_swaps:
         one.wait_send()
 
 
@@ -1993,8 +1987,10 @@
         ((count, DD), HALF),
         ((rows, width), HALF),
         ((count, width), HALF),
-        ((DD, DFF // 2 + PATCH // 2), HALF),
-        ((DD, DFF // 2 + PATCH // 2), HALF),
+        ((DD, PATCH // 2), FLOAT),
+        ((DD, PATCH // 2), FLOAT),
+        ((DD, DFF // 2), HALF),
+        ((DD, DFF // 2), HALF),
         ((DFF // 2 + width, DD), HALF),
         ((DFF // 2 + width, DD), HALF),
         ((rows, HDIM), FLOAT),
@@ -2007,7 +2003,7 @@
         in_specs=[vmem] * 17,
         out_specs=[vmem] * len(shapes),
         scratch_shapes=[pltpu.VMEM(*one) for one in scratch]
-        + [pltpu.SemaphoreType.DMA((12,)), pltpu.SemaphoreType.DMA((12,))],
+        + [pltpu.SemaphoreType.DMA((13,)), pltpu.SemaphoreType.DMA((13,))],
         compiler_params=pltpu.CompilerParams(
             collective_id=number, has_side_effects=True, vmem_limit_bytes=60 << 20
         ),
@@ -2098,7 +2094,8 @@
             hop_both(normed, (HOST, 0)),
             hop_both(activated, (HOST, 2)),
         )
-        pixels_low = lax.dynamic_slice_in_dim(patches[s, 0, 0], side * half_rows, half_rows, 0)
+        pixels_low = lax.dynamic_slice(patches, (s, 0, 0, side * half_rows, 0), (1, 1, 1, half_rows, PATCH))
+        pixels_low = pixels_low.reshape(half_rows, PATCH)
         picked, wide, tall, qkv_grad, small, loss = decoder_round(
             9 + s,
             reduced_clip,

time: 1110 us -> 1130 us (1.018)
  Pallas kernels: 923 us -> 955 us
    pallas_call x2, Pallas kernels: 264 us -> 288 us  [decoder_round(): pl.pallas_call(decoder_kernel, name='decoder', out_shape=[jax.ShapeDtypeS...]
    pallas_call x2, Pallas kernels: 141 us -> 154 us  [update(): pl.pallas_call(functools.partial(update_kernel, number, last), name='upda...]
  transfers between devices with their start and end apart: 18 -> 18, of which waited for: 3 -> 3; matrix products, arithmetic and copies ran while one was open for 7% -> 6% of each run, Pallas kernels for 36% -> 37%
where the time goes in v7:
time: 1130 us; the launch traced here: 1120 us
  Pallas kernels  955 us (85%)
  other arithmetic  63.5 us (6%)
  waiting for transfers between devices  30.1 us (3%)
  local copies, waits for them, and re-layouts  28.3 us (3%)
  starting transfers between devices  24 us (2%)
  matrix products  12.4 us (1%)
    pallas_call x2, Pallas kernels, decoder_round(): pl.pallas_call(decoder_kernel, name='decoder', out_shape=[jax.ShapeDtypeS...  288 us
    pallas_call x2, Pallas kernels, encoder_forward(): pl.pallas_call(functools.partial(forward_kernel, shared), name='encoder_f...  281 us
    pallas_call x2, Pallas kernels, encoder_backward(): pl.pallas_call(encoder_backward_kernel, name='encoder_backward', out_shap...  225 us
    pallas_call x2, Pallas kernels, update(): pl.pallas_call(functools.partial(update_kernel, number, last), name='upda...  154 us
    ppermute x2, waiting for transfers between devices, group_mean(): far = lax.ppermute(part_low, 'group', [(g, g ^ 2) for g in range(4)])  29.3 us
  transfers between devices with their start and end apart: 18, of which 3 were waited for; matrix products, arithmetic and copies ran while one was open for 6% of the time, Pallas kernels for 37%

profile of v7, /device:TPU:0, one launch (start us, length us, event | category | flops | bytes accessed | tf_op | source)
XLA Modules:
  0.0 1117.6 jit_solution(15532206175919813541)
XLA Ops:
  1.4 6.2 fusion.10
  7.6 1.5 collective-permute-start.1
  9.1 5.8 collective-permute-start
  15.5 1.3 collective-permute-start.2
  16.8 6.2 fusion.11
  23.0 1.5 collective-permute-start.8
  27.7 1.6 fusion.73
  29.3 1.8 compare_reduce_fusion.1
  33.6 5.1 dynamic-slice_bitcast_fusion
  38.7 1.7 maximum_select_fusion.places
  41.5 1.9 fusion.71
  45.6 7.4 lay_out.1
  53.0 2.1 collective-permute-start.7
  59.1 1.7 collective-permute-start.4
  60.8 119.6 %encoder_forward.2 = (bf16[768,1152]{1,0:T(8,128)(2,1)}, bf16[384,768]{1,0:T(8,128)(2,1)}, bf16[768,1536]{1,0:T(8,128)(2,1)}, bf16[1536,768]{1,0:T(8,128)(2,1)},...) custom-call(bf16[768,1152]{1,0:T(8,128)(2,1)} %get-tuple-element.147, ...), custom_call_target="tpu_custom_call" | custom-call | tf_op jit(solution)/shard_map/encoder_forward/pallas_call | solution.py:987
  181.4 1.3 broadcast_select_fusion.5
  184.5 1.3 collective-permute-start.5
  186.4 145.8 %decoder.2 = (bf16[160,384]{1,0:T(8,128)(2,1)}, f32[384,1536]{1,0:T(8,128)}, f32[960,384]{1,0:T(8,128)}, f32[384,576]{1,0:T(8,128)}, f32[16,384]{1,0:T(8,128)}, /*index=5*/f32[8,128]{1,0:T(8,128)}) custom-call(f32[160,384]{1,0:T(8,128)} %get-tuple-element.159.reduced, bf16[1568,160]{1,0:T(8,128)(2,1)} %get-tuple-element.305.hot, f32[1568,1]{1,0:T(8,128)} %reshape.394.shown, ...), custom_call_target="tpu_custom_call" | custom-call | tf_op jit(solution)/shard_map/decoder/pallas_call | solution.py:1999
  336.4 2.1 pad_maximum_fusion.2.refs_12_.shown
  338.6 1.3 copy-done.11
  339.9 115.1 %encoder_backward.2 = (bf16[768,1152]{1,0:T(8,128)(2,1)}, bf16[1248,768]{1,0:T(8,128)(2,1)}, bf16[672,1536]{1,0:T(8,128)(2,1)}, bf16[704,384]{1,0:T(8,128)(2,1)}...) custom-call(bf16[160,384]{1,0:T(8,128)(2,1)} %get-tuple-element.173., ...), custom_call_target="tpu_custom_call" | custom-call | tf_op jit(solution)/shard_map/encoder_backward/pallas_call | solution.py:1391
  455.6 78.7 %update.2 = (f32[8,128]{1,0:T(8,128)}, f32[8640,128]{1,0:T(8,128)}, f32[8640,128]{1,0:T(8,128)}, f32[8640,128]{1,0:T(8,128)}, f32[4056,128]{1,0:T(8,128)}, /*ind...) custom-call(f32[8,128]{1,0:T(8,128)} %broadcast_in_dim.116.stats, ...), custom_call_target="tpu_custom_call" | custom-call | tf_op jit(solution)/shard_map/update/pallas_call | solution.py:1726
  534.3 161.6 %encoder_forward.3 = (bf16[768,1152]{1,0:T(8,128)(2,1)}, bf16[384,768]{1,0:T(8,128)(2,1)}, bf16[768,1536]{1,0:T(8,128)(2,1)}, bf16[1536,768]{1,0:T(8,128)(2,1)},...) custom-call(bf16[768,1152]{1,0:T(8,128)(2,1)} %get-tuple-element.208, ...), custom_call_target="tpu_custom_call" | custom-call | tf_op jit(solution)/shard_map/encoder_forward/pallas_call | solution.py:987
  699.0 1.7 collective-permute-start.9
  703.4 1.3 collective-permute-start.10
  704.7 1.3 broadcast_select_fusion.3
  707.2 142.2 %decoder.3 = (bf16[160,384]{1,0:T(8,128)(2,1)}, f32[384,1536]{1,0:T(8,128)}, f32[960,384]{1,0:T(8,128)}, f32[384,576]{1,0:T(8,128)}, f32[16,384]{1,0:T(8,128)}, /*index=5*/f32[8,128]{1,0:T(8,128)}) custom-call(f32[160,384]{1,0:T(8,128)} %get-tuple-element.220.reduced, bf16[1568,160]{1,0:T(8,128)(2,1)} %get-tuple-element.304.hot, f32[1568,1]{1,0:T(8,128)} %reshape.395.shown, ...), custom_call_target="tpu_custom_call" | custom-call | tf_op jit(solution)/shard_map/decoder/pallas_call | solution.py:1999
  850.6 1.3 compare_select_fusion.2
  851.9 1.3 fusion.74
  853.9 1.3 copy-done.10
  855.2 110.1 %encoder_backward.3 = (bf16[768,1152]{1,0:T(8,128)(2,1)}, bf16[1248,768]{1,0:T(8,128)(2,1)}, bf16[672,1536]{1,0:T(8,128)(2,1)}, bf16[704,384]{1,0:T(8,128)(2,1)}...) custom-call(bf16[160,384]{1,0:T(8,128)(2,1)} %get-tuple-element.234., ...), custom_call_target="tpu_custom_call" | custom-call | tf_op jit(solution)/shard_map/encoder_backward/pallas_call | solution.py:1391
  966.0 75.0 %update.3 = (f32[8,128]{1,0:T(8,128)}, f32[8640,128]{1,0:T(8,128)}, f32[8640,128]{1,0:T(8,128)}, f32[8640,128]{1,0:T(8,128)}, f32[4056,128]{1,0:T(8,128)}, /*index=5*/f32[4056,128]{1,0:T(8,128)}, f32[4056,128]{1,0:T(8,128)}) custom-call(f32[8,128]{1,0:T(8,128)} %broadcast_in_dim.122.stats, bf16[768,1152]{1,0:T(8,128)(2,1)} %get-tuple-element.254.qkv, ...), custom_call_target="tpu_custom_call" | custom-call | tf_op jit(solution)/shard_map/update/pallas_call | solution.py:1726
  1041.0 3.8 sub.70
  1047.4 1.4 fusion.75
  1049.5 2.3 broadcast_multiply_fusion
  1051.8 2.2 broadcast_multiply_fusion.1
  1054.3 1.6 collective-permute-start.13
  1055.9 1.4 broadcast_multiply_fusion.2
  1057.3 11.3 %collective-permute-done.13 = bf16[2028,128]{1,0:T(8,128)(2,1)S(1)} collective-permute-done((bf16[2028,128]{1,0:T(8,128)(2,1)S(1)}, bf16[2028,128]{1,0:T(8,128)(2,1)S(1)}, u32[]{:S(2)}, u32[]{:S(2)}) %collective-permute-start.13) | collective-permute-done | bytes 519200 | tf_op jit(solution)/shard_map/ppermute | solution.py:2151
  1069.2 1.6 collective-permute-start.16
  1070.8 1.4 broadcast_multiply_fusion.3
  1072.2 1.9 maximum_bitcast_fusion.3
  1074.1 1.9 maximum_bitcast_fusion.2
  1076.0 1.9 maximum_bitcast_fusion.1
  1078.1 17.9 %collective-permute-done.16 = bf16[4320,128]{1,0:T(8,128)(2,1)S(1)} collective-permute-done((bf16[4320,128]{1,0:T(8,128)(2,1)S(1)}, bf16[4320,128]{1,0:T(8,128)(2,1)S(1)}, u32[]{:S(2)}, u32[]{:S(2)}) %collective-permute-start.16) | collective-permute-done | bytes 1105952 | tf_op jit(solution)/shard_map/ppermute | solution.py:2151
  1096.4 3.5 multiply_subtract_fusion.1
  1101.2 2.6 pad_maximum_fusion
  1103.9 13.3 %multiply_subtract_fusion = (f32[1,1105920]{1,0:T(1,128)}, f32[1,1105920]{1,0:T(1,128)}) fusion(f32[1,1105920]{1,0:T(1,128)S(1)} %bitcast.83, f32[1,1105920]{1,0:T(1,128)S(1)} %bitcast.87, f32[1,1105920]{1,0:T(1,128)S(1)} %bitcast.90), kind=kLoop, calls=%fused_computation.12 | loop fusion | flops 6635520 | bytes 22118400 | tf_op jit(solution)/shard_map/sub | solution.py:2125
  (156 shorter events, 35.8 us)
Async XLA Ops:
  1.4 13.5 %copy-start.17 = (s32[2,1,1,160]{3,2,1,0:T(1,128)S(1)}, s32[2,1,1,160]{3,2,1,0:T(1,128)}, u32[]{:S(2)}) copy-start(s32[2,1,1,160]{3,2,1,0:T(1,128)} %param.13) | copy-start | bytes 3844
  7.6 49.2 %collective-permute-start.1 = (bf16[160,1792]{1,0:T(8,128)(2,1)}, bf16[160,1792]{1,0:T(8,128)(2,1)}, u32[]{:S(2)}, u32[]{:S(2)}) collective-permute-start(bf16[160,1792]{1,0:T(8,128)(2,1)} %fusion.10), channel_id=1, source_target_pairs={{7,3},{15,11},{23,19},{31,27}} | collective-permute-start | bytes 1720328 | tf_op jit(solution)/shard_map/ppermute | solution.py:437
  9.1 48.9 %collective-permute-start = (bf16[160,1792]{1,0:T(8,128)(2,1)}, bf16[160,1792]{1,0:T(8,128)(2,1)}, u32[]{:S(2)}, u32[]{:S(2)}) collective-permute-start(bf16[160,1792]{1,0:T(8,128)(2,1)} %fusion.10), channel_id=1, source_target_pairs={{0,2},{5,3},{8,10},{13,11},{16,18},{21,19},{24,26},{29,27}} | collective-permute-start | bytes 1720328 | tf_op jit(solution)/shard_map/ppermute | solution.py:437
  14.9 38.1 %collective-permute-start.3 = (s32[2,160]{1,0:T(2,128)S(1)}, s32[2,160]{1,0:T(2,128)S(1)}, u32[]{:S(2)}, u32[]{:S(2)}) collective-permute-start(s32[2,160]{1,0:T(2,128)S(1)} %bitcast.119), channel_id=1, source_target_pairs={{7,3},{15,11},{23,19},{31,27}} | collective-permute-start | bytes 3848 | tf_op jit(solution)/shard_map/ppermute | solution.py:437
  15.5 39.6 %collective-permute-start.2 = (s32[2,160]{1,0:T(2,128)S(1)}, s32[2,160]{1,0:T(2,128)S(1)}, u32[]{:S(2)}, u32[]{:S(2)}) collective-permute-start(s32[2,160]{1,0:T(2,128)S(1)} %bitcast.120), channel_id=1, source_target_pairs={{0,2},{5,3},{8,10},{13,11},{16,18},{21,19},{24,26},{29,27}} | collective-permute-start | bytes 3848 | tf_op jit(solution)/shard_map/ppermute | solution.py:437
  23.0 312.3 %collective-permute-start.8 = (bf16[160,1792]{1,0:T(8,128)(2,1)}, bf16[160,1792]{1,0:T(8,128)(2,1)}, u32[]{:S(2)}, u32[]{:S(2)}) collective-permute-start(bf16[160,1792]{1,0:T(8,128)(2,1)} %fusion.11), channel_id=1, source_target_pairs={{7,3},{15,11},{23,19},{31,27}} | collective-permute-start | bytes 1720328 | tf_op jit(solution)/shard_map/ppermute | solution.py:437
  27.7 3.4 copy-start.19
  27.7 5.3 copy-start.20
  33.6 5.1 copy-start.4
  33.6 5.1 copy-start.5
  38.7 1.7 copy-start.12
  53.0 283.5 %collective-permute-start.7 = (bf16[160,1792]{1,0:T(8,128)(2,1)}, bf16[160,1792]{1,0:T(8,128)(2,1)}, u32[]{:S(2)}, u32[]{:S(2)}) collective-permute-start(bf16[160,1792]{1,0:T(8,128)(2,1)} %fusion.11), channel_id=1, source_target_pairs={{0,2},{5,3},{8,10},{13,11},{16,18},{21,19},{24,26},{29,27}} | collective-permute-start | bytes 1720328 | tf_op jit(solution)/shard_map/ppermute | solution.py:437
  59.1 1.7 copy-start.3
  59.1 279.5 %collective-permute-start.4 = (bf16[320,1792]{1,0:T(8,128)(2,1)S(1)}, bf16[320,1792]{1,0:T(8,128)(2,1)}, u32[]{:S(2)}, u32[]{:S(2)}) collective-permute-start(bf16[320,1792]{1,0:T(8,128)(2,1)S(1)} %pad_maximum_fusion.1.refs_12_.shown), channel_id=1, source_target_pairs={{2,3},{3,2},{10,11},{11,10},{18,19},{19,18},{26,27},{27,26}} | collective-permute-start | bytes 3440648 | tf_op jit(solution)/shard_map/ppermute | solution.py:437
  180.4 2.3 copy-start.16
  180.4 158.2 %collective-permute-start.6 = (bf16[640,1536]{1,0:T(8,128)(2,1)}, bf16[640,1536]{1,0:T(8,128)(2,1)S(1)}, u32[]{:S(2)}, u32[]{:S(2)}) collective-permute-start(bf16[640,1536]{1,0:T(8,128)(2,1)} %get-tuple-element.186.activated), channel_id=1, source_target_pairs={{2,4},{3,5},{10,12},{11,13},{18,20},{19,21},{26,28},{27,29}} | collective-permute-start | bytes 5898248 | tf_op jit(solution)/shard_map/ppermute | solution.py:437
  182.7 1.2 copy-start.14
  184.5 154.1 %collective-permute-start.5 = (bf16[640,768]{1,0:T(8,128)(2,1)}, bf16[640,768]{1,0:T(8,128)(2,1)}, u32[]{:S(2)}, u32[]{:S(2)}) collective-permute-start(bf16[640,768]{1,0:T(8,128)(2,1)} %get-tuple-element.180.normed), channel_id=1, source_target_pairs={{2,0},{3,1},{10,8},{11,9},{18,16},{19,17},{26,24},{27,25}} | collective-permute-start | bytes 2949128 | tf_op jit(solution)/shard_map/ppermute | solution.py:437
  186.4 147.0 %copy-start.18 = (pred[16]{0:T(512)(128)(4,1)S(1)}, pred[16]{0:T(512)(128)(4,1)}, u32[]{:S(2)}) copy-start(pred[16]{0:T(512)(128)(4,1)} %constant.142.clone.1) | copy-start | bytes 52
  338.6 1.3 copy-start.11
  534.3 164.7 %copy-start.2 = (bf16[320,1792]{1,0:T(8,128)(2,1)S(1)}, bf16[320,1792]{1,0:T(8,128)(2,1)}, u32[]{:S(2)}) copy-start(bf16[320,1792]{1,0:T(8,128)(2,1)} %pad_maximum_fusion.2.refs_12_.shown) | copy-start | bytes 3440644
  696.0 10.1 copy-start.15
  696.0 157.9 %collective-permute-start.11 = (bf16[640,1536]{1,0:T(8,128)(2,1)}, bf16[640,1536]{1,0:T(8,128)(2,1)S(1)}, u32[]{:S(2)}, u32[]{:S(2)}) collective-permute-start(bf16[640,1536]{1,0:T(8,128)(2,1)} %get-tuple-element.247.activated), channel_id=1, source_target_pairs={{2,4},{3,5},{10,12},{11,13},{18,20},{19,21},{26,28},{27,29}} | collective-permute-start | bytes 5898248 | tf_op jit(solution)/shard_map/ppermute | solution.py:437
  699.0 154.9 %collective-permute-start.9 = (bf16[320,1792]{1,0:T(8,128)(2,1)S(1)}, bf16[320,1792]{1,0:T(8,128)(2,1)}, u32[]{:S(2)}, u32[]{:S(2)}) collective-permute-start(bf16[320,1792]{1,0:T(8,128)(2,1)S(1)} %copy-done.2), channel_id=1, source_target_pairs={{2,3},{3,2},{10,11},{11,10},{18,19},{19,18},{26,27},{27,26}} | collective-permute-start | bytes 3440648 | tf_op jit(solution)/shard_map/ppermute | solution.py:437
  703.4 150.5 %collective-permute-start.10 = (bf16[640,768]{1,0:T(8,128)(2,1)}, bf16[640,768]{1,0:T(8,128)(2,1)}, u32[]{:S(2)}, u32[]{:S(2)}) collective-permute-start(bf16[640,768]{1,0:T(8,128)(2,1)} %get-tuple-element.241.normed), channel_id=1, source_target_pairs={{2,0},{3,1},{10,8},{11,9},{18,16},{19,17},{26,24},{27,25}} | collective-permute-start | bytes 2949128 | tf_op jit(solution)/shard_map/ppermute | solution.py:437
  707.2 146.0 %copy-start.13 = (bf16[16,768]{1,0:T(8,128)(2,1)S(1)}, bf16[16,768]{1,0:T(8,128)(2,1)}, u32[]{:S(2)}) copy-start(bf16[16,768]{1,0:T(8,128)(2,1)} %get-tuple-element.232) | copy-start | bytes 73732
  853.9 1.3 copy-start.10
  1044.8 1.6 copy-start
  1044.8 2.2 copy-start.9
  1045.1 23.8 %collective-permute-start.15 = (f32[4320,128]{1,0:T(8,128)S(1)}, f32[4320,128]{1,0:T(8,128)S(1)}, u32[]{:S(2)}, u32[]{:S(2)}) collective-permute-start(f32[4320,128]{1,0:T(8,128)S(1)} %slice_select_fusion), channel_id=1, source_target_pairs={{0,8},{8,0},{16,24},{24,16},{1,9},{9,1},{17,25},{25,17},{2,10},{10... | collective-permute-start | bytes 6635528 | tf_op jit(solution)/shard_map/ppermute | solution.py:452
  1045.1 4.3 slice-start.6
  1047.0 2.5 slice-start.7
  1047.2 4.5 slice-start.4
  1047.4 6.7 collective-permute-start.12
  1049.5 2.3 slice-start.5
  1054.0 1.8 copy-start.8
  1054.3 14.4 %collective-permute-start.13 = (bf16[2028,128]{1,0:T(8,128)(2,1)S(1)}, bf16[2028,128]{1,0:T(8,128)(2,1)S(1)}, u32[]{:S(2)}, u32[]{:S(2)}) collective-permute-start(bf16[2028,128]{1,0:T(8,128)(2,1)S(1)} %add_convert_fusion.1), channel_id=1, source_target_pairs={{0,16},{8,24},{16,0},{24,8},{1,17},{9,25},{17,1},{25,9},{2,18},{10... | collective-permute-start | bytes 1557512 | tf_op jit(solution)/shard_map/ppermute | solution.py:2151
  1068.8 2.0 copy-start.7
  1068.8 9.1 collective-permute-start.14
  1069.2 26.8 %collective-permute-start.16 = (bf16[4320,128]{1,0:T(8,128)(2,1)S(1)}, bf16[4320,128]{1,0:T(8,128)(2,1)S(1)}, u32[]{:S(2)}, u32[]{:S(2)}) collective-permute-start(bf16[4320,128]{1,0:T(8,128)(2,1)S(1)} %add_convert_fusion), channel_id=1, source_target_pairs={{0,16},{8,24},{16,0},{24,8},{1,17},{9,25},{17,1},{25,9},{2,18},{10... | collective-permute-start | bytes 3317768 | tf_op jit(solution)/shard_map/ppermute | solution.py:2151
  1078.1 18.3 %copy-start.6 = (f32[519168]{0:T(1024)S(1)}, f32[519168]{0:T(1024)}, u32[]{:S(2)}) copy-start(f32[519168]{0:T(1024)} %param.22) | copy-start | bytes 6230020
  1096.3 4.4 collective-permute-start.17
  1096.4 7.4 slice-start.2
  1099.9 3.9 slice-start.3
  1100.7 3.1 slice-start
  1101.2 2.7 slice-start.1
  1103.8 13.4 %copy-start.1 = (f32[8640,128]{1,0:T(8,128)}, f32[8640,128]{1,0:T(8,128)S(1)}, u32[]{:S(2)}) copy-start(f32[8640,128]{1,0:T(8,128)S(1)} %pad_maximum_fusion) | copy-start | bytes 13271044
